TPU v7x, 32 devices: a whole 2x2x4 slice. The times are simulated.
32 devices in a mesh: node: 8 (over z, y), feat: 4 (over x, core).
Axes of the slice: x: 2, y: 2, z: 4, core: 2. Of those that a mesh axis runs over, the one named last changes fastest.
Arguments:
- features: bfloat16 [4096, 128], P('node', 'feat'), may hold values from -10 to 10
- send_rows: int32 [8, 8, 64], P('node'), may hold values from 0 to 511
- send_count: int32 [8, 8], P('node'), may hold values from 1 to 64, 256 in all within a row
- tile_src: int32 [32, 16], P('node'), may hold values from 0 to 7
- tile_val: bfloat16 [32, 16, 128, 128], P('node'), may hold values from 0 to 0.0009765625
- labels: int32 [4096], P('node'), may hold values from 0 to 171
- w_self1: bfloat16 [128, 1024], P('feat'), may hold values from -0.5 to 0.5
- w_neigh1: bfloat16 [128, 1024], P('feat'), may hold values from -0.5 to 0.5
- w_self2: bfloat16 [1024, 172], P('feat'), may hold values from -0.5 to 0.5
- w_neigh2: bfloat16 [1024, 172], P('feat'), may hold values from -0.1875 to 0.1875
Outputs:
- mean_loss: float32 [], replicated
- grad_self1: float32 [128, 1024], P('feat')
- grad_neigh1: float32 [128, 1024], P('feat')
- grad_self2: float32 [1024, 172], P('feat')
- grad_neigh2: float32 [1024, 172], P('feat')
Inputs may be any that keep to these rules, and one draw needn't show every extreme that they name: `send_rows`: row indices within the sending partition's 512 rows. Each row of send_count sums to 256 and holds 64 at least once. `tile_src`: block numbers of the destination partition's source rows: numbers below 4 name its own rows, the others its halo slots.
All inputs are finite; a program needn't handle non-finite values.
Results may differ from a plain program's by a relative error of at most 0.00095.
The roundings to bfloat16 on the way count: a program that leaves them out, or rounds other values in their place, can miss the bound.
Values may be sent and summed in bfloat16 or wider, within the bound.
No kernel may reach another device: no remote copies, remote signals or barrier semaphores. Data moves between devices by JAX's collectives and lax.ppermute only.
A program may use at most 64 MiB of HBM per device.

v0:
```python
import math

import jax
import jax.numpy as jnp
from jax import lax
from jax.sharding import PartitionSpec as P


def pack_rows(own_rows, send_rows, send_count):
    slot_total = send_rows.shape[2]
    picked = jnp.take(own_rows, send_rows[0].reshape(-1), axis=0)
    picked = picked.reshape(send_rows.shape[1], slot_total, own_rows.shape[1])
    in_use = jnp.arange(slot_total, dtype=jnp.int32)[None, :] < send_count[0][:, None]
    return jnp.where(in_use[:, :, None], picked, jnp.zeros_like(picked))


def aggregate(own_rows, arrived, tile_src, tile_val):
    col_count = own_rows.shape[1]
    blocks = jnp.concatenate([own_rows, arrived], axis=0).reshape(-1, 128, col_count)
    chosen = jnp.take(blocks, tile_src, axis=0)
    summed = jnp.einsum("bkij,bkjh->bih", tile_val, chosen, preferred_element_type=jnp.float32)
    return summed.reshape(own_rows.shape[0], col_count).astype(jnp.bfloat16)


def spread_back(grads, tile_src, tile_val, src_total):
    col_count = grads.shape[1]
    per_tile = jnp.einsum(
        "bkij,bih->bkjh",
        tile_val,
        grads.reshape(-1, 128, col_count),
        preferred_element_type=jnp.float32,
    )
    one_hot = (
        tile_src.reshape(-1)[None, :] == jnp.arange(src_total // 128, dtype=jnp.int32)[:, None]
    ).astype(jnp.float32)
    landed = jnp.dot(
        one_hot,
        per_tile.reshape(one_hot.shape[1], -1),
        precision=lax.Precision.HIGHEST,
        preferred_element_type=jnp.float32,
    )
    return landed.reshape(src_total, col_count)


def cross_entropy(logits, labels, grad_scale):
    row_max = jnp.max(logits, axis=1, keepdims=True)
    shifted = logits - row_max
    total_exp = jnp.sum(jnp.exp(shifted), axis=1, keepdims=True)
    classes = jnp.arange(logits.shape[1], dtype=jnp.int32)
    target = (labels[:, None] == classes[None, :]).astype(jnp.float32)
    row_loss = jnp.log(total_exp)[:, 0] - jnp.sum(shifted * target, axis=1)
    grads = ((jnp.exp(shifted) / total_exp - target) * grad_scale).astype(jnp.bfloat16)
    return (row_loss, grads)


def shards(
    features,
    send_rows,
    send_count,
    tile_src,
    tile_val,
    labels,
    w_self1,
    w_neigh1,
    w_self2,
    w_neigh2,
):
    node_count = lax.axis_size("node")
    own_count = features.shape[0]
    slot_total = send_rows.shape[2]
    src_total = own_count + node_count * slot_total
    node_total = own_count * node_count
    grad_scale = 1.0 / math.sqrt(node_total)
    outgoing = pack_rows(features, send_rows, send_count)
    arrived = lax.all_to_all(outgoing, "node", split_axis=0, concat_axis=0, tiled=True).reshape(
        -1, features.shape[1]
    )
    agg_one = aggregate(features, arrived, tile_src, tile_val)
    partial_one = jnp.dot(features, w_self1, preferred_element_type=jnp.float32)
    partial_one = partial_one + jnp.dot(agg_one, w_neigh1, preferred_element_type=jnp.float32)
    pre_act = lax.psum_scatter(partial_one, "feat", scatter_dimension=1, tiled=True)
    activated, pullback = jax.vjp(lambda inner: jax.nn.gelu(inner, approximate=True), pre_act)
    hidden = activated.astype(jnp.bfloat16)
    unit_count = hidden.shape[1]
    outgoing_two = pack_rows(hidden, send_rows, send_count)
    arrived_two = lax.all_to_all(
        outgoing_two, "node", split_axis=0, concat_axis=0, tiled=True
    ).reshape(-1, unit_count)
    agg_two = aggregate(hidden, arrived_two, tile_src, tile_val)
    partial_two = jnp.dot(hidden, w_self2, preferred_element_type=jnp.float32)
    partial_two = partial_two + jnp.dot(agg_two, w_neigh2, preferred_element_type=jnp.float32)
    logits = lax.psum(partial_two, "feat")
    row_loss, dlogits = cross_entropy(logits, labels, grad_scale)
    mean_loss = lax.psum(jnp.sum(row_loss), "node") / node_total
    grad_pair = lax.psum(
        (
            jnp.einsum("nh,nc->hc", hidden, dlogits, preferred_element_type=jnp.float32),
            jnp.einsum("nh,nc->hc", agg_two, dlogits, preferred_element_type=jnp.float32),
        ),
        "node",
    )
    back_grad = jnp.einsum(
        "nc,hc->nh", dlogits, w_neigh2, preferred_element_type=jnp.float32
    ).astype(jnp.bfloat16)
    direct = jnp.einsum("nc,hc->nh", dlogits, w_self2, preferred_element_type=jnp.float32)
    landed = spread_back(back_grad, tile_src, tile_val, src_total)
    halo_back = landed[own_count:].reshape(node_count, slot_total, unit_count)
    returned = lax.all_to_all(
        halo_back.astype(jnp.bfloat16), "node", split_axis=0, concat_axis=0, tiled=True
    ).astype(halo_back.dtype)
    in_use = jnp.arange(slot_total, dtype=jnp.int32)[None, :] < send_count[0][:, None]
    returned = jnp.where(in_use[:, :, None], returned, jnp.zeros_like(returned))
    back_rows = jax.ops.segment_sum(
        returned.reshape(-1, unit_count), send_rows[0].reshape(-1), num_segments=own_count
    )
    back_hidden = direct + landed[:own_count] + back_rows
    pre_grad = pullback(back_hidden)[0].astype(jnp.bfloat16)
    shard_piece = lax.all_gather(pre_grad, "feat", axis=1, tiled=True)
    local_grads = jnp.stack(
        [
            jnp.einsum("nf,nh->fh", features, shard_piece, preferred_element_type=jnp.float32),
            jnp.einsum("nf,nh->fh", agg_one, shard_piece, preferred_element_type=jnp.float32),
        ]
    )
    summed = lax.psum(local_grads, "node")
    return (mean_loss, summed[0], summed[1], grad_pair[0], grad_pair[1])


def solution(mesh):
    in_specs = (
        P("node", "feat"),
        P("node", None, None),
        P("node", None),
        P("node", None),
        P("node", None, None, None),
        P("node"),
        P("feat", None),
        P("feat", None),
        P("feat", None),
        P("feat", None),
    )
    out_specs = (P(), P("feat", None), P("feat", None), P("feat", None), P("feat", None))
    return jax.shard_map(shards, mesh=mesh, in_specs=in_specs, out_specs=out_specs, check_vma=False)
```

profile of v0, /device:TPU:0, one launch (start us, length us, event | category | flops | bytes accessed | tf_op | source)
XLA Modules:
  0.0 273.8 jit_solution(4689654777917767811)
XLA Ops:
  12.0 7.3 %all-to-all-start = ((bf16[8,2,1024]{2,1,0:T(2,128)(2,1)}), bf16[8,2,1024]{2,1,0:T(2,128)(2,1)S(1)}, u32[]{:S(2)}, u32[]{:S(2)}) async-start(bf16[8,2,1024]{2,1,0:T(2,128)(2,1)} %reshape.178), calls=%async_computation | async-start | bytes 65536 | tf_op jit(solution)/shard_map/all_to_all | solution.py:75
  20.8 2.6 fusion.31
  23.4 2.5 all-to-all-done
  28.5 1.8 convolution_add_fusion
  30.3 30.4 %reduce-scatter.2.cloned.1.call-done = f32[512,256]{1,0:T(8,128)} async-done(((f32[512,1024]{1,0:T(8,128)}), f32[512,256]{1,0:T(8,128)}) %reduce-scatter.2.cloned.1.call-update) | async-done | bytes 524304 | tf_op jit(solution)/shard_map/reduce_scatter | solution.py:81
  61.9 2.0 gather_fusion.2
  64.8 5.5 %all-to-all-start.1 = ((bf16[8,64,256]{2,1,0:T(8,128)(2,1)}), bf16[8,64,256]{2,1,0:T(8,128)(2,1)S(1)}, u32[]{:S(2)}, u32[]{:S(2)}) async-start(bf16[8,64,256]{2,1,0:T(8,128)(2,1)} %select_select_fusion), calls=%async_computation.2 | async-start | bytes 524288 | tf_op jit(solution)/shard_map/all_to_all | solution.py:86
  70.8 8.4 %all-to-all-done.1 = bf16[8,64,256]{2,1,0:T(8,128)(2,1)S(1)} async-done(((bf16[8,64,256]{2,1,0:T(8,128)(2,1)}), bf16[8,64,256]{2,1,0:T(8,128)(2,1)S(1)}, u32[]{:S(2)}, u32[]{:S(2)}) %all-to-all-start.1) | async-done | bytes 262176 | tf_op jit(solution)/shard_map/all_to_all | solution.py:86
  79.3 2.8 %gather_fusion.3 = bf16[64,128,256]{2,1,0:T(8,128)(2,1)} fusion(bf16[8,128,256]{2,1,0:T(8,128)(2,1)S(1)} %bitcast.89, s32[1024]{0:T(1024)S(1)} %pad_clamp_fusion), kind=kCustom, calls=%fused_computation.3 | custom fusion | bytes 8388864 | tf_op jit(solution)/shard_map/jit(_take)/gather | solution.py:20
  82.0 3.2 %fusion.7 = bf16[4,256,128]{1,2,0:T(8,128)(2,1)S(1)} fusion(bf16[4,16,128,128]{3,2,1,0:T(8,128)(2,1)S(1)} %copy-done, bf16[4,16,128,256]{3,2,1,0:T(8,128)(2,1)} %bitcast.93, pred[4,16]{1,0:T(4,128)(4,1)S(1)} %compare_and_fusion.1), kind=kOutput, calls=%fused_computation.13 | convolution fusion | flops 539099136 | bytes 6553664 | tf_op jit(solution)/shard_map/bkij,bkjh->bih/dot_general | solution.py:21
  86.4 30.6 %all-reduce.4.cloned.1.call-done = f32[512,172]{0,1:T(8,128)} async-done(((f32[512,172]{0,1:T(8,128)}), f32[512,172]{0,1:T(8,128)}) %all-reduce.4.cloned.1.call-update) | async-done | bytes 352272 | tf_op jit(solution)/shard_map/psum | solution.py:92
  120.5 4.5 %convolution_bitcast_fusion = f32[4,16,128,256]{2,3,1,0:T(8,128)} fusion(bf16[4,128,256,1]{2,1,3,0:T(8,128)(2,1)S(1)} %bitcast.95, bf16[4,16,128,128]{3,2,1,0:T(8,128)(2,1)S(1)} %copy-done), kind=kOutput, calls=%fused_computation.8 | convolution fusion | flops 536870912 | bytes 10747904 | tf_op jit(solution)/shard_map/bkij,bih->bkjh/dot_general | solution.py:27
  125.0 8.7 %copy.42 = f32[4,16,128,256]{3,2,1,0:T(8,128)} copy(f32[4,16,128,256]{2,3,1,0:T(8,128)} %convolution_bitcast_fusion) | data formatting | bytes 16777216 | tf_op jit(solution)/shard_map/bkij,bih->bkjh/dot_general | solution.py:27
  133.7 8.1 %copy.50 = f32[8,8,128,256]{3,1,2,0:T(8,128)S(1)} copy(f32[8,8,128,256]{3,2,1,0:T(8,128)} %bitcast.91) | data formatting | bytes 16777216
  141.8 2.9 %fusion.26 = f32[8,32768]{1,0:T(8,128)S(1)} fusion(f32[64,32768]{1,0:T(8,128)S(1)} %bitcast.90, s32[64]{0:T(128)S(1)} %eq.31), kind=kOutput, calls=%fused_computation.59 | convolution fusion | flops 201327104 | bytes 9437440 | tf_op jit(solution)/shard_map/dot_general | solution.py:36
  146.7 5.5 %all-to-all-start.2 = ((bf16[8,64,256]{2,1,0:T(8,128)(2,1)}), bf16[8,64,256]{2,1,0:T(8,128)(2,1)S(1)}, u32[]{:S(2)}, u32[]{:S(2)}) async-start(bf16[8,64,256]{2,1,0:T(8,128)(2,1)} %convert_element_type.51), calls=%async_computation.3 | async-start | bytes 524288 | tf_op jit(solution)/shard_map/all_to_all | solution.py:108
  155.1 5.4 %all-to-all-done.2 = bf16[8,64,256]{2,1,0:T(8,128)(2,1)S(1)} async-done(((bf16[8,64,256]{2,1,0:T(8,128)(2,1)}), bf16[8,64,256]{2,1,0:T(8,128)(2,1)S(1)}, u32[]{:S(2)}, u32[]{:S(2)}) %all-to-all-start.2) | async-done | bytes 262176 | tf_op jit(solution)/shard_map/all_to_all | solution.py:108
  161.4 4.0 %scatter_fusion = f32[512,256]{1,0:T(8,128)S(1)} fusion(f32[512,256]{1,0:T(8,128)S(1)} %convolution_add_fusion.1, s32[512]{0:T(512)S(1)} %reshape.164, f32[512,256]{1,0:T(8,128)} %bitcast.94), kind=kCustom, calls=%fused_computation.4 | custom fusion | flops 131072 | bytes 1574912 | tf_op jit(solution)/shard_map/scatter-add | solution.py:113
  165.4 2.1 fusion.18
  169.4 13.4 %all-gather.2.cloned.1.call-done = bf16[512,1024]{1,0:T(8,128)(2,1)} async-done(((bf16[512,256]{1,0:T(8,128)(2,1)}), bf16[512,1024]{1,0:T(8,128)(2,1)}) %all-gather.2.cloned.1.call-update) | async-done | bytes 1048592 | tf_op jit(solution)/shard_map/all_gather | solution.py:118
  187.2 22.1 %psum.36 = f32[]{:T(128)} all-reduce(f32[]{:T(128)} %subtract_reduce_fusion), channel_id=1, replica_groups=mesh['node'=8,'feat'=4] {'node'}, use_global_device_ids=true, to_apply=%region_6.7 | all-reduce | flops 1 | bytes 8 | tf_op jit(solution)/shard_map/psum | solution.py:94
  210.0 51.3 %all-reduce.6.cloned.1.call-done = (f32[2,32,1024]{2,1,0:T(8,128)}, f32[256,172]{0,1:T(8,128)}, f32[256,172]{0,1:T(8,128)}) async-done(((f32[2,32,1024]{2,1,0:T(8,128)}, f32[256,172]{0,1:T(8,128)}, f32[256,172]{0,1:T(8,128)}), (f32[2,32,1024]{2,1,0:T(8,128)}, f32[256,172]{0,1:T(8,128)}, f32[256,172]{0,1:T(8,128)})) %all-reduce.6.cloned.1.call-update) | async-done | bytes 614416 | tf_op jit(solution)/shard_map/psum | solution.py:125
  261.2 1.7 slice_bitcast_fusion
  262.9 1.6 copy.65
  (82 shorter events, 29.5 us)
Async XLA Ops:
  7.2 19.8 %copy-start = (bf16[4,16,128,128]{3,2,1,0:T(8,128)(2,1)S(1)}, bf16[4,16,128,128]{3,2,1,0:T(8,128)(2,1)}, u32[]{:S(2)}) copy-start(bf16[4,16,128,128]{3,2,1,0:T(8,128)(2,1)} %param.14) | copy-start | bytes 6291460
  9.8 16.5 %copy-start.5 = (bf16[512,32]{0,1:T(8,128)(2,1)S(1)}, bf16[512,32]{0,1:T(8,128)(2,1)}, u32[]{:S(2)}) copy-start(bf16[512,32]{0,1:T(8,128)(2,1)} %param.10) | copy-start | bytes 98308
  12.0 14.0 %all-to-all-start = ((bf16[8,2,1024]{2,1,0:T(2,128)(2,1)}), bf16[8,2,1024]{2,1,0:T(2,128)(2,1)S(1)}, u32[]{:S(2)}, u32[]{:S(2)}) async-start(bf16[8,2,1024]{2,1,0:T(2,128)(2,1)} %reshape.178), calls=%async_computation | async-start | bytes 65536 | tf_op jit(solution)/shard_map/all_to_all | solution.py:75
  19.3 41.5 %reduce-scatter.2.cloned.1.call-start = ((), (), s32[]{:S(2)}) async-start(), calls=%async_computation.4 | async-start | bytes 2621440 | tf_op jit(solution)/shard_map/reduce_scatter | solution.py:81
  26.9 1.6 copy-start.1
  26.9 1.6 copy-start.11
  28.5 1.8 copy-start.9
  30.3 40.2 %copy-start.7 = (bf16[256,172]{0,1:T(8,128)(2,1)S(1)}, bf16[256,172]{0,1:T(8,128)(2,1)}, u32[]{:S(2)}) copy-start(bf16[256,172]{0,1:T(8,128)(2,1)} %param.18) | copy-start | bytes 264196
  64.8 14.4 %all-to-all-start.1 = ((bf16[8,64,256]{2,1,0:T(8,128)(2,1)}), bf16[8,64,256]{2,1,0:T(8,128)(2,1)S(1)}, u32[]{:S(2)}, u32[]{:S(2)}) async-start(bf16[8,64,256]{2,1,0:T(8,128)(2,1)} %select_select_fusion), calls=%async_computation.2 | async-start | bytes 524288 | tf_op jit(solution)/shard_map/all_to_all | solution.py:86
  70.3 46.7 %all-reduce.4.cloned.1.call-start = ((), (), s32[]{:S(2)}) async-start(), calls=%async_computation.5 | async-start | bytes 720896 | tf_op jit(solution)/shard_map/psum | solution.py:92
  82.0 3.2 %copy-start.6 = (bf16[256,172]{0,1:T(8,128)(2,1)S(1)}, bf16[256,172]{0,1:T(8,128)(2,1)}, u32[]{:S(2)}) copy-start(bf16[256,172]{0,1:T(8,128)(2,1)} %param.19) | copy-start | bytes 264196
  82.0 4.3 %copy-start.13 = (s32[4,16]{1,0:T(4,128)S(1)}, s32[4,16]{1,0:T(4,128)}, u32[]{:S(2)}) copy-start(s32[4,16]{1,0:T(4,128)} %param.13) | copy-start | bytes 772
  82.0 36.0 %copy-start.14 = (s32[512]{0:T(512)S(1)}, s32[512]{0:T(512)}, u32[]{:S(2)}) copy-start(s32[512]{0:T(512)} %param.15) | copy-start | bytes 6148
  85.3 33.9 %copy-start.3 = (bf16[4,256,128]{1,2,0:T(8,128)(2,1)}, bf16[4,256,128]{1,2,0:T(8,128)(2,1)S(1)}, u32[]{:S(2)}) copy-start(bf16[4,256,128]{1,2,0:T(8,128)(2,1)S(1)} %fusion.7) | copy-start | bytes 786436
  141.8 10.7 %copy-start.12 = (s32[1,8,64]{2,1,0:T(8,128)S(1)}, s32[1,8,64]{2,1,0:T(8,128)}, u32[]{:S(2)}) copy-start(s32[1,8,64]{2,1,0:T(8,128)} %param.11) | copy-start | bytes 6148
  144.7 1.0 copy-start.2
  145.7 8.1 %copy-start.8 = (bf16[256,172]{0,1:T(8,128)(2,1)S(1)}, bf16[256,172]{0,1:T(8,128)(2,1)}, u32[]{:S(2)}) copy-start(bf16[256,172]{0,1:T(8,128)(2,1)} %param.18) | copy-start | bytes 264196
  145.8 6.8 %slice-start = ((f32[8,32768]{1,0:T(8,128)}), f32[4,32768]{1,0:T(4,128)S(1)}, s32[]{:S(2)}) async-start(f32[8,32768]{1,0:T(8,128)} %copy-done.2), calls=%async_computation.8 | async-start | bytes 1048576 | tf_op jit(solution)/shard_map/slice | solution.py:116
  146.7 13.7 %all-to-all-start.2 = ((bf16[8,64,256]{2,1,0:T(8,128)(2,1)}), bf16[8,64,256]{2,1,0:T(8,128)(2,1)S(1)}, u32[]{:S(2)}, u32[]{:S(2)}) async-start(bf16[8,64,256]{2,1,0:T(8,128)(2,1)} %convert_element_type.51), calls=%async_computation.3 | async-start | bytes 524288 | tf_op jit(solution)/shard_map/all_to_all | solution.py:108
  152.2 30.6 %all-gather.2.cloned.1.call-start = ((), (), s32[]{:S(2)}) async-start(), calls=%async_computation.6 | async-start | bytes 1310720 | tf_op jit(solution)/shard_map/all_gather | solution.py:118
  161.4 6.2 %copy-start.4 = (bf16[4,256,128]{1,2,0:T(8,128)(2,1)S(1)}, bf16[4,256,128]{1,2,0:T(8,128)(2,1)}, u32[]{:S(2)}) copy-start(bf16[4,256,128]{1,2,0:T(8,128)(2,1)} %copy-done.3) | copy-start | bytes 786436
  165.4 17.4 %copy-start.10 = (bf16[4,4,8,128]{3,2,1,0:T(8,128)(2,1)S(1)}, bf16[4,4,8,128]{3,2,1,0:T(8,128)(2,1)}, u32[]{:S(2)}) copy-start(bf16[4,4,8,128]{3,2,1,0:T(8,128)(2,1)} %copy-done.9) | copy-start | bytes 98308
  167.6 93.7 %all-reduce.6.cloned.1.call-start = ((), (), s32[]{:S(2)}) async-start(), calls=%async_computation.7 | async-start | bytes 1245184 | tf_op jit(solution)/shard_map/psum | solution.py:125
Sparse Core Ops, SparseCore 0:
  30.4 30.2 reduce-scatter.1
  86.4 30.5 all-reduce.3
  167.7 15.0 all-gather.1
  187.4 73.8 all-reduce.5
where the time goes:
time: 275 us; the launch traced here: 274 us
  waiting for transfers between devices  142 us (52%)
  local copies, waits for them, and re-layouts  35.5 us (13%)
  matrix products  23.4 us (9%)
  blocking collectives  22.1 us (8%)
  starting transfers between devices  18.9 us (7%)
  other arithmetic  16 us (6%)
  between operations  15.8 us (6%)
    psum x1, waiting for transfers between devices, shards(): summed = lax.psum(local_grads, 'node')  51.3 us
    psum x1, waiting for transfers between devices, shards(): logits = lax.psum(partial_two, 'feat')  30.6 us
    reduce_scatter x1, waiting for transfers between devices, shards(): lax.psum_scatter(partial_one, 'feat', scatter_dimension=1, tiled=True)  30.4 us
    psum x1, blocking collectives, shards(): mean_loss = lax.psum(jnp.sum(row_loss), 'node') / node_total  22.1 us
    unnamed x36, local copies, waits for them, and re-layouts  14.8 us
    all_gather x1, waiting for transfers between devices, shards(): shard_piece = lax.all_gather(pre_grad, 'feat', axis=1, tiled=True)  13.4 us
    dot_general x1, local copies, waits for them, and re-layouts, spread_back(): jnp.einsum('bkij,bih->bkjh', tile_val, grads.reshape(-1, 128, col_count),...  8.7 us
    all_to_all x1, waiting for transfers between devices, shards(): lax.all_to_all(outgoing_two, 'node', split_axis=0, concat_axis=0, tiled=T...  8.44 us
  transfers between devices with their start and end apart: 7, of which 7 were waited for; matrix products, arithmetic and copies ran while one was open for 3% of the time, Pallas kernels for 0%

commit v1 on v0

v1 whole, which is shorter than its diff:
```python
import functools
import math

import jax
import jax.numpy as jnp
from jax import lax
from jax.experimental import pallas as pl
from jax.experimental.pallas import tpu as pltpu
from jax.sharding import PartitionSpec as P

BLOCK = 128
FEW = 8
F32 = jnp.float32
BF16 = jnp.bfloat16
VMEM = pl.BlockSpec(memory_space=pltpu.VMEM)
SMEM = pl.BlockSpec(memory_space=pltpu.SMEM)


def mm(a, b):
    return lax.dot_general(a, b, (((1,), (0,)), ((), ())), preferred_element_type=F32)


def mm_nt(a, b):
    return lax.dot_general(a, b, (((1,), (1,)), ((), ())), preferred_element_type=F32)


def mm_tn(a, b):
    return lax.dot_general(a, b, (((0,), (0,)), ((), ())), preferred_element_type=F32)


def halves(value):
    high = value.astype(BF16)
    return high, (value - high.astype(F32)).astype(BF16)


def gelu_parts(v):
    inner = math.sqrt(2.0 / math.pi) * (v + 0.044715 * (v * v * v))
    t = jnp.tanh(inner)
    return 0.5 * (1.0 + t), t


def gelu(v):
    return v * gelu_parts(v)[0]


def gelu_slope(v):
    cdf, t = gelu_parts(v)
    inner_slope = math.sqrt(2.0 / math.pi) * (1.0 + 3 * 0.044715 * (v * v))
    return cdf + 0.5 * v * (1.0 - t * t) * inner_slope


def call(body, outs, args, specs, scratch=(), flops=0, moved=0):
    return pl.pallas_call(
        body,
        out_shape=[jax.ShapeDtypeStruct(shape, dtype) for shape, dtype in outs],
        in_specs=specs,
        out_specs=[VMEM] * len(outs),
        scratch_shapes=list(scratch),
        compiler_params=pltpu.CompilerParams(vmem_limit_bytes=56 * 2**20),
        cost_estimate=pl.CostEstimate(flops=flops, bytes_accessed=moved, transcendentals=0),
    )(*args)


def prepare_kernel(tile_src, count, tile_val, send_rows, a_ref, pick_ref, dense):
    blocks, per_block = tile_val.shape[0], tile_val.shape[1]
    own = blocks * BLOCK
    dense[...] = jnp.zeros_like(dense)
    for b in range(blocks):

        def add(k, _, b=b):
            at = pl.ds(pl.multiple_of(tile_src[b, k] * BLOCK, BLOCK), BLOCK)
            rows = pl.ds(b * BLOCK, BLOCK)
            dense[rows, at] = dense[rows, at] + tile_val[b, k].astype(F32)
            return 0

        lax.fori_loop(0, per_block, add, 0)
    for b in range(blocks):
        rows = pl.ds(b * BLOCK, BLOCK)
        high, low = halves(dense[rows, :])
        a_ref[rows, :] = high
        a_ref[pl.ds(own + b * BLOCK, BLOCK), :] = low
    dests, slots = send_rows.shape
    columns = send_rows[...].astype(F32).T
    row_id = lax.broadcasted_iota(jnp.int32, (slots, own), 1).astype(F32)
    slot_id = lax.broadcasted_iota(jnp.int32, (slots, own), 0)
    for d in range(dests):
        hit = (columns[:, d : d + 1] == row_id) & (slot_id < count[0, d])
        pick_ref[pl.ds(d * slots, slots), :] = jnp.where(hit, 1.0, 0.0).astype(BF16)


def spread_out(ids, packed, outs, node_count):
    slots = packed.shape[0] // node_count
    if len(outs) == 1:
        outs[0][...] = packed[...]
        return
    for k, out in enumerate(outs):
        dest = lax.rem(ids[0] + k, node_count)
        out[...] = packed[pl.ds(pl.multiple_of(dest * slots, slots), slots), :]


def bring_in(ids, pieces, landed, node_count):
    slots = landed.shape[0] // node_count
    if len(pieces) == 1:
        landed[...] = pieces[0][...]
        return
    for k, piece in enumerate(pieces):
        source = lax.rem(ids[0] + node_count - k, node_count)
        landed[pl.ds(pl.multiple_of(source * slots, slots), slots), :] = piece[...]


def pack_kernel(node_count, groups, sent, ids, pick, *refs):
    pieces, (full, *outs), (turned, packed) = refs[:groups], refs[groups : groups + 1 + sent], refs[groups + 1 + sent :]
    step = pieces[0].shape[0]
    for k, piece in enumerate(pieces):
        turned[pl.ds(k * step, step), :] = piece[...]
    rows = turned[...].T
    full[...] = rows
    packed[...] = mm(pick[...], rows).astype(BF16)
    spread_out(ids, packed, outs, node_count)


def first_kernel(node_count, sent, ids, pick, a_ref, full, *refs):
    pieces, (agg, source, *outs), (packed,) = refs[:sent], refs[sent : 2 * sent + 2], refs[2 * sent + 2 :]
    own = full.shape[0]
    bring_in(ids, pieces, source, node_count)
    both = mm(a_ref[:, :own], full[...]) + mm(a_ref[:, own:], source[...])
    rounded = (both[:own] + both[own:]).astype(BF16)
    agg[...] = rounded
    packed[...] = mm(pick[...], rounded).astype(BF16)
    spread_out(ids, packed, outs, node_count)


def own_kernel(groups, ids, full, agg, a_ref, turned, *refs):
    selfs, neighs, w_selfs, w_neighs = (refs[i * groups : (i + 1) * groups] for i in range(4))
    w_one, w_two, slope, part, logits, mine, left = refs[4 * groups : 4 * groups + 7]
    (hidden,) = refs[4 * groups + 7 :]
    own, cols = full.shape
    step = selfs[0].shape[0]
    classes, units = w_selfs[0].shape
    w_two[...] = jnp.zeros_like(w_two)
    pad = w_two.shape[0] // 2
    for k in range(groups):
        w_one[pl.ds(k * step, step), :] = selfs[k][...]
        w_one[pl.ds(cols + k * step, step), :] = neighs[k][...]
        group = lax.rem(ids[1] + groups - k, groups)
        at = pl.ds(pl.multiple_of(group * units, units), units)
        w_two[pl.ds(0, classes), at] = w_selfs[k][...]
        w_two[pl.ds(pad, classes), at] = w_neighs[k][...]
    left[pl.ds(0, step), :] = turned[...]
    left[pl.ds(step, step), :] = agg[...].T[:step]
    both = jnp.concatenate([full[...], agg[...]], axis=1)
    total = None
    for j in range(groups):
        at = pl.ds(j * units, units)
        pre = mm(both, w_one[:, at])
        slope[:, at] = gelu_slope(pre)
        out = gelu(pre).astype(BF16)
        hidden[:, at] = out
        spread = mm(a_ref[:, :own], out)
        part[:, at] = spread[:own] + spread[own:]
        term = mm_nt(w_two[:pad, at], out)
        total = term if total is None else total + term
    logits[...] = total
    mine[...] = hidden[:, pl.ds(pl.multiple_of(ids[1] * units, units), units)]


def second_kernel(node_count, groups, sent, class_count, grad_scale, ids, a_ref, source, w_one, w_two, part, logits, labels, *refs):
    pieces = refs[:sent]
    turned, mine, loss, kept, *outs = refs[sent : 2 * sent + 4]
    landed, agg, packed = refs[2 * sent + 4 :]
    own = part.shape[0]
    units = mine.shape[1]
    pad = logits.shape[0]
    bring_in(ids, pieces, landed, node_count)
    chunk = min(own, landed.shape[0])
    total = logits[...]
    for j in range(groups):
        at = pl.ds(j * units, units)

        def one(r, held, at=at):
            rows = pl.ds(pl.multiple_of(r * chunk, chunk), chunk)
            srcs = pl.ds(pl.multiple_of(own + r * chunk, BLOCK), chunk)
            both = jnp.concatenate([source[rows, :], landed[rows, :]], axis=1)
            out = gelu(mm(both, w_one[:, at])).astype(BF16)
            spread = mm(a_ref[:, srcs], out)
            return held + spread[:own] + spread[own:]

        held = part[:, at]
        for r in range(landed.shape[0] // chunk) if landed.shape[0] == chunk else ():
            held = one(r, held)
        if landed.shape[0] != chunk:
            held = lax.fori_loop(0, landed.shape[0] // chunk, one, held)
        rounded = held.astype(BF16)
        agg[:, at] = rounded
        total = total + mm_nt(w_two[pad:, at], rounded)
    class_id = lax.broadcasted_iota(jnp.int32, total.shape, 0)
    real = class_id < class_count
    top = jnp.max(jnp.where(real, total, -jnp.inf), axis=0, keepdims=True)
    shifted = total - top
    powers = jnp.where(real, jnp.exp(shifted), 0.0)
    sums = jnp.sum(powers, axis=0, keepdims=True)
    target = (class_id == labels[...]).astype(F32)
    row_loss = jnp.log(sums) - jnp.sum(shifted * target, axis=0, keepdims=True)
    loss[...] = jnp.broadcast_to(jnp.sum(row_loss, axis=1, keepdims=True), loss.shape)
    grads = ((powers / sums - target) * grad_scale).astype(BF16)
    turned[...] = grads
    back = mm(grads, a_ref[:own, :])
    kept[...] = back[:, :own]
    packed[...] = back[:, own:].T.astype(BF16)
    spread_out(ids, packed, outs, node_count)
    mine[...] = agg[:, pl.ds(pl.multiple_of(ids[1] * units, units), units)]


def weights_kernel(class_count, turned, self_rows, agg_rows, loss, self_out, agg_out):
    own_grads = mm(turned[...], self_rows[...])
    row = lax.broadcasted_iota(jnp.int32, own_grads.shape, 0)
    self_out[...] = jnp.where(row == class_count, loss[0:1, 0:1], own_grads)
    agg_out[...] = mm(turned[...], agg_rows[...])[:class_count]


def direct_kernel(turned, kept, w_two, out):
    pad = turned.shape[0]
    high, low = halves(kept[...].T)
    rows = turned[...].T
    for j in range(out.shape[1] // 256):
        at = pl.ds(j * 256, 256)
        out[:, at] = mm(rows, w_two[:pad, at]) + mm(high, w_two[pad:, at]) + mm(low, w_two[pad:, at])


def back_kernel(node_count, sent, split, ids, pick, direct, slope, w_two, left, *refs):
    pieces = refs[:sent]
    outs, (landed, grads) = refs[sent:-2], refs[-2:]
    pad = w_two.shape[0] // 2
    bring_in(ids, pieces, landed, node_count)
    high, low = halves(mm_tn(pick[...], landed[...]))
    for j in range(direct.shape[1] // 256):
        at = pl.ds(j * 256, 256)
        total = direct[:, at] + mm(high, w_two[pad:, at]) + mm(low, w_two[pad:, at])
        grads[:, at] = mm(left[...], (total * slope[:, at]).astype(BF16))
    if not split:
        step = left.shape[0] // 2
        outs[0][...] = grads[:step]
        outs[1][...] = grads[step:]
        return
    width = grads.shape[1] // node_count
    for k, out in enumerate(outs):
        dest = lax.rem(ids[0] + k, node_count)
        out[...] = grads[:, pl.ds(pl.multiple_of(dest * width, width), width)]


def sum_kernel(*refs):
    *pieces, out = refs
    total = pieces[0][...]
    for piece in pieces[1:]:
        total = total + piece[...]
    out[...] = total


def place_kernel(node_count, ids, *refs):
    pieces, (top, bottom) = refs[:node_count], refs[node_count:]
    step, width = top.shape[0], pieces[0].shape[1]
    for k, piece in enumerate(pieces):
        source = lax.rem(ids[0] + node_count - k, node_count)
        at = pl.ds(pl.multiple_of(source * width, width), width)
        top[:, at] = piece[pl.ds(0, step), :]
        bottom[:, at] = piece[pl.ds(step, step), :]


def shifted(value, axis, count, k):
    return lax.ppermute(value, axis, [(i, (i + k) % count) for i in range(count)])


def exchange(pieces, count):
    if len(pieces) == 1:
        whole = pieces[0]
        return [lax.all_to_all(whole.reshape(count, -1, whole.shape[1]), "node", 0, 0, tiled=True).reshape(whole.shape)]
    return [pieces[0]] + [shifted(pieces[k], "node", count, k) for k in range(1, count)]


def gather_shifted(value, count):
    return [value] + [shifted(value, "feat", count, k) for k in range(1, count)]


def shards(features, send_rows, send_count, tile_src, tile_val, labels, w_self1, w_neigh1, w_self2, w_neigh2):
    nodes, groups = lax.axis_size("node"), lax.axis_size("feat")
    own, step = features.shape
    slots = send_rows.shape[2]
    halo = nodes * slots
    total_src = own + halo
    cols = step * groups
    width = w_self1.shape[1]
    units, classes = w_self2.shape
    pad = -(-(classes + 1) // 16) * 16
    split = nodes <= FEW
    sent = nodes if split else 1
    piece_rows = halo // sent
    grad_scale = 1.0 / math.sqrt(own * nodes)
    ids = jnp.stack([lax.axis_index("node"), lax.axis_index("feat")]).astype(jnp.int32)

    turned = features.T
    turned_all = gather_shifted(turned, groups)
    selfs = gather_shifted(w_self1, groups)
    neighs = gather_shifted(w_neigh1, groups)
    w_selfs = gather_shifted(w_self2.T, groups)
    w_neighs = gather_shifted(w_neigh2.T, groups)

    a_mat, pick = call(
        prepare_kernel,
        [((2 * own, total_src), BF16), ((halo, own), BF16)],
        (tile_src, send_count, tile_val, send_rows[0]),
        [SMEM, SMEM, VMEM, VMEM],
        [pltpu.VMEM((own, total_src), F32)],
        moved=tile_val.size * 4,
    )
    full, *outs = call(
        functools.partial(pack_kernel, nodes, groups, sent),
        [((own, cols), BF16)] + [((piece_rows, cols), BF16)] * sent,
        (ids, pick, *turned_all),
        [SMEM] + [VMEM] * (1 + groups),
        [pltpu.VMEM((cols, own), BF16), pltpu.VMEM((halo, cols), BF16)],
        flops=2 * halo * own * cols,
        moved=halo * own * 2,
    )
    arrived = exchange(outs, nodes)
    agg, source, *outs = call(
        functools.partial(first_kernel, nodes, sent),
        [((own, cols), BF16), ((halo, cols), BF16)] + [((piece_rows, cols), BF16)] * sent,
        (ids, pick, a_mat, full, *arrived),
        [SMEM] + [VMEM] * (3 + sent),
        [pltpu.VMEM((halo, cols), BF16)],
        flops=4 * own * total_src * cols,
        moved=4 * own * total_src,
    )
    arrived = exchange(outs, nodes)
    w_one, w_two, slope, part, logits, mine, left = call(
        functools.partial(own_kernel, groups),
        [
            ((2 * cols, width), BF16),
            ((2 * pad, width), BF16),
            ((own, width), F32),
            ((own, width), F32),
            ((pad, own), F32),
            ((own, units), BF16),
            ((2 * step, own), BF16),
        ],
        (ids, full, agg, a_mat, turned, *selfs, *neighs, *w_selfs, *w_neighs),
        [SMEM] + [VMEM] * (4 + 4 * groups),
        [pltpu.VMEM((own, width), BF16)],
        flops=4 * own * own * width,
        moved=12 * own * width,
    )
    turned_grads, agg_mine, loss, kept, *outs = call(
        functools.partial(second_kernel, nodes, groups, sent, classes, grad_scale),
        [((pad, own), BF16), ((own, units), BF16), ((8, 128), F32), ((pad, own), F32)]
        + [((piece_rows, pad), BF16)] * sent,
        (ids, a_mat, source, w_one, w_two, part, logits, labels.reshape(1, own), *arrived),
        [SMEM] + [VMEM] * (7 + sent),
        [pltpu.VMEM((halo, cols), BF16), pltpu.VMEM((own, width), BF16), pltpu.VMEM((halo, pad), BF16)],
        flops=4 * own * halo * width,
        moved=12 * own * width,
    )
    arrived = exchange(outs, nodes)
    grad_self2, grad_neigh2 = call(
        functools.partial(weights_kernel, classes),
        [((pad, units), F32), ((classes, units), F32)],
        (turned_grads, mine, agg_mine, loss),
        [VMEM] * 4,
        flops=4 * pad * own * units,
        moved=4 * own * units,
    )
    grad_self2, grad_neigh2 = lax.psum((grad_self2, grad_neigh2), "node")
    loss, grad_self2 = grad_self2[classes, 0], grad_self2[:classes]
    (direct,) = call(
        direct_kernel,
        [((own, width), F32)],
        (turned_grads, kept, w_two),
        [VMEM] * 3,
        flops=6 * own * pad * width,
        moved=8 * own * width,
    )
    outs = call(
        functools.partial(back_kernel, nodes, sent, split),
        [((2 * step, width // nodes), F32)] * nodes if split else [((step, width), F32)] * 2,
        (ids, pick, direct, slope, w_two, left, *arrived),
        [SMEM] + [VMEM] * (5 + sent),
        [pltpu.VMEM((halo, pad), BF16), pltpu.VMEM((2 * step, width), F32)],
        flops=6 * own * pad * width,
        moved=12 * own * width,
    )
    if split:
        summed = call(sum_kernel, [((2 * step, width // nodes), F32)], exchange(outs, nodes), [VMEM] * nodes)[0]
        gathered = [summed] + [shifted(summed, "node", nodes, k) for k in range(1, nodes)]
        grad_self1, grad_neigh1 = call(
            functools.partial(place_kernel, nodes),
            [((step, width), F32)] * 2,
            (ids, *gathered),
            [SMEM] + [VMEM] * nodes,
        )
    else:
        grad_self1, grad_neigh1 = lax.psum(tuple(outs), "node")
    return (loss / (own * nodes), grad_self1, grad_neigh1, grad_self2.T, grad_neigh2.T)


def solution(mesh):
    in_specs = (
        P("node", "feat"),
        P("node", None, None),
        P("node", None),
        P("node", None),
        P("node", None, None, None),
        P("node"),
        P("feat", None),
        P("feat", None),
        P("feat", None),
        P("feat", None),
    )
    out_specs = (P(), P("feat", None), P("feat", None), P("feat", None), P("feat", None))
    return jax.shard_map(shards, mesh=mesh, in_specs=in_specs, out_specs=out_specs, check_vma=False)
```

time: 275 us -> 161 us (0.59)
  waiting for transfers between devices: 142 us -> 30 us
  starting transfers between devices: 18.9 us -> 66.8 us
  Pallas kernels: 0 us -> 38.8 us
  local copies, waits for them, and re-layouts: 35.5 us -> 7.5 us
  matrix products: 23.4 us -> 0 us
  blocking collectives: 22.1 us -> 0 us
  other arithmetic: 16 us -> 0.61 us
    ppermute x0 -> x50, starting transfers between devices: none -> 66.8 us  [shifted(): lax.ppermute(value, axis, [(i, (i + k) % count) for i in range(count)])]
    psum x2 -> x1, waiting for transfers between devices: 81.9 us -> 15.2 us  [shards(): grad_self2, grad_neigh2 = lax.psum((grad_self2, grad_neigh2), 'node')]
    pallas_call x0 -> x10, Pallas kernels: none -> 38.8 us  [call(): pl.pallas_call(body, out_shape=[jax.ShapeDtypeStruct(shape, dtype) for sh...]
    reduce_scatter x1 -> x0, waiting for transfers between devices: 30.4 us -> none  [shards(): lax.psum_scatter(partial_one, 'feat', scatter_dimension=1, tiled=True)]
    dot_general x14 -> x0, matrix products: 23.4 us -> none  [the longest x1 4.52 us: spread_back(): jnp.einsum('bkij,bih->bkjh', tile_val, grads.reshape(-1, 128, col_count),...]
    psum x1 -> x0, blocking collectives: 22.1 us -> none  [shards(): mean_loss = lax.psum(jnp.sum(row_loss), 'node') / node_total]
    all_to_all x3 -> x0, starting transfers between devices: 18.3 us -> none  [the longest x1 7.28 us: shards(): lax.all_to_all(outgoing, 'node', split_axis=0, concat_axis=0, tiled=True)]
    all_to_all x3 -> x0, waiting for transfers between devices: 16.4 us -> none  [the longest x1 8.44 us: shards(): lax.all_to_all(outgoing_two, 'node', split_axis=0, concat_axis=0, tiled=T...]
  transfers between devices with their start and end apart: 7 -> 51, of which waited for: 7 -> 13; matrix products, arithmetic and copies ran while one was open for 3% -> 0% of each run, Pallas kernels for 0% -> 18%
where the time goes in v1:
time: 161 us; the launch traced here: 160 us
  starting transfers between devices  66.8 us (41%)
  Pallas kernels  38.8 us (24%)
  waiting for transfers between devices  30 us (19%)
  between operations  16.4 us (10%)
  local copies, waits for them, and re-layouts  7.5 us (5%)
    ppermute x50, starting transfers between devices, shifted(): lax.ppermute(value, axis, [(i, (i + k) % count) for i in range(count)])  66.8 us
    pallas_call x10, Pallas kernels, call(): pl.pallas_call(body, out_shape=[jax.ShapeDtypeStruct(shape, dtype) for sh...  38.8 us
    psum x1, waiting for transfers between devices, shards(): grad_self2, grad_neigh2 = lax.psum((grad_self2, grad_neigh2), 'node')  15.2 us
    ppermute x50, waiting for transfers between devices, shifted(): lax.ppermute(value, axis, [(i, (i + k) % count) for i in range(count)])  14.8 us
    unnamed x109, local copies, waits for them, and re-layouts  4.7 us
  transfers between devices with their start and end apart: 51, of which 13 were waited for; matrix products, arithmetic and copies ran while one was open for 0% of the time, Pallas kernels for 18%

profile of v1, /device:TPU:0, one launch (start us, length us, event | category | flops | bytes accessed | tf_op | source)
XLA Modules:
  0.0 160.2 jit_solution(17951966017182565642)
XLA Ops:
  7.2 2.4 %collective-permute-start.2 = (bf16[32,512]{1,0:T(8,128)(2,1)}, bf16[32,512]{1,0:T(8,128)(2,1)S(1)}, u32[]{:S(2)}, u32[]{:S(2)}) collective-permute-start(bf16[32,512]{1,0:T(8,128)(2,1)} %bitcast.12), channel_id=1, source_target_pairs={{0,3},{1,0},{2,1},{3,2},{4,7},{5,4},{6,5},{7,6},{8,11},{9,8},{10,9... | collective-permute-start | bytes 98312 | tf_op jit(solution)/shard_map/ppermute | solution.py:270
  12.8 4.8 %shard_map.137 = (bf16[1024,1024]{1,0:T(8,128)(2,1)}, bf16[512,512]{1,0:T(8,128)(2,1)}) custom-call(s32[4,16]{1,0:T(4,128)} %tile_src.1, s32[1,8]{1,0:T(1,128)} %count.1, bf16[4,16,128,128]{3,2,1,0:T(8,128)(2,1)} %tile_val.1, s32[8,64]{1,0:T(8,128)} %bitcast.17), custom_call_target="tpu_custom_call" | custom-call | bytes 4194304 | tf_op jit(solution)/shard_map/pallas_call | solution.py:53
  18.2 2.1 %shard_map.138 = (bf16[512,128]{1,0:T(8,128)(2,1)}, bf16[64,128]{1,0:T(8,128)(2,1)}, bf16[64,128]{1,0:T(8,128)(2,1)}, bf16[64,128]{1,0:T(8,128)(2,1)}, bf16[64,1...) custom-call(s32[2]{0:T(128)} %pad_add_fusion.ids, ...), custom_call_target="tpu_custom_call" | custom-call | flops 67108864 | bytes 524288 | tf_op jit(solution)/shard_map/pallas_call | solution.py:53
  23.4 2.5 %collective-permute-start.5 = (bf16[64,128]{1,0:T(8,128)(2,1)}, bf16[64,128]{1,0:T(8,128)(2,1)S(1)}, u32[]{:S(2)}, u32[]{:S(2)}) collective-permute-start(bf16[64,128]{1,0:T(8,128)(2,1)} %get-tuple-element.63), channel_id=1, source_target_pairs={{0,12},{4,16},{8,20},{12,24},{16,28},{20,0},{24,4},{28,8},{1,13},{... | collective-permute-start | bytes 49160 | tf_op jit(solution)/shard_map/ppermute | solution.py:270
  27.8 2.1 %collective-permute-start.7 = (bf16[64,128]{1,0:T(8,128)(2,1)}, bf16[64,128]{1,0:T(8,128)(2,1)S(1)}, u32[]{:S(2)}, u32[]{:S(2)}) collective-permute-start(bf16[64,128]{1,0:T(8,128)(2,1)} %get-tuple-element.65), channel_id=1, source_target_pairs={{0,20},{4,24},{8,28},{12,0},{16,4},{20,8},{24,12},{28,16},{1,21},{... | collective-permute-start | bytes 49160 | tf_op jit(solution)/shard_map/ppermute | solution.py:270
  39.1 3.6 %shard_map.139 = (bf16[512,128]{1,0:T(8,128)(2,1)}, bf16[512,128]{1,0:T(8,128)(2,1)}, bf16[64,128]{1,0:T(8,128)(2,1)}, bf16[64,128]{1,0:T(8,128)(2,1)}, bf16[64,...) custom-call(s32[2]{0:T(128)} %pad_add_fusion.ids, ...), custom_call_target="tpu_custom_call" | custom-call | flops 268435456 | bytes 2097152 | tf_op jit(solution)/shard_map/pallas_call | solution.py:53
  46.0 3.4 %collective-permute-done.22.refs_1_ = bf16[64,128]{1,0:T(8,128)(2,1)S(1)} collective-permute-done((bf16[64,128]{1,0:T(8,128)(2,1)}, bf16[64,128]{1,0:T(8,128)(2,1)S(1)}, u32[]{:S(2)}, u32[]{:S(2)}) %collective-permute-start.22) | collective-permute-done | bytes 16416 | tf_op jit(solution)/shard_map/ppermute | solution.py:270
  54.0 3.7 %collective-permute-start.26 = (bf16[64,128]{1,0:T(8,128)(2,1)}, bf16[64,128]{1,0:T(8,128)(2,1)S(1)}, u32[]{:S(2)}, u32[]{:S(2)}) collective-permute-start(bf16[64,128]{1,0:T(8,128)(2,1)} %get-tuple-element.79), channel_id=1, source_target_pairs={{0,20},{4,24},{8,28},{12,0},{16,4},{20,8},{24,12},{28,16},{1,21},{... | collective-permute-start | bytes 49160 | tf_op jit(solution)/shard_map/ppermute | solution.py:270
  59.3 6.7 %shard_map.140 = (bf16[256,1024]{1,0:T(8,128)(2,1)}, bf16[352,1024]{1,0:T(8,128)(2,1)}, f32[512,1024]{1,0:T(8,128)}, f32[512,1024]{1,0:T(8,128)}, f32[176,512]{1...) custom-call(s32[2]{0:T(128)} %pad_add_fusion.ids, bf16[512,128]{1,0:T(8,128)(2,1)} %get-tuple-element.59.full, ...), custom_call_target="tpu_custom_call" | custom-call | flops 1073741824 | bytes 6291456 | tf_op jit(solution)/shard_map/pallas_call | solution.py:53
  66.8 7.4 %shard_map.141 = (bf16[176,512]{1,0:T(8,128)(2,1)}, bf16[512,256]{1,0:T(8,128)(2,1)}, f32[8,128]{1,0:T(8,128)}, f32[176,512]{1,0:T(8,128)}, bf16[64,176]{1,0:T(8...) custom-call(s32[2]{0:T(128)} %pad_add_fusion.ids, ...), custom_call_target="tpu_custom_call" | custom-call | flops 1073741824 | bytes 6291456 | tf_op jit(solution)/shard_map/pallas_call | solution.py:53
  74.1 2.1 %shard_map.142 = (f32[176,256]{1,0:T(8,128)}, f32[172,256]{1,0:T(8,128)}) custom-call(bf16[176,512]{1,0:T(8,128)(2,1)} %get-tuple-element.82.turned, bf16[512,256]{1,0:T(8,128)(2,1)} %get-tuple-element.83.self_rows, bf16[512,256]{1,0:T(8,128)(2,1)} %get-tuple-element.84.agg_rows, f32[8,128]{1,0:T(8,128)} %get-tuple-element.85.loss), custom_call_target="tpu_custom_call" | custom-call | flops 92274688 | bytes 524288 | tf_op jit(solution)/shard_map/pallas_call | solution.py:53
  76.9 2.0 %collective-permute-start.30 = (bf16[64,176]{1,0:T(8,128)(2,1)}, bf16[64,176]{1,0:T(8,128)(2,1)S(1)}, u32[]{:S(2)}, u32[]{:S(2)}) collective-permute-start(bf16[64,176]{1,0:T(8,128)(2,1)} %get-tuple-element.92), channel_id=1, source_target_pairs={{0,8},{4,12},{8,16},{12,20},{16,24},{20,28},{24,0},{28,4},{1,9},{5... | collective-permute-start | bytes 67592 | tf_op jit(solution)/shard_map/ppermute | solution.py:270
  79.3 3.3 %collective-permute-start.32 = (bf16[64,176]{1,0:T(8,128)(2,1)}, bf16[64,176]{1,0:T(8,128)(2,1)S(1)}, u32[]{:S(2)}, u32[]{:S(2)}) collective-permute-start(bf16[64,176]{1,0:T(8,128)(2,1)} %get-tuple-element.94), channel_id=1, source_target_pairs={{0,16},{4,20},{8,24},{12,28},{16,0},{20,4},{24,8},{28,12},{1,17},{... | collective-permute-start | bytes 67592 | tf_op jit(solution)/shard_map/ppermute | solution.py:270
  83.3 2.3 %collective-permute-start.34 = (bf16[64,176]{1,0:T(8,128)(2,1)}, bf16[64,176]{1,0:T(8,128)(2,1)S(1)}, u32[]{:S(2)}, u32[]{:S(2)}) collective-permute-start(bf16[64,176]{1,0:T(8,128)(2,1)} %get-tuple-element.96), channel_id=1, source_target_pairs={{0,24},{4,28},{8,0},{12,4},{16,8},{20,12},{24,16},{28,20},{1,25},{... | collective-permute-start | bytes 67592 | tf_op jit(solution)/shard_map/ppermute | solution.py:270
  87.5 3.7 %shard_map.143.direct = f32[512,1024]{1,0:T(8,128)} custom-call(bf16[176,512]{1,0:T(8,128)(2,1)} %get-tuple-element.82.turned, f32[176,512]{1,0:T(8,128)} %get-tuple-element.87.kept, bf16[352,1024]{1,0:T(8,128)(2,1)} %get-tuple-element.71.w_two), custom_call_target="tpu_custom_call" | custom-call | flops 553648128 | bytes 4194304 | tf_op jit(solution)/shard_map/pallas_call | solution.py:53
  91.8 5.3 %shard_map.144 = (f32[64,128]{1,0:T(8,128)}, f32[64,128]{1,0:T(8,128)}, f32[64,128]{1,0:T(8,128)}, f32[64,128]{1,0:T(8,128)}, f32[64,128]{1,0:T(8,128)}, /*index...) custom-call(s32[2]{0:T(128)} %pad_add_fusion.ids, bf16[512,512]{1,0:T(8,128)(2,1)} %get-tuple-element.58.pick, ...), custom_call_target="tpu_custom_call" | custom-call | flops 553648128 | bytes 6291456 | tf_op jit(solution)/shard_map/pallas_call | solution.py:53
  100.2 2.5 %collective-permute-start.39 = (f32[64,128]{1,0:T(8,128)}, f32[64,128]{1,0:T(8,128)S(1)}, u32[]{:S(2)}, u32[]{:S(2)}) collective-permute-start(f32[64,128]{1,0:T(8,128)} %get-tuple-element.102), channel_id=1, source_target_pairs={{0,16},{4,20},{8,24},{12,28},{16,0},{20,4},{24,8},{28,12},{1,17},{... | collective-permute-start | bytes 98312 | tf_op jit(solution)/shard_map/ppermute | solution.py:270
  102.7 2.7 %collective-permute-start.40 = (f32[64,128]{1,0:T(8,128)}, f32[64,128]{1,0:T(8,128)S(1)}, u32[]{:S(2)}, u32[]{:S(2)}) collective-permute-start(f32[64,128]{1,0:T(8,128)} %get-tuple-element.103), channel_id=1, source_target_pairs={{0,20},{4,24},{8,28},{12,0},{16,4},{20,8},{24,12},{28,16},{1,21},{... | collective-permute-start | bytes 98312 | tf_op jit(solution)/shard_map/ppermute | solution.py:270
  105.5 2.9 %collective-permute-start.42 = (f32[64,128]{1,0:T(8,128)}, f32[64,128]{1,0:T(8,128)S(1)}, u32[]{:S(2)}, u32[]{:S(2)}) collective-permute-start(f32[64,128]{1,0:T(8,128)} %get-tuple-element.105), channel_id=1, source_target_pairs={{0,28},{4,0},{8,4},{12,8},{16,12},{20,16},{24,20},{28,24},{1,29},{... | collective-permute-start | bytes 98312 | tf_op jit(solution)/shard_map/ppermute | solution.py:270
  112.4 4.9 %collective-permute-start.49 = (f32[64,128]{1,0:T(8,128)}, f32[64,128]{1,0:T(8,128)S(1)}, u32[]{:S(2)}, u32[]{:S(2)}) collective-permute-start(f32[64,128]{1,0:T(8,128)} %shard_map.145.refs_0_), channel_id=1, source_target_pairs={{0,28},{4,0},{8,4},{12,8},{16,12},{20,16},{24,20},{28,24},{1,29},{... | collective-permute-start | bytes 98312 | tf_op jit(solution)/shard_map/ppermute | solution.py:270
  117.3 2.9 %collective-permute-start.46 = (f32[64,128]{1,0:T(8,128)}, f32[64,128]{1,0:T(8,128)S(1)}, u32[]{:S(2)}, u32[]{:S(2)}) collective-permute-start(f32[64,128]{1,0:T(8,128)} %shard_map.145.refs_0_), channel_id=1, source_target_pairs={{0,16},{4,20},{8,24},{12,28},{16,0},{20,4},{24,8},{28,12},{1,17},{... | collective-permute-start | bytes 98312 | tf_op jit(solution)/shard_map/ppermute | solution.py:270
  120.2 2.6 %collective-permute-start.44 = (f32[64,128]{1,0:T(8,128)}, f32[64,128]{1,0:T(8,128)S(1)}, u32[]{:S(2)}, u32[]{:S(2)}) collective-permute-start(f32[64,128]{1,0:T(8,128)} %shard_map.145.refs_0_), channel_id=1, source_target_pairs={{0,8},{4,12},{8,16},{12,20},{16,24},{20,28},{24,0},{28,4},{1,9},{5... | collective-permute-start | bytes 98312 | tf_op jit(solution)/shard_map/ppermute | solution.py:270
  123.7 2.4 %collective-permute-done.45.refs_3_ = f32[64,128]{1,0:T(8,128)S(1)} collective-permute-done((f32[64,128]{1,0:T(8,128)}, f32[64,128]{1,0:T(8,128)S(1)}, u32[]{:S(2)}, u32[]{:S(2)}) %collective-permute-start.45) | collective-permute-done | bytes 32800 | tf_op jit(solution)/shard_map/ppermute | solution.py:270
  131.9 15.2 %all-reduce.3.cloned.1.call-done = (f32[176,256]{1,0:T(8,128)}, f32[256,172]{0,1:T(8,128)}) async-done(((f32[176,256]{1,0:T(8,128)}, f32[256,172]{0,1:T(8,128)}), (f32[176,256]{1,0:T(8,128)}, f32[256,172]{0,1:T(8,128)})) %all-reduce.3.cloned.1.call-update) | async-done | bytes 356368 | tf_op jit(solution)/shard_map/psum | solution.py:371
  (201 shorter events, 50.2 us)
Async XLA Ops:
  7.2 139.9 %all-reduce.3.cloned.1.call-start = ((), (), s32[]{:S(2)}) async-start(), calls=%async_computation | async-start | bytes 720896 | tf_op jit(solution)/shard_map/psum | solution.py:371
  7.2 10.3 %collective-permute-start.2 = (bf16[32,512]{1,0:T(8,128)(2,1)}, bf16[32,512]{1,0:T(8,128)(2,1)S(1)}, u32[]{:S(2)}, u32[]{:S(2)}) collective-permute-start(bf16[32,512]{1,0:T(8,128)(2,1)} %bitcast.12), channel_id=1, source_target_pairs={{0,3},{1,0},{2,1},{3,2},{4,7},{5,4},{6,5},{7,6},{8,11},{9,8},{10,9... | collective-permute-start | bytes 98312 | tf_op jit(solution)/shard_map/ppermute | solution.py:270
  9.7 7.9 %collective-permute-start.1 = (bf16[32,512]{1,0:T(8,128)(2,1)}, bf16[32,512]{1,0:T(8,128)(2,1)S(1)}, u32[]{:S(2)}, u32[]{:S(2)}) collective-permute-start(bf16[32,512]{1,0:T(8,128)(2,1)} %bitcast.13), channel_id=1, source_target_pairs={{0,2},{1,3},{2,0},{3,1},{4,6},{5,7},{6,4},{7,5},{8,10},{9,11},{10,... | collective-permute-start | bytes 98312 | tf_op jit(solution)/shard_map/ppermute | solution.py:270
  10.5 26.8 %collective-permute-start.11 = (bf16[32,1024]{1,0:T(8,128)(2,1)}, bf16[32,1024]{1,0:T(8,128)(2,1)S(1)}, u32[]{:S(2)}, u32[]{:S(2)}) collective-permute-start(bf16[32,1024]{1,0:T(8,128)(2,1)} %refs_0_.1), channel_id=1, source_target_pairs={{0,2},{1,3},{2,0},{3,1},{4,6},{5,7},{6,4},{7,5},{8,10},{9,11},{10,... | collective-permute-start | bytes 196616 | tf_op jit(solution)/shard_map/ppermute | solution.py:270
  11.7 25.6 %collective-permute-start.10 = (bf16[32,1024]{1,0:T(8,128)(2,1)}, bf16[32,1024]{1,0:T(8,128)(2,1)S(1)}, u32[]{:S(2)}, u32[]{:S(2)}) collective-permute-start(bf16[32,1024]{1,0:T(8,128)(2,1)} %refs_0_.1), channel_id=1, source_target_pairs={{0,1},{1,2},{2,3},{3,0},{4,5},{5,6},{6,7},{7,4},{8,9},{9,10},{10,1... | collective-permute-start | bytes 196616 | tf_op jit(solution)/shard_map/ppermute | solution.py:270
  33.8 17.2 %collective-permute-start.18 = (bf16[172,256]{1,0:T(8,128)(2,1)S(1)}, bf16[172,256]{1,0:T(8,128)(2,1)S(1)}, u32[]{:S(2)}, u32[]{:S(2)}) collective-permute-start(bf16[172,256]{1,0:T(8,128)(2,1)S(1)} %bitcast.20), channel_id=1, source_target_pairs={{0,3},{1,0},{2,1},{3,2},{4,7},{5,4},{6,5},{7,6},{8,11},{9,8},{10,9... | collective-permute-start | bytes 264200 | tf_op jit(solution)/shard_map/ppermute | solution.py:270
  34.0 8.8 %collective-permute-start.12 = (bf16[32,1024]{1,0:T(8,128)(2,1)S(1)}, bf16[32,1024]{1,0:T(8,128)(2,1)S(1)}, u32[]{:S(2)}, u32[]{:S(2)}) collective-permute-start(bf16[32,1024]{1,0:T(8,128)(2,1)S(1)} %copy-done.46), channel_id=1, source_target_pairs={{0,3},{1,0},{2,1},{3,2},{4,7},{5,4},{6,5},{7,6},{8,11},{9,8},{10,9... | collective-permute-start | bytes 196616 | tf_op jit(solution)/shard_map/ppermute | solution.py:270
  36.0 8.6 %collective-permute-start.14 = (bf16[32,1024]{1,0:T(8,128)(2,1)S(1)}, bf16[32,1024]{1,0:T(8,128)(2,1)S(1)}, u32[]{:S(2)}, u32[]{:S(2)}) collective-permute-start(bf16[32,1024]{1,0:T(8,128)(2,1)S(1)} %copy-done.47), channel_id=1, source_target_pairs={{0,2},{1,3},{2,0},{3,1},{4,6},{5,7},{6,4},{7,5},{8,10},{9,11},{10,... | collective-permute-start | bytes 196616 | tf_op jit(solution)/shard_map/ppermute | solution.py:270
  37.3 8.1 %collective-permute-start.13 = (bf16[32,1024]{1,0:T(8,128)(2,1)S(1)}, bf16[32,1024]{1,0:T(8,128)(2,1)S(1)}, u32[]{:S(2)}, u32[]{:S(2)}) collective-permute-start(bf16[32,1024]{1,0:T(8,128)(2,1)S(1)} %copy-done.47), channel_id=1, source_target_pairs={{0,1},{1,2},{2,3},{3,0},{4,5},{5,6},{6,7},{7,4},{8,9},{9,10},{10,1... | collective-permute-start | bytes 196616 | tf_op jit(solution)/shard_map/ppermute | solution.py:270
  37.3 8.7 %collective-permute-start.15 = (bf16[32,1024]{1,0:T(8,128)(2,1)S(1)}, bf16[32,1024]{1,0:T(8,128)(2,1)S(1)}, u32[]{:S(2)}, u32[]{:S(2)}) collective-permute-start(bf16[32,1024]{1,0:T(8,128)(2,1)S(1)} %copy-done.47), channel_id=1, source_target_pairs={{0,3},{1,0},{2,1},{3,2},{4,7},{5,4},{6,5},{7,6},{8,11},{9,8},{10,9... | collective-permute-start | bytes 196616 | tf_op jit(solution)/shard_map/ppermute | solution.py:270
  51.0 15.1 %collective-permute-start.24 = (bf16[64,128]{1,0:T(8,128)(2,1)}, bf16[64,128]{1,0:T(8,128)(2,1)S(1)}, u32[]{:S(2)}, u32[]{:S(2)}) collective-permute-start(bf16[64,128]{1,0:T(8,128)(2,1)} %get-tuple-element.77), channel_id=1, source_target_pairs={{0,12},{4,16},{8,20},{12,24},{16,28},{20,0},{24,4},{28,8},{1,13},{... | collective-permute-start | bytes 49160 | tf_op jit(solution)/shard_map/ppermute | solution.py:270
  52.2 13.9 %collective-permute-start.25 = (bf16[64,128]{1,0:T(8,128)(2,1)}, bf16[64,128]{1,0:T(8,128)(2,1)S(1)}, u32[]{:S(2)}, u32[]{:S(2)}) collective-permute-start(bf16[64,128]{1,0:T(8,128)(2,1)} %get-tuple-element.78), channel_id=1, source_target_pairs={{0,16},{4,20},{8,24},{12,28},{16,0},{20,4},{24,8},{28,12},{1,17},{... | collective-permute-start | bytes 49160 | tf_op jit(solution)/shard_map/ppermute | solution.py:270
  54.0 12.1 %collective-permute-start.26 = (bf16[64,128]{1,0:T(8,128)(2,1)}, bf16[64,128]{1,0:T(8,128)(2,1)S(1)}, u32[]{:S(2)}, u32[]{:S(2)}) collective-permute-start(bf16[64,128]{1,0:T(8,128)(2,1)} %get-tuple-element.79), channel_id=1, source_target_pairs={{0,20},{4,24},{8,28},{12,0},{16,4},{20,8},{24,12},{28,16},{1,21},{... | collective-permute-start | bytes 49160 | tf_op jit(solution)/shard_map/ppermute | solution.py:270
  57.7 8.4 %collective-permute-start.27 = (bf16[64,128]{1,0:T(8,128)(2,1)}, bf16[64,128]{1,0:T(8,128)(2,1)S(1)}, u32[]{:S(2)}, u32[]{:S(2)}) collective-permute-start(bf16[64,128]{1,0:T(8,128)(2,1)} %get-tuple-element.80), channel_id=1, source_target_pairs={{0,24},{4,28},{8,0},{12,4},{16,8},{20,12},{24,16},{28,20},{1,25},{... | collective-permute-start | bytes 49160 | tf_op jit(solution)/shard_map/ppermute | solution.py:270
  57.8 8.4 %collective-permute-start.28 = (bf16[64,128]{1,0:T(8,128)(2,1)}, bf16[64,128]{1,0:T(8,128)(2,1)S(1)}, u32[]{:S(2)}, u32[]{:S(2)}) collective-permute-start(bf16[64,128]{1,0:T(8,128)(2,1)} %get-tuple-element.81), channel_id=1, source_target_pairs={{0,28},{4,0},{8,4},{12,8},{16,12},{20,16},{24,20},{28,24},{1,29},{... | collective-permute-start | bytes 49160 | tf_op jit(solution)/shard_map/ppermute | solution.py:270
  76.9 8.7 %collective-permute-start.30 = (bf16[64,176]{1,0:T(8,128)(2,1)}, bf16[64,176]{1,0:T(8,128)(2,1)S(1)}, u32[]{:S(2)}, u32[]{:S(2)}) collective-permute-start(bf16[64,176]{1,0:T(8,128)(2,1)} %get-tuple-element.92), channel_id=1, source_target_pairs={{0,8},{4,12},{8,16},{12,20},{16,24},{20,28},{24,0},{28,4},{1,9},{5... | collective-permute-start | bytes 67592 | tf_op jit(solution)/shard_map/ppermute | solution.py:270
  78.8 12.3 %collective-permute-start.31 = (bf16[64,176]{1,0:T(8,128)(2,1)}, bf16[64,176]{1,0:T(8,128)(2,1)S(1)}, u32[]{:S(2)}, u32[]{:S(2)}) collective-permute-start(bf16[64,176]{1,0:T(8,128)(2,1)} %get-tuple-element.93), channel_id=1, source_target_pairs={{0,12},{4,16},{8,20},{12,24},{16,28},{20,0},{24,4},{28,8},{1,13},{... | collective-permute-start | bytes 67592 | tf_op jit(solution)/shard_map/ppermute | solution.py:270
  79.3 11.9 %collective-permute-start.32 = (bf16[64,176]{1,0:T(8,128)(2,1)}, bf16[64,176]{1,0:T(8,128)(2,1)S(1)}, u32[]{:S(2)}, u32[]{:S(2)}) collective-permute-start(bf16[64,176]{1,0:T(8,128)(2,1)} %get-tuple-element.94), channel_id=1, source_target_pairs={{0,16},{4,20},{8,24},{12,28},{16,0},{20,4},{24,8},{28,12},{1,17},{... | collective-permute-start | bytes 67592 | tf_op jit(solution)/shard_map/ppermute | solution.py:270
  82.6 8.5 %collective-permute-start.33 = (bf16[64,176]{1,0:T(8,128)(2,1)}, bf16[64,176]{1,0:T(8,128)(2,1)S(1)}, u32[]{:S(2)}, u32[]{:S(2)}) collective-permute-start(bf16[64,176]{1,0:T(8,128)(2,1)} %get-tuple-element.95), channel_id=1, source_target_pairs={{0,20},{4,24},{8,28},{12,0},{16,4},{20,8},{24,12},{28,16},{1,21},{... | collective-permute-start | bytes 67592 | tf_op jit(solution)/shard_map/ppermute | solution.py:270
  83.3 7.9 %collective-permute-start.34 = (bf16[64,176]{1,0:T(8,128)(2,1)}, bf16[64,176]{1,0:T(8,128)(2,1)S(1)}, u32[]{:S(2)}, u32[]{:S(2)}) collective-permute-start(bf16[64,176]{1,0:T(8,128)(2,1)} %get-tuple-element.96), channel_id=1, source_target_pairs={{0,24},{4,28},{8,0},{12,4},{16,8},{20,12},{24,16},{28,20},{1,25},{... | collective-permute-start | bytes 67592 | tf_op jit(solution)/shard_map/ppermute | solution.py:270
  97.2 8.2 %collective-permute-start.36 = (f32[64,128]{1,0:T(8,128)}, f32[64,128]{1,0:T(8,128)S(1)}, u32[]{:S(2)}, u32[]{:S(2)}) collective-permute-start(f32[64,128]{1,0:T(8,128)} %get-tuple-element.99), channel_id=1, source_target_pairs={{0,4},{4,8},{8,12},{12,16},{16,20},{20,24},{24,28},{28,0},{1,5},{5... | collective-permute-start | bytes 98312 | tf_op jit(solution)/shard_map/ppermute | solution.py:270
  97.5 8.0 %collective-permute-start.37 = (f32[64,128]{1,0:T(8,128)}, f32[64,128]{1,0:T(8,128)S(1)}, u32[]{:S(2)}, u32[]{:S(2)}) collective-permute-start(f32[64,128]{1,0:T(8,128)} %get-tuple-element.100), channel_id=1, source_target_pairs={{0,8},{4,12},{8,16},{12,20},{16,24},{20,28},{24,0},{28,4},{1,9},{5... | collective-permute-start | bytes 98312 | tf_op jit(solution)/shard_map/ppermute | solution.py:270
  99.2 9.1 %collective-permute-start.38 = (f32[64,128]{1,0:T(8,128)}, f32[64,128]{1,0:T(8,128)S(1)}, u32[]{:S(2)}, u32[]{:S(2)}) collective-permute-start(f32[64,128]{1,0:T(8,128)} %get-tuple-element.101), channel_id=1, source_target_pairs={{0,12},{4,16},{8,20},{12,24},{16,28},{20,0},{24,4},{28,8},{1,13},{... | collective-permute-start | bytes 98312 | tf_op jit(solution)/shard_map/ppermute | solution.py:270
  100.2 8.1 %collective-permute-start.39 = (f32[64,128]{1,0:T(8,128)}, f32[64,128]{1,0:T(8,128)S(1)}, u32[]{:S(2)}, u32[]{:S(2)}) collective-permute-start(f32[64,128]{1,0:T(8,128)} %get-tuple-element.102), channel_id=1, source_target_pairs={{0,16},{4,20},{8,24},{12,28},{16,0},{20,4},{24,8},{28,12},{1,17},{... | collective-permute-start | bytes 98312 | tf_op jit(solution)/shard_map/ppermute | solution.py:270
  (81 other events, 568.6 us)
Sparse Core Ops, SparseCore 0:
  76.4 70.6 all-reduce.2

commit v2 on v1

v2 whole, which is shorter than its diff:
```python
import functools
import math

import jax
import jax.numpy as jnp
from jax import lax
from jax.experimental import pallas as pl
from jax.experimental.pallas import tpu as pltpu
from jax.sharding import PartitionSpec as P

BLOCK = 128
F32 = jnp.float32
BF16 = jnp.bfloat16
VMEM = pl.BlockSpec(memory_space=pltpu.VMEM)
SMEM = pl.BlockSpec(memory_space=pltpu.SMEM)


def mm(a, b):
    return lax.dot_general(a, b, (((1,), (0,)), ((), ())), preferred_element_type=F32)


def mm_nt(a, b):
    return lax.dot_general(a, b, (((1,), (1,)), ((), ())), preferred_element_type=F32)


def mm_tn(a, b):
    return lax.dot_general(a, b, (((0,), (0,)), ((), ())), preferred_element_type=F32)


def halves(value):
    high = value.astype(BF16)
    return high, (value - high.astype(F32)).astype(BF16)


def gelu_parts(v):
    inner = math.sqrt(2.0 / math.pi) * (v + 0.044715 * (v * v * v))
    t = jnp.tanh(inner)
    return 0.5 * (1.0 + t), t


def gelu(v):
    return v * gelu_parts(v)[0]


def gelu_slope(v):
    cdf, t = gelu_parts(v)
    inner_slope = math.sqrt(2.0 / math.pi) * (1.0 + 3 * 0.044715 * (v * v))
    return cdf + 0.5 * v * (1.0 - t * t) * inner_slope


def size_of(shape, dtype):
    rows = -(-shape[-2] // 16) * 16 if len(shape) > 1 else 1
    return math.prod(shape[:-2]) * rows * (-(-shape[-1] // 128) * 128) * jnp.dtype(dtype).itemsize


def call(body, outs, args, specs, scratch=(), flops=0, moved=0):
    room = sum(size_of(shape, dtype) for shape, dtype in outs) + sum(size_of(shape, dtype) for shape, dtype in scratch)
    room += sum(size_of(arg.shape, arg.dtype) for arg, spec in zip(args, specs) if spec is VMEM)
    return pl.pallas_call(
        body,
        out_shape=[jax.ShapeDtypeStruct(shape, dtype) for shape, dtype in outs],
        in_specs=specs,
        out_specs=[VMEM] * len(outs),
        scratch_shapes=[pltpu.VMEM(shape, dtype) for shape, dtype in scratch],
        compiler_params=pltpu.CompilerParams(vmem_limit_bytes=min(room + 8 * 2**20, 56 * 2**20)),
        cost_estimate=pl.CostEstimate(flops=flops, bytes_accessed=moved, transcendentals=0),
    )(*args)


def weights_pack_kernel(w_self1, w_neigh1, w_self2, w_neigh2, out):
    step, units = w_self1.shape[0], out.shape[1]
    classes = w_self2.shape[0]
    groups = w_self1.shape[1] // units
    base = 2 * step * groups
    pad = (out.shape[0] - base) // 2
    for j in range(groups):
        at = pl.ds(j * units, units)
        out[pl.ds(2 * step * j, step), :] = w_self1[:, at]
        out[pl.ds(2 * step * j + step, step), :] = w_neigh1[:, at]
    out[pl.ds(base, 2 * pad), :] = jnp.zeros((2 * pad, units), BF16)
    out[pl.ds(base, classes), :] = w_self2[...]
    out[pl.ds(base + pad, classes), :] = w_neigh2[...]


def pack_kernel(groups, ids, count, send_rows, *refs):
    pieces, (pick, full, packed), (turned,) = refs[:groups], refs[groups : groups + 3], refs[groups + 3 :]
    step, own = pieces[0].shape
    dests, slots = send_rows.shape
    columns = send_rows[...].astype(F32).T
    row_id = lax.broadcasted_iota(jnp.int32, (slots, own), 1).astype(F32)
    slot_id = lax.broadcasted_iota(jnp.int32, (slots, own), 0)
    for d in range(dests):
        hit = (columns[:, d : d + 1] == row_id) & (slot_id < count[0, d])
        pick[pl.ds(d * slots, slots), :] = jnp.where(hit, 1.0, 0.0).astype(BF16)
    for k, piece in enumerate(pieces):
        group = lax.rem(ids[0] + groups - k, groups)
        turned[pl.ds(pl.multiple_of(group * step, step), step), :] = piece[...]
    rows = turned[...].T
    full[...] = rows
    packed[...] = mm(pick[...], rows).astype(BF16)


def prepare_kernel(tile_src, tile_val, a_ref, dense):
    blocks, per_block = tile_val.shape[0], tile_val.shape[1]
    own = blocks * BLOCK
    dense[...] = jnp.zeros_like(dense)
    for b in range(blocks):

        def add(k, _, b=b):
            at = pl.ds(pl.multiple_of(tile_src[b, k] * BLOCK, BLOCK), BLOCK)
            rows = pl.ds(b * BLOCK, BLOCK)
            dense[rows, at] = dense[rows, at] + tile_val[b, k].astype(F32)
            return 0

        lax.fori_loop(0, per_block, add, 0)
    for b in range(blocks):
        rows = pl.ds(b * BLOCK, BLOCK)
        high, low = halves(dense[rows, :])
        a_ref[rows, :] = high
        a_ref[pl.ds(own + b * BLOCK, BLOCK), :] = low


def first_kernel(pick, a_ref, full, source, agg, packed):
    own = full.shape[0]
    both = mm(a_ref[:, :own], full[...]) + mm(a_ref[:, own:], source[...])
    rounded = (both[:own] + both[own:]).astype(BF16)
    agg[...] = rounded
    packed[...] = mm(pick[...], rounded).astype(BF16)


def own_kernel(ids, full, agg, a_ref, turned, weights, w_one, w_two, slope, part, logits, mine, left, hidden, agg_turned):
    groups, _, units = weights.shape
    own, cols = full.shape
    step = turned.shape[0]
    pad = logits.shape[0]
    base = 2 * step * groups
    for g in range(groups):
        for j in range(groups):
            at = pl.ds(j * units, units)
            w_one[pl.ds(g * step, step), at] = weights[g, pl.ds(2 * step * j, step), :]
            w_one[pl.ds(cols + g * step, step), at] = weights[g, pl.ds(2 * step * j + step, step), :]
        w_two[:, pl.ds(g * units, units)] = weights[g, pl.ds(base, 2 * pad), :]
    left[pl.ds(0, step), :] = turned[...]
    agg_turned[...] = agg[...].T
    left[pl.ds(step, step), :] = agg_turned[pl.ds(pl.multiple_of(ids[0] * step, step), step), :]
    both = jnp.concatenate([full[...], agg[...]], axis=1)
    total = None
    for j in range(groups):
        at = pl.ds(j * units, units)
        pre = mm(both, w_one[:, at])
        slope[:, at] = gelu_slope(pre)
        out = gelu(pre).astype(BF16)
        hidden[:, at] = out
        spread = mm(a_ref[:, :own], out)
        part[:, at] = spread[:own] + spread[own:]
        term = mm_nt(w_two[:pad, at], out)
        total = term if total is None else total + term
    logits[...] = total
    mine[...] = hidden[:, pl.ds(pl.multiple_of(ids[0] * units, units), units)]


def second_kernel(
    groups, class_count, grad_scale, ids, a_ref, source, landed, w_one, w_two, part, logits, labels,
    turned, mine, loss, kept, packed, agg,
):
    own = part.shape[0]
    units = mine.shape[1]
    pad = logits.shape[0]
    chunk = min(own, landed.shape[0])
    total = logits[...]
    for j in range(groups):
        at = pl.ds(j * units, units)

        def one(r, held, at=at):
            rows = pl.ds(pl.multiple_of(r * chunk, chunk), chunk)
            srcs = pl.ds(pl.multiple_of(own + r * chunk, BLOCK), chunk)
            both = jnp.concatenate([source[rows, :], landed[rows, :]], axis=1)
            out = gelu(mm(both, w_one[:, at])).astype(BF16)
            spread = mm(a_ref[:, srcs], out)
            return held + spread[:own] + spread[own:]

        if landed.shape[0] == chunk:
            held = one(0, part[:, at])
        else:
            held = lax.fori_loop(0, landed.shape[0] // chunk, one, part[:, at])
        rounded = held.astype(BF16)
        agg[:, at] = rounded
        total = total + mm_nt(w_two[pad:, at], rounded)
    class_id = lax.broadcasted_iota(jnp.int32, total.shape, 0)
    real = class_id < class_count
    top = jnp.max(jnp.where(real, total, -jnp.inf), axis=0, keepdims=True)
    shifted = total - top
    powers = jnp.where(real, jnp.exp(shifted), 0.0)
    sums = jnp.sum(powers, axis=0, keepdims=True)
    target = (class_id == labels[...]).astype(F32)
    row_loss = jnp.log(sums) - jnp.sum(shifted * target, axis=0, keepdims=True)
    loss[...] = jnp.broadcast_to(jnp.sum(row_loss, axis=1, keepdims=True), loss.shape)
    grads = ((powers / sums - target) * grad_scale).astype(BF16)
    turned[...] = grads
    back = mm(grads, a_ref[:own, :])
    kept[...] = back[:, :own]
    packed[...] = back[:, own:].T.astype(BF16)
    mine[...] = agg[:, pl.ds(pl.multiple_of(ids[0] * units, units), units)]


def cut(rows, lanes, parts):
    across = lanes // BLOCK
    down = parts // across
    height = rows // down
    return [(slice(p % down * height, (p % down + 1) * height), slice(p // down * BLOCK, (p // down + 1) * BLOCK)) for p in range(parts)]


def weight_grads_kernel(class_count, parts, turned, self_rows, agg_rows, loss, out, *scratch):
    own_grads = mm(turned[...], self_rows[...])
    row = lax.broadcasted_iota(jnp.int32, own_grads.shape, 0)
    own_grads = jnp.where(row == class_count, loss[0:1, 0:1], own_grads)
    agg_grads = mm(turned[...], agg_rows[...])
    units = own_grads.shape[1]
    if not parts:
        out[:, :units] = own_grads
        out[:, units:] = agg_grads
        return
    (both,) = scratch
    both[:, :units] = own_grads
    both[:, units:] = agg_grads
    for p, (rows, lanes) in enumerate(cut(*both.shape, parts)):
        out[p] = both[rows, lanes]


def direct_kernel(turned, kept, w_two, out):
    pad = turned.shape[0]
    high, low = halves(kept[...].T)
    rows = turned[...].T
    for j in range(out.shape[1] // 256):
        at = pl.ds(j * 256, 256)
        out[:, at] = mm(rows, w_two[:pad, at]) + mm(high, w_two[pad:, at]) + mm(low, w_two[pad:, at])


def back_kernel(parts, pick, direct, slope, w_two, left, landed, out):
    pad = w_two.shape[0] // 2
    high, low = halves(mm_tn(pick[...], landed[...]))
    for j in range(direct.shape[1] // 256):
        at = pl.ds(j * 256, 256)
        total = direct[:, at] + mm(high, w_two[pad:, at]) + mm(low, w_two[pad:, at])
        grads = mm(left[...], (total * slope[:, at]).astype(BF16))
        if parts:
            width = out.shape[2]
            for i in range(256 // width):
                out[j * 256 // width + i] = grads[:, i * width : (i + 1) * width]
        else:
            out[:, at] = grads


def sum_kernel(pieces, out):
    total = pieces[0]
    for k in range(1, pieces.shape[0]):
        total = total + pieces[k]
    for k in range(out.shape[0]):
        out[k] = total


def place_kernel(class_count, node_total, first, second, self1, neigh1, self2, neigh2, loss, both):
    step = self1.shape[0]
    width = first.shape[2]
    for p in range(first.shape[0]):
        self1[:, pl.ds(p * width, width)] = first[p, pl.ds(0, step), :]
        neigh1[:, pl.ds(p * width, width)] = first[p, pl.ds(step, step), :]
    for p, (rows, lanes) in enumerate(cut(*both.shape, second.shape[0])):
        both[rows, lanes] = second[p]
    units = self2.shape[1]
    self2[...] = both[:class_count, :units]
    neigh2[...] = both[:class_count, units:]
    loss[...] = both[class_count : class_count + 1, 0:1] / node_total


def swap(value, count):
    blocks = value.reshape(count, -1, value.shape[-1])
    return lax.all_to_all(blocks, "node", 0, 0, tiled=True)


def gather_shifted(value, count):
    return [value] + [lax.ppermute(value, "feat", [(i, (i + k) % count) for i in range(count)]) for k in range(1, count)]


def shards(features, send_rows, send_count, tile_src, tile_val, labels, w_self1, w_neigh1, w_self2, w_neigh2):
    nodes, groups = lax.axis_size("node"), lax.axis_size("feat")
    own, step = features.shape
    slots = send_rows.shape[2]
    halo = nodes * slots
    total_src = own + halo
    cols = step * groups
    width = w_self1.shape[1]
    units, classes = w_self2.shape
    pad = -(-(classes + 1) // 16) * 16
    across = 2 * units // BLOCK
    parts = nodes if nodes % across == 0 and pad % (8 * (nodes // across)) == 0 and width % (nodes * BLOCK) == 0 else 0
    node_total = own * nodes
    grad_scale = 1.0 / math.sqrt(node_total)
    ids = lax.axis_index("feat").astype(jnp.int32).reshape(1)

    turned = features.T
    turned_all = gather_shifted(turned, groups)
    (packed_weights,) = call(
        weights_pack_kernel,
        [((2 * step * groups + 2 * pad, units), BF16)],
        (w_self1, w_neigh1, w_self2.T, w_neigh2.T),
        [VMEM] * 4,
        moved=4 * 2**20,
    )
    weights = lax.all_gather(packed_weights, "feat")
    pick, full, packed = call(
        functools.partial(pack_kernel, groups),
        [((halo, own), BF16), ((own, cols), BF16), ((halo, cols), BF16)],
        (ids, send_count, send_rows[0], *turned_all),
        [SMEM] * 2 + [VMEM] * (1 + groups),
        [((cols, own), BF16)],
        flops=2 * halo * own * cols,
        moved=halo * own * 2,
    )
    source = swap(packed, nodes).reshape(halo, cols)
    (a_mat,) = call(
        prepare_kernel,
        [((2 * own, total_src), BF16)],
        (tile_src, tile_val),
        [SMEM, VMEM],
        [((own, total_src), F32)],
        moved=tile_val.size * 8,
    )
    agg, packed = call(
        first_kernel,
        [((own, cols), BF16), ((halo, cols), BF16)],
        (pick, a_mat, full, source),
        [VMEM] * 4,
        flops=4 * own * total_src * cols,
        moved=4 * own * total_src,
    )
    landed = swap(packed, nodes).reshape(halo, cols)
    w_one, w_two, slope, part, logits, mine, left = call(
        own_kernel,
        [
            ((2 * cols, width), BF16),
            ((2 * pad, width), BF16),
            ((own, width), F32),
            ((own, width), F32),
            ((pad, own), F32),
            ((own, units), BF16),
            ((2 * step, own), BF16),
        ],
        (ids, full, agg, a_mat, turned, weights),
        [SMEM] + [VMEM] * 5,
        [((own, width), BF16), ((cols, own), BF16)],
        flops=8 * own * own * width,
        moved=16 * own * width,
    )
    turned_grads, agg_mine, loss, kept, packed = call(
        functools.partial(second_kernel, groups, classes, grad_scale),
        [((pad, own), BF16), ((own, units), BF16), ((8, 128), F32), ((pad, own), F32), ((halo, pad), BF16)],
        (ids, a_mat, source, landed, w_one, w_two, part, logits, labels.reshape(1, own)),
        [SMEM] + [VMEM] * 8,
        [((own, width), BF16)],
        flops=4 * own * halo * width,
        moved=12 * own * width,
    )
    landed = swap(packed, nodes).reshape(halo, pad)
    shape = (parts, pad * 2 * units // (BLOCK * parts), BLOCK) if parts else (pad, 2 * units)
    (grads2,) = call(
        functools.partial(weight_grads_kernel, classes, parts),
        [(shape, F32)],
        (turned_grads, mine, agg_mine, loss),
        [VMEM] * 4,
        [((pad, 2 * units), F32)] if parts else [],
        flops=4 * pad * own * units,
        moved=4 * own * units,
    )
    if parts:
        grads2 = swap(grads2, nodes)
    (direct,) = call(
        direct_kernel,
        [((own, width), F32)],
        (turned_grads, kept, w_two),
        [VMEM] * 3,
        flops=6 * own * pad * width,
        moved=8 * own * width,
    )
    (grads1,) = call(
        functools.partial(back_kernel, parts),
        [((parts, 2 * step, width // parts) if parts else (2 * step, width), F32)],
        (pick, direct, slope, w_two, left, landed),
        [VMEM] * 6,
        flops=6 * own * pad * width,
        moved=12 * own * width,
    )
    if not parts:
        grads1, grads2 = lax.psum((grads1, grads2), "node")
        loss = grads2[classes, 0] / node_total
        return (loss, grads1[:step], grads1[step:], grads2[:classes, :units].T, grads2[:classes, units:].T)
    first = swap(grads1, nodes)
    (second,) = call(sum_kernel, [(grads2.shape, F32)], (grads2,), [VMEM], moved=2**20)
    second = swap(second, nodes)
    (first,) = call(sum_kernel, [(first.shape, F32)], (first,), [VMEM], moved=2**20)
    first = swap(first, nodes)
    grad_self1, grad_neigh1, grad_self2, grad_neigh2, loss = call(
        functools.partial(place_kernel, classes, node_total),
        [((step, width), F32)] * 2 + [((classes, units), F32)] * 2 + [((1, 1), F32)],
        (first, second),
        [VMEM] * 2,
        [((pad, 2 * units), F32)],
    )
    return (loss.reshape(()), grad_self1, grad_neigh1, grad_self2.T, grad_neigh2.T)


def solution(mesh):
    in_specs = (
        P("node", "feat"),
        P("node", None, None),
        P("node", None),
        P("node", None),
        P("node", None, None, None),
        P("node"),
        P("feat", None),
        P("feat", None),
        P("feat", None),
        P("feat", None),
    )
    out_specs = (P(), P("feat", None), P("feat", None), P("feat", None), P("feat", None))
    return jax.shard_map(shards, mesh=mesh, in_specs=in_specs, out_specs=out_specs, check_vma=False)
```

time: 161 us -> 143 us (0.89)
  starting transfers between devices: 66.8 us -> 29.2 us
  local copies, waits for them, and re-layouts: 7.5 us -> 30.8 us
  Pallas kernels: 38.8 us -> 20.7 us
  blocking collectives: 0 us -> 14.3 us
  waiting for transfers between devices: 30 us -> 32.7 us
  between operations: 16.4 us -> 14.2 us
    ppermute x50 -> x3, starting transfers between devices: 66.8 us -> 3.23 us  [gather_shifted(): lax.ppermute(value, 'feat', [(i, (i + k) % count) for i in range(count)])]
    all_to_all x0 -> x6, waiting for transfers between devices: none -> 29 us  [swap(): return lax.all_to_all(blocks, 'node', 0, 0, tiled=True)]
    unnamed x109 -> x70, local copies, waits for them, and re-layouts: 4.7 us -> 30.8 us
    all_to_all x0 -> x6, starting transfers between devices: none -> 26 us  [swap(): return lax.all_to_all(blocks, 'node', 0, 0, tiled=True)]
    pallas_call x10 -> x12, Pallas kernels: 38.8 us -> 20.7 us  [call(): pl.pallas_call(body, out_shape=[jax.ShapeDtypeStruct(shape, dtype) for sh...]
    psum x1 -> x0, waiting for transfers between devices: 15.2 us -> none  [shards(): grad_self2, grad_neigh2 = lax.psum((grad_self2, grad_neigh2), 'node')]
    all_to_all x0 -> x1, blocking collectives: none -> 14.3 us  [swap(): return lax.all_to_all(blocks, 'node', 0, 0, tiled=True)]
    ppermute x50 -> x3, waiting for transfers between devices: 14.8 us -> 3.67 us  [gather_shifted(): lax.ppermute(value, 'feat', [(i, (i + k) % count) for i in range(count)])]
  transfers between devices with their start and end apart: 51 -> 10, of which waited for: 13 -> 8; matrix products, arithmetic and copies ran while one was open for 0% -> 0% of each run, Pallas kernels for 18% -> 8%
where the time goes in v2:
time: 143 us; the launch traced here: 142 us
  waiting for transfers between devices  32.7 us (23%)
  local copies, waits for them, and re-layouts  30.8 us (22%)
  starting transfers between devices  29.2 us (20%)
  Pallas kernels  20.7 us (14%)
  blocking collectives  14.3 us (10%)
  between operations  14.2 us (10%)
    unnamed x70, local copies, waits for them, and re-layouts  30.8 us
    all_to_all x6, waiting for transfers between devices, swap(): return lax.all_to_all(blocks, 'node', 0, 0, tiled=True)  29 us
    all_to_all x6, starting transfers between devices, swap(): return lax.all_to_all(blocks, 'node', 0, 0, tiled=True)  26 us
    pallas_call x12, Pallas kernels, call(): pl.pallas_call(body, out_shape=[jax.ShapeDtypeStruct(shape, dtype) for sh...  20.7 us
    all_to_all x1, blocking collectives, swap(): return lax.all_to_all(blocks, 'node', 0, 0, tiled=True)  14.3 us
    ppermute x3, waiting for transfers between devices, gather_shifted(): lax.ppermute(value, 'feat', [(i, (i + k) % count) for i in range(count)])  3.67 us
    ppermute x3, starting transfers between devices, gather_shifted(): lax.ppermute(value, 'feat', [(i, (i + k) % count) for i in range(count)])  3.23 us
  transfers between devices with their start and end apart: 10, of which 8 were waited for; matrix products, arithmetic and copies ran while one was open for 0% of the time, Pallas kernels for 8%

profile of v2, /device:TPU:0, one launch (start us, length us, event | category | flops | bytes accessed | tf_op | source)
XLA Modules:
  0.0 141.9 jit_solution(16856981701764860309)
XLA Ops:
  11.4 2.4 %collective-permute-start.2 = (bf16[32,512]{1,0:T(8,128)(2,1)}, bf16[32,512]{1,0:T(8,128)(2,1)S(1)}, u32[]{:S(2)}, u32[]{:S(2)}) collective-permute-start(bf16[32,512]{1,0:T(8,128)(2,1)} %bitcast.23), channel_id=1, source_target_pairs={{0,3},{1,0},{2,1},{3,2},{4,7},{5,4},{6,5},{7,6},{8,11},{9,8},{10,9... | collective-permute-start | bytes 98312 | tf_op jit(solution)/shard_map/ppermute | solution.py:282
  15.8 2.4 %collective-permute-done.1.refs_2_ = bf16[32,512]{1,0:T(8,128)(2,1)S(1)} collective-permute-done((bf16[32,512]{1,0:T(8,128)(2,1)}, bf16[32,512]{1,0:T(8,128)(2,1)S(1)}, u32[]{:S(2)}, u32[]{:S(2)}) %collective-permute-start.1) | collective-permute-done | bytes 32800 | tf_op jit(solution)/shard_map/ppermute | solution.py:282
  20.4 1.6 %shard_map.137 = (bf16[512,512]{1,0:T(8,128)(2,1)S(1)}, bf16[512,128]{1,0:T(8,128)(2,1)S(1)}, bf16[512,128]{1,0:T(8,128)(2,1)}) custom-call(s32[1]{0:T(128)} %bitcast.ids, s32[1,8]{1,0:T(1,128)S(1)} %copy-done.34, s32[8,64]{1,0:T(8,128)S(1)} %bitcast.28, bf16[32,512]{1,0:T(8,128)(2,1)S(1)} %bitcast.26, bf16[32,512]{1,0:T(8,128)(2,1)S(1)} %collective-permute-done.refs_1_, ...), custom_call_target="tpu_custom_call" | custom-call | flops 67108864 | bytes 524288 | tf_op jit(solution)/shard_map/pallas_call | solution.py:59
  22.1 5.8 %all-to-all-start = ((bf16[8,64,128]{2,1,0:T(8,128)(2,1)}), bf16[8,64,128]{2,1,0:T(8,128)(2,1)S(1)}, u32[]{:S(2)}, u32[]{:S(2)}) async-start(bf16[8,64,128]{2,1,0:T(8,128)(2,1)} %bitcast.3), calls=%async_computation | async-start | bytes 262144 | tf_op jit(solution)/shard_map/all_to_all | solution.py:278
  27.9 1.6 %copy-done.4 = bf16[4,16,128,128]{3,2,1,0:T(8,128)(2,1)S(1)} copy-done((bf16[4,16,128,128]{3,2,1,0:T(8,128)(2,1)S(1)}, bf16[4,16,128,128]{3,2,1,0:T(8,128)(2,1)}, u32[]{:S(2)}) %copy-start.4) | copy-done | bytes 2097176
  30.2 2.2 %shard_map.138.a_ref = bf16[1024,1024]{1,0:T(8,128)(2,1)S(1)} custom-call(s32[4,16]{1,0:T(4,128)S(1)} %copy-done.26, bf16[4,16,128,128]{3,2,1,0:T(8,128)(2,1)S(1)} %copy-done.4), custom_call_target="tpu_custom_call" | custom-call | bytes 8388608 | tf_op jit(solution)/shard_map/pallas_call | solution.py:59
  32.4 2.9 %all-to-all-done = bf16[8,64,128]{2,1,0:T(8,128)(2,1)S(1)} async-done(((bf16[8,64,128]{2,1,0:T(8,128)(2,1)}), bf16[8,64,128]{2,1,0:T(8,128)(2,1)S(1)}, u32[]{:S(2)}, u32[]{:S(2)}) %all-to-all-start) | async-done | bytes 131104 | tf_op jit(solution)/shard_map/all_to_all | solution.py:278
  35.3 1.8 %shard_map.139 = (bf16[512,128]{1,0:T(8,128)(2,1)S(1)}, bf16[512,128]{1,0:T(8,128)(2,1)}) custom-call(bf16[512,512]{1,0:T(8,128)(2,1)S(1)} %get-tuple-element.27.pick, bf16[1024,1024]{1,0:T(8,128)(2,1)S(1)} %shard_map.138.a_ref, bf16[512,128]{1,0:T(8,128)(2,1)S(1)} %get-tuple-element.29.full, bf16[512,128]{1,0:T(8,128)(2,1)S(1)} %bitcast.16), custom_call_target="tpu_custom_call" | custom-call | flops 268435456 | bytes 2097152 | tf_op jit(solution)/shard_map/pallas_call | solution.py:59
  37.7 4.0 %all-to-all-start.1 = ((bf16[8,64,128]{2,1,0:T(8,128)(2,1)}), bf16[8,64,128]{2,1,0:T(8,128)(2,1)}, u32[]{:S(2)}, u32[]{:S(2)}) async-start(bf16[8,64,128]{2,1,0:T(8,128)(2,1)} %bitcast.5), calls=%async_computation.1 | async-start | bytes 262144 | tf_op jit(solution)/shard_map/all_to_all | solution.py:278
  45.6 3.1 %shard_map.141 = (bf16[256,1024]{1,0:T(8,128)(2,1)S(1)}, bf16[352,1024]{1,0:T(8,128)(2,1)S(1)}, f32[512,1024]{1,0:T(8,128)S(1)}, f32[512,1024]{1,0:T(8,128)S(1)}...) custom-call(s32[1]{0:T(128)} %bitcast.ids, bf16[512,128]{1,0:T(8,128)(2,1)S(1)} %copy-done.21, ...), custom_call_target="tpu_custom_call" | custom-call | flops 2147483648 | bytes 8388608 | tf_op jit(solution)/shard_map/pallas_call | solution.py:59
  50.1 1.4 copy-done.2
  53.8 1.6 %copy-done.3 = f32[512,1024]{1,0:T(8,128)S(1)} copy-done((f32[512,1024]{1,0:T(8,128)S(1)}, f32[512,1024]{1,0:T(8,128)}, u32[]{:S(2)}) %copy-start.3) | copy-done | bytes 2097176
  57.4 4.7 %shard_map.142 = (bf16[176,512]{1,0:T(8,128)(2,1)S(1)}, bf16[512,256]{1,0:T(8,128)(2,1)S(1)}, f32[8,128]{1,0:T(8,128)S(1)}, f32[176,512]{1,0:T(8,128)S(1)}, bf16[512,176]{1,0:T(8,128)(2,1)S(1)}) custom-call(s32[1]{0:T(128)} %bitcast.ids, bf16[1024,1024]{1,0:T(8,128)(2,1)S(1)} %shard_map.138.a_ref, bf16[512,128]{1,0:T(8,128)(2,1)S(1)} %bitcast.17, ...), custom_call_target="tpu_custom_call" | custom-call | flops 1073741824 | bytes 6291456 | tf_op jit(solution)/shard_map/pallas_call | solution.py:59
  65.0 5.9 %all-to-all-start.2 = ((bf16[8,64,176]{2,1,0:T(8,128)(2,1)}), bf16[8,64,176]{2,1,0:T(8,128)(2,1)}, u32[]{:S(2)}, u32[]{:S(2)}) async-start(bf16[8,64,176]{2,1,0:T(8,128)(2,1)} %bitcast.18), calls=%async_computation.2 | async-start | bytes 524288 | tf_op jit(solution)/shard_map/all_to_all | solution.py:278
  73.8 5.4 %all-to-all-done.2 = bf16[8,64,176]{2,1,0:T(8,128)(2,1)} async-done(((bf16[8,64,176]{2,1,0:T(8,128)(2,1)}), bf16[8,64,176]{2,1,0:T(8,128)(2,1)}, u32[]{:S(2)}, u32[]{:S(2)}) %all-to-all-start.2) | async-done | bytes 180256 | tf_op jit(solution)/shard_map/all_to_all | solution.py:278
  79.2 1.6 %copy-done.1 = f32[512,1024]{1,0:T(8,128)S(1)} copy-done((f32[512,1024]{1,0:T(8,128)S(1)}, f32[512,1024]{1,0:T(8,128)}, u32[]{:S(2)}) %copy-start.1) | copy-done | bytes 2097176
  80.8 2.8 %shard_map.144 = f32[8,64,128]{2,1,0:T(8,128)S(1)} custom-call(bf16[512,512]{1,0:T(8,128)(2,1)S(1)} %get-tuple-element.27.pick, f32[512,1024]{1,0:T(8,128)S(1)} %shard_map.143.direct, f32[512,1024]{1,0:T(8,128)S(1)} %copy-done.1, bf16[352,1024]{1,0:T(8,128)(2,1)S(1)} %get-tuple-element.33.w_two, bf16[64,512]{1,0:T(8,128)(2,1)S(1)} %get-tuple-element.39.left, ...), custom_call_target="tpu_custom_call" | custom-call | flops 553648128 | bytes 6291456 | tf_op jit(solution)/shard_map/pallas_call | solution.py:59
  84.3 3.4 %all-to-all-start.3 = ((f32[8,64,128]{2,1,0:T(8,128)}), f32[8,64,128]{2,1,0:T(8,128)S(1)}, u32[]{:S(2)}, u32[]{:S(2)}) async-start(f32[8,64,128]{2,1,0:T(8,128)} %copy-done.5), calls=%async_computation.3 | async-start | bytes 524288 | tf_op jit(solution)/shard_map/all_to_all | solution.py:278
  91.6 4.3 %all-to-all-done.3.pieces = f32[8,64,128]{2,1,0:T(8,128)S(1)} async-done(((f32[8,64,128]{2,1,0:T(8,128)}), f32[8,64,128]{2,1,0:T(8,128)S(1)}, u32[]{:S(2)}, u32[]{:S(2)}) %all-to-all-start.3) | async-done | bytes 262176 | tf_op jit(solution)/shard_map/all_to_all | solution.py:278
  95.9 3.4 %all-to-all-start.5 = ((f32[8,88,128]{2,1,0:T(8,128)}), f32[8,88,128]{2,1,0:T(8,128)S(1)}, u32[]{:S(2)}, u32[]{:S(2)}) async-start(f32[8,88,128]{2,1,0:T(8,128)} %shard_map.146), calls=%async_computation.5 | async-start | bytes 720896 | tf_op jit(solution)/shard_map/all_to_all | solution.py:278
  100.1 8.1 %all-to-all-done.5.pieces = f32[8,88,128]{2,1,0:T(8,128)S(1)} async-done(((f32[8,88,128]{2,1,0:T(8,128)}), f32[8,88,128]{2,1,0:T(8,128)S(1)}, u32[]{:S(2)}, u32[]{:S(2)}) %all-to-all-start.5) | async-done | bytes 360480 | tf_op jit(solution)/shard_map/all_to_all | solution.py:278
  108.3 3.4 %all-to-all-start.4 = ((f32[8,64,128]{2,1,0:T(8,128)}), f32[8,64,128]{2,1,0:T(8,128)S(1)}, u32[]{:S(2)}, u32[]{:S(2)}) async-start(f32[8,64,128]{2,1,0:T(8,128)} %shard_map.145), calls=%async_computation.4 | async-start | bytes 524288 | tf_op jit(solution)/shard_map/all_to_all | solution.py:278
  111.7 8.2 %all-to-all-done.4.first = f32[8,64,128]{2,1,0:T(8,128)S(1)} async-done(((f32[8,64,128]{2,1,0:T(8,128)}), f32[8,64,128]{2,1,0:T(8,128)S(1)}, u32[]{:S(2)}, u32[]{:S(2)}) %all-to-all-start.4) | async-done | bytes 262176 | tf_op jit(solution)/shard_map/all_to_all | solution.py:278
  119.9 14.3 %all_to_all.35.second = f32[8,88,128]{2,1,0:T(8,128)S(1)} all-to-all(f32[8,88,128]{2,1,0:T(8,128)S(1)} %shard_map.147), channel_id=1, replica_groups=mesh['node'=8,'feat'=4] {'node'}, dimensions={0} | all-to-all | bytes 720896 | tf_op jit(solution)/shard_map/all_to_all | solution.py:278
  (80 shorter events, 31.2 us)
Async XLA Ops:
  7.2 34.6 %all-gather.3.cloned.1.call-start = ((), (), s32[]{:S(2)}) async-start(), calls=%async_computation.7 | async-start | bytes 1556480 | tf_op jit(solution)/shard_map/all_gather | solution.py:310
  11.4 4.4 %collective-permute-start.2 = (bf16[32,512]{1,0:T(8,128)(2,1)}, bf16[32,512]{1,0:T(8,128)(2,1)S(1)}, u32[]{:S(2)}, u32[]{:S(2)}) collective-permute-start(bf16[32,512]{1,0:T(8,128)(2,1)} %bitcast.23), channel_id=1, source_target_pairs={{0,3},{1,0},{2,1},{3,2},{4,7},{5,4},{6,5},{7,6},{8,11},{9,8},{10,9... | collective-permute-start | bytes 98312 | tf_op jit(solution)/shard_map/ppermute | solution.py:282
  13.9 4.4 %collective-permute-start.1 = (bf16[32,512]{1,0:T(8,128)(2,1)}, bf16[32,512]{1,0:T(8,128)(2,1)S(1)}, u32[]{:S(2)}, u32[]{:S(2)}) collective-permute-start(bf16[32,512]{1,0:T(8,128)(2,1)} %bitcast.24), channel_id=1, source_target_pairs={{0,2},{1,3},{2,0},{3,1},{4,6},{5,7},{6,4},{7,5},{8,10},{9,11},{10,... | collective-permute-start | bytes 98312 | tf_op jit(solution)/shard_map/ppermute | solution.py:282
  14.5 3.8 %collective-permute-start = (bf16[32,512]{1,0:T(8,128)(2,1)}, bf16[32,512]{1,0:T(8,128)(2,1)S(1)}, u32[]{:S(2)}, u32[]{:S(2)}) collective-permute-start(bf16[32,512]{1,0:T(8,128)(2,1)} %bitcast.25), channel_id=1, source_target_pairs={{0,1},{1,2},{2,3},{3,0},{4,5},{5,6},{6,7},{7,4},{8,9},{9,10},{10,1... | collective-permute-start | bytes 98312 | tf_op jit(solution)/shard_map/ppermute | solution.py:282
  22.1 13.2 %copy-start.20 = (bf16[512,128]{1,0:T(8,128)(2,1)}, bf16[512,128]{1,0:T(8,128)(2,1)S(1)}, u32[]{:S(2)}) copy-start(bf16[512,128]{1,0:T(8,128)(2,1)S(1)} %get-tuple-element.29.full) | copy-start | bytes 393220
  22.1 13.2 %all-to-all-start = ((bf16[8,64,128]{2,1,0:T(8,128)(2,1)}), bf16[8,64,128]{2,1,0:T(8,128)(2,1)S(1)}, u32[]{:S(2)}, u32[]{:S(2)}) async-start(bf16[8,64,128]{2,1,0:T(8,128)(2,1)} %bitcast.3), calls=%async_computation | async-start | bytes 262144 | tf_op jit(solution)/shard_map/all_to_all | solution.py:278
  27.9 1.6 %copy-start.4 = (bf16[4,16,128,128]{3,2,1,0:T(8,128)(2,1)S(1)}, bf16[4,16,128,128]{3,2,1,0:T(8,128)(2,1)}, u32[]{:S(2)}) copy-start(bf16[4,16,128,128]{3,2,1,0:T(8,128)(2,1)} %tile_val.1) | copy-start | bytes 6291460
  37.7 16.0 %all-to-all-start.1 = ((bf16[8,64,128]{2,1,0:T(8,128)(2,1)}), bf16[8,64,128]{2,1,0:T(8,128)(2,1)}, u32[]{:S(2)}, u32[]{:S(2)}) async-start(bf16[8,64,128]{2,1,0:T(8,128)(2,1)} %bitcast.5), calls=%async_computation.1 | async-start | bytes 262144 | tf_op jit(solution)/shard_map/all_to_all | solution.py:278
  42.7 1.3 copy-start.28
  45.6 8.1 %copy-start.27 = (s32[512]{0:T(512)S(1)}, s32[512]{0:T(512)}, u32[]{:S(2)}) copy-start(s32[512]{0:T(512)} %param.15) | copy-start | bytes 6148
  48.8 1.3 copy-start
  50.1 1.4 copy-start.2
  53.8 1.6 %copy-start.3 = (f32[512,1024]{1,0:T(8,128)S(1)}, f32[512,1024]{1,0:T(8,128)}, u32[]{:S(2)}) copy-start(f32[512,1024]{1,0:T(8,128)} %copy-done.2) | copy-start | bytes 6291460
  55.4 1.0 copy-start.10
  56.4 1.0 copy-start.14
  65.0 14.2 %all-to-all-start.2 = ((bf16[8,64,176]{2,1,0:T(8,128)(2,1)}), bf16[8,64,176]{2,1,0:T(8,128)(2,1)}, u32[]{:S(2)}, u32[]{:S(2)}) async-start(bf16[8,64,176]{2,1,0:T(8,128)(2,1)} %bitcast.18), calls=%async_computation.2 | async-start | bytes 524288 | tf_op jit(solution)/shard_map/all_to_all | solution.py:278
  71.8 1.0 copy-start.12
  79.2 1.6 %copy-start.1 = (f32[512,1024]{1,0:T(8,128)S(1)}, f32[512,1024]{1,0:T(8,128)}, u32[]{:S(2)}) copy-start(f32[512,1024]{1,0:T(8,128)} %copy-done) | copy-start | bytes 6291460
  84.3 11.6 %all-to-all-start.3 = ((f32[8,64,128]{2,1,0:T(8,128)}), f32[8,64,128]{2,1,0:T(8,128)S(1)}, u32[]{:S(2)}, u32[]{:S(2)}) async-start(f32[8,64,128]{2,1,0:T(8,128)} %copy-done.5), calls=%async_computation.3 | async-start | bytes 524288 | tf_op jit(solution)/shard_map/all_to_all | solution.py:278
  87.8 0.9 copy-start.8
  88.7 0.9 copy-start.17
  89.6 0.9 copy-start.19
  95.9 12.3 %all-to-all-start.5 = ((f32[8,88,128]{2,1,0:T(8,128)}), f32[8,88,128]{2,1,0:T(8,128)S(1)}, u32[]{:S(2)}, u32[]{:S(2)}) async-start(f32[8,88,128]{2,1,0:T(8,128)} %shard_map.146), calls=%async_computation.5 | async-start | bytes 720896 | tf_op jit(solution)/shard_map/all_to_all | solution.py:278
  108.3 11.7 %all-to-all-start.4 = ((f32[8,64,128]{2,1,0:T(8,128)}), f32[8,64,128]{2,1,0:T(8,128)S(1)}, u32[]{:S(2)}, u32[]{:S(2)}) async-start(f32[8,64,128]{2,1,0:T(8,128)} %shard_map.145), calls=%async_computation.4 | async-start | bytes 524288 | tf_op jit(solution)/shard_map/all_to_all | solution.py:278
  (21 other events, 16.2 us)
Sparse Core Ops, SparseCore 0:
  11.6 20.5 all-gather.2

commit v3 on v2

v3 whole, which is shorter than its diff:
```python
import functools
import math

import jax
import jax.numpy as jnp
from jax import lax
from jax.experimental import pallas as pl
from jax.experimental.pallas import tpu as pltpu
from jax.sharding import PartitionSpec as P

BLOCK = 128
F32 = jnp.float32
BF16 = jnp.bfloat16
VMEM = pl.BlockSpec(memory_space=pltpu.VMEM)
HBM = pl.BlockSpec(memory_space=pltpu.HBM)
SMEM = pl.BlockSpec(memory_space=pltpu.SMEM)


def mm(a, b):
    return lax.dot_general(a, b, (((1,), (0,)), ((), ())), preferred_element_type=F32)


def mm_nt(a, b):
    return lax.dot_general(a, b, (((1,), (1,)), ((), ())), preferred_element_type=F32)


def mm_tn(a, b):
    return lax.dot_general(a, b, (((0,), (0,)), ((), ())), preferred_element_type=F32)


def halves(value):
    high = value.astype(BF16)
    return high, (value - high.astype(F32)).astype(BF16)


def gelu_parts(v):
    inner = math.sqrt(2.0 / math.pi) * (v + 0.044715 * (v * v * v))
    t = jnp.tanh(inner)
    return 0.5 * (1.0 + t), t


def gelu(v):
    return v * gelu_parts(v)[0]


def gelu_slope(v):
    cdf, t = gelu_parts(v)
    inner_slope = math.sqrt(2.0 / math.pi) * (1.0 + 3 * 0.044715 * (v * v))
    return cdf + 0.5 * v * (1.0 - t * t) * inner_slope


def call(body, outs, args, scratch, copies, flops=0, moved=0, out_specs=None):
    return pl.pallas_call(
        body,
        out_shape=[jax.ShapeDtypeStruct(shape, dtype) for shape, dtype in outs],
        in_specs=[SMEM if arg.dtype == jnp.int32 and arg.size < 512 else HBM for arg in args],
        out_specs=out_specs or [HBM] * len(outs),
        scratch_shapes=[pltpu.VMEM(shape, dtype) for shape, dtype in scratch] + [pltpu.SemaphoreType.DMA((copies,))],
        compiler_params=pltpu.CompilerParams(vmem_limit_bytes=58 * 2**20),
        cost_estimate=pl.CostEstimate(flops=flops, bytes_accessed=moved, transcendentals=0),
    )(*args)


class Copies:
    def __init__(self, sems):
        self.sems, self.used, self.open = sems, 0, []

    def __call__(self, src, dst):
        copy = pltpu.make_async_copy(src, dst, self.sems.at[self.used])
        copy.start()
        self.used += 1
        return copy

    def later(self, src, dst):
        self.open.append(self(src, dst))

    def finish(self):
        for copy in self.open:
            copy.wait()


def prepare_kernel(tile_src, count, tile_val, send_rows, a_out, pick_out, tiles, rows_in, dense, a_ref, pick, sems):
    copies = Copies(sems)
    blocks, per_block = tile_val.shape[0], tile_val.shape[1]
    own = blocks * BLOCK
    rows_copy = copies(send_rows, rows_in)
    tile_copies = [copies(tile_val.at[b], tiles.at[b]) for b in range(blocks)]
    dense[...] = jnp.zeros_like(dense)
    rows_copy.wait()
    dests, slots = rows_in.shape
    columns = rows_in[...].astype(F32).T
    row_id = lax.broadcasted_iota(jnp.int32, (slots, own), 1).astype(F32)
    slot_id = lax.broadcasted_iota(jnp.int32, (slots, own), 0)
    for d in range(dests):
        hit = (columns[:, d : d + 1] == row_id) & (slot_id < count[0, d])
        pick[pl.ds(d * slots, slots), :] = jnp.where(hit, 1.0, 0.0).astype(BF16)
    copies.later(pick, pick_out)
    for b in range(blocks):
        rows = pl.ds(b * BLOCK, BLOCK)
        low_rows = pl.ds(own + b * BLOCK, BLOCK)
        tile_copies[b].wait()

        def add(k, _, b=b, rows=rows):
            at = pl.ds(pl.multiple_of(tile_src[b, k] * BLOCK, BLOCK), BLOCK)
            dense[rows, at] = dense[rows, at] + tiles[b, k].astype(F32)
            return 0

        lax.fori_loop(0, per_block, add, 0)
        high, low = halves(dense[rows, :])
        a_ref[rows, :] = high
        a_ref[low_rows, :] = low
        copies.later(a_ref.at[rows], a_out.at[rows])
        copies.later(a_ref.at[low_rows], a_out.at[low_rows])
    copies.finish()


def pack_kernel(
    groups, ids, pick_in, w_self1, w_neigh1, w_self2, w_neigh2, *refs
):
    pieces = refs[:groups]
    full_out, packed_out, weights_out, pick, turned, full, packed, firsts, seconds, weights, sems = refs[groups:]
    copies = Copies(sems)
    step = pieces[0].shape[0]
    classes, units = w_self2.shape
    base = 2 * step * groups
    pad = (weights.shape[0] - base) // 2
    loads = [copies(pick_in, pick)]
    for k, piece in enumerate(pieces):
        group = lax.rem(ids[0] + groups - k, groups)
        loads.append(copies(piece, turned.at[pl.ds(pl.multiple_of(group * step, step), step)]))
    w_loads = [copies(w_self1, firsts.at[0]), copies(w_neigh1, firsts.at[1]), copies(w_self2, seconds.at[0]), copies(w_neigh2, seconds.at[1])]
    weights[pl.ds(base, 2 * pad), :] = jnp.zeros((2 * pad, units), BF16)
    for load in loads:
        load.wait()
    rows = turned[...].T
    full[...] = rows
    copies.later(full, full_out)
    packed[...] = mm(pick[...], rows).astype(BF16)
    copies.later(packed, packed_out)
    for load in w_loads:
        load.wait()
    for j in range(groups):
        at = pl.ds(j * units, units)
        weights[pl.ds(2 * step * j, step), :] = firsts[0, :, at]
        weights[pl.ds(2 * step * j + step, step), :] = firsts[1, :, at]
    weights[pl.ds(base, classes), :] = seconds[0]
    weights[pl.ds(base + pad, classes), :] = seconds[1]
    copies.later(weights, weights_out)
    copies.finish()


def first_kernel(pick_in, a_in, full_in, source_in, agg_out, packed_out, pick, a_ref, full, source, agg, packed, sems):
    copies = Copies(sems)
    own, total = full.shape[0], a_ref.shape[1]
    front, rest = pl.ds(0, own), pl.ds(own, total - own)
    loads = [
        copies(full_in, full),
        copies(a_in.at[:, front], a_ref.at[:, front]),
        copies(source_in, source),
        copies(a_in.at[:, rest], a_ref.at[:, rest]),
        copies(pick_in, pick),
    ]
    loads[0].wait()
    loads[1].wait()
    both = mm(a_ref[:, :own], full[...])
    loads[2].wait()
    loads[3].wait()
    both = both + mm(a_ref[:, own:], source[...])
    agg[...] = (both[:own] + both[own:]).astype(BF16)
    copies.later(agg, agg_out)
    loads[4].wait()
    packed[...] = mm(pick[...], agg[...]).astype(BF16)
    copies.later(packed, packed_out)
    copies.finish()


def own_kernel(
    ids, full_in, agg_in, a_in, turned_in, weights_in,
    w_one_out, w_two_out, slope_out, part_out, logits_out, mine_out, left_out,
    full, agg, a_ref, left, weights, w_one, w_two, slope, part, logits, hidden, agg_turned, sems,
):
    copies = Copies(sems)
    groups, _, units = weights.shape
    own, cols = full.shape
    step = turned_in.shape[0]
    pad = logits.shape[0]
    base = 2 * step * groups
    loads = [
        copies(weights_in, weights),
        copies(full_in, full),
        copies(agg_in, agg),
        copies(a_in.at[:, pl.ds(0, own)], a_ref),
        copies(turned_in, left.at[pl.ds(0, step)]),
    ]
    loads[0].wait()
    for g in range(groups):
        for j in range(groups):
            w_one[j, pl.ds(g * step, step), :] = weights[g, pl.ds(2 * step * j, step), :]
            w_one[j, pl.ds(cols + g * step, step), :] = weights[g, pl.ds(2 * step * j + step, step), :]
        w_two[g] = weights[g, pl.ds(base, 2 * pad), :]
    copies.later(w_one, w_one_out)
    copies.later(w_two, w_two_out)
    loads[1].wait()
    loads[2].wait()
    agg_turned[...] = agg[...].T
    loads[4].wait()
    left[pl.ds(step, step), :] = agg_turned[pl.ds(pl.multiple_of(ids[0] * step, step), step), :]
    copies.later(left, left_out)
    both = jnp.concatenate([full[...], agg[...]], axis=1)
    total = None
    for j in range(groups):
        pre = mm(both, w_one[j])
        slope[j] = gelu_slope(pre)
        copies.later(slope.at[j], slope_out.at[j])
        out = gelu(pre).astype(BF16)
        hidden[j] = out
        if j == 0:
            loads[3].wait()
        spread = mm(a_ref[...], out)
        part[j] = spread[:own] + spread[own:]
        copies.later(part.at[j], part_out.at[j])
        term = mm_nt(w_two[j, :pad], out)
        total = term if total is None else total + term
    logits[...] = total
    copies.later(logits, logits_out)
    copies.later(hidden.at[ids[0]], mine_out)
    copies.finish()


def second_kernel(
    class_count, grad_scale, ids, a_in, source_in, landed_in, w_one_in, w_two_in, part_in, logits_in, labels_in,
    turned_out, mine_out, loss_out, kept_out, packed_out,
    a_ref, source, landed, w_one, w_two, part, logits, labels, turned, loss, kept, packed, agg, sems,
):
    copies = Copies(sems)
    groups, own, units = part.shape
    pad = logits.shape[0]
    halo = landed.shape[0]
    slots = halo // packed.shape[0]
    chunk = min(own, halo)
    loads = [
        copies(source_in, source),
        copies(landed_in, landed),
        copies(w_one_in, w_one),
        copies(a_in.at[:, pl.ds(own, halo)], a_ref.at[:, pl.ds(own, halo)]),
        copies(logits_in, logits),
        copies(w_two_in, w_two),
        copies(labels_in, labels),
        copies(a_in.at[pl.ds(0, own), pl.ds(0, own)], a_ref.at[pl.ds(0, own), pl.ds(0, own)]),
    ]
    part_loads = [copies(part_in.at[j], part.at[j]) for j in range(groups)]
    for load in loads[:3]:
        load.wait()
    total = None
    for j in range(groups):

        def one(r, held, j=j):
            rows = pl.ds(pl.multiple_of(r * chunk, chunk), chunk)
            srcs = pl.ds(pl.multiple_of(own + r * chunk, BLOCK), chunk)
            both = jnp.concatenate([source[rows, :], landed[rows, :]], axis=1)
            out = gelu(mm(both, w_one[j])).astype(BF16)
            if j == 0 and halo == chunk:
                loads[3].wait()
            spread = mm(a_ref[:, srcs], out)
            spread = spread[:own] + spread[own:]
            if halo == chunk:
                part_loads[j].wait()
                return part[j] + spread
            return held + spread

        if halo == chunk:
            held = one(0, None)
        else:
            if j == 0:
                loads[3].wait()
            part_loads[j].wait()
            held = lax.fori_loop(0, halo // chunk, one, part[j])
        agg[j] = held.astype(BF16)
        if j == 0:
            loads[4].wait()
            loads[5].wait()
            total = logits[...]
        total = total + mm_nt(w_two[j, pad:], agg[j])
    copies.later(agg.at[ids[0]], mine_out)
    class_id = lax.broadcasted_iota(jnp.int32, total.shape, 0)
    real = class_id < class_count
    top = jnp.max(jnp.where(real, total, -jnp.inf), axis=0, keepdims=True)
    shifted = total - top
    powers = jnp.where(real, jnp.exp(shifted), 0.0)
    sums = jnp.sum(powers, axis=0, keepdims=True)
    loads[6].wait()
    target = (class_id == labels[...]).astype(F32)
    turned[...] = ((powers / sums - target) * grad_scale).astype(BF16)
    copies.later(turned, turned_out)
    loads[7].wait()
    back = mm(turned[...], a_ref[:own, own:]).T.astype(BF16)
    for d in range(packed.shape[0]):
        put_message(packed, d, back[d * slots : (d + 1) * slots])
    copies.later(packed, packed_out)
    kept[...] = mm(turned[...], a_ref[:own, :own])
    copies.later(kept, kept_out)
    row_loss = jnp.log(sums) - jnp.sum(shifted * target, axis=0, keepdims=True)
    loss[...] = jnp.broadcast_to(jnp.sum(row_loss, axis=1, keepdims=True), loss.shape)
    copies.later(loss, loss_out)
    copies.finish()


def message_shape(slots, pad):
    compact = BLOCK < pad <= BLOCK + BLOCK // 2 and slots % 32 == 0
    return (slots + slots // 2, BLOCK) if compact else (slots, pad)


def put_message(packed, d, rows):
    slots, pad = rows.shape
    if packed.shape[1:] == (slots, pad):
        packed[d] = rows
        return
    half, tail = slots // 2, pad - BLOCK
    packed[d, :slots, :] = rows[:, :BLOCK]
    filler = jnp.zeros((half, BLOCK // 2 - tail), BF16)
    packed[d, slots:, :] = jnp.concatenate([rows[:half, BLOCK:], filler, rows[half:, BLOCK:], filler], axis=1)


def take_message(packed, d, landed):
    slots, pad = landed.shape[0] // packed.shape[0], landed.shape[1]
    if packed.shape[1:] == (slots, pad):
        landed[pl.ds(d * slots, slots), :] = packed[d]
        return
    half, tail = slots // 2, pad - BLOCK
    landed[pl.ds(d * slots, slots), :BLOCK] = packed[d, :slots, :]
    landed[pl.ds(d * slots, half), BLOCK:] = packed[d, slots:, :tail]
    landed[pl.ds(d * slots + half, half), BLOCK:] = packed[d, slots:, BLOCK // 2 : BLOCK // 2 + tail]


def cut(rows, lanes, parts):
    across = lanes // BLOCK
    down = parts // across
    height = rows // down
    return [(slice(p % down * height, (p % down + 1) * height), slice(p // down * BLOCK, (p // down + 1) * BLOCK)) for p in range(parts)]


def middle_kernel(
    class_count, parts, turned_in, self_in, agg_in, loss_in, kept_in, w_two_in,
    second_out, direct_out,
    turned, self_rows, agg_rows, loss, kept, w_two, both, direct, sems,
):
    copies = Copies(sems)
    loads = [
        copies(turned_in, turned),
        copies(kept_in, kept),
        copies(w_two_in, w_two),
        copies(self_in, self_rows),
        copies(agg_in, agg_rows),
        copies(loss_in, loss),
    ]
    pad = turned.shape[0]
    units = self_rows.shape[1]
    loads[0].wait()
    loads[1].wait()
    high, low = halves(kept[...].T)
    rows = turned[...].T
    loads[2].wait()
    for j in range(direct.shape[0]):
        direct[j] = mm(rows, w_two[j, :pad]) + mm(high, w_two[j, pad:]) + mm(low, w_two[j, pad:])
        copies.later(direct.at[j], direct_out.at[j])
    for load in loads[3:]:
        load.wait()
    own_grads = mm(turned[...], self_rows[...])
    row = lax.broadcasted_iota(jnp.int32, own_grads.shape, 0)
    both[:, :units] = jnp.where(row == class_count, loss[0:1, 0:1], own_grads)
    both[:, units:] = mm(turned[...], agg_rows[...])
    if parts:
        for p, (rows, lanes) in enumerate(cut(*both.shape, parts)):
            copies.later(both.at[rows, lanes], second_out.at[p])
    else:
        copies.later(both, second_out)
    copies.finish()


def back_kernel(
    parts, pick_in, direct_in, slope_in, w_two_in, left_in, landed_in, second_in, out,
    pick, direct, slope, w_two, left, landed, rows, grads, sems,
):
    copies = Copies(sems)
    step = left.shape[0]
    groups, _, units = direct.shape
    pad = landed.shape[1] if w_two.ndim == 2 else w_two.shape[1] // 2
    loads = [copies(landed_in, landed), copies(pick_in, pick), copies(w_two_in, w_two)]
    both_loads = [(copies(direct_in.at[j], direct.at[j]), copies(slope_in.at[j], slope.at[j])) for j in range(groups)]
    left_load = copies(left_in, left)
    if parts:
        copies.later(second_in, out.at[:, pl.ds(step, second_in.shape[1])])
    loads[0].wait()
    for d in range(landed.shape[0]):
        take_message(landed, d, rows)
    loads[1].wait()
    high, low = halves(mm_tn(pick[...], rows[...]))
    loads[2].wait()
    for j in range(groups):
        for load in both_loads[j]:
            load.wait()
        total = direct[j] + mm(high, w_two[j, pad:]) + mm(low, w_two[j, pad:])
        if j == 0:
            left_load.wait()
        grads[j] = mm(left[...], (total * slope[j]).astype(BF16))
        if parts:
            width = BLOCK
            for i in range(units // width):
                copies.later(grads.at[j, :, pl.ds(i * width, width)], out.at[j * units // width + i, pl.ds(0, step)])
        else:
            copies.later(grads.at[j], out.at[:, pl.ds(j * units, units)])
    copies.finish()


def sum_kernel(pieces_in, out, pieces, total, sems):
    copies = Copies(sems)
    count = pieces.shape[0]
    loads = [copies(pieces_in.at[k], pieces.at[k]) for k in range(count)]
    for load in loads:
        load.wait()
    held = pieces[0]
    for k in range(1, count):
        held = held + pieces[k]
    total[...] = held
    for k in range(count):
        copies.later(total, out.at[k])
    copies.finish()


def place_kernel(class_count, node_total, pieces, self1, neigh1, self2, neigh2, loss, both, sems):
    copies = Copies(sems)
    step = self1.shape[0]
    loads = []
    for p, (rows, lanes) in enumerate(cut(*both.shape, pieces.shape[0])):
        loads.append(copies(pieces.at[p, pl.ds(2 * step, pieces.shape[1] - 2 * step)], both.at[rows, lanes]))
    for p in range(pieces.shape[0]):
        at = pl.ds(p * BLOCK, BLOCK)
        copies.later(pieces.at[p, pl.ds(0, step)], self1.at[:, at])
        copies.later(pieces.at[p, pl.ds(step, step)], neigh1.at[:, at])
    for load in loads:
        load.wait()
    units = self2.shape[1]
    self2[...] = both[:class_count, :units]
    neigh2[...] = both[:class_count, units:]
    loss[...] = both[class_count : class_count + 1, 0:1] / node_total
    copies.finish()


def swap(value, count):
    blocks = value.reshape(count, -1, value.shape[-1])
    return lax.all_to_all(blocks, "node", 0, 0, tiled=True)


def gather_shifted(value, count):
    return [value] + [lax.ppermute(value, "feat", [(i, (i + k) % count) for i in range(count)]) for k in range(1, count)]


def shards(features, send_rows, send_count, tile_src, tile_val, labels, w_self1, w_neigh1, w_self2, w_neigh2):
    nodes, groups = lax.axis_size("node"), lax.axis_size("feat")
    own, step = features.shape
    slots = send_rows.shape[2]
    halo = nodes * slots
    total_src = own + halo
    cols = step * groups
    width = w_self1.shape[1]
    units, classes = w_self2.shape
    pad = -(-(classes + 1) // 16) * 16
    across = 2 * units // BLOCK
    parts = nodes if nodes % across == 0 and pad % (8 * (nodes // across)) == 0 and width == nodes * BLOCK else 0
    node_total = own * nodes
    grad_scale = 1.0 / math.sqrt(node_total)
    ids = lax.axis_index("feat").astype(jnp.int32).reshape(1)
    blocks = own // BLOCK
    packed_rows = 2 * step * groups + 2 * pad

    turned = features.T
    turned_all = gather_shifted(turned, groups)
    a_mat, pick = call(
        prepare_kernel,
        [((2 * own, total_src), BF16), ((halo, own), BF16)],
        (tile_src, send_count, tile_val, send_rows[0]),
        [(tile_val.shape, BF16), ((nodes, slots), jnp.int32), ((own, total_src), F32), ((2 * own, total_src), BF16), ((halo, own), BF16)],
        2 + 3 * blocks,
        moved=tile_val.size * 4,
    )
    full, packed, packed_weights = call(
        functools.partial(pack_kernel, groups),
        [((own, cols), BF16), ((halo, cols), BF16), ((packed_rows, units), BF16)],
        (ids, pick, w_self1, w_neigh1, w_self2.T, w_neigh2.T, *turned_all),
        [
            ((halo, own), BF16),
            ((cols, own), BF16),
            ((own, cols), BF16),
            ((halo, cols), BF16),
            ((2, step, width), BF16),
            ((2, classes, units), BF16),
            ((packed_rows, units), BF16),
        ],
        8 + groups,
        flops=2 * halo * own * cols,
        moved=halo * own * 2,
    )
    weights = lax.all_gather(packed_weights, "feat")
    source = swap(packed, nodes).reshape(halo, cols)
    agg, packed = call(
        first_kernel,
        [((own, cols), BF16), ((halo, cols), BF16)],
        (pick, a_mat, full, source),
        [((halo, own), BF16), ((2 * own, total_src), BF16), ((own, cols), BF16), ((halo, cols), BF16), ((own, cols), BF16), ((halo, cols), BF16)],
        7,
        flops=4 * own * total_src * cols,
        moved=4 * own * total_src,
    )
    landed = swap(packed, nodes).reshape(halo, cols)
    chunked = (groups, own, units)
    w_one, w_two, slope, part, logits, mine, left = call(
        own_kernel,
        [
            ((groups, 2 * cols, units), BF16),
            ((groups, 2 * pad, units), BF16),
            (chunked, F32),
            (chunked, F32),
            ((pad, own), F32),
            ((own, units), BF16),
            ((2 * step, own), BF16),
        ],
        (ids, full, agg, a_mat, turned, weights),
        [
            ((own, cols), BF16),
            ((own, cols), BF16),
            ((2 * own, own), BF16),
            ((2 * step, own), BF16),
            ((groups, packed_rows, units), BF16),
            ((groups, 2 * cols, units), BF16),
            ((groups, 2 * pad, units), BF16),
            (chunked, F32),
            (chunked, F32),
            ((pad, own), F32),
            (chunked, BF16),
            ((cols, own), BF16),
        ],
        10 + 2 * groups,
        flops=8 * own * own * width,
        moved=16 * own * width,
    )
    message = (nodes, *message_shape(slots, pad))
    turned_grads, agg_mine, loss, kept, packed = call(
        functools.partial(second_kernel, classes, grad_scale),
        [((pad, own), BF16), ((own, units), BF16), ((8, 128), F32), ((pad, own), F32), (message, BF16)],
        (ids, a_mat, source, landed, w_one, w_two, part, logits, labels.reshape(1, own)),
        [
            ((2 * own, total_src), BF16),
            ((halo, cols), BF16),
            ((halo, cols), BF16),
            ((groups, 2 * cols, units), BF16),
            ((groups, 2 * pad, units), BF16),
            (chunked, F32),
            ((pad, own), F32),
            ((1, own), jnp.int32),
            ((pad, own), BF16),
            ((8, 128), F32),
            ((pad, own), F32),
            (message, BF16),
            (chunked, BF16),
        ],
        13 + groups,
        flops=4 * own * halo * width,
        moved=12 * own * width,
    )
    landed = swap(packed, nodes)
    second_shape = (parts, pad * 2 * units // (BLOCK * parts), BLOCK) if parts else (pad, 2 * units)
    second, direct = call(
        functools.partial(middle_kernel, classes, parts),
        [(second_shape, F32), (chunked, F32)],
        (turned_grads, mine, agg_mine, loss, kept, w_two),
        [
            ((pad, own), BF16),
            ((own, units), BF16),
            ((own, units), BF16),
            ((8, 128), F32),
            ((pad, own), F32),
            ((groups, 2 * pad, units), BF16),
            ((pad, 2 * units), F32),
            (chunked, F32),
        ],
        6 + groups + max(parts, 1),
        flops=10 * own * pad * width,
        moved=8 * own * width,
    )
    out_shape = (parts, 2 * step + second_shape[1], BLOCK) if parts else (2 * step, width)
    (grads,) = call(
        functools.partial(back_kernel, parts),
        [(out_shape, F32)],
        (pick, direct, slope, w_two, left, landed, second),
        [
            ((halo, own), BF16),
            (chunked, F32),
            (chunked, F32),
            ((groups, 2 * pad, units), BF16),
            ((2 * step, own), BF16),
            (message, BF16),
            ((halo, pad), BF16),
            ((groups, 2 * step, units), F32),
        ],
        5 + 2 * groups + max(parts, groups),
        flops=6 * own * pad * width,
        moved=12 * own * width,
    )
    if not parts:
        grads, second = lax.psum((grads, second), "node")
        loss = second[classes, 0] / node_total
        return (loss, grads[:step], grads[step:], second[:classes, :units].T, second[:classes, units:].T)
    grads = swap(grads, nodes)
    (grads,) = call(sum_kernel, [(out_shape, F32)], (grads,), [(out_shape, F32), (out_shape[1:], F32)], 2 * nodes, moved=2**20)
    grads = swap(grads, nodes)
    grad_self1, grad_neigh1, grad_self2, grad_neigh2, loss = call(
        functools.partial(place_kernel, classes, node_total),
        [((step, width), F32)] * 2 + [((classes, units), F32)] * 2 + [((1, 1), F32)],
        (grads,),
        [((pad, 2 * units), F32)],
        3 * nodes,
        out_specs=[HBM, HBM, VMEM, VMEM, VMEM],
    )
    return (loss.reshape(()), grad_self1, grad_neigh1, grad_self2.T, grad_neigh2.T)


def solution(mesh):
    in_specs = (
        P("node", "feat"),
        P("node", None, None),
        P("node", None),
        P("node", None),
        P("node", None, None, None),
        P("node"),
        P("feat", None),
        P("feat", None),
        P("feat", None),
        P("feat", None),
    )
    out_specs = (P(), P("feat", None), P("feat", None), P("feat", None), P("feat", None))
    return jax.shard_map(shards, mesh=mesh, in_specs=in_specs, out_specs=out_specs, check_vma=False)
```

time: 143 us -> 139 us (0.972)
  blocking collectives: 14.3 us -> 54 us
  Pallas kernels: 20.7 us -> 51 us
  local copies, waits for them, and re-layouts: 30.8 us -> 1.94 us
  waiting for transfers between devices: 32.7 us -> 6.06 us
  starting transfers between devices: 29.2 us -> 10.9 us
    all_to_all x1 -> x3, blocking collectives: 14.3 us -> 54 us  [swap(): return lax.all_to_all(blocks, 'node', 0, 0, tiled=True)]
    pallas_call x12 -> x9, Pallas kernels: 20.7 us -> 51 us  [call(): pl.pallas_call(body, out_shape=[jax.ShapeDtypeStruct(shape, dtype) for sh...]
    unnamed x70 -> x10, local copies, waits for them, and re-layouts: 30.8 us -> 1.94 us
    all_to_all x6 -> x2, waiting for transfers between devices: 29 us -> 6.02 us  [swap(): return lax.all_to_all(blocks, 'node', 0, 0, tiled=True)]
    all_to_all x6 -> x2, starting transfers between devices: 26 us -> 7.6 us  [swap(): return lax.all_to_all(blocks, 'node', 0, 0, tiled=True)]
    ppermute x3, waiting for transfers between devices: 3.67 us -> 0.01 us  [gather_shifted(): lax.ppermute(value, 'feat', [(i, (i + k) % count) for i in range(count)])]
  transfers between devices with their start and end apart: 10 -> 6, of which waited for: 8 -> 2; matrix products, arithmetic and copies ran while one was open for 0% -> 0% of each run, Pallas kernels for 8% -> 12%
where the time goes in v3:
time: 139 us; the launch traced here: 138 us
  blocking collectives  54 us (39%)
  Pallas kernels  51 us (37%)
  between operations  14.2 us (10%)
  starting transfers between devices  10.9 us (8%)
  waiting for transfers between devices  6.06 us (4%)
  local copies, waits for them, and re-layouts  1.94 us (1%)
    all_to_all x3, blocking collectives, swap(): return lax.all_to_all(blocks, 'node', 0, 0, tiled=True)  54 us
    pallas_call x9, Pallas kernels, call(): pl.pallas_call(body, out_shape=[jax.ShapeDtypeStruct(shape, dtype) for sh...  51 us
    all_to_all x2, starting transfers between devices, swap(): return lax.all_to_all(blocks, 'node', 0, 0, tiled=True)  7.6 us
    all_to_all x2, waiting for transfers between devices, swap(): return lax.all_to_all(blocks, 'node', 0, 0, tiled=True)  6.02 us
    ppermute x3, starting transfers between devices, gather_shifted(): lax.ppermute(value, 'feat', [(i, (i + k) % count) for i in range(count)])  3.23 us
  transfers between devices with their start and end apart: 6, of which 2 were waited for; matrix products, arithmetic and copies ran while one was open for 0% of the time, Pallas kernels for 12%

profile of v3, /device:TPU:0, one launch (start us, length us, event | category | flops | bytes accessed | tf_op | source)
XLA Modules:
  0.0 138.0 jit_solution(94437570698893025)
XLA Ops:
  7.2 0.0 all-gather.3.cloned.1.call-start
  7.2 2.4 %collective-permute-start.2 = (bf16[32,512]{1,0:T(8,128)(2,1)}, bf16[32,512]{1,0:T(8,128)(2,1)S(1)}, u32[]{:S(2)}, u32[]{:S(2)}) collective-permute-start(bf16[32,512]{1,0:T(8,128)(2,1)} %bitcast.21), channel_id=1, source_target_pairs={{0,3},{1,0},{2,1},{3,2},{4,7},{5,4},{6,5},{7,6},{8,11},{9,8},{10,9... | collective-permute-start | bytes 98312 | tf_op jit(solution)/shard_map/ppermute | solution.py:455
  9.6 0.6 collective-permute-start.1
  10.3 0.2 collective-permute-start
  10.4 4.0 %shard_map.137 = (bf16[1024,1024]{1,0:T(8,128)(2,1)}, bf16[512,512]{1,0:T(8,128)(2,1)}) custom-call(s32[4,16]{1,0:T(4,128)} %tile_src.1, s32[1,8]{1,0:T(1,128)} %count.1, bf16[4,16,128,128]{3,2,1,0:T(8,128)(2,1)} %tile_val.1, s32[8,64]{1,0:T(8,128)} %bitcast.26), custom_call_target="tpu_custom_call" | custom-call | bytes 4194304 | tf_op jit(solution)/shard_map/pallas_call | solution.py:53
  14.6 0.6 copy-done.2
  15.1 0.0 copy-done.3
  15.2 2.3 %shard_map.138 = (bf16[512,128]{1,0:T(8,128)(2,1)}, bf16[512,128]{1,0:T(8,128)(2,1)}, bf16[608,256]{1,0:T(8,128)(2,1)}) custom-call(s32[1]{0:T(128)} %bitcast.1.ids, bf16[512,512]{1,0:T(8,128)(2,1)} %get-tuple-element.31.pick_in, bf16[32,1024]{1,0:T(8,128)(2,1)} %w_self1.1, bf16[32,1024]{1,0:T(8,128)(2,1)} %w_neigh1.1, bf16[172,256]{1,0:T(8,128)(2,1)} %bitcast.19, ...), custom_call_target="tpu_custom_call" | custom-call | flops 67108864 | bytes 524288 | tf_op jit(solution)/shard_map/pallas_call | solution.py:53
  17.5 14.1 %all_to_all.25 = bf16[8,64,128]{2,1,0:T(8,128)(2,1)} all-to-all(bf16[8,64,128]{2,1,0:T(8,128)(2,1)} %bitcast.18), channel_id=1, replica_groups=mesh['node'=8,'feat'=4] {'node'}, dimensions={0} | all-to-all | bytes 262144 | tf_op jit(solution)/shard_map/all_to_all | solution.py:451
  31.6 3.7 %shard_map.139 = (bf16[512,128]{1,0:T(8,128)(2,1)}, bf16[512,128]{1,0:T(8,128)(2,1)}) custom-call(bf16[512,512]{1,0:T(8,128)(2,1)} %get-tuple-element.31.pick_in, bf16[1024,1024]{1,0:T(8,128)(2,1)} %get-tuple-element.32.a_in, bf16[512,128]{1,0:T(8,128)(2,1)} %get-tuple-element.34.full_in, bf16[512,128]{1,0:T(8,128)(2,1)} %bitcast.14), custom_call_target="tpu_custom_call" | custom-call | flops 268435456 | bytes 2097152 | tf_op jit(solution)/shard_map/pallas_call | solution.py:53
  35.2 3.4 %all-to-all-start.1 = ((bf16[8,64,128]{2,1,0:T(8,128)(2,1)}), bf16[8,64,128]{2,1,0:T(8,128)(2,1)S(1)}, u32[]{:S(2)}, u32[]{:S(2)}) async-start(bf16[8,64,128]{2,1,0:T(8,128)(2,1)} %bitcast.17), calls=%async_computation.1 | async-start | bytes 262144 | tf_op jit(solution)/shard_map/all_to_all | solution.py:451
  38.6 5.7 %shard_map.140 = (bf16[4,256,256]{2,1,0:T(8,128)(2,1)}, bf16[4,352,256]{2,1,0:T(8,128)(2,1)}, f32[4,512,256]{2,1,0:T(8,128)}, f32[4,512,256]{2,1,0:T(8,128)}, f3...) custom-call(s32[1]{0:T(128)} %bitcast.1.ids, bf16[512,128]{1,0:T(8,128)(2,1)} %get-tuple-element.34.full_in, ...), custom_call_target="tpu_custom_call" | custom-call | flops 2147483648 | bytes 8388608 | tf_op jit(solution)/shard_map/pallas_call | solution.py:53
  44.4 1.7 %all-to-all-done.1 = bf16[8,64,128]{2,1,0:T(8,128)(2,1)S(1)} async-done(((bf16[8,64,128]{2,1,0:T(8,128)(2,1)}), bf16[8,64,128]{2,1,0:T(8,128)(2,1)S(1)}, u32[]{:S(2)}, u32[]{:S(2)}) %all-to-all-start.1) | async-done | bytes 131104 | tf_op jit(solution)/shard_map/all_to_all | solution.py:451
  46.1 0.7 copy-done.1
  46.8 7.3 %shard_map.141 = (bf16[176,512]{1,0:T(8,128)(2,1)}, bf16[512,256]{1,0:T(8,128)(2,1)}, f32[8,128]{1,0:T(8,128)}, f32[176,512]{1,0:T(8,128)}, bf16[8,96,128]{2,1,0:T(8,128)(2,1)}) custom-call(s32[1]{0:T(128)} %bitcast.1.ids, bf16[1024,1024]{1,0:T(8,128)(2,1)} %get-tuple-element.32.a_in, bf16[512,128]{1,0:T(8,128)(2,1)} %bitcast.15, bf16[512,128]{1,0:T(8,128)(2,1)} %bitcast.16, ...), custom_call_target="tpu_custom_call" | custom-call | flops 1073741824 | bytes 6291456 | tf_op jit(solution)/shard_map/pallas_call | solution.py:53
  54.0 4.2 %all-to-all-start.2 = ((bf16[8,96,128]{2,1,0:T(8,128)(2,1)}), bf16[8,96,128]{2,1,0:T(8,128)(2,1)S(1)}, u32[]{:S(2)}, u32[]{:S(2)}) async-start(bf16[8,96,128]{2,1,0:T(8,128)(2,1)} %get-tuple-element.50), calls=%async_computation.2 | async-start | bytes 393216 | tf_op jit(solution)/shard_map/all_to_all | solution.py:451
  58.2 3.6 %shard_map.142 = (f32[8,88,128]{2,1,0:T(8,128)}, f32[4,512,256]{2,1,0:T(8,128)}) custom-call(bf16[176,512]{1,0:T(8,128)(2,1)} %get-tuple-element.42.turned_in, bf16[512,256]{1,0:T(8,128)(2,1)} %get-tuple-element.43.self_in, bf16[512,256]{1,0:T(8,128)(2,1)} %get-tuple-element.44.agg_in, f32[8,128]{1,0:T(8,128)} %get-tuple-element.45.loss_in, ...), custom_call_target="tpu_custom_call" | custom-call | flops 922746880 | bytes 4194304 | tf_op jit(solution)/shard_map/pallas_call | solution.py:53
  61.9 4.3 %all-to-all-done.2.landed_in = bf16[8,96,128]{2,1,0:T(8,128)(2,1)S(1)} async-done(((bf16[8,96,128]{2,1,0:T(8,128)(2,1)}), bf16[8,96,128]{2,1,0:T(8,128)(2,1)S(1)}, u32[]{:S(2)}, u32[]{:S(2)}) %all-to-all-start.2) | async-done | bytes 196640 | tf_op jit(solution)/shard_map/all_to_all | solution.py:451
  66.2 0.7 copy-done
  66.9 12.2 %shard_map.143 = f32[8,152,128]{2,1,0:T(8,128)} custom-call(bf16[512,512]{1,0:T(8,128)(2,1)} %get-tuple-element.31.pick_in, f32[4,512,256]{2,1,0:T(8,128)} %get-tuple-element.47.direct_in, f32[4,512,256]{2,1,0:T(8,128)} %get-tuple-element.48.slope_in, bf16[4,352,256]{2,1,0:T(8,128)(2,1)} %get-tuple-element.39.w_two_in, ...), custom_call_target="tpu_custom_call" | custom-call | flops 553648128 | bytes 6291456 | tf_op jit(solution)/shard_map/pallas_call | solution.py:53
  79.1 20.1 %all_to_all.26.pieces_in = f32[8,152,128]{2,1,0:T(8,128)} all-to-all(f32[8,152,128]{2,1,0:T(8,128)} %shard_map.143), channel_id=1, replica_groups=mesh['node'=8,'feat'=4] {'node'}, dimensions={0} | all-to-all | bytes 1245184 | tf_op jit(solution)/shard_map/all_to_all | solution.py:451
  99.2 2.2 %shard_map.144 = f32[8,152,128]{2,1,0:T(8,128)} custom-call(f32[8,152,128]{2,1,0:T(8,128)} %all_to_all.26.pieces_in), custom_call_target="tpu_custom_call" | custom-call | bytes 1048576 | tf_op jit(solution)/shard_map/pallas_call | solution.py:53
  101.3 19.9 %all_to_all.27.pieces = f32[8,152,128]{2,1,0:T(8,128)} all-to-all(f32[8,152,128]{2,1,0:T(8,128)} %shard_map.144), channel_id=1, replica_groups=mesh['node'=8,'feat'=4] {'node'}, dimensions={0} | all-to-all | bytes 1245184 | tf_op jit(solution)/shard_map/all_to_all | solution.py:451
  121.2 10.0 %shard_map.145 = (f32[32,1024]{1,0:T(8,128)}, f32[32,1024]{1,0:T(8,128)}, f32[172,256]{1,0:T(8,128)}, f32[172,256]{1,0:T(8,128)}, f32[1,1]{1,0:T(1,128)}) custom-call(f32[8,152,128]{2,1,0:T(8,128)} %all_to_all.27.pieces), custom_call_target="tpu_custom_call" | custom-call | tf_op jit(solution)/shard_map/pallas_call | solution.py:53
  (11 shorter events, 0.1 us)
Async XLA Ops:
  7.2 31.5 %all-gather.3.cloned.1.call-start = ((), (), s32[]{:S(2)}) async-start(), calls=%async_computation.5 | async-start | bytes 1556480 | tf_op jit(solution)/shard_map/all_gather | solution.py:503
  7.2 7.3 %collective-permute-start.2 = (bf16[32,512]{1,0:T(8,128)(2,1)}, bf16[32,512]{1,0:T(8,128)(2,1)S(1)}, u32[]{:S(2)}, u32[]{:S(2)}) collective-permute-start(bf16[32,512]{1,0:T(8,128)(2,1)} %bitcast.21), channel_id=1, source_target_pairs={{0,3},{1,0},{2,1},{3,2},{4,7},{5,4},{6,5},{7,6},{8,11},{9,8},{10,9... | collective-permute-start | bytes 98312 | tf_op jit(solution)/shard_map/ppermute | solution.py:455
  9.6 4.9 %collective-permute-start.1 = (bf16[32,512]{1,0:T(8,128)(2,1)}, bf16[32,512]{1,0:T(8,128)(2,1)S(1)}, u32[]{:S(2)}, u32[]{:S(2)}) collective-permute-start(bf16[32,512]{1,0:T(8,128)(2,1)} %bitcast.22), channel_id=1, source_target_pairs={{0,2},{1,3},{2,0},{3,1},{4,6},{5,7},{6,4},{7,5},{8,10},{9,11},{10,... | collective-permute-start | bytes 98312 | tf_op jit(solution)/shard_map/ppermute | solution.py:455
  10.3 4.3 %collective-permute-start = (bf16[32,512]{1,0:T(8,128)(2,1)}, bf16[32,512]{1,0:T(8,128)(2,1)S(1)}, u32[]{:S(2)}, u32[]{:S(2)}) collective-permute-start(bf16[32,512]{1,0:T(8,128)(2,1)} %bitcast.23), channel_id=1, source_target_pairs={{0,1},{1,2},{2,3},{3,0},{4,5},{5,6},{6,7},{7,4},{8,9},{9,10},{10,1... | collective-permute-start | bytes 98312 | tf_op jit(solution)/shard_map/ppermute | solution.py:455
  14.5 0.6 copy-start.2
  14.5 0.6 copy-start.3
  14.6 0.6 copy-start.4
  35.2 10.9 %all-to-all-start.1 = ((bf16[8,64,128]{2,1,0:T(8,128)(2,1)}), bf16[8,64,128]{2,1,0:T(8,128)(2,1)S(1)}, u32[]{:S(2)}, u32[]{:S(2)}) async-start(bf16[8,64,128]{2,1,0:T(8,128)(2,1)} %bitcast.17), calls=%async_computation.1 | async-start | bytes 262144 | tf_op jit(solution)/shard_map/all_to_all | solution.py:451
  46.1 0.7 copy-start.1
  54.0 12.2 %all-to-all-start.2 = ((bf16[8,96,128]{2,1,0:T(8,128)(2,1)}), bf16[8,96,128]{2,1,0:T(8,128)(2,1)S(1)}, u32[]{:S(2)}, u32[]{:S(2)}) async-start(bf16[8,96,128]{2,1,0:T(8,128)(2,1)} %get-tuple-element.50), calls=%async_computation.2 | async-start | bytes 393216 | tf_op jit(solution)/shard_map/all_to_all | solution.py:451
  66.2 0.7 copy-start
Sparse Core Ops, SparseCore 0:
  17.6 19.2 all-gather.2

commit v4 on v3

--- a/solution.py
+++ b/solution.py
@@ -49,14 +49,14 @@
     return cdf + 0.5 * v * (1.0 - t * t) * inner_slope
 
 
-def call(body, outs, args, scratch, copies, flops=0, moved=0, out_specs=None):
+def call(body, outs, args, scratch, copies, flops=0, moved=0, out_specs=None, near=0, room=58):
     return pl.pallas_call(
         body,
         out_shape=[jax.ShapeDtypeStruct(shape, dtype) for shape, dtype in outs],
-        in_specs=[SMEM if arg.dtype == jnp.int32 and arg.size < 512 else HBM for arg in args],
+        in_specs=[SMEM if arg.dtype == jnp.int32 and arg.size < 512 else HBM for arg in args[: len(args) - near]] + [VMEM] * near,
         out_specs=out_specs or [HBM] * len(outs),
         scratch_shapes=[pltpu.VMEM(shape, dtype) for shape, dtype in scratch] + [pltpu.SemaphoreType.DMA((copies,))],
-        compiler_params=pltpu.CompilerParams(vmem_limit_bytes=58 * 2**20),
+        compiler_params=pltpu.CompilerParams(vmem_limit_bytes=room * 2**20),
         cost_estimate=pl.CostEstimate(flops=flops, bytes_accessed=moved, transcendentals=0),
     )(*args)
 
@@ -125,9 +125,10 @@
     base = 2 * step * groups
     pad = (weights.shape[0] - base) // 2
     loads = [copies(pick_in, pick)]
-    for k, piece in enumerate(pieces):
+    loads.append(copies(pieces[0], turned.at[pl.ds(pl.multiple_of(ids[0] * step, step), step)]))
+    for k, piece in enumerate(pieces[1:], 1):
         group = lax.rem(ids[0] + groups - k, groups)
-        loads.append(copies(piece, turned.at[pl.ds(pl.multiple_of(group * step, step), step)]))
+        turned[pl.ds(pl.multiple_of(group * step, step), step), :] = piece[...]
     w_loads = [copies(w_self1, firsts.at[0]), copies(w_neigh1, firsts.at[1]), copies(w_self2, seconds.at[0]), copies(w_neigh2, seconds.at[1])]
     weights[pl.ds(base, 2 * pad), :] = jnp.zeros((2 * pad, units), BF16)
     for load in loads:
@@ -149,26 +150,32 @@
     copies.finish()
 
 
-def first_kernel(pick_in, a_in, full_in, source_in, agg_out, packed_out, pick, a_ref, full, source, agg, packed, sems):
-    copies = Copies(sems)
-    own, total = full.shape[0], a_ref.shape[1]
-    front, rest = pl.ds(0, own), pl.ds(own, total - own)
+def near_kernel(a_in, full_in, out, a_ref, full, near, sems):
+    copies = Copies(sems)
+    own = full.shape[0]
+    loads = [copies(full_in, full), copies(a_in.at[:, pl.ds(0, own)], a_ref)]
+    for load in loads:
+        load.wait()
+    both = mm(a_ref[...], full[...])
+    near[...] = both[:own] + both[own:]
+    copies(near, out).wait()
+
+
+def first_kernel(pick_in, a_in, near_in, source_in, agg_out, packed_out, pick, a_ref, near, source, agg, packed, sems):
+    copies = Copies(sems)
+    own = near.shape[0]
     loads = [
-        copies(full_in, full),
-        copies(a_in.at[:, front], a_ref.at[:, front]),
         copies(source_in, source),
-        copies(a_in.at[:, rest], a_ref.at[:, rest]),
+        copies(a_in.at[:, pl.ds(own, source.shape[0])], a_ref),
+        copies(near_in, near),
         copies(pick_in, pick),
     ]
-    loads[0].wait()
-    loads[1].wait()
-    both = mm(a_ref[:, :own], full[...])
-    loads[2].wait()
+    for load in loads[:3]:
+        load.wait()
+    both = mm(a_ref[...], source[...])
+    agg[...] = (near[...] + both[:own] + both[own:]).astype(BF16)
+    copies.later(agg, agg_out)
     loads[3].wait()
-    both = both + mm(a_ref[:, own:], source[...])
-    agg[...] = (both[:own] + both[own:]).astype(BF16)
-    copies.later(agg, agg_out)
-    loads[4].wait()
     packed[...] = mm(pick[...], agg[...]).astype(BF16)
     copies.later(packed, packed_out)
     copies.finish()
@@ -229,8 +236,8 @@
 
 def second_kernel(
     class_count, grad_scale, ids, a_in, source_in, landed_in, w_one_in, w_two_in, part_in, logits_in, labels_in,
-    turned_out, mine_out, loss_out, kept_out, packed_out,
-    a_ref, source, landed, w_one, w_two, part, logits, labels, turned, loss, kept, packed, agg, sems,
+    turned_out, mine_out, loss_out, packed_out,
+    a_ref, source, landed, w_one, w_two, part, logits, labels, turned, loss, packed, agg, sems,
 ):
     copies = Copies(sems)
     groups, own, units = part.shape
@@ -242,11 +249,10 @@
         copies(source_in, source),
         copies(landed_in, landed),
         copies(w_one_in, w_one),
-        copies(a_in.at[:, pl.ds(own, halo)], a_ref.at[:, pl.ds(own, halo)]),
+        copies(a_in.at[:, pl.ds(own, halo)], a_ref),
         copies(logits_in, logits),
         copies(w_two_in, w_two),
         copies(labels_in, labels),
-        copies(a_in.at[pl.ds(0, own), pl.ds(0, own)], a_ref.at[pl.ds(0, own), pl.ds(0, own)]),
     ]
     part_loads = [copies(part_in.at[j], part.at[j]) for j in range(groups)]
     for load in loads[:3]:
@@ -256,7 +262,7 @@
 
         def one(r, held, j=j):
             rows = pl.ds(pl.multiple_of(r * chunk, chunk), chunk)
-            srcs = pl.ds(pl.multiple_of(own + r * chunk, BLOCK), chunk)
+            srcs = pl.ds(pl.multiple_of(r * chunk, chunk), chunk)
             both = jnp.concatenate([source[rows, :], landed[rows, :]], axis=1)
             out = gelu(mm(both, w_one[j])).astype(BF16)
             if j == 0 and halo == chunk:
@@ -292,16 +298,13 @@
     target = (class_id == labels[...]).astype(F32)
     turned[...] = ((powers / sums - target) * grad_scale).astype(BF16)
     copies.later(turned, turned_out)
-    loads[7].wait()
-    back = mm(turned[...], a_ref[:own, own:]).T.astype(BF16)
+    row_loss = jnp.log(sums) - jnp.sum(shifted * target, axis=0, keepdims=True)
+    loss[...] = jnp.broadcast_to(jnp.sum(row_loss, axis=1, keepdims=True), loss.shape)
+    copies.later(loss, loss_out)
+    back = mm(turned[...], a_ref[:own, :]).T.astype(BF16)
     for d in range(packed.shape[0]):
         put_message(packed, d, back[d * slots : (d + 1) * slots])
     copies.later(packed, packed_out)
-    kept[...] = mm(turned[...], a_ref[:own, :own])
-    copies.later(kept, kept_out)
-    row_loss = jnp.log(sums) - jnp.sum(shifted * target, axis=0, keepdims=True)
-    loss[...] = jnp.broadcast_to(jnp.sum(row_loss, axis=1, keepdims=True), loss.shape)
-    copies.later(loss, loss_out)
     copies.finish()
 
 
@@ -340,14 +343,14 @@
 
 
 def middle_kernel(
-    class_count, parts, turned_in, self_in, agg_in, loss_in, kept_in, w_two_in,
+    class_count, parts, turned_in, self_in, agg_in, loss_in, a_in, w_two_in,
     second_out, direct_out,
-    turned, self_rows, agg_rows, loss, kept, w_two, both, direct, sems,
+    turned, self_rows, agg_rows, loss, a_ref, w_two, both, direct, sems,
 ):
     copies = Copies(sems)
     loads = [
         copies(turned_in, turned),
-        copies(kept_in, kept),
+        copies(a_in.at[pl.ds(0, a_ref.shape[0]), pl.ds(0, a_ref.shape[1])], a_ref),
         copies(w_two_in, w_two),
         copies(self_in, self_rows),
         copies(agg_in, agg_rows),
@@ -357,7 +360,7 @@
     units = self_rows.shape[1]
     loads[0].wait()
     loads[1].wait()
-    high, low = halves(kept[...].T)
+    high, low = halves(mm(turned[...], a_ref[...]).T)
     rows = turned[...].T
     loads[2].wait()
     for j in range(direct.shape[0]):
@@ -389,7 +392,7 @@
     both_loads = [(copies(direct_in.at[j], direct.at[j]), copies(slope_in.at[j], slope.at[j])) for j in range(groups)]
     left_load = copies(left_in, left)
     if parts:
-        copies.later(second_in, out.at[:, pl.ds(step, second_in.shape[1])])
+        second_load = copies(second_in, grads.at[:, pl.ds(step, second_in.shape[1])])
     loads[0].wait()
     for d in range(landed.shape[0]):
         take_message(landed, d, rows)
@@ -402,12 +405,16 @@
         total = direct[j] + mm(high, w_two[j, pad:]) + mm(low, w_two[j, pad:])
         if j == 0:
             left_load.wait()
-        grads[j] = mm(left[...], (total * slope[j]).astype(BF16))
+        result = mm(left[...], (total * slope[j]).astype(BF16))
         if parts:
-            width = BLOCK
-            for i in range(units // width):
-                copies.later(grads.at[j, :, pl.ds(i * width, width)], out.at[j * units // width + i, pl.ds(0, step)])
+            if j == 0:
+                second_load.wait()
+            for i in range(units // BLOCK):
+                p = j * units // BLOCK + i
+                grads[p, :step, :] = result[:, i * BLOCK : (i + 1) * BLOCK]
+                copies.later(grads.at[p], out.at[p])
         else:
+            grads[j] = result
             copies.later(grads.at[j], out.at[:, pl.ds(j * units, units)])
     copies.finish()
 
@@ -496,18 +503,29 @@
             ((2, classes, units), BF16),
             ((packed_rows, units), BF16),
         ],
-        8 + groups,
+        9,
         flops=2 * halo * own * cols,
         moved=halo * own * 2,
+        near=groups - 1,
+        room=12 + halo * own // 2**18,
     )
     weights = lax.all_gather(packed_weights, "feat")
     source = swap(packed, nodes).reshape(halo, cols)
+    (near,) = call(
+        near_kernel,
+        [((own, cols), F32)],
+        (a_mat, full),
+        [((2 * own, own), BF16), ((own, cols), BF16), ((own, cols), F32)],
+        3,
+        flops=4 * own * own * cols,
+        moved=4 * own * own,
+    )
     agg, packed = call(
         first_kernel,
         [((own, cols), BF16), ((halo, cols), BF16)],
-        (pick, a_mat, full, source),
-        [((halo, own), BF16), ((2 * own, total_src), BF16), ((own, cols), BF16), ((halo, cols), BF16), ((own, cols), BF16), ((halo, cols), BF16)],
-        7,
+        (pick, a_mat, near, source),
+        [((halo, own), BF16), ((2 * own, halo), BF16), ((own, cols), F32), ((halo, cols), BF16), ((own, cols), BF16), ((halo, cols), BF16)],
+        6,
         flops=4 * own * total_src * cols,
         moved=4 * own * total_src,
     )
@@ -544,12 +562,12 @@
         moved=16 * own * width,
     )
     message = (nodes, *message_shape(slots, pad))
-    turned_grads, agg_mine, loss, kept, packed = call(
+    turned_grads, agg_mine, loss, packed = call(
         functools.partial(second_kernel, classes, grad_scale),
-        [((pad, own), BF16), ((own, units), BF16), ((8, 128), F32), ((pad, own), F32), (message, BF16)],
+        [((pad, own), BF16), ((own, units), BF16), ((8, 128), F32), (message, BF16)],
         (ids, a_mat, source, landed, w_one, w_two, part, logits, labels.reshape(1, own)),
         [
-            ((2 * own, total_src), BF16),
+            ((2 * own, halo), BF16),
             ((halo, cols), BF16),
             ((halo, cols), BF16),
             ((groups, 2 * cols, units), BF16),
@@ -559,11 +577,10 @@
             ((1, own), jnp.int32),
             ((pad, own), BF16),
             ((8, 128), F32),
-            ((pad, own), F32),
             (message, BF16),
             (chunked, BF16),
         ],
-        13 + groups,
+        11 + groups,
         flops=4 * own * halo * width,
         moved=12 * own * width,
     )
@@ -572,13 +589,13 @@
     second, direct = call(
         functools.partial(middle_kernel, classes, parts),
         [(second_shape, F32), (chunked, F32)],
-        (turned_grads, mine, agg_mine, loss, kept, w_two),
+        (turned_grads, mine, agg_mine, loss, a_mat, w_two),
         [
             ((pad, own), BF16),
             ((own, units), BF16),
             ((own, units), BF16),
             ((8, 128), F32),
-            ((pad, own), F32),
+            ((own, own), BF16),
             ((groups, 2 * pad, units), BF16),
             ((pad, 2 * units), F32),
             (chunked, F32),
@@ -600,7 +617,7 @@
             ((2 * step, own), BF16),
             (message, BF16),
             ((halo, pad), BF16),
-            ((groups, 2 * step, units), F32),
+            (out_shape, F32) if parts else ((groups, 2 * step, units), F32),
         ],
         5 + 2 * groups + max(parts, groups),
         flops=6 * own * pad * width,
@@ -619,7 +636,7 @@
         (grads,),
         [((pad, 2 * units), F32)],
         3 * nodes,
-        out_specs=[HBM, HBM, VMEM, VMEM, VMEM],
+        out_specs=[VMEM] * 5,
     )
     return (loss.reshape(()), grad_self1, grad_neigh1, grad_self2.T, grad_neigh2.T)
 

time: 139 us -> 125 us (0.90)
  blocking collectives: 54 us -> 39.9 us
  Pallas kernels: 51 us -> 37.8 us
  starting transfers between devices: 10.9 us -> 16.9 us
  waiting for transfers between devices: 6.06 us -> 11.3 us
  local copies, waits for them, and re-layouts: 1.94 us -> 3.68 us
    all_to_all x3 -> x2, blocking collectives: 54 us -> 39.9 us  [swap(): return lax.all_to_all(blocks, 'node', 0, 0, tiled=True)]
    pallas_call x9 -> x10, Pallas kernels: 51 us -> 37.8 us  [call(): pl.pallas_call(body, out_shape=[jax.ShapeDtypeStruct(shape, dtype) for sh...]
    all_to_all x2 -> x3, starting transfers between devices: 7.6 us -> 13.6 us  [swap(): return lax.all_to_all(blocks, 'node', 0, 0, tiled=True)]
    all_to_all x2 -> x3, waiting for transfers between devices: 6.02 us -> 11.2 us  [swap(): return lax.all_to_all(blocks, 'node', 0, 0, tiled=True)]
    unnamed x10 -> x20, local copies, waits for them, and re-layouts: 1.94 us -> 3.68 us
  transfers between devices with their start and end apart: 6 -> 7, of which waited for: 2 -> 3; matrix products, arithmetic and copies ran while one was open for 0% -> 0% of each run, Pallas kernels for 12% -> 16%
where the time goes in v4:
time: 125 us; the launch traced here: 124 us
  blocking collectives  39.9 us (32%)
  Pallas kernels  37.8 us (30%)
  starting transfers between devices  16.9 us (14%)
  between operations  14.3 us (11%)
  waiting for transfers between devices  11.3 us (9%)
  local copies, waits for them, and re-layouts  3.68 us (3%)
    all_to_all x2, blocking collectives, swap(): return lax.all_to_all(blocks, 'node', 0, 0, tiled=True)  39.9 us
    pallas_call x10, Pallas kernels, call(): pl.pallas_call(body, out_shape=[jax.ShapeDtypeStruct(shape, dtype) for sh...  37.8 us
    all_to_all x3, starting transfers between devices, swap(): return lax.all_to_all(blocks, 'node', 0, 0, tiled=True)  13.6 us
    all_to_all x3, waiting for transfers between devices, swap(): return lax.all_to_all(blocks, 'node', 0, 0, tiled=True)  11.2 us
    unnamed x20, local copies, waits for them, and re-layouts  3.68 us
    ppermute x3, starting transfers between devices, gather_shifted(): lax.ppermute(value, 'feat', [(i, (i + k) % count) for i in range(count)])  3.23 us
  transfers between devices with their start and end apart: 7, of which 3 were waited for; matrix products, arithmetic and copies ran while one was open for 0% of the time, Pallas kernels for 16%

profile of v4, /device:TPU:0, one launch (start us, length us, event | category | flops | bytes accessed | tf_op | source)
XLA Modules:
  0.0 123.9 jit_solution(2954953728065732953)
XLA Ops:
  7.3 2.4 %collective-permute-start.2 = (bf16[32,512]{1,0:T(8,128)(2,1)}, bf16[32,512]{1,0:T(8,128)(2,1)S(1)}, u32[]{:S(2)}, u32[]{:S(2)}) collective-permute-start(bf16[32,512]{1,0:T(8,128)(2,1)} %bitcast.16), channel_id=1, source_target_pairs={{0,3},{1,0},{2,1},{3,2},{4,7},{5,4},{6,5},{7,6},{8,11},{9,8},{10,9... | collective-permute-start | bytes 98312 | tf_op jit(solution)/shard_map/ppermute | solution.py:462
  10.5 4.0 %shard_map.137 = (bf16[1024,1024]{1,0:T(8,128)(2,1)}, bf16[512,512]{1,0:T(8,128)(2,1)}) custom-call(s32[4,16]{1,0:T(4,128)} %tile_src.1, s32[1,8]{1,0:T(1,128)} %count.1, bf16[4,16,128,128]{3,2,1,0:T(8,128)(2,1)} %tile_val.1, s32[8,64]{1,0:T(8,128)} %bitcast.25), custom_call_target="tpu_custom_call" | custom-call | bytes 4194304 | tf_op jit(solution)/shard_map/pallas_call | solution.py:53
  14.6 1.0 copy-done
  15.7 1.9 %shard_map.138 = (bf16[512,128]{1,0:T(8,128)(2,1)S(1)}, bf16[512,128]{1,0:T(8,128)(2,1)}, bf16[608,256]{1,0:T(8,128)(2,1)}) custom-call(s32[1]{0:T(128)} %bitcast.1.ids, bf16[512,512]{1,0:T(8,128)(2,1)S(1)} %copy-done, bf16[32,1024]{1,0:T(8,128)(2,1)S(1)} %copy-done.4, bf16[32,1024]{1,0:T(8,128)(2,1)S(1)} %copy-done.5, bf16[172,256]{1,0:T(8,128)(2,1)S(1)} %bitcast.14, ...), custom_call_target="tpu_custom_call" | custom-call | flops 67108864 | bytes 524288 | tf_op jit(solution)/shard_map/pallas_call | solution.py:53
  17.6 0.6 copy-done.1
  18.3 5.8 %all-to-all-start = ((bf16[8,64,128]{2,1,0:T(8,128)(2,1)}), bf16[8,64,128]{2,1,0:T(8,128)(2,1)S(1)}, u32[]{:S(2)}, u32[]{:S(2)}) async-start(bf16[8,64,128]{2,1,0:T(8,128)(2,1)} %bitcast.5), calls=%async_computation | async-start | bytes 262144 | tf_op jit(solution)/shard_map/all_to_all | solution.py:458
  24.1 2.5 %shard_map.139.near_in = f32[512,128]{1,0:T(8,128)} custom-call(bf16[1024,1024]{1,0:T(8,128)(2,1)} %get-tuple-element.31.a_in, bf16[512,128]{1,0:T(8,128)(2,1)} %copy-done.1), custom_call_target="tpu_custom_call" | custom-call | flops 134217728 | bytes 1048576 | tf_op jit(solution)/shard_map/pallas_call | solution.py:53
  26.6 5.6 %all-to-all-done = bf16[8,64,128]{2,1,0:T(8,128)(2,1)S(1)} async-done(((bf16[8,64,128]{2,1,0:T(8,128)(2,1)}), bf16[8,64,128]{2,1,0:T(8,128)(2,1)S(1)}, u32[]{:S(2)}, u32[]{:S(2)}) %all-to-all-start) | async-done | bytes 131104 | tf_op jit(solution)/shard_map/all_to_all | solution.py:458
  32.3 0.7 copy-done.7
  32.9 3.0 %shard_map.140 = (bf16[512,128]{1,0:T(8,128)(2,1)}, bf16[512,128]{1,0:T(8,128)(2,1)}) custom-call(bf16[512,512]{1,0:T(8,128)(2,1)} %get-tuple-element.30.pick_in, bf16[1024,1024]{1,0:T(8,128)(2,1)} %get-tuple-element.31.a_in, f32[512,128]{1,0:T(8,128)} %shard_map.139.near_in, bf16[512,128]{1,0:T(8,128)(2,1)} %bitcast.21), custom_call_target="tpu_custom_call" | custom-call | flops 268435456 | bytes 2097152 | tf_op jit(solution)/shard_map/pallas_call | solution.py:53
  36.0 3.4 %all-to-all-start.1 = ((bf16[8,64,128]{2,1,0:T(8,128)(2,1)}), bf16[8,64,128]{2,1,0:T(8,128)(2,1)S(1)}, u32[]{:S(2)}, u32[]{:S(2)}) async-start(bf16[8,64,128]{2,1,0:T(8,128)(2,1)} %bitcast.24), calls=%async_computation.1 | async-start | bytes 262144 | tf_op jit(solution)/shard_map/all_to_all | solution.py:458
  39.4 5.9 %shard_map.141 = (bf16[4,256,256]{2,1,0:T(8,128)(2,1)}, bf16[4,352,256]{2,1,0:T(8,128)(2,1)}, f32[4,512,256]{2,1,0:T(8,128)}, f32[4,512,256]{2,1,0:T(8,128)}, f3...) custom-call(s32[1]{0:T(128)} %bitcast.1.ids, bf16[512,128]{1,0:T(8,128)(2,1)} %copy-done.1, ...), custom_call_target="tpu_custom_call" | custom-call | flops 2147483648 | bytes 8388608 | tf_op jit(solution)/shard_map/pallas_call | solution.py:53
  45.3 1.5 %all-to-all-done.1 = bf16[8,64,128]{2,1,0:T(8,128)(2,1)S(1)} async-done(((bf16[8,64,128]{2,1,0:T(8,128)(2,1)}), bf16[8,64,128]{2,1,0:T(8,128)(2,1)S(1)}, u32[]{:S(2)}, u32[]{:S(2)}) %all-to-all-start.1) | async-done | bytes 131104 | tf_op jit(solution)/shard_map/all_to_all | solution.py:458
  46.8 0.7 copy-done.9
  47.5 7.1 %shard_map.142 = (bf16[176,512]{1,0:T(8,128)(2,1)}, bf16[512,256]{1,0:T(8,128)(2,1)}, f32[8,128]{1,0:T(8,128)}, bf16[8,96,128]{2,1,0:T(8,128)(2,1)}) custom-call(s32[1]{0:T(128)} %bitcast.1.ids, bf16[1024,1024]{1,0:T(8,128)(2,1)} %get-tuple-element.31.a_in, bf16[512,128]{1,0:T(8,128)(2,1)} %bitcast.22, bf16[512,128]{1,0:T(8,128)(2,1)} %bitcast.23, ...), custom_call_target="tpu_custom_call" | custom-call | flops 1073741824 | bytes 6291456 | tf_op jit(solution)/shard_map/pallas_call | solution.py:53
  54.6 4.4 %all-to-all-start.2 = ((bf16[8,96,128]{2,1,0:T(8,128)(2,1)}), bf16[8,96,128]{2,1,0:T(8,128)(2,1)S(1)}, u32[]{:S(2)}, u32[]{:S(2)}) async-start(bf16[8,96,128]{2,1,0:T(8,128)(2,1)} %get-tuple-element.48), calls=%async_computation.2 | async-start | bytes 393216 | tf_op jit(solution)/shard_map/all_to_all | solution.py:458
  59.0 3.9 %shard_map.143 = (f32[8,88,128]{2,1,0:T(8,128)}, f32[4,512,256]{2,1,0:T(8,128)}) custom-call(bf16[176,512]{1,0:T(8,128)(2,1)} %get-tuple-element.41.turned_in, bf16[512,256]{1,0:T(8,128)(2,1)} %get-tuple-element.42.self_in, bf16[512,256]{1,0:T(8,128)(2,1)} %get-tuple-element.43.agg_in, f32[8,128]{1,0:T(8,128)} %get-tuple-element.44.loss_in, ...), custom_call_target="tpu_custom_call" | custom-call | flops 922746880 | bytes 4194304 | tf_op jit(solution)/shard_map/pallas_call | solution.py:53
  62.9 4.1 %all-to-all-done.2.landed_in = bf16[8,96,128]{2,1,0:T(8,128)(2,1)S(1)} async-done(((bf16[8,96,128]{2,1,0:T(8,128)(2,1)}), bf16[8,96,128]{2,1,0:T(8,128)(2,1)S(1)}, u32[]{:S(2)}, u32[]{:S(2)}) %all-to-all-start.2) | async-done | bytes 196640 | tf_op jit(solution)/shard_map/all_to_all | solution.py:458
  67.0 0.7 copy-done.8
  67.7 5.2 %shard_map.144 = f32[8,152,128]{2,1,0:T(8,128)} custom-call(bf16[512,512]{1,0:T(8,128)(2,1)} %get-tuple-element.30.pick_in, f32[4,512,256]{2,1,0:T(8,128)} %get-tuple-element.45.direct_in, f32[4,512,256]{2,1,0:T(8,128)} %get-tuple-element.46.slope_in, bf16[4,352,256]{2,1,0:T(8,128)(2,1)} %get-tuple-element.38.w_two_in, ...), custom_call_target="tpu_custom_call" | custom-call | flops 553648128 | bytes 6291456 | tf_op jit(solution)/shard_map/pallas_call | solution.py:53
  72.9 20.1 %all_to_all.25.pieces_in = f32[8,152,128]{2,1,0:T(8,128)} all-to-all(f32[8,152,128]{2,1,0:T(8,128)} %shard_map.144), channel_id=1, replica_groups=mesh['node'=8,'feat'=4] {'node'}, dimensions={0} | all-to-all | bytes 1245184 | tf_op jit(solution)/shard_map/all_to_all | solution.py:458
  93.0 2.2 %shard_map.145 = f32[8,152,128]{2,1,0:T(8,128)} custom-call(f32[8,152,128]{2,1,0:T(8,128)} %all_to_all.25.pieces_in), custom_call_target="tpu_custom_call" | custom-call | bytes 1048576 | tf_op jit(solution)/shard_map/pallas_call | solution.py:53
  95.2 19.9 %all_to_all.26.pieces = f32[8,152,128]{2,1,0:T(8,128)} all-to-all(f32[8,152,128]{2,1,0:T(8,128)} %shard_map.145), channel_id=1, replica_groups=mesh['node'=8,'feat'=4] {'node'}, dimensions={0} | all-to-all | bytes 1245184 | tf_op jit(solution)/shard_map/all_to_all | solution.py:458
  115.0 2.0 %shard_map.146 = (f32[32,1024]{1,0:T(8,128)}, f32[32,1024]{1,0:T(8,128)}, f32[172,256]{1,0:T(8,128)}, f32[172,256]{1,0:T(8,128)}, f32[1,1]{1,0:T(1,128)}) custom-call(f32[8,152,128]{2,1,0:T(8,128)} %all_to_all.26.pieces), custom_call_target="tpu_custom_call" | custom-call | tf_op jit(solution)/shard_map/pallas_call | solution.py:53
  (23 shorter events, 0.9 us)
Async XLA Ops:
  7.2 7.4 %copy-start.6 = (bf16[512,32]{0,1:T(8,128)(2,1)S(1)}, bf16[512,32]{0,1:T(8,128)(2,1)}, u32[]{:S(2)}) copy-start(bf16[512,32]{0,1:T(8,128)(2,1)} %param.10) | copy-start | bytes 98308
  7.2 7.4 %copy-start.3 = (bf16[256,172]{0,1:T(8,128)(2,1)S(1)}, bf16[256,172]{0,1:T(8,128)(2,1)}, u32[]{:S(2)}) copy-start(bf16[256,172]{0,1:T(8,128)(2,1)} %param.19) | copy-start | bytes 264196
  7.2 7.4 %copy-start.2 = (bf16[256,172]{0,1:T(8,128)(2,1)S(1)}, bf16[256,172]{0,1:T(8,128)(2,1)}, u32[]{:S(2)}) copy-start(bf16[256,172]{0,1:T(8,128)(2,1)} %param.18) | copy-start | bytes 264196
  7.2 7.4 %copy-start.5 = (bf16[32,1024]{1,0:T(8,128)(2,1)S(1)}, bf16[32,1024]{1,0:T(8,128)(2,1)}, u32[]{:S(2)}) copy-start(bf16[32,1024]{1,0:T(8,128)(2,1)} %w_neigh1.1) | copy-start | bytes 196612
  7.2 7.4 %copy-start.4 = (bf16[32,1024]{1,0:T(8,128)(2,1)S(1)}, bf16[32,1024]{1,0:T(8,128)(2,1)}, u32[]{:S(2)}) copy-start(bf16[32,1024]{1,0:T(8,128)(2,1)} %w_self1.1) | copy-start | bytes 196612
  7.2 32.1 %all-gather.3.cloned.1.call-start = ((), (), s32[]{:S(2)}) async-start(), calls=%async_computation.5 | async-start | bytes 1556480 | tf_op jit(solution)/shard_map/all_gather | solution.py:512
  7.3 7.3 %collective-permute-start.2 = (bf16[32,512]{1,0:T(8,128)(2,1)}, bf16[32,512]{1,0:T(8,128)(2,1)S(1)}, u32[]{:S(2)}, u32[]{:S(2)}) collective-permute-start(bf16[32,512]{1,0:T(8,128)(2,1)} %bitcast.16), channel_id=1, source_target_pairs={{0,3},{1,0},{2,1},{3,2},{4,7},{5,4},{6,5},{7,6},{8,11},{9,8},{10,9... | collective-permute-start | bytes 98312 | tf_op jit(solution)/shard_map/ppermute | solution.py:462
  9.7 4.9 %collective-permute-start.1 = (bf16[32,512]{1,0:T(8,128)(2,1)}, bf16[32,512]{1,0:T(8,128)(2,1)S(1)}, u32[]{:S(2)}, u32[]{:S(2)}) collective-permute-start(bf16[32,512]{1,0:T(8,128)(2,1)} %bitcast.17), channel_id=1, source_target_pairs={{0,2},{1,3},{2,0},{3,1},{4,6},{5,7},{6,4},{7,5},{8,10},{9,11},{10,... | collective-permute-start | bytes 98312 | tf_op jit(solution)/shard_map/ppermute | solution.py:462
  10.3 4.2 %collective-permute-start = (bf16[32,512]{1,0:T(8,128)(2,1)}, bf16[32,512]{1,0:T(8,128)(2,1)S(1)}, u32[]{:S(2)}, u32[]{:S(2)}) collective-permute-start(bf16[32,512]{1,0:T(8,128)(2,1)} %bitcast.18), channel_id=1, source_target_pairs={{0,1},{1,2},{2,3},{3,0},{4,5},{5,6},{6,7},{7,4},{8,9},{9,10},{10,1... | collective-permute-start | bytes 98312 | tf_op jit(solution)/shard_map/ppermute | solution.py:462
  14.6 1.0 copy-start
  17.6 0.7 copy-start.1
  18.3 14.0 %all-to-all-start = ((bf16[8,64,128]{2,1,0:T(8,128)(2,1)}), bf16[8,64,128]{2,1,0:T(8,128)(2,1)S(1)}, u32[]{:S(2)}, u32[]{:S(2)}) async-start(bf16[8,64,128]{2,1,0:T(8,128)(2,1)} %bitcast.5), calls=%async_computation | async-start | bytes 262144 | tf_op jit(solution)/shard_map/all_to_all | solution.py:458
  32.3 0.7 copy-start.7
  36.0 10.9 %all-to-all-start.1 = ((bf16[8,64,128]{2,1,0:T(8,128)(2,1)}), bf16[8,64,128]{2,1,0:T(8,128)(2,1)S(1)}, u32[]{:S(2)}, u32[]{:S(2)}) async-start(bf16[8,64,128]{2,1,0:T(8,128)(2,1)} %bitcast.24), calls=%async_computation.1 | async-start | bytes 262144 | tf_op jit(solution)/shard_map/all_to_all | solution.py:458
  46.8 0.7 copy-start.9
  54.6 12.4 %all-to-all-start.2 = ((bf16[8,96,128]{2,1,0:T(8,128)(2,1)}), bf16[8,96,128]{2,1,0:T(8,128)(2,1)S(1)}, u32[]{:S(2)}, u32[]{:S(2)}) async-start(bf16[8,96,128]{2,1,0:T(8,128)(2,1)} %get-tuple-element.48), calls=%async_computation.2 | async-start | bytes 393216 | tf_op jit(solution)/shard_map/all_to_all | solution.py:458
  67.0 0.7 copy-start.8
Sparse Core Ops, SparseCore 0:
  18.4 19.1 all-gather.2

commit v5 on v4

--- a/solution.py
+++ b/solution.py
@@ -49,14 +49,14 @@
     return cdf + 0.5 * v * (1.0 - t * t) * inner_slope
 
 
-def call(body, outs, args, scratch, copies, flops=0, moved=0, out_specs=None, near=0, room=58):
+def call(body, outs, args, scratch, copies, flops=0, moved=0, out_specs=None, near=0):
     return pl.pallas_call(
         body,
         out_shape=[jax.ShapeDtypeStruct(shape, dtype) for shape, dtype in outs],
         in_specs=[SMEM if arg.dtype == jnp.int32 and arg.size < 512 else HBM for arg in args[: len(args) - near]] + [VMEM] * near,
         out_specs=out_specs or [HBM] * len(outs),
         scratch_shapes=[pltpu.VMEM(shape, dtype) for shape, dtype in scratch] + [pltpu.SemaphoreType.DMA((copies,))],
-        compiler_params=pltpu.CompilerParams(vmem_limit_bytes=room * 2**20),
+        compiler_params=pltpu.CompilerParams(vmem_limit_bytes=58 * 2**20),
         cost_estimate=pl.CostEstimate(flops=flops, bytes_accessed=moved, transcendentals=0),
     )(*args)
 
@@ -335,29 +335,27 @@
     landed[pl.ds(d * slots + half, half), BLOCK:] = packed[d, slots:, BLOCK // 2 : BLOCK // 2 + tail]
 
 
-def cut(rows, lanes, parts):
-    across = lanes // BLOCK
-    down = parts // across
-    height = rows // down
-    return [(slice(p % down * height, (p % down + 1) * height), slice(p // down * BLOCK, (p // down + 1) * BLOCK)) for p in range(parts)]
-
-
-def middle_kernel(
-    class_count, parts, turned_in, self_in, agg_in, loss_in, a_in, w_two_in,
-    second_out, direct_out,
-    turned, self_rows, agg_rows, loss, a_ref, w_two, both, direct, sems,
-):
-    copies = Copies(sems)
-    loads = [
-        copies(turned_in, turned),
-        copies(a_in.at[pl.ds(0, a_ref.shape[0]), pl.ds(0, a_ref.shape[1])], a_ref),
-        copies(w_two_in, w_two),
-        copies(self_in, self_rows),
-        copies(agg_in, agg_rows),
-        copies(loss_in, loss),
-    ]
+def second_grads_kernel(class_count, turned_in, self_in, agg_in, loss_in, out, turned, self_rows, agg_rows, loss, both, sems):
+    copies = Copies(sems)
+    loads = [copies(turned_in, turned), copies(self_in, self_rows), copies(loss_in, loss), copies(agg_in, agg_rows)]
+    units = self_rows.shape[1]
+    for load in loads[:3]:
+        load.wait()
+    own_grads = mm(turned[...], self_rows[...])
+    row = lax.broadcasted_iota(jnp.int32, own_grads.shape, 0)
+    both[:, :units] = jnp.where(row == class_count, loss[0:1, 0:1], own_grads)
+    copies.later(both.at[:, pl.ds(0, units)], out.at[:, pl.ds(0, units)])
+    loads[3].wait()
+    both[:, units:] = mm(turned[...], agg_rows[...])
+    copies.later(both.at[:, pl.ds(units, units)], out.at[:, pl.ds(units, units)])
+    copies.finish()
+
+
+def direct_kernel(turned_in, a_in, w_two_in, after, out, turned, a_ref, w_two, direct, sems):
+    copies = Copies(sems)
+    own = a_ref.shape[0]
     pad = turned.shape[0]
-    units = self_rows.shape[1]
+    loads = [copies(turned_in, turned), copies(a_in.at[pl.ds(0, own), pl.ds(0, own)], a_ref), copies(w_two_in, w_two)]
     loads[0].wait()
     loads[1].wait()
     high, low = halves(mm(turned[...], a_ref[...]).T)
@@ -365,34 +363,20 @@
     loads[2].wait()
     for j in range(direct.shape[0]):
         direct[j] = mm(rows, w_two[j, :pad]) + mm(high, w_two[j, pad:]) + mm(low, w_two[j, pad:])
-        copies.later(direct.at[j], direct_out.at[j])
-    for load in loads[3:]:
-        load.wait()
-    own_grads = mm(turned[...], self_rows[...])
-    row = lax.broadcasted_iota(jnp.int32, own_grads.shape, 0)
-    both[:, :units] = jnp.where(row == class_count, loss[0:1, 0:1], own_grads)
-    both[:, units:] = mm(turned[...], agg_rows[...])
-    if parts:
-        for p, (rows, lanes) in enumerate(cut(*both.shape, parts)):
-            copies.later(both.at[rows, lanes], second_out.at[p])
-    else:
-        copies.later(both, second_out)
+        copies.later(direct.at[j], out.at[j])
     copies.finish()
 
 
 def back_kernel(
-    parts, pick_in, direct_in, slope_in, w_two_in, left_in, landed_in, second_in, out,
+    parts, pick_in, direct_in, slope_in, w_two_in, left_in, landed_in, out,
     pick, direct, slope, w_two, left, landed, rows, grads, sems,
 ):
     copies = Copies(sems)
-    step = left.shape[0]
     groups, _, units = direct.shape
-    pad = landed.shape[1] if w_two.ndim == 2 else w_two.shape[1] // 2
+    pad = w_two.shape[1] // 2
     loads = [copies(landed_in, landed), copies(pick_in, pick), copies(w_two_in, w_two)]
     both_loads = [(copies(direct_in.at[j], direct.at[j]), copies(slope_in.at[j], slope.at[j])) for j in range(groups)]
     left_load = copies(left_in, left)
-    if parts:
-        second_load = copies(second_in, grads.at[:, pl.ds(step, second_in.shape[1])])
     loads[0].wait()
     for d in range(landed.shape[0]):
         take_message(landed, d, rows)
@@ -407,11 +391,9 @@
             left_load.wait()
         result = mm(left[...], (total * slope[j]).astype(BF16))
         if parts:
-            if j == 0:
-                second_load.wait()
             for i in range(units // BLOCK):
                 p = j * units // BLOCK + i
-                grads[p, :step, :] = result[:, i * BLOCK : (i + 1) * BLOCK]
+                grads[p] = result[:, i * BLOCK : (i + 1) * BLOCK]
                 copies.later(grads.at[p], out.at[p])
         else:
             grads[j] = result
@@ -434,22 +416,21 @@
     copies.finish()
 
 
-def place_kernel(class_count, node_total, pieces, self1, neigh1, self2, neigh2, loss, both, sems):
+def place_kernel(class_count, node_total, pieces, second, other, self1, neigh1, self2, neigh2, loss, one, two, sems):
     copies = Copies(sems)
     step = self1.shape[0]
-    loads = []
-    for p, (rows, lanes) in enumerate(cut(*both.shape, pieces.shape[0])):
-        loads.append(copies(pieces.at[p, pl.ds(2 * step, pieces.shape[1] - 2 * step)], both.at[rows, lanes]))
+    units = self2.shape[1]
+    loads = [copies(second, one), copies(other, two)]
     for p in range(pieces.shape[0]):
         at = pl.ds(p * BLOCK, BLOCK)
         copies.later(pieces.at[p, pl.ds(0, step)], self1.at[:, at])
         copies.later(pieces.at[p, pl.ds(step, step)], neigh1.at[:, at])
     for load in loads:
         load.wait()
-    units = self2.shape[1]
-    self2[...] = both[:class_count, :units]
-    neigh2[...] = both[:class_count, units:]
-    loss[...] = both[class_count : class_count + 1, 0:1] / node_total
+    self2[...] = one[:class_count, :units] + two[:class_count, :units]
+    neigh2[...] = one[:class_count, units:] + two[:class_count, units:]
+    row = slice(class_count, class_count + 1)
+    loss[...] = (one[row, 0:1] + two[row, 0:1]) / node_total
     copies.finish()
 
 
@@ -472,8 +453,7 @@
     width = w_self1.shape[1]
     units, classes = w_self2.shape
     pad = -(-(classes + 1) // 16) * 16
-    across = 2 * units // BLOCK
-    parts = nodes if nodes % across == 0 and pad % (8 * (nodes // across)) == 0 and width == nodes * BLOCK else 0
+    parts = nodes if nodes % 2 == 0 and width == nodes * BLOCK else 0
     node_total = own * nodes
     grad_scale = 1.0 / math.sqrt(node_total)
     ids = lax.axis_index("feat").astype(jnp.int32).reshape(1)
@@ -507,7 +487,6 @@
         flops=2 * halo * own * cols,
         moved=halo * own * 2,
         near=groups - 1,
-        room=12 + halo * own // 2**18,
     )
     weights = lax.all_gather(packed_weights, "feat")
     source = swap(packed, nodes).reshape(halo, cols)
@@ -585,30 +564,32 @@
         moved=12 * own * width,
     )
     landed = swap(packed, nodes)
-    second_shape = (parts, pad * 2 * units // (BLOCK * parts), BLOCK) if parts else (pad, 2 * units)
-    second, direct = call(
-        functools.partial(middle_kernel, classes, parts),
-        [(second_shape, F32), (chunked, F32)],
-        (turned_grads, mine, agg_mine, loss, a_mat, w_two),
-        [
-            ((pad, own), BF16),
-            ((own, units), BF16),
-            ((own, units), BF16),
-            ((8, 128), F32),
-            ((own, own), BF16),
-            ((groups, 2 * pad, units), BF16),
-            ((pad, 2 * units), F32),
-            (chunked, F32),
-        ],
-        6 + groups + max(parts, 1),
-        flops=10 * own * pad * width,
+    (local_second,) = call(
+        functools.partial(second_grads_kernel, classes),
+        [((pad, 2 * units), F32)],
+        (turned_grads, mine, agg_mine, loss),
+        [((pad, own), BF16), ((own, units), BF16), ((own, units), BF16), ((8, 128), F32), ((pad, 2 * units), F32)],
+        6,
+        flops=4 * own * pad * units,
+        moved=4 * own * units,
+    )
+    second = local_second
+    if parts:
+        second = lax.psum(second, "node", axis_index_groups=[list(range(y, nodes, 2)) for y in range(2)])
+    (direct,) = call(
+        direct_kernel,
+        [(chunked, F32)],
+        (turned_grads, a_mat, w_two, local_second),
+        [((pad, own), BF16), ((own, own), BF16), ((groups, 2 * pad, units), BF16), (chunked, F32)],
+        3 + groups,
+        flops=6 * own * pad * width,
         moved=8 * own * width,
     )
-    out_shape = (parts, 2 * step + second_shape[1], BLOCK) if parts else (2 * step, width)
+    out_shape = (parts, 2 * step, BLOCK) if parts else (2 * step, width)
     (grads,) = call(
         functools.partial(back_kernel, parts),
         [(out_shape, F32)],
-        (pick, direct, slope, w_two, left, landed, second),
+        (pick, direct, slope, w_two, left, landed),
         [
             ((halo, own), BF16),
             (chunked, F32),
@@ -619,7 +600,7 @@
             ((halo, pad), BF16),
             (out_shape, F32) if parts else ((groups, 2 * step, units), F32),
         ],
-        5 + 2 * groups + max(parts, groups),
+        4 + 2 * groups + max(parts, groups),
         flops=6 * own * pad * width,
         moved=12 * own * width,
     )
@@ -630,12 +611,13 @@
     grads = swap(grads, nodes)
     (grads,) = call(sum_kernel, [(out_shape, F32)], (grads,), [(out_shape, F32), (out_shape[1:], F32)], 2 * nodes, moved=2**20)
     grads = swap(grads, nodes)
+    other = lax.ppermute(second, "node", [(i, i ^ 1) for i in range(nodes)])
     grad_self1, grad_neigh1, grad_self2, grad_neigh2, loss = call(
         functools.partial(place_kernel, classes, node_total),
         [((step, width), F32)] * 2 + [((classes, units), F32)] * 2 + [((1, 1), F32)],
-        (grads,),
-        [((pad, 2 * units), F32)],
-        3 * nodes,
+        (grads, second, other),
+        [((pad, 2 * units), F32)] * 2,
+        2 + 2 * nodes,
         out_specs=[VMEM] * 5,
     )
     return (loss.reshape(()), grad_self1, grad_neigh1, grad_self2.T, grad_neigh2.T)

time: 125 us -> 140 us (1.12)
  waiting for transfers between devices: 11.3 us -> 53.6 us
  blocking collectives: 39.9 us -> 0 us
  starting transfers between devices: 16.9 us -> 25.9 us
  Pallas kernels: 37.8 us -> 40.7 us
    all_to_all x2 -> x0, blocking collectives: 39.9 us -> none  [swap(): return lax.all_to_all(blocks, 'node', 0, 0, tiled=True)]
    psum x0 -> x1, waiting for transfers between devices: none -> 28.6 us  [shards(): lax.psum(second, 'node', axis_index_groups=[list(range(y, nodes, 2)) for...]
    all_to_all x3 -> x5, starting transfers between devices: 13.6 us -> 21.1 us  [swap(): return lax.all_to_all(blocks, 'node', 0, 0, tiled=True)]
    ppermute x0 -> x1, waiting for transfers between devices: none -> 7.39 us  [shards(): other = lax.ppermute(second, 'node', [(i, i ^ 1) for i in range(nodes)])]
    all_to_all x3 -> x5, waiting for transfers between devices: 11.2 us -> 16.9 us  [swap(): return lax.all_to_all(blocks, 'node', 0, 0, tiled=True)]
    pallas_call x10 -> x11, Pallas kernels: 37.8 us -> 40.7 us  [call(): pl.pallas_call(body, out_shape=[jax.ShapeDtypeStruct(shape, dtype) for sh...]
    ppermute x0 -> x1, starting transfers between devices: none -> 1.47 us  [shards(): other = lax.ppermute(second, 'node', [(i, i ^ 1) for i in range(nodes)])]
    unnamed x20 -> x18, local copies, waits for them, and re-layouts: 3.68 us -> 4.76 us
  transfers between devices with their start and end apart: 7 -> 11, of which waited for: 3 -> 6; matrix products, arithmetic and copies ran while one was open for 0% -> 0% of each run, Pallas kernels for 16% -> 17%
where the time goes in v5:
time: 140 us; the launch traced here: 139 us
  waiting for transfers between devices  53.6 us (38%)
  Pallas kernels  40.7 us (29%)
  starting transfers between devices  25.9 us (18%)
  between operations  14.2 us (10%)
  local copies, waits for them, and re-layouts  4.76 us (3%)
    pallas_call x11, Pallas kernels, call(): pl.pallas_call(body, out_shape=[jax.ShapeDtypeStruct(shape, dtype) for sh...  40.7 us
    psum x1, waiting for transfers between devices, shards(): lax.psum(second, 'node', axis_index_groups=[list(range(y, nodes, 2)) for...  28.6 us
    all_to_all x5, starting transfers between devices, swap(): return lax.all_to_all(blocks, 'node', 0, 0, tiled=True)  21.1 us
    all_to_all x5, waiting for transfers between devices, swap(): return lax.all_to_all(blocks, 'node', 0, 0, tiled=True)  16.9 us
    ppermute x1, waiting for transfers between devices, shards(): other = lax.ppermute(second, 'node', [(i, i ^ 1) for i in range(nodes)])  7.39 us
    unnamed x18, local copies, waits for them, and re-layouts  4.76 us
    ppermute x3, starting transfers between devices, gather_shifted(): lax.ppermute(value, 'feat', [(i, (i + k) % count) for i in range(count)])  3.23 us
  transfers between devices with their start and end apart: 11, of which 6 were waited for; matrix products, arithmetic and copies ran while one was open for 0% of the time, Pallas kernels for 17%

profile of v5, /device:TPU:0, one launch (start us, length us, event | category | flops | bytes accessed | tf_op | source)
XLA Modules:
  0.0 139.2 jit_solution(1068437637106005120)
XLA Ops:
  7.2 2.4 %collective-permute-start.2 = (bf16[32,512]{1,0:T(8,128)(2,1)}, bf16[32,512]{1,0:T(8,128)(2,1)S(1)}, u32[]{:S(2)}, u32[]{:S(2)}) collective-permute-start(bf16[32,512]{1,0:T(8,128)(2,1)} %bitcast.21), channel_id=1, source_target_pairs={{0,3},{1,0},{2,1},{3,2},{4,7},{5,4},{6,5},{7,6},{8,11},{9,8},{10,9... | collective-permute-start | bytes 98312 | tf_op jit(solution)/shard_map/ppermute | solution.py:443
  10.4 4.1 %shard_map.137 = (bf16[1024,1024]{1,0:T(8,128)(2,1)}, bf16[512,512]{1,0:T(8,128)(2,1)}) custom-call(s32[4,16]{1,0:T(4,128)} %tile_src.1, s32[1,8]{1,0:T(1,128)} %count.1, bf16[4,16,128,128]{3,2,1,0:T(8,128)(2,1)} %tile_val.1, s32[8,64]{1,0:T(8,128)} %bitcast.26), custom_call_target="tpu_custom_call" | custom-call | bytes 4194304 | tf_op jit(solution)/shard_map/pallas_call | solution.py:53
  15.2 3.0 %shard_map.138 = (bf16[512,128]{1,0:T(8,128)(2,1)}, bf16[512,128]{1,0:T(8,128)(2,1)}, bf16[608,256]{1,0:T(8,128)(2,1)}) custom-call(s32[1]{0:T(128)} %bitcast.1.ids, bf16[512,512]{1,0:T(8,128)(2,1)} %get-tuple-element.28.pick_in, bf16[32,1024]{1,0:T(8,128)(2,1)} %w_self1.1, bf16[32,1024]{1,0:T(8,128)(2,1)} %w_neigh1.1, bf16[172,256]{1,0:T(8,128)(2,1)} %bitcast.19, ...), custom_call_target="tpu_custom_call" | custom-call | flops 67108864 | bytes 524288 | tf_op jit(solution)/shard_map/pallas_call | solution.py:53
  18.3 5.8 %all-to-all-start = ((bf16[8,64,128]{2,1,0:T(8,128)(2,1)}), bf16[8,64,128]{2,1,0:T(8,128)(2,1)S(1)}, u32[]{:S(2)}, u32[]{:S(2)}) async-start(bf16[8,64,128]{2,1,0:T(8,128)(2,1)} %bitcast.18), calls=%async_computation | async-start | bytes 262144 | tf_op jit(solution)/shard_map/all_to_all | solution.py:439
  24.1 2.5 %shard_map.139.near_in = f32[512,128]{1,0:T(8,128)} custom-call(bf16[1024,1024]{1,0:T(8,128)(2,1)} %get-tuple-element.29.a_in, bf16[512,128]{1,0:T(8,128)(2,1)} %get-tuple-element.31.full_in), custom_call_target="tpu_custom_call" | custom-call | flops 134217728 | bytes 1048576 | tf_op jit(solution)/shard_map/pallas_call | solution.py:53
  26.6 5.7 %all-to-all-done = bf16[8,64,128]{2,1,0:T(8,128)(2,1)S(1)} async-done(((bf16[8,64,128]{2,1,0:T(8,128)(2,1)}), bf16[8,64,128]{2,1,0:T(8,128)(2,1)S(1)}, u32[]{:S(2)}, u32[]{:S(2)}) %all-to-all-start) | async-done | bytes 131104 | tf_op jit(solution)/shard_map/all_to_all | solution.py:439
  32.9 3.0 %shard_map.140 = (bf16[512,128]{1,0:T(8,128)(2,1)}, bf16[512,128]{1,0:T(8,128)(2,1)}) custom-call(bf16[512,512]{1,0:T(8,128)(2,1)} %get-tuple-element.28.pick_in, bf16[1024,1024]{1,0:T(8,128)(2,1)} %get-tuple-element.29.a_in, f32[512,128]{1,0:T(8,128)} %shard_map.139.near_in, bf16[512,128]{1,0:T(8,128)(2,1)} %bitcast.14), custom_call_target="tpu_custom_call" | custom-call | flops 268435456 | bytes 2097152 | tf_op jit(solution)/shard_map/pallas_call | solution.py:53
  35.9 3.4 %all-to-all-start.1 = ((bf16[8,64,128]{2,1,0:T(8,128)(2,1)}), bf16[8,64,128]{2,1,0:T(8,128)(2,1)S(1)}, u32[]{:S(2)}, u32[]{:S(2)}) async-start(bf16[8,64,128]{2,1,0:T(8,128)(2,1)} %bitcast.17), calls=%async_computation.1 | async-start | bytes 262144 | tf_op jit(solution)/shard_map/all_to_all | solution.py:439
  39.4 6.0 %shard_map.141 = (bf16[4,256,256]{2,1,0:T(8,128)(2,1)}, bf16[4,352,256]{2,1,0:T(8,128)(2,1)}, f32[4,512,256]{2,1,0:T(8,128)}, f32[4,512,256]{2,1,0:T(8,128)}, f3...) custom-call(s32[1]{0:T(128)} %bitcast.1.ids, bf16[512,128]{1,0:T(8,128)(2,1)} %get-tuple-element.31.full_in, ...), custom_call_target="tpu_custom_call" | custom-call | flops 2147483648 | bytes 8388608 | tf_op jit(solution)/shard_map/pallas_call | solution.py:53
  45.4 1.5 %all-to-all-done.1 = bf16[8,64,128]{2,1,0:T(8,128)(2,1)S(1)} async-done(((bf16[8,64,128]{2,1,0:T(8,128)(2,1)}), bf16[8,64,128]{2,1,0:T(8,128)(2,1)S(1)}, u32[]{:S(2)}, u32[]{:S(2)}) %all-to-all-start.1) | async-done | bytes 131104 | tf_op jit(solution)/shard_map/all_to_all | solution.py:439
  47.5 7.1 %shard_map.142 = (bf16[176,512]{1,0:T(8,128)(2,1)}, bf16[512,256]{1,0:T(8,128)(2,1)}, f32[8,128]{1,0:T(8,128)}, bf16[8,96,128]{2,1,0:T(8,128)(2,1)}) custom-call(s32[1]{0:T(128)} %bitcast.1.ids, bf16[1024,1024]{1,0:T(8,128)(2,1)} %get-tuple-element.29.a_in, bf16[512,128]{1,0:T(8,128)(2,1)} %bitcast.15, bf16[512,128]{1,0:T(8,128)(2,1)} %bitcast.16, ...), custom_call_target="tpu_custom_call" | custom-call | flops 1073741824 | bytes 6291456 | tf_op jit(solution)/shard_map/pallas_call | solution.py:53
  54.6 4.5 %all-to-all-start.2 = ((bf16[8,96,128]{2,1,0:T(8,128)(2,1)}), bf16[8,96,128]{2,1,0:T(8,128)(2,1)S(1)}, u32[]{:S(2)}, u32[]{:S(2)}) async-start(bf16[8,96,128]{2,1,0:T(8,128)(2,1)} %get-tuple-element.45), calls=%async_computation.2 | async-start | bytes 393216 | tf_op jit(solution)/shard_map/all_to_all | solution.py:439
  59.1 2.3 %shard_map.143.after = f32[176,512]{1,0:T(8,128)} custom-call(bf16[176,512]{1,0:T(8,128)(2,1)} %get-tuple-element.39.turned_in, bf16[512,256]{1,0:T(8,128)(2,1)} %get-tuple-element.40.self_in, bf16[512,256]{1,0:T(8,128)(2,1)} %get-tuple-element.41.agg_in, f32[8,128]{1,0:T(8,128)} %get-tuple-element.42.loss_in), custom_call_target="tpu_custom_call" | custom-call | flops 92274688 | bytes 524288 | tf_op jit(solution)/shard_map/pallas_call | solution.py:53
  61.4 3.6 %shard_map.144.direct_in = f32[4,512,256]{2,1,0:T(8,128)} custom-call(bf16[176,512]{1,0:T(8,128)(2,1)} %get-tuple-element.39.turned_in, bf16[1024,1024]{1,0:T(8,128)(2,1)} %get-tuple-element.29.a_in, bf16[4,352,256]{2,1,0:T(8,128)(2,1)} %get-tuple-element.36.w_two_in, f32[176,512]{1,0:T(8,128)} %shard_map.143.after), custom_call_target="tpu_custom_call" | custom-call | flops 553648128 | bytes 4194304 | tf_op jit(solution)/shard_map/pallas_call | solution.py:53
  65.0 2.0 %all-to-all-done.2.landed_in = bf16[8,96,128]{2,1,0:T(8,128)(2,1)S(1)} async-done(((bf16[8,96,128]{2,1,0:T(8,128)(2,1)}), bf16[8,96,128]{2,1,0:T(8,128)(2,1)S(1)}, u32[]{:S(2)}, u32[]{:S(2)}) %all-to-all-start.2) | async-done | bytes 196640 | tf_op jit(solution)/shard_map/all_to_all | solution.py:439
  67.7 5.1 %shard_map.145 = f32[8,64,128]{2,1,0:T(8,128)} custom-call(bf16[512,512]{1,0:T(8,128)(2,1)} %get-tuple-element.28.pick_in, f32[4,512,256]{2,1,0:T(8,128)} %shard_map.144.direct_in, f32[4,512,256]{2,1,0:T(8,128)} %get-tuple-element.43.slope_in, bf16[4,352,256]{2,1,0:T(8,128)(2,1)} %get-tuple-element.36.w_two_in, bf16[64,512]{1,0:T(8,128)(2,1)} %get-tuple-element.44.left_in, ...), custom_call_target="tpu_custom_call" | custom-call | flops 553648128 | bytes 6291456 | tf_op jit(solution)/shard_map/pallas_call | solution.py:53
  72.9 4.0 %all-to-all-start.3 = ((f32[8,64,128]{2,1,0:T(8,128)}), f32[8,64,128]{2,1,0:T(8,128)S(1)}, u32[]{:S(2)}, u32[]{:S(2)}) async-start(f32[8,64,128]{2,1,0:T(8,128)} %shard_map.145), calls=%async_computation.3 | async-start | bytes 524288 | tf_op jit(solution)/shard_map/all_to_all | solution.py:439
  77.6 7.8 %all-to-all-done.3.pieces_in = f32[8,64,128]{2,1,0:T(8,128)S(1)} async-done(((f32[8,64,128]{2,1,0:T(8,128)}), f32[8,64,128]{2,1,0:T(8,128)S(1)}, u32[]{:S(2)}, u32[]{:S(2)}) %all-to-all-start.3) | async-done | bytes 262176 | tf_op jit(solution)/shard_map/all_to_all | solution.py:439
  86.1 1.7 %shard_map.146 = f32[8,64,128]{2,1,0:T(8,128)} custom-call(f32[8,64,128]{2,1,0:T(8,128)} %copy-done.1), custom_call_target="tpu_custom_call" | custom-call | bytes 1048576 | tf_op jit(solution)/shard_map/pallas_call | solution.py:53
  87.8 3.4 %all-to-all-start.4 = ((f32[8,64,128]{2,1,0:T(8,128)}), f32[8,64,128]{2,1,0:T(8,128)S(1)}, u32[]{:S(2)}, u32[]{:S(2)}) async-start(f32[8,64,128]{2,1,0:T(8,128)} %shard_map.146), calls=%async_computation.4 | async-start | bytes 524288 | tf_op jit(solution)/shard_map/all_to_all | solution.py:439
  91.3 28.6 %all-reduce.2.cloned.1.call-done.second = f32[176,512]{1,0:T(8,128)} async-done(((f32[176,512]{1,0:T(8,128)}), f32[176,512]{1,0:T(8,128)}) %all-reduce.2.cloned.1.call-update) | async-done | bytes 360464 | tf_op jit(solution)/shard_map/psum | solution.py:578
  119.9 1.5 %collective-permute-start.3 = (f32[176,512]{1,0:T(8,128)}, f32[176,512]{1,0:T(8,128)S(1)}, u32[]{:S(2)}, u32[]{:S(2)}) collective-permute-start(f32[176,512]{1,0:T(8,128)} %all-reduce.2.cloned.1.call-done.second), channel_id=1, source_target_pairs={{0,4},{4,0},{8,12},{12,8},{16,20},{20,16},{24,28},{28,24},{1,5},{5... | collective-permute-start | bytes 1081352 | tf_op jit(solution)/shard_map/ppermute | solution.py:614
  121.3 7.4 %collective-permute-done.3.other = f32[176,512]{1,0:T(8,128)S(1)} collective-permute-done((f32[176,512]{1,0:T(8,128)}, f32[176,512]{1,0:T(8,128)S(1)}, u32[]{:S(2)}, u32[]{:S(2)}) %collective-permute-start.3) | collective-permute-done | bytes 360480 | tf_op jit(solution)/shard_map/ppermute | solution.py:614
  130.2 2.1 %shard_map.147 = (f32[32,1024]{1,0:T(8,128)}, f32[32,1024]{1,0:T(8,128)}, f32[172,256]{1,0:T(8,128)}, f32[172,256]{1,0:T(8,128)}, f32[1,1]{1,0:T(1,128)}) custom-call(f32[8,64,128]{2,1,0:T(8,128)} %copy-done.2, f32[176,512]{1,0:T(8,128)} %all-reduce.2.cloned.1.call-done.second, f32[176,512]{1,0:T(8,128)} %copy-done.5), custom_call_target="tpu_custom_call" | custom-call | tf_op jit(solution)/shard_map/pallas_call | solution.py:53
  (29 shorter events, 6.4 us)
Async XLA Ops:
  7.2 32.2 %all-gather.3.cloned.1.call-start = ((), (), s32[]{:S(2)}) async-start(), calls=%async_computation.6 | async-start | bytes 1556480 | tf_op jit(solution)/shard_map/all_gather | solution.py:491
  7.2 7.3 %collective-permute-start.2 = (bf16[32,512]{1,0:T(8,128)(2,1)}, bf16[32,512]{1,0:T(8,128)(2,1)S(1)}, u32[]{:S(2)}, u32[]{:S(2)}) collective-permute-start(bf16[32,512]{1,0:T(8,128)(2,1)} %bitcast.21), channel_id=1, source_target_pairs={{0,3},{1,0},{2,1},{3,2},{4,7},{5,4},{6,5},{7,6},{8,11},{9,8},{10,9... | collective-permute-start | bytes 98312 | tf_op jit(solution)/shard_map/ppermute | solution.py:443
  9.6 4.9 %collective-permute-start.1 = (bf16[32,512]{1,0:T(8,128)(2,1)}, bf16[32,512]{1,0:T(8,128)(2,1)S(1)}, u32[]{:S(2)}, u32[]{:S(2)}) collective-permute-start(bf16[32,512]{1,0:T(8,128)(2,1)} %bitcast.22), channel_id=1, source_target_pairs={{0,2},{1,3},{2,0},{3,1},{4,6},{5,7},{6,4},{7,5},{8,10},{9,11},{10,... | collective-permute-start | bytes 98312 | tf_op jit(solution)/shard_map/ppermute | solution.py:443
  10.3 4.3 %collective-permute-start = (bf16[32,512]{1,0:T(8,128)(2,1)}, bf16[32,512]{1,0:T(8,128)(2,1)S(1)}, u32[]{:S(2)}, u32[]{:S(2)}) collective-permute-start(bf16[32,512]{1,0:T(8,128)(2,1)} %bitcast.23), channel_id=1, source_target_pairs={{0,1},{1,2},{2,3},{3,0},{4,5},{5,6},{6,7},{7,4},{8,9},{9,10},{10,1... | collective-permute-start | bytes 98312 | tf_op jit(solution)/shard_map/ppermute | solution.py:443
  14.5 0.6 copy-start.6
  14.5 0.6 copy-start.7
  14.6 0.6 copy-start.8
  18.3 14.0 %all-to-all-start = ((bf16[8,64,128]{2,1,0:T(8,128)(2,1)}), bf16[8,64,128]{2,1,0:T(8,128)(2,1)S(1)}, u32[]{:S(2)}, u32[]{:S(2)}) async-start(bf16[8,64,128]{2,1,0:T(8,128)(2,1)} %bitcast.18), calls=%async_computation | async-start | bytes 262144 | tf_op jit(solution)/shard_map/all_to_all | solution.py:439
  32.2 0.7 copy-start
  35.9 10.9 %all-to-all-start.1 = ((bf16[8,64,128]{2,1,0:T(8,128)(2,1)}), bf16[8,64,128]{2,1,0:T(8,128)(2,1)S(1)}, u32[]{:S(2)}, u32[]{:S(2)}) async-start(bf16[8,64,128]{2,1,0:T(8,128)(2,1)} %bitcast.17), calls=%async_computation.1 | async-start | bytes 262144 | tf_op jit(solution)/shard_map/all_to_all | solution.py:439
  46.8 0.7 copy-start.4
  54.6 12.4 %all-to-all-start.2 = ((bf16[8,96,128]{2,1,0:T(8,128)(2,1)}), bf16[8,96,128]{2,1,0:T(8,128)(2,1)S(1)}, u32[]{:S(2)}, u32[]{:S(2)}) async-start(bf16[8,96,128]{2,1,0:T(8,128)(2,1)} %get-tuple-element.45), calls=%async_computation.2 | async-start | bytes 393216 | tf_op jit(solution)/shard_map/all_to_all | solution.py:439
  67.1 0.7 copy-start.3
  72.9 12.5 %all-to-all-start.3 = ((f32[8,64,128]{2,1,0:T(8,128)}), f32[8,64,128]{2,1,0:T(8,128)S(1)}, u32[]{:S(2)}, u32[]{:S(2)}) async-start(f32[8,64,128]{2,1,0:T(8,128)} %shard_map.145), calls=%async_computation.3 | async-start | bytes 524288 | tf_op jit(solution)/shard_map/all_to_all | solution.py:439
  76.9 43.0 %all-reduce.2.cloned.1.call-start = ((), (), s32[]{:S(2)}) async-start(), calls=%async_computation.5 | async-start | bytes 720896 | tf_op jit(solution)/shard_map/psum | solution.py:578
  85.4 0.7 copy-start.1
  87.8 40.9 %all-to-all-start.4 = ((f32[8,64,128]{2,1,0:T(8,128)}), f32[8,64,128]{2,1,0:T(8,128)S(1)}, u32[]{:S(2)}, u32[]{:S(2)}) async-start(f32[8,64,128]{2,1,0:T(8,128)} %shard_map.146), calls=%async_computation.4 | async-start | bytes 524288 | tf_op jit(solution)/shard_map/all_to_all | solution.py:439
  119.9 8.9 %collective-permute-start.3 = (f32[176,512]{1,0:T(8,128)}, f32[176,512]{1,0:T(8,128)S(1)}, u32[]{:S(2)}, u32[]{:S(2)}) collective-permute-start(f32[176,512]{1,0:T(8,128)} %all-reduce.2.cloned.1.call-done.second), channel_id=1, source_target_pairs={{0,4},{4,0},{8,12},{12,8},{16,20},{20,16},{24,28},{28,24},{1,5},{5... | collective-permute-start | bytes 1081352 | tf_op jit(solution)/shard_map/ppermute | solution.py:614
  128.7 0.7 copy-start.5
  129.5 0.7 copy-start.2
Sparse Core Ops, SparseCore 0:
  18.4 19.1 all-gather.2
  80.1 39.7 all-reduce.1

commit v6 on v4

--- a/solution.py
+++ b/solution.py
@@ -33,6 +33,15 @@
     return high, (value - high.astype(F32)).astype(BF16)
 
 
+def spread(a, rows):
+    own = a.shape[0]
+    parts = []
+    for c in range(rows.shape[0] // own):
+        part = rows[c * own : (c + 1) * own]
+        parts += [part, part]
+    return mm(a, jnp.concatenate(parts, axis=0))
+
+
 def gelu_parts(v):
     inner = math.sqrt(2.0 / math.pi) * (v + 0.044715 * (v * v * v))
     t = jnp.tanh(inner)
@@ -49,14 +58,15 @@
     return cdf + 0.5 * v * (1.0 - t * t) * inner_slope
 
 
-def call(body, outs, args, scratch, copies, flops=0, moved=0, out_specs=None, near=0, room=58):
+def call(body, outs, args, scratch, copies, flops=0, moved=0, out_specs=None, near=0):
+    beside = sum(arg.size * arg.dtype.itemsize for arg in args[len(args) - near :]) if near else -4 * 2**20
     return pl.pallas_call(
         body,
         out_shape=[jax.ShapeDtypeStruct(shape, dtype) for shape, dtype in outs],
         in_specs=[SMEM if arg.dtype == jnp.int32 and arg.size < 512 else HBM for arg in args[: len(args) - near]] + [VMEM] * near,
         out_specs=out_specs or [HBM] * len(outs),
         scratch_shapes=[pltpu.VMEM(shape, dtype) for shape, dtype in scratch] + [pltpu.SemaphoreType.DMA((copies,))],
-        compiler_params=pltpu.CompilerParams(vmem_limit_bytes=room * 2**20),
+        compiler_params=pltpu.CompilerParams(vmem_limit_bytes=54 * 2**20 - beside - 2048),
         cost_estimate=pl.CostEstimate(flops=flops, bytes_accessed=moved, transcendentals=0),
     )(*args)
 
@@ -97,7 +107,6 @@
     copies.later(pick, pick_out)
     for b in range(blocks):
         rows = pl.ds(b * BLOCK, BLOCK)
-        low_rows = pl.ds(own + b * BLOCK, BLOCK)
         tile_copies[b].wait()
 
         def add(k, _, b=b, rows=rows):
@@ -106,11 +115,11 @@
             return 0
 
         lax.fori_loop(0, per_block, add, 0)
-        high, low = halves(dense[rows, :])
-        a_ref[rows, :] = high
-        a_ref[low_rows, :] = low
+        for c in range(dense.shape[1] // own):
+            high, low = halves(dense[rows, pl.ds(c * own, own)])
+            a_ref[rows, pl.ds(2 * c * own, own)] = high
+            a_ref[rows, pl.ds((2 * c + 1) * own, own)] = low
         copies.later(a_ref.at[rows], a_out.at[rows])
-        copies.later(a_ref.at[low_rows], a_out.at[low_rows])
     copies.finish()
 
 
@@ -153,29 +162,27 @@
 def near_kernel(a_in, full_in, out, a_ref, full, near, sems):
     copies = Copies(sems)
     own = full.shape[0]
-    loads = [copies(full_in, full), copies(a_in.at[:, pl.ds(0, own)], a_ref)]
+    loads = [copies(full_in, full), copies(a_in.at[:, pl.ds(0, 2 * own)], a_ref)]
     for load in loads:
         load.wait()
-    both = mm(a_ref[...], full[...])
-    near[...] = both[:own] + both[own:]
+    near[...] = spread(a_ref[...], full[...])
     copies(near, out).wait()
 
 
-def first_kernel(pick_in, a_in, near_in, source_in, agg_out, packed_out, pick, a_ref, near, source, agg, packed, sems):
+def first_kernel(pick_in, a_in, near_in, source, agg_out, packed_out, source_out, pick, a_ref, near, agg, packed, sems):
     copies = Copies(sems)
     own = near.shape[0]
+    copies.later(source, source_out)
     loads = [
-        copies(source_in, source),
-        copies(a_in.at[:, pl.ds(own, source.shape[0])], a_ref),
+        copies(a_in.at[:, pl.ds(2 * own, 2 * source.shape[0])], a_ref),
         copies(near_in, near),
         copies(pick_in, pick),
     ]
-    for load in loads[:3]:
-        load.wait()
-    both = mm(a_ref[...], source[...])
-    agg[...] = (near[...] + both[:own] + both[own:]).astype(BF16)
+    for load in loads[:2]:
+        load.wait()
+    agg[...] = (near[...] + spread(a_ref[...], source[...])).astype(BF16)
     copies.later(agg, agg_out)
-    loads[3].wait()
+    loads[2].wait()
     packed[...] = mm(pick[...], agg[...]).astype(BF16)
     copies.later(packed, packed_out)
     copies.finish()
@@ -196,7 +203,7 @@
         copies(weights_in, weights),
         copies(full_in, full),
         copies(agg_in, agg),
-        copies(a_in.at[:, pl.ds(0, own)], a_ref),
+        copies(a_in.at[:, pl.ds(0, 2 * own)], a_ref),
         copies(turned_in, left.at[pl.ds(0, step)]),
     ]
     loads[0].wait()
@@ -223,8 +230,7 @@
         hidden[j] = out
         if j == 0:
             loads[3].wait()
-        spread = mm(a_ref[...], out)
-        part[j] = spread[:own] + spread[own:]
+        part[j] = spread(a_ref[...], out)
         copies.later(part.at[j], part_out.at[j])
         term = mm_nt(w_two[j, :pad], out)
         total = term if total is None else total + term
@@ -235,56 +241,54 @@
 
 
 def second_kernel(
-    class_count, grad_scale, ids, a_in, source_in, landed_in, w_one_in, w_two_in, part_in, logits_in, labels_in,
+    class_count, grad_scale, ids, a_in, source_in, w_one_in, w_two_in, part_in, logits_in, labels_in, landed,
     turned_out, mine_out, loss_out, packed_out,
-    a_ref, source, landed, w_one, w_two, part, logits, labels, turned, loss, packed, agg, sems,
+    a_ref, source, w_one, w_two, part, logits, labels, turned, loss, packed, agg, sems,
 ):
     copies = Copies(sems)
     groups, own, units = part.shape
     pad = logits.shape[0]
     halo = landed.shape[0]
     slots = halo // packed.shape[0]
-    chunk = min(own, halo)
+    chunk = own
     loads = [
         copies(source_in, source),
-        copies(landed_in, landed),
         copies(w_one_in, w_one),
-        copies(a_in.at[:, pl.ds(own, halo)], a_ref),
+        copies(a_in.at[:, pl.ds(2 * own, 2 * halo)], a_ref),
         copies(logits_in, logits),
         copies(w_two_in, w_two),
         copies(labels_in, labels),
     ]
     part_loads = [copies(part_in.at[j], part.at[j]) for j in range(groups)]
-    for load in loads[:3]:
+    for load in loads[:2]:
         load.wait()
     total = None
     for j in range(groups):
 
         def one(r, held, j=j):
             rows = pl.ds(pl.multiple_of(r * chunk, chunk), chunk)
-            srcs = pl.ds(pl.multiple_of(r * chunk, chunk), chunk)
+            srcs = pl.ds(pl.multiple_of(2 * r * chunk, chunk), 2 * chunk)
             both = jnp.concatenate([source[rows, :], landed[rows, :]], axis=1)
             out = gelu(mm(both, w_one[j])).astype(BF16)
             if j == 0 and halo == chunk:
-                loads[3].wait()
-            spread = mm(a_ref[:, srcs], out)
-            spread = spread[:own] + spread[own:]
+                loads[2].wait()
+            more = spread(a_ref[:, srcs], out)
             if halo == chunk:
                 part_loads[j].wait()
-                return part[j] + spread
-            return held + spread
+                return part[j] + more
+            return held + more
 
         if halo == chunk:
             held = one(0, None)
         else:
             if j == 0:
-                loads[3].wait()
+                loads[2].wait()
             part_loads[j].wait()
             held = lax.fori_loop(0, halo // chunk, one, part[j])
         agg[j] = held.astype(BF16)
         if j == 0:
+            loads[3].wait()
             loads[4].wait()
-            loads[5].wait()
             total = logits[...]
         total = total + mm_nt(w_two[j, pad:], agg[j])
     copies.later(agg.at[ids[0]], mine_out)
@@ -294,16 +298,18 @@
     shifted = total - top
     powers = jnp.where(real, jnp.exp(shifted), 0.0)
     sums = jnp.sum(powers, axis=0, keepdims=True)
-    loads[6].wait()
+    loads[5].wait()
     target = (class_id == labels[...]).astype(F32)
     turned[...] = ((powers / sums - target) * grad_scale).astype(BF16)
     copies.later(turned, turned_out)
     row_loss = jnp.log(sums) - jnp.sum(shifted * target, axis=0, keepdims=True)
     loss[...] = jnp.broadcast_to(jnp.sum(row_loss, axis=1, keepdims=True), loss.shape)
     copies.later(loss, loss_out)
-    back = mm(turned[...], a_ref[:own, :]).T.astype(BF16)
-    for d in range(packed.shape[0]):
-        put_message(packed, d, back[d * slots : (d + 1) * slots])
+    per_chunk = own // slots
+    for c in range(halo // own):
+        back = mm(turned[...], a_ref[:, pl.ds(2 * c * own, own)]).T.astype(BF16)
+        for d in range(per_chunk):
+            put_message(packed, c * per_chunk + d, back[d * slots : (d + 1) * slots])
     copies.later(packed, packed_out)
     copies.finish()
 
@@ -360,11 +366,11 @@
     units = self_rows.shape[1]
     loads[0].wait()
     loads[1].wait()
-    high, low = halves(mm(turned[...], a_ref[...]).T)
-    rows = turned[...].T
+    high, low = halves(mm(turned[...], a_ref[...]))
+    rows = jnp.concatenate([turned[...], high, low], axis=0).T
     loads[2].wait()
     for j in range(direct.shape[0]):
-        direct[j] = mm(rows, w_two[j, :pad]) + mm(high, w_two[j, pad:]) + mm(low, w_two[j, pad:])
+        direct[j] = mm(rows, jnp.concatenate([w_two[j], w_two[j, pad:]], axis=0))
         copies.later(direct.at[j], direct_out.at[j])
     for load in loads[3:]:
         load.wait()
@@ -381,28 +387,29 @@
 
 
 def back_kernel(
-    parts, pick_in, direct_in, slope_in, w_two_in, left_in, landed_in, second_in, out,
-    pick, direct, slope, w_two, left, landed, rows, grads, sems,
+    parts, pick_in, direct_in, slope_in, w_two_in, left_in, second_in, landed, out,
+    pick, direct, slope, w_two, left, rows, grads, sems,
 ):
     copies = Copies(sems)
     step = left.shape[0]
     groups, _, units = direct.shape
     pad = landed.shape[1] if w_two.ndim == 2 else w_two.shape[1] // 2
-    loads = [copies(landed_in, landed), copies(pick_in, pick), copies(w_two_in, w_two)]
+    loads = [copies(pick_in, pick), copies(w_two_in, w_two)]
     both_loads = [(copies(direct_in.at[j], direct.at[j]), copies(slope_in.at[j], slope.at[j])) for j in range(groups)]
     left_load = copies(left_in, left)
     if parts:
         second_load = copies(second_in, grads.at[:, pl.ds(step, second_in.shape[1])])
-    loads[0].wait()
     for d in range(landed.shape[0]):
         take_message(landed, d, rows)
+    loads[0].wait()
+    high, low = halves(mm_tn(rows[...], pick[...]))
+    both = jnp.concatenate([high, low], axis=0).T
     loads[1].wait()
-    high, low = halves(mm_tn(pick[...], rows[...]))
-    loads[2].wait()
     for j in range(groups):
+        more = mm(both, jnp.concatenate([w_two[j, pad:], w_two[j, pad:]], axis=0))
         for load in both_loads[j]:
             load.wait()
-        total = direct[j] + mm(high, w_two[j, pad:]) + mm(low, w_two[j, pad:])
+        total = direct[j] + more
         if j == 0:
             left_load.wait()
         result = mm(left[...], (total * slope[j]).astype(BF16))
@@ -484,10 +491,10 @@
     turned_all = gather_shifted(turned, groups)
     a_mat, pick = call(
         prepare_kernel,
-        [((2 * own, total_src), BF16), ((halo, own), BF16)],
+        [((own, 2 * total_src), BF16), ((halo, own), BF16)],
         (tile_src, send_count, tile_val, send_rows[0]),
-        [(tile_val.shape, BF16), ((nodes, slots), jnp.int32), ((own, total_src), F32), ((2 * own, total_src), BF16), ((halo, own), BF16)],
-        2 + 3 * blocks,
+        [(tile_val.shape, BF16), ((nodes, slots), jnp.int32), ((own, total_src), F32), ((own, 2 * total_src), BF16), ((halo, own), BF16)],
+        2 + 2 * blocks,
         moved=tile_val.size * 4,
     )
     full, packed, packed_weights = call(
@@ -507,7 +514,6 @@
         flops=2 * halo * own * cols,
         moved=halo * own * 2,
         near=groups - 1,
-        room=12 + halo * own // 2**18,
     )
     weights = lax.all_gather(packed_weights, "feat")
     source = swap(packed, nodes).reshape(halo, cols)
@@ -515,19 +521,20 @@
         near_kernel,
         [((own, cols), F32)],
         (a_mat, full),
-        [((2 * own, own), BF16), ((own, cols), BF16), ((own, cols), F32)],
+        [((own, 2 * own), BF16), ((own, cols), BF16), ((own, cols), F32)],
         3,
         flops=4 * own * own * cols,
         moved=4 * own * own,
     )
-    agg, packed = call(
+    agg, packed, source = call(
         first_kernel,
-        [((own, cols), BF16), ((halo, cols), BF16)],
+        [((own, cols), BF16), ((halo, cols), BF16), ((halo, cols), BF16)],
         (pick, a_mat, near, source),
-        [((halo, own), BF16), ((2 * own, halo), BF16), ((own, cols), F32), ((halo, cols), BF16), ((own, cols), BF16), ((halo, cols), BF16)],
+        [((halo, own), BF16), ((own, 2 * halo), BF16), ((own, cols), F32), ((own, cols), BF16), ((halo, cols), BF16)],
         6,
         flops=4 * own * total_src * cols,
         moved=4 * own * total_src,
+        near=1,
     )
     landed = swap(packed, nodes).reshape(halo, cols)
     chunked = (groups, own, units)
@@ -546,7 +553,7 @@
         [
             ((own, cols), BF16),
             ((own, cols), BF16),
-            ((2 * own, own), BF16),
+            ((own, 2 * own), BF16),
             ((2 * step, own), BF16),
             ((groups, packed_rows, units), BF16),
             ((groups, 2 * cols, units), BF16),
@@ -565,10 +572,9 @@
     turned_grads, agg_mine, loss, packed = call(
         functools.partial(second_kernel, classes, grad_scale),
         [((pad, own), BF16), ((own, units), BF16), ((8, 128), F32), (message, BF16)],
-        (ids, a_mat, source, landed, w_one, w_two, part, logits, labels.reshape(1, own)),
+        (ids, a_mat, source, w_one, w_two, part, logits, labels.reshape(1, own), landed),
         [
-            ((2 * own, halo), BF16),
-            ((halo, cols), BF16),
+            ((own, 2 * halo), BF16),
             ((halo, cols), BF16),
             ((groups, 2 * cols, units), BF16),
             ((groups, 2 * pad, units), BF16),
@@ -580,9 +586,10 @@
             (message, BF16),
             (chunked, BF16),
         ],
-        11 + groups,
+        10 + groups,
         flops=4 * own * halo * width,
         moved=12 * own * width,
+        near=1,
     )
     landed = swap(packed, nodes)
     second_shape = (parts, pad * 2 * units // (BLOCK * parts), BLOCK) if parts else (pad, 2 * units)
@@ -608,20 +615,20 @@
     (grads,) = call(
         functools.partial(back_kernel, parts),
         [(out_shape, F32)],
-        (pick, direct, slope, w_two, left, landed, second),
+        (pick, direct, slope, w_two, left, second, landed),
         [
             ((halo, own), BF16),
             (chunked, F32),
             (chunked, F32),
             ((groups, 2 * pad, units), BF16),
             ((2 * step, own), BF16),
-            (message, BF16),
             ((halo, pad), BF16),
             (out_shape, F32) if parts else ((groups, 2 * step, units), F32),
         ],
-        5 + 2 * groups + max(parts, groups),
+        4 + 2 * groups + max(parts, groups),
         flops=6 * own * pad * width,
         moved=12 * own * width,
+        near=1,
     )
     if not parts:
         grads, second = lax.psum((grads, second), "node")

time: 125 us -> 128 us (1.024)
  Pallas kernels: 37.8 us -> 41.7 us
    pallas_call x10, Pallas kernels: 37.8 us -> 41.7 us  [call(): pl.pallas_call(body, out_shape=[jax.ShapeDtypeStruct(shape, dtype) for sh...]
    unnamed x20 -> x18, local copies, waits for them, and re-layouts: 3.68 us -> 3.19 us
where the time goes in v6:
time: 128 us; the launch traced here: 127 us
  Pallas kernels  41.7 us (33%)
  blocking collectives  39.9 us (31%)
  starting transfers between devices  17 us (13%)
  between operations  14.2 us (11%)
  waiting for transfers between devices  11.3 us (9%)
  local copies, waits for them, and re-layouts  3.19 us (2%)
    pallas_call x10, Pallas kernels, call(): pl.pallas_call(body, out_shape=[jax.ShapeDtypeStruct(shape, dtype) for sh...  41.7 us
    all_to_all x2, blocking collectives, swap(): return lax.all_to_all(blocks, 'node', 0, 0, tiled=True)  39.9 us
    all_to_all x3, starting transfers between devices, swap(): return lax.all_to_all(blocks, 'node', 0, 0, tiled=True)  13.8 us
    all_to_all x3, waiting for transfers between devices, swap(): return lax.all_to_all(blocks, 'node', 0, 0, tiled=True)  11.2 us
    ppermute x3, starting transfers between devices, gather_shifted(): lax.ppermute(value, 'feat', [(i, (i + k) % count) for i in range(count)])  3.23 us
    unnamed x18, local copies, waits for them, and re-layouts  3.19 us
  transfers between devices with their start and end apart: 7, of which 3 were waited for; matrix products, arithmetic and copies ran while one was open for 0% of the time, Pallas kernels for 16%

profile of v6, /device:TPU:0, one launch (start us, length us, event | category | flops | bytes accessed | tf_op | source)
XLA Modules:
  0.0 127.3 jit_solution(8649323020769960534)
XLA Ops:
  7.2 2.4 %collective-permute-start.2 = (bf16[32,512]{1,0:T(8,128)(2,1)}, bf16[32,512]{1,0:T(8,128)(2,1)S(1)}, u32[]{:S(2)}, u32[]{:S(2)}) collective-permute-start(bf16[32,512]{1,0:T(8,128)(2,1)} %bitcast.21), channel_id=1, source_target_pairs={{0,3},{1,0},{2,1},{3,2},{4,7},{5,4},{6,5},{7,6},{8,11},{9,8},{10,9... | collective-permute-start | bytes 98312 | tf_op jit(solution)/shard_map/ppermute | solution.py:469
  9.6 0.6 collective-permute-start.1
  10.4 4.0 %shard_map.137 = (bf16[512,2048]{1,0:T(8,128)(2,1)}, bf16[512,512]{1,0:T(8,128)(2,1)}) custom-call(s32[4,16]{1,0:T(4,128)} %tile_src.1, s32[1,8]{1,0:T(1,128)} %count.1, bf16[4,16,128,128]{3,2,1,0:T(8,128)(2,1)} %tile_val.1, s32[8,64]{1,0:T(8,128)} %bitcast.26), custom_call_target="tpu_custom_call" | custom-call | bytes 4194304 | tf_op jit(solution)/shard_map/pallas_call | solution.py:63
  15.1 3.0 %shard_map.138 = (bf16[512,128]{1,0:T(8,128)(2,1)}, bf16[512,128]{1,0:T(8,128)(2,1)}, bf16[608,256]{1,0:T(8,128)(2,1)}) custom-call(s32[1]{0:T(128)} %bitcast.1.ids, bf16[512,512]{1,0:T(8,128)(2,1)} %get-tuple-element.31.pick_in, bf16[32,1024]{1,0:T(8,128)(2,1)} %w_self1.1, bf16[32,1024]{1,0:T(8,128)(2,1)} %w_neigh1.1, bf16[172,256]{1,0:T(8,128)(2,1)} %bitcast.19, ...), custom_call_target="tpu_custom_call" | custom-call | flops 67108864 | bytes 524288 | tf_op jit(solution)/shard_map/pallas_call | solution.py:63
  18.2 5.8 %all-to-all-start = ((bf16[8,64,128]{2,1,0:T(8,128)(2,1)}), bf16[8,64,128]{2,1,0:T(8,128)(2,1)S(1)}, u32[]{:S(2)}, u32[]{:S(2)}) async-start(bf16[8,64,128]{2,1,0:T(8,128)(2,1)} %bitcast.18), calls=%async_computation | async-start | bytes 262144 | tf_op jit(solution)/shard_map/all_to_all | solution.py:465
  24.0 2.5 %shard_map.139.near_in = f32[512,128]{1,0:T(8,128)} custom-call(bf16[512,2048]{1,0:T(8,128)(2,1)} %get-tuple-element.32.a_in, bf16[512,128]{1,0:T(8,128)(2,1)} %get-tuple-element.33.full_in), custom_call_target="tpu_custom_call" | custom-call | flops 134217728 | bytes 1048576 | tf_op jit(solution)/shard_map/pallas_call | solution.py:63
  26.5 5.6 %all-to-all-done = bf16[8,64,128]{2,1,0:T(8,128)(2,1)S(1)} async-done(((bf16[8,64,128]{2,1,0:T(8,128)(2,1)}), bf16[8,64,128]{2,1,0:T(8,128)(2,1)S(1)}, u32[]{:S(2)}, u32[]{:S(2)}) %all-to-all-start) | async-done | bytes 131104 | tf_op jit(solution)/shard_map/all_to_all | solution.py:465
  32.1 0.7 copy-done.5
  32.8 3.9 %shard_map.140 = (bf16[512,128]{1,0:T(8,128)(2,1)}, bf16[512,128]{1,0:T(8,128)(2,1)}, bf16[512,128]{1,0:T(8,128)(2,1)}) custom-call(bf16[512,512]{1,0:T(8,128)(2,1)} %get-tuple-element.31.pick_in, bf16[512,2048]{1,0:T(8,128)(2,1)} %get-tuple-element.32.a_in, f32[512,128]{1,0:T(8,128)} %shard_map.139.near_in, bf16[512,128]{1,0:T(8,128)(2,1)} %bitcast.16), custom_call_target="tpu_custom_call" | custom-call | flops 268435456 | bytes 2097152 | tf_op jit(solution)/shard_map/pallas_call | solution.py:63
  36.7 3.4 %all-to-all-start.1 = ((bf16[8,64,128]{2,1,0:T(8,128)(2,1)}), bf16[8,64,128]{2,1,0:T(8,128)(2,1)S(1)}, u32[]{:S(2)}, u32[]{:S(2)}) async-start(bf16[8,64,128]{2,1,0:T(8,128)(2,1)} %bitcast.17), calls=%async_computation.1 | async-start | bytes 262144 | tf_op jit(solution)/shard_map/all_to_all | solution.py:465
  40.1 5.9 %shard_map.141 = (bf16[4,256,256]{2,1,0:T(8,128)(2,1)}, bf16[4,352,256]{2,1,0:T(8,128)(2,1)}, f32[4,512,256]{2,1,0:T(8,128)}, f32[4,512,256]{2,1,0:T(8,128)}, f3...) custom-call(s32[1]{0:T(128)} %bitcast.1.ids, bf16[512,128]{1,0:T(8,128)(2,1)} %get-tuple-element.33.full_in, ...), custom_call_target="tpu_custom_call" | custom-call | flops 2147483648 | bytes 8388608 | tf_op jit(solution)/shard_map/pallas_call | solution.py:63
  46.1 1.5 %all-to-all-done.1 = bf16[8,64,128]{2,1,0:T(8,128)(2,1)S(1)} async-done(((bf16[8,64,128]{2,1,0:T(8,128)(2,1)}), bf16[8,64,128]{2,1,0:T(8,128)(2,1)S(1)}, u32[]{:S(2)}, u32[]{:S(2)}) %all-to-all-start.1) | async-done | bytes 131104 | tf_op jit(solution)/shard_map/all_to_all | solution.py:465
  47.6 0.7 copy-done.4
  48.2 8.3 %shard_map.142 = (bf16[176,512]{1,0:T(8,128)(2,1)}, bf16[512,256]{1,0:T(8,128)(2,1)}, f32[8,128]{1,0:T(8,128)S(1)}, bf16[8,96,128]{2,1,0:T(8,128)(2,1)}) custom-call(s32[1]{0:T(128)} %bitcast.1.ids, bf16[512,2048]{1,0:T(8,128)(2,1)} %get-tuple-element.32.a_in, bf16[512,128]{1,0:T(8,128)(2,1)} %get-tuple-element.35.source_in, ...), custom_call_target="tpu_custom_call" | custom-call | flops 1073741824 | bytes 6291456 | tf_op jit(solution)/shard_map/pallas_call | solution.py:63
  56.5 0.6 copy-done.1
  57.1 4.5 %all-to-all-start.2 = ((bf16[8,96,128]{2,1,0:T(8,128)(2,1)}), bf16[8,96,128]{2,1,0:T(8,128)(2,1)S(1)}, u32[]{:S(2)}, u32[]{:S(2)}) async-start(bf16[8,96,128]{2,1,0:T(8,128)(2,1)} %get-tuple-element.51), calls=%async_computation.2 | async-start | bytes 393216 | tf_op jit(solution)/shard_map/all_to_all | solution.py:465
  61.7 3.8 %shard_map.143 = (f32[8,88,128]{2,1,0:T(8,128)}, f32[4,512,256]{2,1,0:T(8,128)}) custom-call(bf16[176,512]{1,0:T(8,128)(2,1)} %get-tuple-element.43.turned_in, bf16[512,256]{1,0:T(8,128)(2,1)} %get-tuple-element.44.self_in, bf16[512,256]{1,0:T(8,128)(2,1)} %get-tuple-element.45.agg_in, f32[8,128]{1,0:T(8,128)} %copy-done.1, ...), custom_call_target="tpu_custom_call" | custom-call | flops 922746880 | bytes 4194304 | tf_op jit(solution)/shard_map/pallas_call | solution.py:63
  65.5 4.1 %all-to-all-done.2.landed = bf16[8,96,128]{2,1,0:T(8,128)(2,1)S(1)} async-done(((bf16[8,96,128]{2,1,0:T(8,128)(2,1)}), bf16[8,96,128]{2,1,0:T(8,128)(2,1)S(1)}, u32[]{:S(2)}, u32[]{:S(2)}) %all-to-all-start.2) | async-done | bytes 196640 | tf_op jit(solution)/shard_map/all_to_all | solution.py:465
  69.6 0.7 copy-done.3
  70.3 6.0 %shard_map.144 = f32[8,152,128]{2,1,0:T(8,128)} custom-call(bf16[512,512]{1,0:T(8,128)(2,1)} %get-tuple-element.31.pick_in, f32[4,512,256]{2,1,0:T(8,128)} %get-tuple-element.47.direct_in, f32[4,512,256]{2,1,0:T(8,128)} %get-tuple-element.48.slope_in, bf16[4,352,256]{2,1,0:T(8,128)(2,1)} %get-tuple-element.39.w_two_in, bf16[64,512]{1,0:T(8,128)(2,1)S(1)} %copy-done, ...), custom_call_target="tpu_custom_call" | custom-call | flops 553648128 | bytes 6291456 | tf_op jit(solution)/shard_map/pallas_call | solution.py:63
  76.3 20.1 %all_to_all.25.pieces_in = f32[8,152,128]{2,1,0:T(8,128)} all-to-all(f32[8,152,128]{2,1,0:T(8,128)} %shard_map.144), channel_id=1, replica_groups=mesh['node'=8,'feat'=4] {'node'}, dimensions={0} | all-to-all | bytes 1245184 | tf_op jit(solution)/shard_map/all_to_all | solution.py:465
  96.4 2.2 %shard_map.145 = f32[8,152,128]{2,1,0:T(8,128)} custom-call(f32[8,152,128]{2,1,0:T(8,128)} %all_to_all.25.pieces_in), custom_call_target="tpu_custom_call" | custom-call | bytes 1048576 | tf_op jit(solution)/shard_map/pallas_call | solution.py:63
  98.6 19.9 %all_to_all.26.pieces = f32[8,152,128]{2,1,0:T(8,128)} all-to-all(f32[8,152,128]{2,1,0:T(8,128)} %shard_map.145), channel_id=1, replica_groups=mesh['node'=8,'feat'=4] {'node'}, dimensions={0} | all-to-all | bytes 1245184 | tf_op jit(solution)/shard_map/all_to_all | solution.py:465
  118.4 2.0 %shard_map.146 = (f32[32,1024]{1,0:T(8,128)}, f32[32,1024]{1,0:T(8,128)}, f32[172,256]{1,0:T(8,128)}, f32[172,256]{1,0:T(8,128)}, f32[1,1]{1,0:T(1,128)}) custom-call(f32[8,152,128]{2,1,0:T(8,128)} %all_to_all.26.pieces), custom_call_target="tpu_custom_call" | custom-call | tf_op jit(solution)/shard_map/pallas_call | solution.py:63
  (21 shorter events, 0.9 us)
Async XLA Ops:
  7.2 33.0 %all-gather.3.cloned.1.call-start = ((), (), s32[]{:S(2)}) async-start(), calls=%async_computation.5 | async-start | bytes 1556480 | tf_op jit(solution)/shard_map/all_gather | solution.py:518
  7.2 7.2 %collective-permute-start.2 = (bf16[32,512]{1,0:T(8,128)(2,1)}, bf16[32,512]{1,0:T(8,128)(2,1)S(1)}, u32[]{:S(2)}, u32[]{:S(2)}) collective-permute-start(bf16[32,512]{1,0:T(8,128)(2,1)} %bitcast.21), channel_id=1, source_target_pairs={{0,3},{1,0},{2,1},{3,2},{4,7},{5,4},{6,5},{7,6},{8,11},{9,8},{10,9... | collective-permute-start | bytes 98312 | tf_op jit(solution)/shard_map/ppermute | solution.py:469
  9.6 4.8 %collective-permute-start.1 = (bf16[32,512]{1,0:T(8,128)(2,1)}, bf16[32,512]{1,0:T(8,128)(2,1)S(1)}, u32[]{:S(2)}, u32[]{:S(2)}) collective-permute-start(bf16[32,512]{1,0:T(8,128)(2,1)} %bitcast.22), channel_id=1, source_target_pairs={{0,2},{1,3},{2,0},{3,1},{4,6},{5,7},{6,4},{7,5},{8,10},{9,11},{10,... | collective-permute-start | bytes 98312 | tf_op jit(solution)/shard_map/ppermute | solution.py:469
  10.3 4.2 %collective-permute-start = (bf16[32,512]{1,0:T(8,128)(2,1)}, bf16[32,512]{1,0:T(8,128)(2,1)S(1)}, u32[]{:S(2)}, u32[]{:S(2)}) collective-permute-start(bf16[32,512]{1,0:T(8,128)(2,1)} %bitcast.23), channel_id=1, source_target_pairs={{0,1},{1,2},{2,3},{3,0},{4,5},{5,6},{6,7},{7,4},{8,9},{9,10},{10,1... | collective-permute-start | bytes 98312 | tf_op jit(solution)/shard_map/ppermute | solution.py:469
  14.4 0.6 copy-start.6
  14.5 0.6 copy-start.7
  14.5 0.6 copy-start.8
  18.2 14.0 %all-to-all-start = ((bf16[8,64,128]{2,1,0:T(8,128)(2,1)}), bf16[8,64,128]{2,1,0:T(8,128)(2,1)S(1)}, u32[]{:S(2)}, u32[]{:S(2)}) async-start(bf16[8,64,128]{2,1,0:T(8,128)(2,1)} %bitcast.18), calls=%async_computation | async-start | bytes 262144 | tf_op jit(solution)/shard_map/all_to_all | solution.py:465
  32.1 0.7 copy-start.5
  36.7 10.9 %all-to-all-start.1 = ((bf16[8,64,128]{2,1,0:T(8,128)(2,1)}), bf16[8,64,128]{2,1,0:T(8,128)(2,1)S(1)}, u32[]{:S(2)}, u32[]{:S(2)}) async-start(bf16[8,64,128]{2,1,0:T(8,128)(2,1)} %bitcast.17), calls=%async_computation.1 | async-start | bytes 262144 | tf_op jit(solution)/shard_map/all_to_all | solution.py:465
  40.1 8.1 %copy-start.2 = (s32[512]{0:T(512)S(1)}, s32[512]{0:T(512)}, u32[]{:S(2)}) copy-start(s32[512]{0:T(512)} %param.15) | copy-start | bytes 6148
  47.6 0.7 copy-start.4
  56.5 0.6 copy-start.1
  57.1 13.2 %copy-start = (bf16[64,512]{1,0:T(8,128)(2,1)S(1)}, bf16[64,512]{1,0:T(8,128)(2,1)}, u32[]{:S(2)}) copy-start(bf16[64,512]{1,0:T(8,128)(2,1)} %get-tuple-element.49.left_in) | copy-start | bytes 196612
  57.1 12.5 %all-to-all-start.2 = ((bf16[8,96,128]{2,1,0:T(8,128)(2,1)}), bf16[8,96,128]{2,1,0:T(8,128)(2,1)S(1)}, u32[]{:S(2)}, u32[]{:S(2)}) async-start(bf16[8,96,128]{2,1,0:T(8,128)(2,1)} %get-tuple-element.51), calls=%async_computation.2 | async-start | bytes 393216 | tf_op jit(solution)/shard_map/all_to_all | solution.py:465
  69.6 0.7 copy-start.3
Sparse Core Ops, SparseCore 0:
  18.3 19.1 all-gather.2

commit v7 on v0

v7 whole, which is shorter than its diff:
```python
import functools
import math

import jax
import jax.numpy as jnp
from jax import lax
from jax.experimental import pallas as pl
from jax.experimental.pallas import tpu as pltpu
from jax.sharding import PartitionSpec as P

BLOCK = 128
F32 = jnp.float32
BF16 = jnp.bfloat16
VMEM = pl.BlockSpec(memory_space=pltpu.VMEM)
HBM = pl.BlockSpec(memory_space=pltpu.HBM)
SMEM = pl.BlockSpec(memory_space=pltpu.SMEM)


def mm(a, b):
    return lax.dot_general(a, b, (((1,), (0,)), ((), ())), preferred_element_type=F32)


def mm_nt(a, b):
    return lax.dot_general(a, b, (((1,), (1,)), ((), ())), preferred_element_type=F32)


def mm_tn(a, b):
    return lax.dot_general(a, b, (((0,), (0,)), ((), ())), preferred_element_type=F32)


def halves(value):
    high = value.astype(BF16)
    return high, (value - high.astype(F32)).astype(BF16)


def spread(a, rows):
    own = a.shape[0]
    parts = []
    for c in range(rows.shape[0] // own):
        part = rows[c * own : (c + 1) * own]
        parts += [part, part]
    return mm(a, jnp.concatenate(parts, axis=0))


def gelu_parts(v):
    inner = math.sqrt(2.0 / math.pi) * (v + 0.044715 * (v * v * v))
    t = jnp.tanh(inner)
    return 0.5 * (1.0 + t), t


def gelu(v):
    return v * gelu_parts(v)[0]


def gelu_slope(v):
    cdf, t = gelu_parts(v)
    inner_slope = math.sqrt(2.0 / math.pi) * (1.0 + 3 * 0.044715 * (v * v))
    return cdf + 0.5 * v * (1.0 - t * t) * inner_slope


def size_of(shape, dtype):
    rows = -(-shape[-2] // 16) * 16 if len(shape) > 1 else 1
    return math.prod(shape[:-2]) * rows * (-(-shape[-1] // 128) * 128) * jnp.dtype(dtype).itemsize


def call(body, outs, args, scratch=(), copies=0, flops=0, moved=0, grant=0):
    specs = [SMEM if arg.dtype == jnp.int32 and arg.size < 512 else VMEM for arg in args]
    if copies:
        specs = [spec if spec is SMEM else HBM for spec in specs]
    room = sum(size_of(shape, dtype) for shape, dtype in [*outs, *scratch])
    room += sum(size_of(arg.shape, arg.dtype) for arg, spec in zip(args, specs) if spec is VMEM)
    return pl.pallas_call(
        body,
        out_shape=[jax.ShapeDtypeStruct(shape, dtype) for shape, dtype in outs],
        in_specs=specs,
        out_specs=[HBM if copies else VMEM] * len(outs),
        scratch_shapes=[pltpu.VMEM(shape, dtype) for shape, dtype in scratch]
        + ([pltpu.SemaphoreType.DMA((copies,))] if copies else []),
        compiler_params=pltpu.CompilerParams(vmem_limit_bytes=grant or min(room + 8 * 2**20, 56 * 2**20)),
        cost_estimate=pl.CostEstimate(flops=flops, bytes_accessed=moved, transcendentals=0),
    )(*args)


def prepare_kernel(
    tile_src, tile_val, w_self1, w_neigh1, w_self2, w_neigh2,
    a_out, weights_out, a_ref, weights, tiles, firsts, seconds, dense, sems,
):
    started = []

    def copy(src, dst):
        started.append(pltpu.make_async_copy(src, dst, sems.at[len(started)]))
        started[-1].start()
        return started[-1]

    blocks, per_block = tile_val.shape[0], tile_val.shape[1]
    own = blocks * BLOCK
    pairs = [(w_self1, firsts.at[0]), (w_neigh1, firsts.at[1]), (w_self2, seconds.at[0]), (w_neigh2, seconds.at[1])]
    w_copies = [copy(src, dst) for src, dst in pairs]
    tile_copies = [copy(tile_val.at[b], tiles.at[b]) for b in range(blocks)]
    dense[...] = jnp.zeros_like(dense)
    step = firsts.shape[1]
    classes, units = seconds.shape[1:]
    groups = firsts.shape[2] // units
    base = 2 * step * groups
    pad = (weights.shape[0] - base) // 2
    weights[pl.ds(base, 2 * pad), :] = jnp.zeros((2 * pad, units), BF16)
    for load in w_copies:
        load.wait()
    for j in range(groups):
        at = pl.ds(j * units, units)
        weights[pl.ds(2 * step * j, step), :] = firsts[0, :, at]
        weights[pl.ds(2 * step * j + step, step), :] = firsts[1, :, at]
    weights[pl.ds(base, classes), :] = seconds[0]
    weights[pl.ds(base + pad, classes), :] = seconds[1]
    stores = [copy(weights, weights_out)]
    for b in range(blocks):
        rows = pl.ds(b * BLOCK, BLOCK)
        tile_copies[b].wait()

        def add(k, _, b=b, rows=rows):
            at = pl.ds(pl.multiple_of(tile_src[b, k] * BLOCK, BLOCK), BLOCK)
            dense[rows, at] = dense[rows, at] + tiles[b, k].astype(F32)
            return 0

        lax.fori_loop(0, per_block, add, 0)
        for c in range(dense.shape[1] // own):
            high, low = halves(dense[rows, pl.ds(c * own, own)])
            a_ref[rows, pl.ds(2 * c * own, own)] = high
            a_ref[rows, pl.ds((2 * c + 1) * own, own)] = low
        stores.append(copy(a_ref.at[rows], a_out.at[rows]))
    for store in stores:
        store.wait()


def pack_kernel(groups, count, send_rows, *refs):
    pieces, (pick, full, packed), (turned,) = refs[:groups], refs[groups : groups + 3], refs[groups + 3 :]
    step, own = pieces[0].shape
    dests, slots = send_rows.shape
    columns = send_rows[...].astype(F32).T
    row_id = lax.broadcasted_iota(jnp.int32, (slots, own), 1).astype(F32)
    slot_id = lax.broadcasted_iota(jnp.int32, (slots, own), 0)
    for d in range(dests):
        hit = (columns[:, d : d + 1] == row_id) & (slot_id < count[0, d])
        pick[pl.ds(d * slots, slots), :] = jnp.where(hit, 1.0, 0.0).astype(BF16)
    for k, piece in enumerate(pieces):
        turned[pl.ds(k * step, step), :] = piece[...]
    full[...] = turned[...].T
    packed[...] = mm(pick[...], full[...]).astype(BF16)


def first_kernel(pick, a_ref, full, source, turned, agg, left, packed):
    own = full.shape[0]
    step = turned.shape[0]
    total = spread(a_ref[:, : 2 * own], full[...]) + spread(a_ref[:, 2 * own :], source[...])
    agg[...] = total.astype(BF16)
    packed[...] = mm(pick[...], agg[...]).astype(BF16)
    left[:step] = turned[...]
    left[step:] = agg[...].T[:step]


def forward_kernel(
    class_count, grad_scale, groups, ids, a_ref, full, agg, source, landed, labels, *refs
):
    weights = refs[:groups]
    turned, mine, agg_mine, loss, slope, packed = refs[groups:]
    own, cols = full.shape
    units = weights[0].shape[1]
    halo = landed.shape[0]
    step = cols // groups
    base = 2 * step * groups
    pad = turned.shape[0]
    slots = halo // packed.shape[0]
    near = jnp.concatenate([full[...], agg[...]], axis=1)
    total = jnp.zeros((pad, own), F32)
    for k in range(groups):
        group = lax.rem(ids[0] + groups - k, groups)
        begin = [pl.multiple_of(2 * step * group + part * step, step) for part in (0, 1)]
        w_one = jnp.concatenate([w[pl.ds(at, step), :] for at in begin for w in weights], axis=0)
        pre = mm(near, w_one)
        slope[k] = gelu_slope(pre)
        out = gelu(pre).astype(BF16)
        if halo == own:
            both = jnp.concatenate([source[...], landed[...]], axis=1)
            far = gelu(mm(both, w_one)).astype(BF16)
            held = spread(a_ref[...], jnp.concatenate([out, far], axis=0))
        else:

            def one(r, held, w_one=w_one):
                rows = pl.ds(pl.multiple_of(r * own, own), own)
                srcs = pl.ds(pl.multiple_of(2 * (r + 1) * own, own), 2 * own)
                both = jnp.concatenate([source[rows, :], landed[rows, :]], axis=1)
                return held + spread(a_ref[:, srcs], gelu(mm(both, w_one)).astype(BF16))

            held = lax.fori_loop(0, halo // own, one, spread(a_ref[:, : 2 * own], out))
        rounded = held.astype(BF16)
        if k == 0:
            mine[...] = out
            agg_mine[...] = rounded
        total = total + mm_nt(weights[k][pl.ds(base, pad), :], out) + mm_nt(weights[k][pl.ds(base + pad, pad), :], rounded)
    class_id = lax.broadcasted_iota(jnp.int32, total.shape, 0)
    real = class_id < class_count
    top = jnp.max(jnp.where(real, total, -jnp.inf), axis=0, keepdims=True)
    shifted = total - top
    powers = jnp.where(real, jnp.exp(shifted), 0.0)
    sums = jnp.sum(powers, axis=0, keepdims=True)
    target = (class_id == labels[...]).astype(F32)
    turned[...] = ((powers / sums - target) * grad_scale).astype(BF16)
    row_loss = jnp.log(sums) - jnp.sum(shifted * target, axis=0, keepdims=True)
    loss[...] = jnp.broadcast_to(jnp.sum(row_loss, axis=1, keepdims=True), loss.shape)
    per_chunk = own // slots
    for c in range(halo // own):
        back = mm(turned[...], a_ref[:, pl.ds(2 * (c + 1) * own, own)]).T.astype(BF16)
        for d in range(per_chunk):
            put_message(packed, c * per_chunk + d, back[d * slots : (d + 1) * slots])


def message_shape(slots, pad):
    compact = BLOCK < pad <= BLOCK + BLOCK // 2 and slots % 32 == 0
    return (slots + slots // 2, BLOCK) if compact else (slots, pad)


def put_message(packed, d, rows):
    slots, pad = rows.shape
    if packed.shape[1:] == (slots, pad):
        packed[d] = rows
        return
    half, tail = slots // 2, pad - BLOCK
    packed[d, :slots, :] = rows[:, :BLOCK]
    filler = jnp.zeros((half, BLOCK // 2 - tail), BF16)
    packed[d, slots:, :] = jnp.concatenate([rows[:half, BLOCK:], filler, rows[half:, BLOCK:], filler], axis=1)


def take_message(packed, d, landed):
    slots, pad = landed.shape[0] // packed.shape[0], landed.shape[1]
    if packed.shape[1:] == (slots, pad):
        landed[pl.ds(d * slots, slots), :] = packed[d]
        return
    half, tail = slots // 2, pad - BLOCK
    landed[pl.ds(d * slots, slots), :BLOCK] = packed[d, :slots, :]
    landed[pl.ds(d * slots, half), BLOCK:] = packed[d, slots:, :tail]
    landed[pl.ds(d * slots + half, half), BLOCK:] = packed[d, slots:, BLOCK // 2 : BLOCK // 2 + tail]


def cut(rows, lanes, parts):
    across = lanes // BLOCK
    down = parts // across
    height = rows // down
    return [(slice(p % down * height, (p % down + 1) * height), slice(p // down * BLOCK, (p // down + 1) * BLOCK)) for p in range(parts)]


def backward_kernel(
    class_count, parts, groups, ids, turned, pick, a_ref, slope, left, mine, agg_mine, loss, landed, *refs
):
    weights = refs[:groups]
    if parts:
        out, rows, both = refs[groups:]
    else:
        out, both, rows = refs[groups:]
    own, units = mine.shape
    pad = turned.shape[0]
    step = left.shape[0] // 2
    base = 2 * step * groups
    own_grads = mm(turned[...], mine[...])
    row = lax.broadcasted_iota(jnp.int32, own_grads.shape, 0)
    both[:, :units] = jnp.where(row == class_count, loss[0:1, 0:1], own_grads)
    both[:, units:] = mm(turned[...], agg_mine[...])
    for d in range(landed.shape[0]):
        take_message(landed, d, rows)
    high, low = halves(mm(turned[...], a_ref[:, :own]) + mm_tn(rows[...], pick[...]))
    wide = jnp.concatenate([turned[...], high, low], axis=0).T
    for k in range(groups):
        group = lax.rem(ids[0] + groups - k, groups)
        w_neigh = weights[k][pl.ds(base + pad, pad), :]
        total = mm(wide, jnp.concatenate([weights[k][pl.ds(base, pad), :], w_neigh, w_neigh], axis=0))
        result = mm(left[...], (total * slope[k]).astype(BF16))
        if parts:
            for i in range(units // BLOCK):
                out[group * (units // BLOCK) + i, pl.ds(0, 2 * step), :] = result[:, i * BLOCK : (i + 1) * BLOCK]
        else:
            out[:, pl.ds(pl.multiple_of(group * units, units), units)] = result
    if parts:
        for p, (height, lanes) in enumerate(cut(*both.shape, parts)):
            out[p, pl.ds(2 * step, out.shape[1] - 2 * step), :] = both[height, lanes]


def sum_kernel(pieces, out):
    held = pieces[0]
    for k in range(1, pieces.shape[0]):
        held = held + pieces[k]
    for k in range(pieces.shape[0]):
        out[k] = held


def place_kernel(class_count, node_total, pieces, self1, neigh1, self2, neigh2, loss, both):
    step = self1.shape[0]
    for p, (rows, lanes) in enumerate(cut(*both.shape, pieces.shape[0])):
        both[rows, lanes] = pieces[p, pl.ds(2 * step, pieces.shape[1] - 2 * step), :]
    for p in range(pieces.shape[0]):
        at = pl.ds(p * BLOCK, BLOCK)
        self1[:, at] = pieces[p, pl.ds(0, step), :]
        neigh1[:, at] = pieces[p, pl.ds(step, step), :]
    units = self2.shape[1]
    self2[...] = both[:class_count, :units]
    neigh2[...] = both[:class_count, units:]
    loss[...] = both[class_count : class_count + 1, 0:1] / node_total


def swap(value, count):
    blocks = value.reshape(count, -1, value.shape[-1])
    return lax.all_to_all(blocks, "node", 0, 0, tiled=True)


def gather_shifted(value, count):
    return [value] + [lax.ppermute(value, "feat", [(i, (i + k) % count) for i in range(count)]) for k in range(1, count)]


def shards(features, send_rows, send_count, tile_src, tile_val, labels, w_self1, w_neigh1, w_self2, w_neigh2):
    nodes, groups = lax.axis_size("node"), lax.axis_size("feat")
    own, step = features.shape
    slots = send_rows.shape[2]
    halo = nodes * slots
    total_src = own + halo
    cols = step * groups
    width = w_self1.shape[1]
    units, classes = w_self2.shape
    pad = -(-(classes + 1) // 16) * 16
    across = 2 * units // BLOCK
    parts = nodes if nodes % across == 0 and pad % (8 * (nodes // across)) == 0 and width == nodes * BLOCK else 0
    node_total = own * nodes
    grad_scale = 1.0 / math.sqrt(node_total)
    ids = lax.axis_index("feat").astype(jnp.int32).reshape(1)
    blocks = own // BLOCK
    packed_rows = 2 * step * groups + 2 * pad

    turned = features.T
    turned_all = gather_shifted(turned, groups)
    a_mat, packed_weights = call(
        prepare_kernel,
        [((own, 2 * total_src), BF16), ((packed_rows, units), BF16)],
        (tile_src, tile_val, w_self1, w_neigh1, w_self2.T, w_neigh2.T),
        [
            ((own, 2 * total_src), BF16),
            ((packed_rows, units), BF16),
            (tile_val.shape, BF16),
            ((2, step, width), BF16),
            ((2, classes, units), BF16),
            ((own, total_src), F32),
        ],
        copies=5 + 2 * blocks,
        moved=tile_val.size * 4,
        grant=58 * 2**20,
    )
    weights = gather_shifted(packed_weights, groups)
    pick, full, packed = call(
        functools.partial(pack_kernel, groups),
        [((halo, own), BF16), ((own, cols), BF16), ((halo, cols), BF16)],
        (send_count, send_rows[0], *turned_all),
        [((cols, own), BF16)],
        flops=2 * halo * own * cols,
        moved=halo * own * 2,
    )
    source = swap(packed, nodes).reshape(halo, cols)
    agg, left, packed = call(
        first_kernel,
        [((own, cols), BF16), ((2 * step, own), BF16), ((halo, cols), BF16)],
        (pick, a_mat, full, source, turned),
        flops=4 * own * total_src * cols,
        moved=4 * own * total_src,
    )
    landed = swap(packed, nodes).reshape(halo, cols)
    message = (nodes, *message_shape(slots, pad))
    turned_grads, mine, agg_mine, loss, slope, packed = call(
        functools.partial(forward_kernel, classes, grad_scale, groups),
        [
            ((pad, own), BF16),
            ((own, units), BF16),
            ((own, units), BF16),
            ((8, 128), F32),
            ((groups, own, units), F32),
            (message, BF16),
        ],
        (ids, a_mat, full, agg, source, landed, labels.reshape(1, own), *weights),
        flops=8 * own * total_src * width,
        moved=16 * own * width,
    )
    landed = swap(packed, nodes)
    second_shape = (pad, 2 * units)
    grads_shape = (parts, 2 * step + pad * 2 * units // (BLOCK * parts), BLOCK) if parts else (2 * step, width)
    grads, *second = call(
        functools.partial(backward_kernel, classes, parts, groups),
        [(grads_shape, F32)] + ([] if parts else [(second_shape, F32)]),
        (ids, turned_grads, pick, a_mat, slope, left, mine, agg_mine, loss, landed, *weights),
        [((halo, pad), BF16)] + ([(second_shape, F32)] if parts else []),
        flops=8 * own * pad * width,
        moved=12 * own * width,
    )
    if not parts:
        grads, second = lax.psum((grads, second[0]), "node")
        loss = second[classes, 0] / node_total
        return (loss, grads[:step], grads[step:], second[:classes, :units].T, second[:classes, units:].T)
    grads = swap(grads, nodes)
    (grads,) = call(sum_kernel, [(grads_shape, F32)], (grads,), moved=2**20)
    grads = swap(grads, nodes)
    grad_self1, grad_neigh1, grad_self2, grad_neigh2, loss = call(
        functools.partial(place_kernel, classes, node_total),
        [((step, width), F32)] * 2 + [((classes, units), F32)] * 2 + [((1, 1), F32)],
        (grads,),
        [(second_shape, F32)],
    )
    return (loss.reshape(()), grad_self1, grad_neigh1, grad_self2.T, grad_neigh2.T)


def solution(mesh):
    in_specs = (
        P("node", "feat"),
        P("node", None, None),
        P("node", None),
        P("node", None),
        P("node", None, None, None),
        P("node"),
        P("feat", None),
        P("feat", None),
        P("feat", None),
        P("feat", None),
    )
    out_specs = (P(), P("feat", None), P("feat", None), P("feat", None), P("feat", None))
    return jax.shard_map(shards, mesh=mesh, in_specs=in_specs, out_specs=out_specs, check_vma=False)
```

time: 275 us -> 106 us (0.39)
  waiting for transfers between devices: 142 us -> 13.6 us
  local copies, waits for them, and re-layouts: 35.5 us -> 6.54 us
  blocking collectives: 22.1 us -> 50.2 us
  matrix products: 23.4 us -> 0 us
  Pallas kernels: 0 us -> 19.2 us
  other arithmetic: 16 us -> 0 us
  between operations: 15.8 us -> 0.72 us
  starting transfers between devices: 18.9 us -> 14.7 us
    psum x2 -> x0, waiting for transfers between devices: 81.9 us -> none  [the longest x1 51.3 us: shards(): summed = lax.psum(local_grads, 'node')]
    all_to_all x0 -> x3, blocking collectives: none -> 50.2 us  [swap(): return lax.all_to_all(blocks, 'node', 0, 0, tiled=True)]
    reduce_scatter x1 -> x0, waiting for transfers between devices: 30.4 us -> none  [shards(): lax.psum_scatter(partial_one, 'feat', scatter_dimension=1, tiled=True)]
    dot_general x14 -> x0, matrix products: 23.4 us -> none  [the longest x1 4.52 us: spread_back(): jnp.einsum('bkij,bih->bkjh', tile_val, grads.reshape(-1, 128, col_count),...]
    psum x1 -> x0, blocking collectives: 22.1 us -> none  [shards(): mean_loss = lax.psum(jnp.sum(row_loss), 'node') / node_total]
    pallas_call x0 -> x7, Pallas kernels: none -> 19.2 us  [call(): pl.pallas_call(body, out_shape=[jax.ShapeDtypeStruct(shape, dtype) for sh...]
    all_gather x1 -> x0, waiting for transfers between devices: 13.4 us -> none  [shards(): shard_piece = lax.all_gather(pre_grad, 'feat', axis=1, tiled=True)]
    all_to_all x3 -> x2, waiting for transfers between devices: 16.4 us -> 5.72 us  [swap(): return lax.all_to_all(blocks, 'node', 0, 0, tiled=True)]
  transfers between devices with their start and end apart: 7 -> 8, of which waited for: 7 -> 7; matrix products, arithmetic and copies ran while one was open for 3% -> 0% of each run, Pallas kernels for 0% -> 5%
where the time goes in v7:
time: 106 us; the launch traced here: 105 us
  blocking collectives  50.2 us (47%)
  Pallas kernels  19.2 us (18%)
  starting transfers between devices  14.7 us (14%)
  waiting for transfers between devices  13.6 us (13%)
  local copies, waits for them, and re-layouts  6.54 us (6%)
    all_to_all x3, blocking collectives, swap(): return lax.all_to_all(blocks, 'node', 0, 0, tiled=True)  50.2 us
    pallas_call x7, Pallas kernels, call(): pl.pallas_call(body, out_shape=[jax.ShapeDtypeStruct(shape, dtype) for sh...  19.2 us
    all_to_all x2, starting transfers between devices, swap(): return lax.all_to_all(blocks, 'node', 0, 0, tiled=True)  10.1 us
    ppermute x6, waiting for transfers between devices, gather_shifted(): lax.ppermute(value, 'feat', [(i, (i + k) % count) for i in range(count)])  7.86 us
    unnamed x26, local copies, waits for them, and re-layouts  6.54 us
    all_to_all x2, waiting for transfers between devices, swap(): return lax.all_to_all(blocks, 'node', 0, 0, tiled=True)  5.72 us
    ppermute x6, starting transfers between devices, gather_shifted(): lax.ppermute(value, 'feat', [(i, (i + k) % count) for i in range(count)])  4.62 us
  transfers between devices with their start and end apart: 8, of which 7 were waited for; matrix products, arithmetic and copies ran while one was open for 0% of the time, Pallas kernels for 5%

profile of v7, /device:TPU:0, one launch (start us, length us, event | category | flops | bytes accessed | tf_op | source)
XLA Modules:
  0.0 104.9 jit_solution(15705984545747016464)
XLA Ops:
  0.6 2.4 %collective-permute-start.2 = (bf16[32,512]{1,0:T(8,128)(2,1)}, bf16[32,512]{1,0:T(8,128)(2,1)S(1)}, u32[]{:S(2)}, u32[]{:S(2)}) collective-permute-start(bf16[32,512]{1,0:T(8,128)(2,1)} %bitcast.16), channel_id=1, source_target_pairs={{0,3},{1,0},{2,1},{3,2},{4,7},{5,4},{6,5},{7,6},{8,11},{9,8},{10,9... | collective-permute-start | bytes 98312 | tf_op jit(solution)/shard_map/ppermute | solution.py:314
  3.9 1.2 %collective-permute-done.2.refs_3_ = bf16[32,512]{1,0:T(8,128)(2,1)S(1)} collective-permute-done((bf16[32,512]{1,0:T(8,128)(2,1)}, bf16[32,512]{1,0:T(8,128)(2,1)S(1)}, u32[]{:S(2)}, u32[]{:S(2)}) %collective-permute-start.2) | collective-permute-done | bytes 32800 | tf_op jit(solution)/shard_map/ppermute | solution.py:314
  5.0 2.4 %collective-permute-done.1.refs_2_ = bf16[32,512]{1,0:T(8,128)(2,1)S(1)} collective-permute-done((bf16[32,512]{1,0:T(8,128)(2,1)}, bf16[32,512]{1,0:T(8,128)(2,1)S(1)}, u32[]{:S(2)}, u32[]{:S(2)}) %collective-permute-start.1) | collective-permute-done | bytes 32800 | tf_op jit(solution)/shard_map/ppermute | solution.py:314
  7.5 0.8 copy-done.6
  8.3 0.7 copy-done.10
  9.0 0.7 copy-done.12
  9.6 1.7 %shard_map.138 = (bf16[512,512]{1,0:T(8,128)(2,1)S(1)}, bf16[512,128]{1,0:T(8,128)(2,1)S(1)}, bf16[512,128]{1,0:T(8,128)(2,1)}) custom-call(s32[1,8]{1,0:T(1,128)S(1)} %copy-done.12, s32[8,64]{1,0:T(8,128)S(1)} %bitcast.21, bf16[32,512]{1,0:T(8,128)(2,1)S(1)} %bitcast.19, bf16[32,512]{1,0:T(8,128)(2,1)S(1)} %collective-permute-done.refs_1_, ...), custom_call_target="tpu_custom_call" | custom-call | flops 67108864 | bytes 524288 | tf_op jit(solution)/shard_map/pallas_call | solution.py:72
  11.3 5.8 %all-to-all-start = ((bf16[8,64,128]{2,1,0:T(8,128)(2,1)}), bf16[8,64,128]{2,1,0:T(8,128)(2,1)S(1)}, u32[]{:S(2)}, u32[]{:S(2)}) async-start(bf16[8,64,128]{2,1,0:T(8,128)(2,1)} %bitcast.5), calls=%async_computation | async-start | bytes 262144 | tf_op jit(solution)/shard_map/all_to_all | solution.py:310
  17.1 4.1 %shard_map.137 = (bf16[512,2048]{1,0:T(8,128)(2,1)}, bf16[608,256]{1,0:T(8,128)(2,1)}) custom-call(s32[4,16]{1,0:T(4,128)} %tile_src.1, bf16[4,16,128,128]{3,2,1,0:T(8,128)(2,1)} %tile_val.1, bf16[32,1024]{1,0:T(8,128)(2,1)} %w_self1.1, bf16[32,1024]{1,0:T(8,128)(2,1)} %w_neigh1.1, bf16[172,256]{1,0:T(8,128)(2,1)} %bitcast.23, bf16[172,256]{1,0:T(8,128)(2,1)} %bitcast.24), custom_call_target="tpu_custom_call" | custom-call | bytes 4194304 | tf_op jit(solution)/shard_map/pallas_call | solution.py:72
  21.4 1.2 %collective-permute-start.4 = (bf16[608,256]{1,0:T(8,128)(2,1)}, bf16[608,256]{1,0:T(8,128)(2,1)}, u32[]{:S(2)}, u32[]{:S(2)}) collective-permute-start(bf16[608,256]{1,0:T(8,128)(2,1)} %get-tuple-element.30.refs_0_), channel_id=1, source_target_pairs={{0,2},{1,3},{2,0},{3,1},{4,6},{5,7},{6,4},{7,5},{8,10},{9,11},{10,... | collective-permute-start | bytes 933896 | tf_op jit(solution)/shard_map/ppermute | solution.py:314
  22.7 1.8 %all-to-all-done = bf16[8,64,128]{2,1,0:T(8,128)(2,1)S(1)} async-done(((bf16[8,64,128]{2,1,0:T(8,128)(2,1)}), bf16[8,64,128]{2,1,0:T(8,128)(2,1)S(1)}, u32[]{:S(2)}, u32[]{:S(2)}) %all-to-all-start) | async-done | bytes 131104 | tf_op jit(solution)/shard_map/all_to_all | solution.py:310
  24.5 1.6 %copy-done = bf16[512,2048]{1,0:T(8,128)(2,1)S(1)} copy-done((bf16[512,2048]{1,0:T(8,128)(2,1)S(1)}, bf16[512,2048]{1,0:T(8,128)(2,1)}, u32[]{:S(2)}) %copy-start) | copy-done | bytes 2097176
  26.1 1.2 %shard_map.139 = (bf16[512,128]{1,0:T(8,128)(2,1)S(1)}, bf16[64,512]{1,0:T(8,128)(2,1)S(1)}, bf16[512,128]{1,0:T(8,128)(2,1)S(1)}) custom-call(bf16[512,512]{1,0:T(8,128)(2,1)S(1)} %get-tuple-element.26.pick, bf16[512,2048]{1,0:T(8,128)(2,1)S(1)} %copy-done, bf16[512,128]{1,0:T(8,128)(2,1)S(1)} %get-tuple-element.25.full, bf16[512,128]{1,0:T(8,128)(2,1)S(1)} %bitcast.13, ...), custom_call_target="tpu_custom_call" | custom-call | flops 268435456 | bytes 2097152 | tf_op jit(solution)/shard_map/pallas_call | solution.py:72
  28.6 0.7 copy-done.8
  29.2 4.2 %all-to-all-start.1 = ((bf16[8,64,128]{2,1,0:T(8,128)(2,1)}), bf16[8,64,128]{2,1,0:T(8,128)(2,1)}, u32[]{:S(2)}, u32[]{:S(2)}) async-start(bf16[8,64,128]{2,1,0:T(8,128)(2,1)} %bitcast.15), calls=%async_computation.1 | async-start | bytes 262144 | tf_op jit(solution)/shard_map/all_to_all | solution.py:310
  33.5 3.8 %collective-permute-done.4.refs_2_ = bf16[608,256]{1,0:T(8,128)(2,1)} collective-permute-done((bf16[608,256]{1,0:T(8,128)(2,1)}, bf16[608,256]{1,0:T(8,128)(2,1)}, u32[]{:S(2)}, u32[]{:S(2)}) %collective-permute-start.4) | collective-permute-done | bytes 311328 | tf_op jit(solution)/shard_map/ppermute | solution.py:314
  37.6 3.9 %all-to-all-done.1 = bf16[8,64,128]{2,1,0:T(8,128)(2,1)} async-done(((bf16[8,64,128]{2,1,0:T(8,128)(2,1)}), bf16[8,64,128]{2,1,0:T(8,128)(2,1)}, u32[]{:S(2)}, u32[]{:S(2)}) %all-to-all-start.1) | async-done | bytes 131104 | tf_op jit(solution)/shard_map/all_to_all | solution.py:310
  41.6 0.9 copy-done.9
  42.5 7.4 %shard_map.140 = (bf16[176,512]{1,0:T(8,128)(2,1)S(1)}, bf16[512,256]{1,0:T(8,128)(2,1)S(1)}, bf16[512,256]{1,0:T(8,128)(2,1)S(1)}, f32[8,128]{1,0:T(8,128)S(1)}...) custom-call(s32[1]{0:T(128)} %bitcast.ids, bf16[512,2048]{1,0:T(8,128)(2,1)S(1)} %copy-done.1, ...), custom_call_target="tpu_custom_call" | custom-call | flops 4294967296 | bytes 8388608 | tf_op jit(solution)/shard_map/pallas_call | solution.py:72
  50.0 10.7 %all_to_all.25.landed = bf16[8,96,128]{2,1,0:T(8,128)(2,1)S(1)} all-to-all(bf16[8,96,128]{2,1,0:T(8,128)(2,1)S(1)} %get-tuple-element.37), channel_id=1, replica_groups=mesh['node'=8,'feat'=4] {'node'}, dimensions={0} | all-to-all | bytes 393216 | tf_op jit(solution)/shard_map/all_to_all | solution.py:310
  60.7 3.9 %shard_map.141 = f32[8,152,128]{2,1,0:T(8,128)S(1)} custom-call(s32[1]{0:T(128)} %bitcast.ids, bf16[176,512]{1,0:T(8,128)(2,1)S(1)} %get-tuple-element.31.turned, bf16[512,512]{1,0:T(8,128)(2,1)S(1)} %get-tuple-element.26.pick, bf16[512,2048]{1,0:T(8,128)(2,1)S(1)} %copy-done.1, f32[4,512,256]{2,1,0:T(8,128)S(1)} %get-tuple-element.32.slope, ...), custom_call_target="tpu_custom_call" | custom-call | flops 738197504 | bytes 6291456 | tf_op jit(solution)/shard_map/pallas_call | solution.py:72
  64.6 19.8 %all_to_all.26.pieces = f32[8,152,128]{2,1,0:T(8,128)S(1)} all-to-all(f32[8,152,128]{2,1,0:T(8,128)S(1)} %shard_map.141), channel_id=1, replica_groups=mesh['node'=8,'feat'=4] {'node'}, dimensions={0} | all-to-all | bytes 1245184 | tf_op jit(solution)/shard_map/all_to_all | solution.py:310
  84.5 19.6 %all_to_all.27.pieces = f32[8,152,128]{2,1,0:T(8,128)S(1)} all-to-all(f32[8,152,128]{2,1,0:T(8,128)S(1)} %shard_map.142), channel_id=1, replica_groups=mesh['node'=8,'feat'=4] {'node'}, dimensions={0} | all-to-all | bytes 1245184 | tf_op jit(solution)/shard_map/all_to_all | solution.py:310
  104.1 0.8 shard_map.143
  (28 shorter events, 2.9 us)
Async XLA Ops:
  0.6 4.4 %collective-permute-start.2 = (bf16[32,512]{1,0:T(8,128)(2,1)}, bf16[32,512]{1,0:T(8,128)(2,1)S(1)}, u32[]{:S(2)}, u32[]{:S(2)}) collective-permute-start(bf16[32,512]{1,0:T(8,128)(2,1)} %bitcast.16), channel_id=1, source_target_pairs={{0,3},{1,0},{2,1},{3,2},{4,7},{5,4},{6,5},{7,6},{8,11},{9,8},{10,9... | collective-permute-start | bytes 98312 | tf_op jit(solution)/shard_map/ppermute | solution.py:314
  3.1 4.4 %collective-permute-start.1 = (bf16[32,512]{1,0:T(8,128)(2,1)}, bf16[32,512]{1,0:T(8,128)(2,1)S(1)}, u32[]{:S(2)}, u32[]{:S(2)}) collective-permute-start(bf16[32,512]{1,0:T(8,128)(2,1)} %bitcast.17), channel_id=1, source_target_pairs={{0,2},{1,3},{2,0},{3,1},{4,6},{5,7},{6,4},{7,5},{8,10},{9,11},{10,... | collective-permute-start | bytes 98312 | tf_op jit(solution)/shard_map/ppermute | solution.py:314
  3.7 3.8 %collective-permute-start = (bf16[32,512]{1,0:T(8,128)(2,1)}, bf16[32,512]{1,0:T(8,128)(2,1)S(1)}, u32[]{:S(2)}, u32[]{:S(2)}) collective-permute-start(bf16[32,512]{1,0:T(8,128)(2,1)} %bitcast.18), channel_id=1, source_target_pairs={{0,1},{1,2},{2,3},{3,0},{4,5},{5,6},{6,7},{7,4},{8,9},{9,10},{10,1... | collective-permute-start | bytes 98312 | tf_op jit(solution)/shard_map/ppermute | solution.py:314
  7.5 0.8 copy-start.6
  8.3 0.7 copy-start.10
  9.0 0.7 copy-start.12
  9.6 14.8 %copy-start.7 = (bf16[512,32]{0,1:T(8,128)(2,1)S(1)}, bf16[512,32]{0,1:T(8,128)(2,1)}, u32[]{:S(2)}) copy-start(bf16[512,32]{0,1:T(8,128)(2,1)} %param.10) | copy-start | bytes 98308
  11.3 13.2 %all-to-all-start = ((bf16[8,64,128]{2,1,0:T(8,128)(2,1)}), bf16[8,64,128]{2,1,0:T(8,128)(2,1)S(1)}, u32[]{:S(2)}, u32[]{:S(2)}) async-start(bf16[8,64,128]{2,1,0:T(8,128)(2,1)} %bitcast.5), calls=%async_computation | async-start | bytes 262144 | tf_op jit(solution)/shard_map/all_to_all | solution.py:310
  21.3 20.3 %copy-start.11 = (s32[512]{0:T(512)S(1)}, s32[512]{0:T(512)}, u32[]{:S(2)}) copy-start(s32[512]{0:T(512)} %param.15) | copy-start | bytes 6148
  21.3 12.2 %collective-permute-start.5 = (bf16[608,256]{1,0:T(8,128)(2,1)}, bf16[608,256]{1,0:T(8,128)(2,1)S(1)}, u32[]{:S(2)}, u32[]{:S(2)}) collective-permute-start(bf16[608,256]{1,0:T(8,128)(2,1)} %get-tuple-element.30.refs_0_), channel_id=1, source_target_pairs={{0,3},{1,0},{2,1},{3,2},{4,7},{5,4},{6,5},{7,6},{8,11},{9,8},{10,9... | collective-permute-start | bytes 933896 | tf_op jit(solution)/shard_map/ppermute | solution.py:314
  21.4 15.9 %collective-permute-start.4 = (bf16[608,256]{1,0:T(8,128)(2,1)}, bf16[608,256]{1,0:T(8,128)(2,1)}, u32[]{:S(2)}, u32[]{:S(2)}) collective-permute-start(bf16[608,256]{1,0:T(8,128)(2,1)} %get-tuple-element.30.refs_0_), channel_id=1, source_target_pairs={{0,2},{1,3},{2,0},{3,1},{4,6},{5,7},{6,4},{7,5},{8,10},{9,11},{10,... | collective-permute-start | bytes 933896 | tf_op jit(solution)/shard_map/ppermute | solution.py:314
  22.5 15.1 %collective-permute-start.3 = (bf16[608,256]{1,0:T(8,128)(2,1)}, bf16[608,256]{1,0:T(8,128)(2,1)}, u32[]{:S(2)}, u32[]{:S(2)}) collective-permute-start(bf16[608,256]{1,0:T(8,128)(2,1)} %get-tuple-element.30.refs_0_), channel_id=1, source_target_pairs={{0,1},{1,2},{2,3},{3,0},{4,5},{5,6},{6,7},{7,4},{8,9},{9,10},{10,1... | collective-permute-start | bytes 933896 | tf_op jit(solution)/shard_map/ppermute | solution.py:314
  24.5 1.6 %copy-start = (bf16[512,2048]{1,0:T(8,128)(2,1)S(1)}, bf16[512,2048]{1,0:T(8,128)(2,1)}, u32[]{:S(2)}) copy-start(bf16[512,2048]{1,0:T(8,128)(2,1)} %get-tuple-element.24.a_ref) | copy-start | bytes 6291460
  26.1 15.5 %copy-start.1 = (bf16[512,2048]{1,0:T(8,128)(2,1)S(1)}, bf16[512,2048]{1,0:T(8,128)(2,1)}, u32[]{:S(2)}) copy-start(bf16[512,2048]{1,0:T(8,128)(2,1)} %get-tuple-element.24.a_ref) | copy-start | bytes 6291460
  26.1 15.5 %copy-start.2 = (bf16[608,256]{1,0:T(8,128)(2,1)S(1)}, bf16[608,256]{1,0:T(8,128)(2,1)}, u32[]{:S(2)}) copy-start(bf16[608,256]{1,0:T(8,128)(2,1)} %get-tuple-element.30.refs_0_) | copy-start | bytes 933892
  27.3 0.7 copy-start.3
  28.0 0.6 copy-start.4
  28.6 0.7 copy-start.8
  29.2 12.3 %all-to-all-start.1 = ((bf16[8,64,128]{2,1,0:T(8,128)(2,1)}), bf16[8,64,128]{2,1,0:T(8,128)(2,1)}, u32[]{:S(2)}, u32[]{:S(2)}) async-start(bf16[8,64,128]{2,1,0:T(8,128)(2,1)} %bitcast.15), calls=%async_computation.1 | async-start | bytes 262144 | tf_op jit(solution)/shard_map/all_to_all | solution.py:310
  41.6 0.9 copy-start.9
  42.5 18.2 %copy-start.5 = (bf16[64,512]{1,0:T(8,128)(2,1)S(1)}, bf16[64,512]{1,0:T(8,128)(2,1)}, u32[]{:S(2)}) copy-start(bf16[64,512]{1,0:T(8,128)(2,1)} %copy-done.4) | copy-start | bytes 196612

commit v8 on v7

--- a/solution.py
+++ b/solution.py
@@ -42,20 +42,15 @@
     return mm(a, jnp.concatenate(parts, axis=0))
 
 
-def gelu_parts(v):
-    inner = math.sqrt(2.0 / math.pi) * (v + 0.044715 * (v * v * v))
-    t = jnp.tanh(inner)
-    return 0.5 * (1.0 + t), t
-
-
-def gelu(v):
-    return v * gelu_parts(v)[0]
-
-
-def gelu_slope(v):
-    cdf, t = gelu_parts(v)
-    inner_slope = math.sqrt(2.0 / math.pi) * (1.0 + 3 * 0.044715 * (v * v))
-    return cdf + 0.5 * v * (1.0 - t * t) * inner_slope
+def activate(v, with_slope):
+    scale = math.sqrt(2.0 / math.pi)
+    square = v * v
+    t = jnp.tanh(v * (scale + (scale * 0.044715) * square))
+    half = 0.5 * v
+    out = (half + half * t).astype(BF16)
+    if not with_slope:
+        return out
+    return out, (0.5 + 0.5 * t) + half * (1.0 - t * t) * (scale + (scale * 3 * 0.044715) * square)
 
 
 def size_of(shape, dtype):
@@ -148,48 +143,48 @@
     packed[...] = mm(pick[...], full[...]).astype(BF16)
 
 
-def first_kernel(pick, a_ref, full, source, turned, agg, left, packed):
-    own = full.shape[0]
-    step = turned.shape[0]
+def first_kernel(pick, a_ref, full, source, state, packed):
+    own, cols = full.shape
     total = spread(a_ref[:, : 2 * own], full[...]) + spread(a_ref[:, 2 * own :], source[...])
-    agg[...] = total.astype(BF16)
-    packed[...] = mm(pick[...], agg[...]).astype(BF16)
-    left[:step] = turned[...]
-    left[step:] = agg[...].T[:step]
+    agg = total.astype(BF16)
+    packed[...] = mm(pick[...], agg).astype(BF16)
+    state[:own, :cols] = full[...]
+    state[:own, cols:] = agg
+    state[own:, :cols] = source[...]
+    state[own:, cols:] = jnp.zeros_like(source)
 
 
 def forward_kernel(
-    class_count, grad_scale, groups, ids, a_ref, full, agg, source, landed, labels, *refs
+    class_count, grad_scale, groups, ids, a_ref, state, landed, labels, *refs
 ):
     weights = refs[:groups]
     turned, mine, agg_mine, loss, slope, packed = refs[groups:]
-    own, cols = full.shape
+    halo, cols = landed.shape
+    own = state.shape[0] - halo
     units = weights[0].shape[1]
-    halo = landed.shape[0]
     step = cols // groups
     base = 2 * step * groups
     pad = turned.shape[0]
     slots = halo // packed.shape[0]
-    near = jnp.concatenate([full[...], agg[...]], axis=1)
+    near = state[:own, :]
     total = jnp.zeros((pad, own), F32)
     for k in range(groups):
         group = lax.rem(ids[0] + groups - k, groups)
         begin = [pl.multiple_of(2 * step * group + part * step, step) for part in (0, 1)]
         w_one = jnp.concatenate([w[pl.ds(at, step), :] for at in begin for w in weights], axis=0)
-        pre = mm(near, w_one)
-        slope[k] = gelu_slope(pre)
-        out = gelu(pre).astype(BF16)
+        out, slope[k] = activate(mm(near, w_one), True)
         if halo == own:
-            both = jnp.concatenate([source[...], landed[...]], axis=1)
-            far = gelu(mm(both, w_one)).astype(BF16)
+            both = jnp.concatenate([state[own:, :cols], landed[...]], axis=1)
+            far = activate(mm(both, w_one), False)
             held = spread(a_ref[...], jnp.concatenate([out, far], axis=0))
         else:
 
             def one(r, held, w_one=w_one):
                 rows = pl.ds(pl.multiple_of(r * own, own), own)
                 srcs = pl.ds(pl.multiple_of(2 * (r + 1) * own, own), 2 * own)
-                both = jnp.concatenate([source[rows, :], landed[rows, :]], axis=1)
-                return held + spread(a_ref[:, srcs], gelu(mm(both, w_one)).astype(BF16))
+                lower = pl.ds(pl.multiple_of((r + 1) * own, own), own)
+                both = jnp.concatenate([state[lower, :cols], landed[rows, :]], axis=1)
+                return held + spread(a_ref[:, srcs], activate(mm(both, w_one), False))
 
             held = lax.fori_loop(0, halo // own, one, spread(a_ref[:, : 2 * own], out))
         rounded = held.astype(BF16)
@@ -249,7 +244,7 @@
 
 
 def backward_kernel(
-    class_count, parts, groups, ids, turned, pick, a_ref, slope, left, mine, agg_mine, loss, landed, *refs
+    class_count, parts, groups, ids, turned, pick, a_ref, slope, features, state, mine, agg_mine, loss, landed, *refs
 ):
     weights = refs[:groups]
     if parts:
@@ -258,7 +253,7 @@
         out, both, rows = refs[groups:]
     own, units = mine.shape
     pad = turned.shape[0]
-    step = left.shape[0] // 2
+    step = features.shape[0]
     base = 2 * step * groups
     own_grads = mm(turned[...], mine[...])
     row = lax.broadcasted_iota(jnp.int32, own_grads.shape, 0)
@@ -268,11 +263,13 @@
         take_message(landed, d, rows)
     high, low = halves(mm(turned[...], a_ref[:, :own]) + mm_tn(rows[...], pick[...]))
     wide = jnp.concatenate([turned[...], high, low], axis=0).T
+    cols = state.shape[1] // 2
+    left = jnp.concatenate([features[...], state[:own, cols:].T[:step]], axis=0)
     for k in range(groups):
         group = lax.rem(ids[0] + groups - k, groups)
         w_neigh = weights[k][pl.ds(base + pad, pad), :]
         total = mm(wide, jnp.concatenate([weights[k][pl.ds(base, pad), :], w_neigh, w_neigh], axis=0))
-        result = mm(left[...], (total * slope[k]).astype(BF16))
+        result = mm(left, (total * slope[k]).astype(BF16))
         if parts:
             for i in range(units // BLOCK):
                 out[group * (units // BLOCK) + i, pl.ds(0, 2 * step), :] = result[:, i * BLOCK : (i + 1) * BLOCK]
@@ -350,6 +347,7 @@
         moved=tile_val.size * 4,
         grant=58 * 2**20,
     )
+    packed_weights, *turned_all = lax.optimization_barrier((packed_weights, *turned_all))
     weights = gather_shifted(packed_weights, groups)
     pick, full, packed = call(
         functools.partial(pack_kernel, groups),
@@ -360,13 +358,14 @@
         moved=halo * own * 2,
     )
     source = swap(packed, nodes).reshape(halo, cols)
-    agg, left, packed = call(
+    state, packed = call(
         first_kernel,
-        [((own, cols), BF16), ((2 * step, own), BF16), ((halo, cols), BF16)],
-        (pick, a_mat, full, source, turned),
+        [((total_src, 2 * cols), BF16), ((halo, cols), BF16)],
+        (pick, a_mat, full, source),
         flops=4 * own * total_src * cols,
         moved=4 * own * total_src,
     )
+    packed, *weights = lax.optimization_barrier((packed, *weights))
     landed = swap(packed, nodes).reshape(halo, cols)
     message = (nodes, *message_shape(slots, pad))
     turned_grads, mine, agg_mine, loss, slope, packed = call(
@@ -379,7 +378,7 @@
             ((groups, own, units), F32),
             (message, BF16),
         ],
-        (ids, a_mat, full, agg, source, landed, labels.reshape(1, own), *weights),
+        (ids, a_mat, state, landed, labels.reshape(1, own), *weights),
         flops=8 * own * total_src * width,
         moved=16 * own * width,
     )
@@ -389,7 +388,7 @@
     grads, *second = call(
         functools.partial(backward_kernel, classes, parts, groups),
         [(grads_shape, F32)] + ([] if parts else [(second_shape, F32)]),
-        (ids, turned_grads, pick, a_mat, slope, left, mine, agg_mine, loss, landed, *weights),
+        (ids, turned_grads, pick, a_mat, slope, turned, state, mine, agg_mine, loss, landed, *weights),
         [((halo, pad), BF16)] + ([(second_shape, F32)] if parts else []),
         flops=8 * own * pad * width,
         moved=12 * own * width,

time: 106 us -> 105 us (level)
  the two profiles are of different devices: /device:TPU:0 before, /device:TPU:2 now
where the time goes in v8:
time: 105 us; the launch traced here: 104 us
  blocking collectives  63.3 us (60%)
  Pallas kernels  17.2 us (16%)
  starting transfers between devices  7.94 us (8%)
  waiting for transfers between devices  7.69 us (7%)
  local copies, waits for them, and re-layouts  7.33 us (7%)
    all_to_all x4, blocking collectives, swap(): return lax.all_to_all(blocks, 'node', 0, 0, tiled=True)  63.3 us
    pallas_call x7, Pallas kernels, call(): pl.pallas_call(body, out_shape=[jax.ShapeDtypeStruct(shape, dtype) for sh...  17.2 us
    all_to_all x1, waiting for transfers between devices, swap(): return lax.all_to_all(blocks, 'node', 0, 0, tiled=True)  7.68 us
    unnamed x28, local copies, waits for them, and re-layouts  7.33 us
    all_to_all x1, starting transfers between devices, swap(): return lax.all_to_all(blocks, 'node', 0, 0, tiled=True)  3.99 us
    ppermute x6, starting transfers between devices, gather_shifted(): lax.ppermute(value, 'feat', [(i, (i + k) % count) for i in range(count)])  3.95 us
  transfers between devices with their start and end apart: 7, of which 1 were waited for; matrix products, arithmetic and copies ran while one was open for 0% of the time, Pallas kernels for 6%

profile of v8, /device:TPU:2, one launch (start us, length us, event | category | flops | bytes accessed | tf_op | source)
XLA Modules:
  0.0 104.3 jit_solution(502630869854723260)
XLA Ops:
  0.7 0.1 collective-permute-start.2
  0.7 1.5 %collective-permute-start.1 = (bf16[32,512]{1,0:T(8,128)(2,1)}, bf16[32,512]{1,0:T(8,128)(2,1)S(1)}, u32[]{:S(2)}, u32[]{:S(2)}) collective-permute-start(bf16[32,512]{1,0:T(8,128)(2,1)} %bitcast.17), channel_id=1, source_target_pairs={{0,2},{1,3},{2,0},{3,1},{4,6},{5,7},{6,4},{7,5},{8,10},{9,11},{10,... | collective-permute-start | bytes 98312 | tf_op jit(solution)/shard_map/ppermute | solution.py:311
  2.2 4.2 %shard_map.137 = (bf16[512,2048]{1,0:T(8,128)(2,1)}, bf16[608,256]{1,0:T(8,128)(2,1)}) custom-call(s32[4,16]{1,0:T(4,128)} %tile_src.1, bf16[4,16,128,128]{3,2,1,0:T(8,128)(2,1)} %tile_val.1, bf16[32,1024]{1,0:T(8,128)(2,1)} %w_self1.1, bf16[32,1024]{1,0:T(8,128)(2,1)} %w_neigh1.1, bf16[172,256]{1,0:T(8,128)(2,1)} %bitcast.23, bf16[172,256]{1,0:T(8,128)(2,1)} %bitcast.24), custom_call_target="tpu_custom_call" | custom-call | bytes 4194304 | tf_op jit(solution)/shard_map/pallas_call | solution.py:67
  6.4 1.8 %collective-permute-start.5 = (bf16[608,256]{1,0:T(8,128)(2,1)}, bf16[608,256]{1,0:T(8,128)(2,1)S(1)}, u32[]{:S(2)}, u32[]{:S(2)}) collective-permute-start(bf16[608,256]{1,0:T(8,128)(2,1)} %get-tuple-element.46.refs_0_), channel_id=1, source_target_pairs={{0,3},{1,0},{2,1},{3,2},{4,7},{5,4},{6,5},{7,6},{8,11},{9,8},{10,9... | collective-permute-start | bytes 933896 | tf_op jit(solution)/shard_map/ppermute | solution.py:311
  8.2 0.6 collective-permute-start.4
  8.9 1.0 shard_map.138
  9.9 13.6 %all_to_all.25 = bf16[8,64,128]{2,1,0:T(8,128)(2,1)S(1)} all-to-all(bf16[8,64,128]{2,1,0:T(8,128)(2,1)S(1)} %bitcast.15), channel_id=1, replica_groups=mesh['node'=8,'feat'=4] {'node'}, dimensions={0} | all-to-all | bytes 262144 | tf_op jit(solution)/shard_map/all_to_all | solution.py:307
  23.5 1.6 %copy-done = bf16[512,2048]{1,0:T(8,128)(2,1)S(1)} copy-done((bf16[512,2048]{1,0:T(8,128)(2,1)S(1)}, bf16[512,2048]{1,0:T(8,128)(2,1)}, u32[]{:S(2)}) %copy-start) | copy-done | bytes 2097176
  25.1 1.2 %shard_map.139 = (bf16[1024,256]{1,0:T(8,128)(2,1)S(1)}, bf16[512,128]{1,0:T(8,128)(2,1)S(1)}) custom-call(bf16[512,512]{1,0:T(8,128)(2,1)S(1)} %get-tuple-element.39.pick, bf16[512,2048]{1,0:T(8,128)(2,1)S(1)} %copy-done, bf16[512,128]{1,0:T(8,128)(2,1)S(1)} %get-tuple-element.40.full, bf16[512,128]{1,0:T(8,128)(2,1)S(1)} %bitcast.13), custom_call_target="tpu_custom_call" | custom-call | flops 268435456 | bytes 2097152 | tf_op jit(solution)/shard_map/pallas_call | solution.py:67
  26.2 0.6 copy-done.9
  26.9 0.7 copy-done.3
  27.6 0.7 copy-done.5
  28.3 0.7 copy-done.7
  29.1 4.0 %all-to-all-start.1 = ((bf16[8,64,128]{2,1,0:T(8,128)(2,1)}), bf16[8,64,128]{2,1,0:T(8,128)(2,1)}, u32[]{:S(2)}, u32[]{:S(2)}) async-start(bf16[8,64,128]{2,1,0:T(8,128)(2,1)} %bitcast.14), calls=%async_computation.1 | async-start | bytes 262144 | tf_op jit(solution)/shard_map/all_to_all | solution.py:307
  33.1 7.7 %all-to-all-done.1 = bf16[8,64,128]{2,1,0:T(8,128)(2,1)} async-done(((bf16[8,64,128]{2,1,0:T(8,128)(2,1)}), bf16[8,64,128]{2,1,0:T(8,128)(2,1)}, u32[]{:S(2)}, u32[]{:S(2)}) %all-to-all-start.1) | async-done | bytes 131104 | tf_op jit(solution)/shard_map/all_to_all | solution.py:307
  40.8 1.0 copy-done.4
  41.7 1.0 copy-done.6
  42.7 1.0 copy-done.8
  43.7 7.2 %shard_map.140 = (bf16[176,512]{1,0:T(8,128)(2,1)S(1)}, bf16[512,256]{1,0:T(8,128)(2,1)S(1)}, bf16[512,256]{1,0:T(8,128)(2,1)S(1)}, f32[8,128]{1,0:T(8,128)S(1)}...) custom-call(s32[1]{0:T(128)} %bitcast.ids, bf16[512,2048]{1,0:T(8,128)(2,1)S(1)} %copy-done.1, ...), custom_call_target="tpu_custom_call" | custom-call | flops 4294967296 | bytes 8388608 | tf_op jit(solution)/shard_map/pallas_call | solution.py:67
  50.9 10.4 %all_to_all.26.landed = bf16[8,96,128]{2,1,0:T(8,128)(2,1)S(1)} all-to-all(bf16[8,96,128]{2,1,0:T(8,128)(2,1)S(1)} %get-tuple-element.55), channel_id=1, replica_groups=mesh['node'=8,'feat'=4] {'node'}, dimensions={0} | all-to-all | bytes 393216 | tf_op jit(solution)/shard_map/all_to_all | solution.py:307
  61.2 2.8 %shard_map.141 = f32[8,152,128]{2,1,0:T(8,128)S(1)} custom-call(s32[1]{0:T(128)} %bitcast.ids, bf16[176,512]{1,0:T(8,128)(2,1)S(1)} %get-tuple-element.50.turned, bf16[512,512]{1,0:T(8,128)(2,1)S(1)} %get-tuple-element.39.pick, bf16[512,2048]{1,0:T(8,128)(2,1)S(1)} %copy-done.1, f32[4,512,256]{2,1,0:T(8,128)S(1)} %get-tuple-element.51.slope, ...), custom_call_target="tpu_custom_call" | custom-call | flops 738197504 | bytes 6291456 | tf_op jit(solution)/shard_map/pallas_call | solution.py:67
  64.1 19.8 %all_to_all.27.pieces = f32[8,152,128]{2,1,0:T(8,128)S(1)} all-to-all(f32[8,152,128]{2,1,0:T(8,128)S(1)} %shard_map.141), channel_id=1, replica_groups=mesh['node'=8,'feat'=4] {'node'}, dimensions={0} | all-to-all | bytes 1245184 | tf_op jit(solution)/shard_map/all_to_all | solution.py:307
  83.9 19.6 %all_to_all.28.pieces = f32[8,152,128]{2,1,0:T(8,128)S(1)} all-to-all(f32[8,152,128]{2,1,0:T(8,128)S(1)} %shard_map.142), channel_id=1, replica_groups=mesh['node'=8,'feat'=4] {'node'}, dimensions={0} | all-to-all | bytes 1245184 | tf_op jit(solution)/shard_map/all_to_all | solution.py:307
  103.5 0.8 shard_map.143
  (29 shorter events, 0.1 us)
Async XLA Ops:
  0.6 8.2 %copy-start.10 = (bf16[512,32]{0,1:T(8,128)(2,1)S(1)}, bf16[512,32]{0,1:T(8,128)(2,1)}, u32[]{:S(2)}) copy-start(bf16[512,32]{0,1:T(8,128)(2,1)} %param.10) | copy-start | bytes 98308
  0.6 8.2 %copy-start.13 = (s32[1,8]{1,0:T(1,128)S(1)}, s32[1,8]{1,0:T(1,128)}, u32[]{:S(2)}) copy-start(s32[1,8]{1,0:T(1,128)} %count.1) | copy-start | bytes 100
  0.7 8.2 %copy-start.11 = (s32[1,8,64]{2,1,0:T(8,128)S(1)}, s32[1,8,64]{2,1,0:T(8,128)}, u32[]{:S(2)}) copy-start(s32[1,8,64]{2,1,0:T(8,128)} %param.11) | copy-start | bytes 6148
  0.7 5.7 %collective-permute-start.2 = (bf16[32,512]{1,0:T(8,128)(2,1)}, bf16[32,512]{1,0:T(8,128)(2,1)S(1)}, u32[]{:S(2)}, u32[]{:S(2)}) collective-permute-start(bf16[32,512]{1,0:T(8,128)(2,1)} %bitcast.16), channel_id=1, source_target_pairs={{0,3},{1,0},{2,1},{3,2},{4,7},{5,4},{6,5},{7,6},{8,11},{9,8},{10,9... | collective-permute-start | bytes 98312 | tf_op jit(solution)/shard_map/ppermute | solution.py:311
  0.7 5.7 %collective-permute-start.1 = (bf16[32,512]{1,0:T(8,128)(2,1)}, bf16[32,512]{1,0:T(8,128)(2,1)S(1)}, u32[]{:S(2)}, u32[]{:S(2)}) collective-permute-start(bf16[32,512]{1,0:T(8,128)(2,1)} %bitcast.17), channel_id=1, source_target_pairs={{0,2},{1,3},{2,0},{3,1},{4,6},{5,7},{6,4},{7,5},{8,10},{9,11},{10,... | collective-permute-start | bytes 98312 | tf_op jit(solution)/shard_map/ppermute | solution.py:311
  2.2 4.2 %collective-permute-start = (bf16[32,512]{1,0:T(8,128)(2,1)}, bf16[32,512]{1,0:T(8,128)(2,1)S(1)}, u32[]{:S(2)}, u32[]{:S(2)}) collective-permute-start(bf16[32,512]{1,0:T(8,128)(2,1)} %bitcast.18), channel_id=1, source_target_pairs={{0,1},{1,2},{2,3},{3,0},{4,5},{5,6},{6,7},{7,4},{8,9},{9,10},{10,1... | collective-permute-start | bytes 98312 | tf_op jit(solution)/shard_map/ppermute | solution.py:311
  6.3 34.4 %copy-start.2 = (bf16[608,256]{1,0:T(8,128)(2,1)S(1)}, bf16[608,256]{1,0:T(8,128)(2,1)}, u32[]{:S(2)}) copy-start(bf16[608,256]{1,0:T(8,128)(2,1)} %get-tuple-element.46.refs_0_) | copy-start | bytes 933892
  6.4 34.4 %copy-start.12 = (s32[512]{0:T(512)S(1)}, s32[512]{0:T(512)}, u32[]{:S(2)}) copy-start(s32[512]{0:T(512)} %param.15) | copy-start | bytes 6148
  6.4 20.5 %collective-permute-start.5 = (bf16[608,256]{1,0:T(8,128)(2,1)}, bf16[608,256]{1,0:T(8,128)(2,1)S(1)}, u32[]{:S(2)}, u32[]{:S(2)}) collective-permute-start(bf16[608,256]{1,0:T(8,128)(2,1)} %get-tuple-element.46.refs_0_), channel_id=1, source_target_pairs={{0,3},{1,0},{2,1},{3,2},{4,7},{5,4},{6,5},{7,6},{8,11},{9,8},{10,9... | collective-permute-start | bytes 933896 | tf_op jit(solution)/shard_map/ppermute | solution.py:311
  8.2 19.4 %collective-permute-start.4 = (bf16[608,256]{1,0:T(8,128)(2,1)}, bf16[608,256]{1,0:T(8,128)(2,1)S(1)}, u32[]{:S(2)}, u32[]{:S(2)}) collective-permute-start(bf16[608,256]{1,0:T(8,128)(2,1)} %get-tuple-element.46.refs_0_), channel_id=1, source_target_pairs={{0,2},{1,3},{2,0},{3,1},{4,6},{5,7},{6,4},{7,5},{8,10},{9,11},{10,... | collective-permute-start | bytes 933896 | tf_op jit(solution)/shard_map/ppermute | solution.py:311
  8.8 19.5 %collective-permute-start.3 = (bf16[608,256]{1,0:T(8,128)(2,1)}, bf16[608,256]{1,0:T(8,128)(2,1)S(1)}, u32[]{:S(2)}, u32[]{:S(2)}) collective-permute-start(bf16[608,256]{1,0:T(8,128)(2,1)} %get-tuple-element.46.refs_0_), channel_id=1, source_target_pairs={{0,1},{1,2},{2,3},{3,0},{4,5},{5,6},{6,7},{7,4},{8,9},{9,10},{10,1... | collective-permute-start | bytes 933896 | tf_op jit(solution)/shard_map/ppermute | solution.py:311
  23.5 1.6 %copy-start = (bf16[512,2048]{1,0:T(8,128)(2,1)S(1)}, bf16[512,2048]{1,0:T(8,128)(2,1)}, u32[]{:S(2)}) copy-start(bf16[512,2048]{1,0:T(8,128)(2,1)} %get-tuple-element.33.a_ref) | copy-start | bytes 6291460
  25.1 15.7 %copy-start.1 = (bf16[512,2048]{1,0:T(8,128)(2,1)S(1)}, bf16[512,2048]{1,0:T(8,128)(2,1)}, u32[]{:S(2)}) copy-start(bf16[512,2048]{1,0:T(8,128)(2,1)} %get-tuple-element.33.a_ref) | copy-start | bytes 6291460
  26.2 0.7 copy-start.9
  26.9 0.7 copy-start.3
  27.6 0.7 copy-start.5
  28.3 0.7 copy-start.7
  29.1 11.7 %all-to-all-start.1 = ((bf16[8,64,128]{2,1,0:T(8,128)(2,1)}), bf16[8,64,128]{2,1,0:T(8,128)(2,1)}, u32[]{:S(2)}, u32[]{:S(2)}) async-start(bf16[8,64,128]{2,1,0:T(8,128)(2,1)} %bitcast.14), calls=%async_computation.1 | async-start | bytes 262144 | tf_op jit(solution)/shard_map/all_to_all | solution.py:307
  40.8 1.0 copy-start.4
  41.7 1.0 copy-start.6
  42.7 1.0 copy-start.8

commit v9 on v8

--- a/solution.py
+++ b/solution.py
@@ -68,7 +68,7 @@
         body,
         out_shape=[jax.ShapeDtypeStruct(shape, dtype) for shape, dtype in outs],
         in_specs=specs,
-        out_specs=[HBM if copies else VMEM] * len(outs),
+        out_specs=[VMEM] * len(outs),
         scratch_shapes=[pltpu.VMEM(shape, dtype) for shape, dtype in scratch]
         + ([pltpu.SemaphoreType.DMA((copies,))] if copies else []),
         compiler_params=pltpu.CompilerParams(vmem_limit_bytes=grant or min(room + 8 * 2**20, 56 * 2**20)),
@@ -76,41 +76,16 @@
     )(*args)
 
 
-def prepare_kernel(
-    tile_src, tile_val, w_self1, w_neigh1, w_self2, w_neigh2,
-    a_out, weights_out, a_ref, weights, tiles, firsts, seconds, dense, sems,
-):
-    started = []
-
-    def copy(src, dst):
-        started.append(pltpu.make_async_copy(src, dst, sems.at[len(started)]))
-        started[-1].start()
-        return started[-1]
-
+def prepare_kernel(tile_src, tile_val, a_ref, tiles, dense, sems):
     blocks, per_block = tile_val.shape[0], tile_val.shape[1]
     own = blocks * BLOCK
-    pairs = [(w_self1, firsts.at[0]), (w_neigh1, firsts.at[1]), (w_self2, seconds.at[0]), (w_neigh2, seconds.at[1])]
-    w_copies = [copy(src, dst) for src, dst in pairs]
-    tile_copies = [copy(tile_val.at[b], tiles.at[b]) for b in range(blocks)]
+    copies = [pltpu.make_async_copy(tile_val.at[b], tiles.at[b], sems.at[b]) for b in range(blocks)]
+    for copy in copies:
+        copy.start()
     dense[...] = jnp.zeros_like(dense)
-    step = firsts.shape[1]
-    classes, units = seconds.shape[1:]
-    groups = firsts.shape[2] // units
-    base = 2 * step * groups
-    pad = (weights.shape[0] - base) // 2
-    weights[pl.ds(base, 2 * pad), :] = jnp.zeros((2 * pad, units), BF16)
-    for load in w_copies:
-        load.wait()
-    for j in range(groups):
-        at = pl.ds(j * units, units)
-        weights[pl.ds(2 * step * j, step), :] = firsts[0, :, at]
-        weights[pl.ds(2 * step * j + step, step), :] = firsts[1, :, at]
-    weights[pl.ds(base, classes), :] = seconds[0]
-    weights[pl.ds(base + pad, classes), :] = seconds[1]
-    stores = [copy(weights, weights_out)]
     for b in range(blocks):
         rows = pl.ds(b * BLOCK, BLOCK)
-        tile_copies[b].wait()
+        copies[b].wait()
 
         def add(k, _, b=b, rows=rows):
             at = pl.ds(pl.multiple_of(tile_src[b, k] * BLOCK, BLOCK), BLOCK)
@@ -122,14 +97,21 @@
             high, low = halves(dense[rows, pl.ds(c * own, own)])
             a_ref[rows, pl.ds(2 * c * own, own)] = high
             a_ref[rows, pl.ds((2 * c + 1) * own, own)] = low
-        stores.append(copy(a_ref.at[rows], a_out.at[rows]))
-    for store in stores:
-        store.wait()
-
-
-def pack_kernel(groups, count, send_rows, *refs):
-    pieces, (pick, full, packed), (turned,) = refs[:groups], refs[groups : groups + 3], refs[groups + 3 :]
+
+
+def pack_kernel(groups, count, send_rows, w_self1, w_neigh1, w_self2, w_neigh2, *refs):
+    pieces, (pick, full, packed, weights), (turned,) = refs[:groups], refs[groups : groups + 4], refs[groups + 4 :]
     step, own = pieces[0].shape
+    classes, units = w_self2.shape
+    base = 2 * step * groups
+    pad = (weights.shape[0] - base) // 2
+    for j in range(groups):
+        at = pl.ds(j * units, units)
+        weights[pl.ds(2 * step * j, step), :] = w_self1[:, at]
+        weights[pl.ds(2 * step * j + step, step), :] = w_neigh1[:, at]
+    weights[pl.ds(base, 2 * pad), :] = jnp.zeros((2 * pad, units), BF16)
+    weights[pl.ds(base, classes), :] = w_self2[...]
+    weights[pl.ds(base + pad, classes), :] = w_neigh2[...]
     dests, slots = send_rows.shape
     columns = send_rows[...].astype(F32).T
     row_id = lax.broadcasted_iota(jnp.int32, (slots, own), 1).astype(F32)
@@ -331,32 +313,25 @@
 
     turned = features.T
     turned_all = gather_shifted(turned, groups)
-    a_mat, packed_weights = call(
+    (a_mat,) = call(
         prepare_kernel,
-        [((own, 2 * total_src), BF16), ((packed_rows, units), BF16)],
-        (tile_src, tile_val, w_self1, w_neigh1, w_self2.T, w_neigh2.T),
-        [
-            ((own, 2 * total_src), BF16),
-            ((packed_rows, units), BF16),
-            (tile_val.shape, BF16),
-            ((2, step, width), BF16),
-            ((2, classes, units), BF16),
-            ((own, total_src), F32),
-        ],
-        copies=5 + 2 * blocks,
+        [((own, 2 * total_src), BF16)],
+        (tile_src, tile_val),
+        [(tile_val.shape, BF16), ((own, total_src), F32)],
+        copies=blocks,
         moved=tile_val.size * 4,
-        grant=58 * 2**20,
-    )
-    packed_weights, *turned_all = lax.optimization_barrier((packed_weights, *turned_all))
-    weights = gather_shifted(packed_weights, groups)
-    pick, full, packed = call(
+        grant=54 * 2**20 - 4 * own * total_src - 3 * 10**5,
+    )
+    a_mat, ids, *turned_all = lax.optimization_barrier((a_mat, ids, *turned_all))
+    pick, full, packed, packed_weights = call(
         functools.partial(pack_kernel, groups),
-        [((halo, own), BF16), ((own, cols), BF16), ((halo, cols), BF16)],
-        (send_count, send_rows[0], *turned_all),
+        [((halo, own), BF16), ((own, cols), BF16), ((halo, cols), BF16), ((packed_rows, units), BF16)],
+        (send_count, send_rows[0], w_self1, w_neigh1, w_self2.T, w_neigh2.T, *turned_all),
         [((cols, own), BF16)],
         flops=2 * halo * own * cols,
         moved=halo * own * 2,
     )
+    weights = gather_shifted(packed_weights, groups)
     source = swap(packed, nodes).reshape(halo, cols)
     state, packed = call(
         first_kernel,
@@ -365,7 +340,7 @@
         flops=4 * own * total_src * cols,
         moved=4 * own * total_src,
     )
-    packed, *weights = lax.optimization_barrier((packed, *weights))
+    packed, ids, *weights = lax.optimization_barrier((packed, ids, *weights))
     landed = swap(packed, nodes).reshape(halo, cols)
     message = (nodes, *message_shape(slots, pad))
     turned_grads, mine, agg_mine, loss, slope, packed = call(

time: 105 us -> 92.8 us (0.88)
  the two profiles are of different devices: /device:TPU:2 before, /device:TPU:0 now
where the time goes in v9:
time: 92.8 us; the launch traced here: 92.4 us
  blocking collectives  69.4 us (75%)
  Pallas kernels  15.3 us (16%)
  starting transfers between devices  6.25 us (7%)
    all_to_all x5, blocking collectives, swap(): return lax.all_to_all(blocks, 'node', 0, 0, tiled=True)  69.4 us
    pallas_call x7, Pallas kernels, call(): pl.pallas_call(body, out_shape=[jax.ShapeDtypeStruct(shape, dtype) for sh...  15.3 us
    ppermute x6, starting transfers between devices, gather_shifted(): lax.ppermute(value, 'feat', [(i, (i + k) % count) for i in range(count)])  6.25 us
  transfers between devices with their start and end apart: 6, of which 0 were waited for; matrix products, arithmetic and copies ran while one was open for 0% of the time, Pallas kernels for 5%

profile of v9, /device:TPU:0, one launch (start us, length us, event | category | flops | bytes accessed | tf_op | source)
XLA Modules:
  0.0 92.4 jit_solution(15098822922239292321)
XLA Ops:
  0.6 2.4 %collective-permute-start.2 = (bf16[32,512]{1,0:T(8,128)(2,1)}, bf16[32,512]{1,0:T(8,128)(2,1)S(1)}, u32[]{:S(2)}, u32[]{:S(2)}) collective-permute-start(bf16[32,512]{1,0:T(8,128)(2,1)} %bitcast.17), channel_id=1, source_target_pairs={{0,3},{1,0},{2,1},{3,2},{4,7},{5,4},{6,5},{7,6},{8,11},{9,8},{10,9... | collective-permute-start | bytes 98312 | tf_op jit(solution)/shard_map/ppermute | solution.py:293
  3.1 0.6 collective-permute-start.1
  3.7 0.2 collective-permute-start
  3.9 0.7 copy-done.6
  4.6 3.0 %shard_map.137.a_ref = bf16[512,2048]{1,0:T(8,128)(2,1)S(1)} custom-call(s32[4,16]{1,0:T(4,128)S(1)} %copy-done.6, bf16[4,16,128,128]{3,2,1,0:T(8,128)(2,1)} %tile_val.1), custom_call_target="tpu_custom_call" | custom-call | bytes 4194304 | tf_op jit(solution)/shard_map/pallas_call | solution.py:67
  7.6 0.0 copy-start.8
  7.7 0.0 collective-permute-done.2.refs_3_
  7.7 0.0 collective-permute-done.1.refs_2_
  7.7 0.0 collective-permute-done.refs_1_
  7.8 1.0 %shard_map.138 = (bf16[512,512]{1,0:T(8,128)(2,1)S(1)}, bf16[512,128]{1,0:T(8,128)(2,1)S(1)}, bf16[512,128]{1,0:T(8,128)(2,1)S(1)}, bf16[608,256]{1,0:T(8,128)(2,1)S(1)}) custom-call(s32[1,8]{1,0:T(1,128)S(1)} %copy-done.7, s32[8,64]{1,0:T(8,128)S(1)} %bitcast.24, bf16[32,1024]{1,0:T(8,128)(2,1)S(1)} %copy-done.3, bf16[32,1024]{1,0:T(8,128)(2,1)S(1)} %copy-done.4, ...), custom_call_target="tpu_custom_call" | custom-call | flops 67108864 | bytes 524288 | tf_op jit(solution)/shard_map/pallas_call | solution.py:67
  8.8 1.6 %collective-permute-start.5 = (bf16[608,256]{1,0:T(8,128)(2,1)S(1)}, bf16[608,256]{1,0:T(8,128)(2,1)S(1)}, u32[]{:S(2)}, u32[]{:S(2)}) collective-permute-start(bf16[608,256]{1,0:T(8,128)(2,1)S(1)} %get-tuple-element.48.refs_0_), channel_id=1, source_target_pairs={{0,3},{1,0},{2,1},{3,2},{4,7},{5,4},{6,5},{7,6},{8,11},{9,8},{10,9... | collective-permute-start | bytes 933896 | tf_op jit(solution)/shard_map/ppermute | solution.py:293
  10.4 1.4 %collective-permute-start.4 = (bf16[608,256]{1,0:T(8,128)(2,1)S(1)}, bf16[608,256]{1,0:T(8,128)(2,1)S(1)}, u32[]{:S(2)}, u32[]{:S(2)}) collective-permute-start(bf16[608,256]{1,0:T(8,128)(2,1)S(1)} %get-tuple-element.48.refs_0_), channel_id=1, source_target_pairs={{0,2},{1,3},{2,0},{3,1},{4,6},{5,7},{6,4},{7,5},{8,10},{9,11},{10,... | collective-permute-start | bytes 933896 | tf_op jit(solution)/shard_map/ppermute | solution.py:293
  11.8 0.0 collective-permute-start.3
  11.8 13.5 %all_to_all.25 = bf16[8,64,128]{2,1,0:T(8,128)(2,1)S(1)} all-to-all(bf16[8,64,128]{2,1,0:T(8,128)(2,1)S(1)} %bitcast.14), channel_id=1, replica_groups=mesh['node'=8,'feat'=4] {'node'}, dimensions={0} | all-to-all | bytes 262144 | tf_op jit(solution)/shard_map/all_to_all | solution.py:289
  25.3 1.2 %shard_map.139 = (bf16[1024,256]{1,0:T(8,128)(2,1)S(1)}, bf16[512,128]{1,0:T(8,128)(2,1)S(1)}) custom-call(bf16[512,512]{1,0:T(8,128)(2,1)S(1)} %get-tuple-element.38.pick, bf16[512,2048]{1,0:T(8,128)(2,1)S(1)} %shard_map.137.a_ref, bf16[512,128]{1,0:T(8,128)(2,1)S(1)} %get-tuple-element.40.full, bf16[512,128]{1,0:T(8,128)(2,1)S(1)} %bitcast.13), custom_call_target="tpu_custom_call" | custom-call | flops 268435456 | bytes 2097152 | tf_op jit(solution)/shard_map/pallas_call | solution.py:67
  26.5 0.0 collective-permute-done.5.refs_3_
  26.5 0.0 collective-permute-done.3.refs_1_
  26.5 12.6 %all_to_all.26 = bf16[8,64,128]{2,1,0:T(8,128)(2,1)S(1)} all-to-all(bf16[8,64,128]{2,1,0:T(8,128)(2,1)S(1)} %bitcast.15), channel_id=1, replica_groups=mesh['node'=8,'feat'=4] {'node'}, dimensions={0} | all-to-all | bytes 262144 | tf_op jit(solution)/shard_map/all_to_all | solution.py:289
  39.1 6.3 %shard_map.140 = (bf16[176,512]{1,0:T(8,128)(2,1)S(1)}, bf16[512,256]{1,0:T(8,128)(2,1)S(1)}, bf16[512,256]{1,0:T(8,128)(2,1)S(1)}, f32[8,128]{1,0:T(8,128)S(1)}...) custom-call(s32[1]{0:T(128)} %bitcast.3.ids, bf16[512,2048]{1,0:T(8,128)(2,1)S(1)} %shard_map.137.a_ref, ...), custom_call_target="tpu_custom_call" | custom-call | flops 4294967296 | bytes 8388608 | tf_op jit(solution)/shard_map/pallas_call | solution.py:67
  45.5 10.2 %all_to_all.27.landed = bf16[8,96,128]{2,1,0:T(8,128)(2,1)S(1)} all-to-all(bf16[8,96,128]{2,1,0:T(8,128)(2,1)S(1)} %get-tuple-element.57), channel_id=1, replica_groups=mesh['node'=8,'feat'=4] {'node'}, dimensions={0} | all-to-all | bytes 393216 | tf_op jit(solution)/shard_map/all_to_all | solution.py:289
  55.6 2.9 %shard_map.141 = f32[8,152,128]{2,1,0:T(8,128)S(1)} custom-call(s32[1]{0:T(128)} %bitcast.3.ids, bf16[176,512]{1,0:T(8,128)(2,1)S(1)} %get-tuple-element.52.turned, bf16[512,512]{1,0:T(8,128)(2,1)S(1)} %get-tuple-element.38.pick, bf16[512,2048]{1,0:T(8,128)(2,1)S(1)} %shard_map.137.a_ref, f32[4,512,256]{2,1,0:T(8,128)S(1)} %get-tuple-element.53.slope, ...), custom_call_target="tpu_custom_call" | custom-call | flops 738197504 | bytes 6291456 | tf_op jit(solution)/shard_map/pallas_call | solution.py:67
  58.5 15.2 %all_to_all.28.pieces = f32[8,152,128]{2,1,0:T(8,128)S(1)} all-to-all(f32[8,152,128]{2,1,0:T(8,128)S(1)} %shard_map.141), channel_id=1, replica_groups=mesh['node'=8,'feat'=4] {'node'}, dimensions={0} | all-to-all | bytes 1245184 | tf_op jit(solution)/shard_map/all_to_all | solution.py:289
  73.8 17.8 %all_to_all.29.pieces = f32[8,152,128]{2,1,0:T(8,128)S(1)} all-to-all(f32[8,152,128]{2,1,0:T(8,128)S(1)} %shard_map.142), channel_id=1, replica_groups=mesh['node'=8,'feat'=4] {'node'}, dimensions={0} | all-to-all | bytes 1245184 | tf_op jit(solution)/shard_map/all_to_all | solution.py:289
  91.6 0.8 shard_map.143
  (18 shorter events, 0.1 us)
Async XLA Ops:
  0.6 7.0 %collective-permute-start.2 = (bf16[32,512]{1,0:T(8,128)(2,1)}, bf16[32,512]{1,0:T(8,128)(2,1)S(1)}, u32[]{:S(2)}, u32[]{:S(2)}) collective-permute-start(bf16[32,512]{1,0:T(8,128)(2,1)} %bitcast.17), channel_id=1, source_target_pairs={{0,3},{1,0},{2,1},{3,2},{4,7},{5,4},{6,5},{7,6},{8,11},{9,8},{10,9... | collective-permute-start | bytes 98312 | tf_op jit(solution)/shard_map/ppermute | solution.py:293
  3.1 4.6 %collective-permute-start.1 = (bf16[32,512]{1,0:T(8,128)(2,1)}, bf16[32,512]{1,0:T(8,128)(2,1)S(1)}, u32[]{:S(2)}, u32[]{:S(2)}) collective-permute-start(bf16[32,512]{1,0:T(8,128)(2,1)} %bitcast.18), channel_id=1, source_target_pairs={{0,2},{1,3},{2,0},{3,1},{4,6},{5,7},{6,4},{7,5},{8,10},{9,11},{10,... | collective-permute-start | bytes 98312 | tf_op jit(solution)/shard_map/ppermute | solution.py:293
  3.7 4.0 %collective-permute-start = (bf16[32,512]{1,0:T(8,128)(2,1)}, bf16[32,512]{1,0:T(8,128)(2,1)S(1)}, u32[]{:S(2)}, u32[]{:S(2)}) collective-permute-start(bf16[32,512]{1,0:T(8,128)(2,1)} %bitcast.19), channel_id=1, source_target_pairs={{0,1},{1,2},{2,3},{3,0},{4,5},{5,6},{6,7},{7,4},{8,9},{9,10},{10,1... | collective-permute-start | bytes 98312 | tf_op jit(solution)/shard_map/ppermute | solution.py:293
  3.9 0.7 copy-start.6
  4.6 3.1 %copy-start = (bf16[512,32]{0,1:T(8,128)(2,1)S(1)}, bf16[512,32]{0,1:T(8,128)(2,1)}, u32[]{:S(2)}) copy-start(bf16[512,32]{0,1:T(8,128)(2,1)} %param.10) | copy-start | bytes 98308
  4.6 3.1 %copy-start.1 = (bf16[256,172]{0,1:T(8,128)(2,1)S(1)}, bf16[256,172]{0,1:T(8,128)(2,1)}, u32[]{:S(2)}) copy-start(bf16[256,172]{0,1:T(8,128)(2,1)} %param.18) | copy-start | bytes 264196
  4.6 3.2 %copy-start.2 = (bf16[256,172]{0,1:T(8,128)(2,1)S(1)}, bf16[256,172]{0,1:T(8,128)(2,1)}, u32[]{:S(2)}) copy-start(bf16[256,172]{0,1:T(8,128)(2,1)} %param.19) | copy-start | bytes 264196
  4.6 3.2 %copy-start.3 = (bf16[32,1024]{1,0:T(8,128)(2,1)S(1)}, bf16[32,1024]{1,0:T(8,128)(2,1)}, u32[]{:S(2)}) copy-start(bf16[32,1024]{1,0:T(8,128)(2,1)} %w_self1.1) | copy-start | bytes 196612
  4.6 3.2 %copy-start.4 = (bf16[32,1024]{1,0:T(8,128)(2,1)S(1)}, bf16[32,1024]{1,0:T(8,128)(2,1)}, u32[]{:S(2)}) copy-start(bf16[32,1024]{1,0:T(8,128)(2,1)} %w_neigh1.1) | copy-start | bytes 196612
  4.6 3.2 %copy-start.5 = (s32[1,8,64]{2,1,0:T(8,128)S(1)}, s32[1,8,64]{2,1,0:T(8,128)}, u32[]{:S(2)}) copy-start(s32[1,8,64]{2,1,0:T(8,128)} %param.11) | copy-start | bytes 6148
  4.6 3.2 %copy-start.7 = (s32[1,8]{1,0:T(1,128)S(1)}, s32[1,8]{1,0:T(1,128)}, u32[]{:S(2)}) copy-start(s32[1,8]{1,0:T(1,128)} %count.1) | copy-start | bytes 100
  7.6 31.5 %copy-start.8 = (s32[512]{0:T(512)S(1)}, s32[512]{0:T(512)}, u32[]{:S(2)}) copy-start(s32[512]{0:T(512)} %param.15) | copy-start | bytes 6148
  8.8 17.7 %collective-permute-start.5 = (bf16[608,256]{1,0:T(8,128)(2,1)S(1)}, bf16[608,256]{1,0:T(8,128)(2,1)S(1)}, u32[]{:S(2)}, u32[]{:S(2)}) collective-permute-start(bf16[608,256]{1,0:T(8,128)(2,1)S(1)} %get-tuple-element.48.refs_0_), channel_id=1, source_target_pairs={{0,3},{1,0},{2,1},{3,2},{4,7},{5,4},{6,5},{7,6},{8,11},{9,8},{10,9... | collective-permute-start | bytes 933896 | tf_op jit(solution)/shard_map/ppermute | solution.py:293
  10.4 16.1 %collective-permute-start.4 = (bf16[608,256]{1,0:T(8,128)(2,1)S(1)}, bf16[608,256]{1,0:T(8,128)(2,1)S(1)}, u32[]{:S(2)}, u32[]{:S(2)}) collective-permute-start(bf16[608,256]{1,0:T(8,128)(2,1)S(1)} %get-tuple-element.48.refs_0_), channel_id=1, source_target_pairs={{0,2},{1,3},{2,0},{3,1},{4,6},{5,7},{6,4},{7,5},{8,10},{9,11},{10,... | collective-permute-start | bytes 933896 | tf_op jit(solution)/shard_map/ppermute | solution.py:293
  11.8 14.7 %collective-permute-start.3 = (bf16[608,256]{1,0:T(8,128)(2,1)S(1)}, bf16[608,256]{1,0:T(8,128)(2,1)S(1)}, u32[]{:S(2)}, u32[]{:S(2)}) collective-permute-start(bf16[608,256]{1,0:T(8,128)(2,1)S(1)} %get-tuple-element.48.refs_0_), channel_id=1, source_target_pairs={{0,1},{1,2},{2,3},{3,0},{4,5},{5,6},{6,7},{7,4},{8,9},{9,10},{10,1... | collective-permute-start | bytes 933896 | tf_op jit(solution)/shard_map/ppermute | solution.py:293

commit v10 on v9

--- a/solution.py
+++ b/solution.py
@@ -151,7 +151,7 @@
     near = state[:own, :]
     total = jnp.zeros((pad, own), F32)
     for k in range(groups):
-        group = lax.rem(ids[0] + groups - k, groups)
+        group = jnp.bitwise_xor(ids[0], k)
         begin = [pl.multiple_of(2 * step * group + part * step, step) for part in (0, 1)]
         w_one = jnp.concatenate([w[pl.ds(at, step), :] for at in begin for w in weights], axis=0)
         out, slope[k] = activate(mm(near, w_one), True)
@@ -248,7 +248,7 @@
     cols = state.shape[1] // 2
     left = jnp.concatenate([features[...], state[:own, cols:].T[:step]], axis=0)
     for k in range(groups):
-        group = lax.rem(ids[0] + groups - k, groups)
+        group = jnp.bitwise_xor(ids[0], k)
         w_neigh = weights[k][pl.ds(base + pad, pad), :]
         total = mm(wide, jnp.concatenate([weights[k][pl.ds(base, pad), :], w_neigh, w_neigh], axis=0))
         result = mm(left, (total * slope[k]).astype(BF16))
@@ -289,8 +289,8 @@
     return lax.all_to_all(blocks, "node", 0, 0, tiled=True)
 
 
-def gather_shifted(value, count):
-    return [value] + [lax.ppermute(value, "feat", [(i, (i + k) % count) for i in range(count)]) for k in range(1, count)]
+def crossed(value, count, k):
+    return lax.ppermute(value, "feat", [(i, i ^ k) for i in range(count)])
 
 
 def shards(features, send_rows, send_count, tile_src, tile_val, labels, w_self1, w_neigh1, w_self2, w_neigh2):
@@ -312,7 +312,7 @@
     packed_rows = 2 * step * groups + 2 * pad
 
     turned = features.T
-    turned_all = gather_shifted(turned, groups)
+    turned_all = [turned] + [crossed(turned, groups, k) for k in range(1, groups)]
     (a_mat,) = call(
         prepare_kernel,
         [((own, 2 * total_src), BF16)],
@@ -331,7 +331,7 @@
         flops=2 * halo * own * cols,
         moved=halo * own * 2,
     )
-    weights = gather_shifted(packed_weights, groups)
+    weights = [packed_weights] + [crossed(packed_weights, groups, 1 << i) for i in range(groups.bit_length() - 1)]
     source = swap(packed, nodes).reshape(halo, cols)
     state, packed = call(
         first_kernel,
@@ -341,6 +341,10 @@
         moved=4 * own * total_src,
     )
     packed, ids, *weights = lax.optimization_barrier((packed, ids, *weights))
+    pieces = weights[:2]
+    for i, half in enumerate(weights[2:], 1):
+        pieces += [half] + [crossed(half, groups, k) for k in range(1, 1 << i)]
+    packed, *weights = lax.optimization_barrier((packed, *pieces))
     landed = swap(packed, nodes).reshape(halo, cols)
     message = (nodes, *message_shape(slots, pad))
     turned_grads, mine, agg_mine, loss, slope, packed = call(

time: 92.8 us -> 96.7 us (1.042)
  blocking collectives: 69.4 us -> 72.9 us
  waiting for transfers between devices: 0.02 us -> 1.61 us
  starting transfers between devices: 6.25 us -> 5.01 us
    all_to_all x5, blocking collectives: 69.4 us -> 72.9 us  [swap(): return lax.all_to_all(blocks, 'node', 0, 0, tiled=True)]
    ppermute x6, waiting for transfers between devices: 0.02 us -> 1.61 us  [crossed(): return lax.ppermute(value, 'feat', [(i, i ^ k) for i in range(count)])]
    ppermute x6, starting transfers between devices: 6.25 us -> 5.01 us  [crossed(): return lax.ppermute(value, 'feat', [(i, i ^ k) for i in range(count)])]
  transfers between devices with their start and end apart: 6 -> 6, of which waited for: 0 -> 1; matrix products, arithmetic and copies ran while one was open for 0% -> 0% of each run, Pallas kernels for 5% -> 4%
where the time goes in v10:
time: 96.7 us; the launch traced here: 96.4 us
  blocking collectives  72.9 us (75%)
  Pallas kernels  15.3 us (16%)
  starting transfers between devices  5.01 us (5%)
  waiting for transfers between devices  1.61 us (2%)
    all_to_all x5, blocking collectives, swap(): return lax.all_to_all(blocks, 'node', 0, 0, tiled=True)  72.9 us
    pallas_call x7, Pallas kernels, call(): pl.pallas_call(body, out_shape=[jax.ShapeDtypeStruct(shape, dtype) for sh...  15.3 us
    ppermute x6, starting transfers between devices, crossed(): return lax.ppermute(value, 'feat', [(i, i ^ k) for i in range(count)])  5.01 us
  transfers between devices with their start and end apart: 6, of which 1 were waited for; matrix products, arithmetic and copies ran while one was open for 0% of the time, Pallas kernels for 4%

profile of v10, /device:TPU:0, one launch (start us, length us, event | category | flops | bytes accessed | tf_op | source)
XLA Modules:
  0.0 96.4 jit_solution(10723706052835189216)
XLA Ops:
  0.6 2.4 %collective-permute-start.2 = (bf16[32,512]{1,0:T(8,128)(2,1)}, bf16[32,512]{1,0:T(8,128)(2,1)S(1)}, u32[]{:S(2)}, u32[]{:S(2)}) collective-permute-start(bf16[32,512]{1,0:T(8,128)(2,1)} %bitcast.17), channel_id=1, source_target_pairs={{0,3},{1,2},{2,1},{3,0},{4,7},{5,6},{6,5},{7,4},{8,11},{9,10},{10,... | collective-permute-start | bytes 98312 | tf_op jit(solution)/shard_map/ppermute | solution.py:293
  3.1 0.6 collective-permute-start.1
  3.7 0.0 collective-permute-start
  3.8 0.7 copy-done.6
  4.5 3.0 %shard_map.137.a_ref = bf16[512,2048]{1,0:T(8,128)(2,1)S(1)} custom-call(s32[4,16]{1,0:T(4,128)S(1)} %copy-done.6, bf16[4,16,128,128]{3,2,1,0:T(8,128)(2,1)} %tile_val.1), custom_call_target="tpu_custom_call" | custom-call | bytes 4194304 | tf_op jit(solution)/shard_map/pallas_call | solution.py:67
  7.5 0.0 copy-start.8
  7.5 0.0 collective-permute-done.2.refs_3_
  7.6 0.0 collective-permute-done.1.refs_2_
  7.6 0.0 collective-permute-done.refs_1_
  7.6 1.0 %shard_map.138 = (bf16[512,512]{1,0:T(8,128)(2,1)S(1)}, bf16[512,128]{1,0:T(8,128)(2,1)S(1)}, bf16[512,128]{1,0:T(8,128)(2,1)S(1)}, bf16[608,256]{1,0:T(8,128)(2,1)S(1)}) custom-call(s32[1,8]{1,0:T(1,128)S(1)} %copy-done.7, s32[8,64]{1,0:T(8,128)S(1)} %bitcast.24, bf16[32,1024]{1,0:T(8,128)(2,1)S(1)} %copy-done.3, bf16[32,1024]{1,0:T(8,128)(2,1)S(1)} %copy-done.4, ...), custom_call_target="tpu_custom_call" | custom-call | flops 67108864 | bytes 524288 | tf_op jit(solution)/shard_map/pallas_call | solution.py:67
  8.7 1.8 %collective-permute-start.4 = (bf16[608,256]{1,0:T(8,128)(2,1)S(1)}, bf16[608,256]{1,0:T(8,128)(2,1)S(1)}, u32[]{:S(2)}, u32[]{:S(2)}) collective-permute-start(bf16[608,256]{1,0:T(8,128)(2,1)S(1)} %get-tuple-element.56.refs_0_), channel_id=1, source_target_pairs={{0,2},{1,3},{2,0},{3,1},{4,6},{5,7},{6,4},{7,5},{8,10},{9,11},{10,... | collective-permute-start | bytes 933896 | tf_op jit(solution)/shard_map/ppermute | solution.py:293
  10.5 0.0 collective-permute-start.3
  10.5 13.3 %all_to_all.25 = bf16[8,64,128]{2,1,0:T(8,128)(2,1)S(1)} all-to-all(bf16[8,64,128]{2,1,0:T(8,128)(2,1)S(1)} %bitcast.15), channel_id=1, replica_groups=mesh['node'=8,'feat'=4] {'node'}, dimensions={0} | all-to-all | bytes 262144 | tf_op jit(solution)/shard_map/all_to_all | solution.py:289
  23.7 1.2 %shard_map.139 = (bf16[1024,256]{1,0:T(8,128)(2,1)S(1)}, bf16[512,128]{1,0:T(8,128)(2,1)S(1)}) custom-call(bf16[512,512]{1,0:T(8,128)(2,1)S(1)} %get-tuple-element.42.pick, bf16[512,2048]{1,0:T(8,128)(2,1)S(1)} %shard_map.137.a_ref, bf16[512,128]{1,0:T(8,128)(2,1)S(1)} %get-tuple-element.44.full, bf16[512,128]{1,0:T(8,128)(2,1)S(1)} %bitcast.13), custom_call_target="tpu_custom_call" | custom-call | flops 268435456 | bytes 2097152 | tf_op jit(solution)/shard_map/pallas_call | solution.py:67
  24.9 0.0 collective-permute-done.4.refs_2_
  24.9 0.1 collective-permute-start.5
  25.0 1.6 %collective-permute-done.5.refs_3_ = bf16[608,256]{1,0:T(8,128)(2,1)S(1)} collective-permute-done((bf16[608,256]{1,0:T(8,128)(2,1)S(1)}, bf16[608,256]{1,0:T(8,128)(2,1)S(1)}, u32[]{:S(2)}, u32[]{:S(2)}) %collective-permute-start.5) | collective-permute-done | bytes 311328 | tf_op jit(solution)/shard_map/ppermute | solution.py:293
  26.6 9.9 %all_to_all.26 = bf16[8,64,128]{2,1,0:T(8,128)(2,1)S(1)} all-to-all(bf16[8,64,128]{2,1,0:T(8,128)(2,1)S(1)} %bitcast.14), channel_id=1, replica_groups=mesh['node'=8,'feat'=4] {'node'}, dimensions={0} | all-to-all | bytes 262144 | tf_op jit(solution)/shard_map/all_to_all | solution.py:289
  36.5 6.3 %shard_map.140 = (bf16[176,512]{1,0:T(8,128)(2,1)S(1)}, bf16[512,256]{1,0:T(8,128)(2,1)S(1)}, bf16[512,256]{1,0:T(8,128)(2,1)S(1)}, f32[8,128]{1,0:T(8,128)S(1)}...) custom-call(s32[1]{0:T(128)} %bitcast.3.ids, bf16[512,2048]{1,0:T(8,128)(2,1)S(1)} %shard_map.137.a_ref, ...), custom_call_target="tpu_custom_call" | custom-call | flops 4294967296 | bytes 8388608 | tf_op jit(solution)/shard_map/pallas_call | solution.py:67
  42.9 10.4 %all_to_all.27.landed = bf16[8,96,128]{2,1,0:T(8,128)(2,1)S(1)} all-to-all(bf16[8,96,128]{2,1,0:T(8,128)(2,1)S(1)} %get-tuple-element.65), channel_id=1, replica_groups=mesh['node'=8,'feat'=4] {'node'}, dimensions={0} | all-to-all | bytes 393216 | tf_op jit(solution)/shard_map/all_to_all | solution.py:289
  53.2 2.9 %shard_map.141 = f32[8,152,128]{2,1,0:T(8,128)S(1)} custom-call(s32[1]{0:T(128)} %bitcast.3.ids, bf16[176,512]{1,0:T(8,128)(2,1)S(1)} %get-tuple-element.60.turned, bf16[512,512]{1,0:T(8,128)(2,1)S(1)} %get-tuple-element.42.pick, bf16[512,2048]{1,0:T(8,128)(2,1)S(1)} %shard_map.137.a_ref, f32[4,512,256]{2,1,0:T(8,128)S(1)} %get-tuple-element.61.slope, ...), custom_call_target="tpu_custom_call" | custom-call | flops 738197504 | bytes 6291456 | tf_op jit(solution)/shard_map/pallas_call | solution.py:67
  56.1 19.8 %all_to_all.28.pieces = f32[8,152,128]{2,1,0:T(8,128)S(1)} all-to-all(f32[8,152,128]{2,1,0:T(8,128)S(1)} %shard_map.141), channel_id=1, replica_groups=mesh['node'=8,'feat'=4] {'node'}, dimensions={0} | all-to-all | bytes 1245184 | tf_op jit(solution)/shard_map/all_to_all | solution.py:289
  76.0 19.6 %all_to_all.29.pieces = f32[8,152,128]{2,1,0:T(8,128)S(1)} all-to-all(f32[8,152,128]{2,1,0:T(8,128)S(1)} %shard_map.142), channel_id=1, replica_groups=mesh['node'=8,'feat'=4] {'node'}, dimensions={0} | all-to-all | bytes 1245184 | tf_op jit(solution)/shard_map/all_to_all | solution.py:289
  95.5 0.8 shard_map.143
  (18 shorter events, 0.1 us)
Async XLA Ops:
  0.6 6.9 %collective-permute-start.2 = (bf16[32,512]{1,0:T(8,128)(2,1)}, bf16[32,512]{1,0:T(8,128)(2,1)S(1)}, u32[]{:S(2)}, u32[]{:S(2)}) collective-permute-start(bf16[32,512]{1,0:T(8,128)(2,1)} %bitcast.17), channel_id=1, source_target_pairs={{0,3},{1,2},{2,1},{3,0},{4,7},{5,6},{6,5},{7,4},{8,11},{9,10},{10,... | collective-permute-start | bytes 98312 | tf_op jit(solution)/shard_map/ppermute | solution.py:293
  3.1 4.5 %collective-permute-start.1 = (bf16[32,512]{1,0:T(8,128)(2,1)}, bf16[32,512]{1,0:T(8,128)(2,1)S(1)}, u32[]{:S(2)}, u32[]{:S(2)}) collective-permute-start(bf16[32,512]{1,0:T(8,128)(2,1)} %bitcast.18), channel_id=1, source_target_pairs={{0,2},{1,3},{2,0},{3,1},{4,6},{5,7},{6,4},{7,5},{8,10},{9,11},{10,... | collective-permute-start | bytes 98312 | tf_op jit(solution)/shard_map/ppermute | solution.py:293
  3.7 3.9 %collective-permute-start = (bf16[32,512]{1,0:T(8,128)(2,1)}, bf16[32,512]{1,0:T(8,128)(2,1)S(1)}, u32[]{:S(2)}, u32[]{:S(2)}) collective-permute-start(bf16[32,512]{1,0:T(8,128)(2,1)} %bitcast.19), channel_id=1, source_target_pairs={{0,1},{1,0},{2,3},{3,2},{4,5},{5,4},{6,7},{7,6},{8,9},{9,8},{10,11... | collective-permute-start | bytes 98312 | tf_op jit(solution)/shard_map/ppermute | solution.py:293
  3.8 0.7 copy-start.6
  4.4 3.1 %copy-start = (bf16[512,32]{0,1:T(8,128)(2,1)S(1)}, bf16[512,32]{0,1:T(8,128)(2,1)}, u32[]{:S(2)}) copy-start(bf16[512,32]{0,1:T(8,128)(2,1)} %param.10) | copy-start | bytes 98308
  4.4 3.1 %copy-start.1 = (bf16[256,172]{0,1:T(8,128)(2,1)S(1)}, bf16[256,172]{0,1:T(8,128)(2,1)}, u32[]{:S(2)}) copy-start(bf16[256,172]{0,1:T(8,128)(2,1)} %param.18) | copy-start | bytes 264196
  4.4 3.2 %copy-start.2 = (bf16[256,172]{0,1:T(8,128)(2,1)S(1)}, bf16[256,172]{0,1:T(8,128)(2,1)}, u32[]{:S(2)}) copy-start(bf16[256,172]{0,1:T(8,128)(2,1)} %param.19) | copy-start | bytes 264196
  4.4 3.2 %copy-start.3 = (bf16[32,1024]{1,0:T(8,128)(2,1)S(1)}, bf16[32,1024]{1,0:T(8,128)(2,1)}, u32[]{:S(2)}) copy-start(bf16[32,1024]{1,0:T(8,128)(2,1)} %w_self1.1) | copy-start | bytes 196612
  4.5 3.2 %copy-start.4 = (bf16[32,1024]{1,0:T(8,128)(2,1)S(1)}, bf16[32,1024]{1,0:T(8,128)(2,1)}, u32[]{:S(2)}) copy-start(bf16[32,1024]{1,0:T(8,128)(2,1)} %w_neigh1.1) | copy-start | bytes 196612
  4.5 3.2 %copy-start.5 = (s32[1,8,64]{2,1,0:T(8,128)S(1)}, s32[1,8,64]{2,1,0:T(8,128)}, u32[]{:S(2)}) copy-start(s32[1,8,64]{2,1,0:T(8,128)} %param.11) | copy-start | bytes 6148
  4.5 3.2 %copy-start.7 = (s32[1,8]{1,0:T(1,128)S(1)}, s32[1,8]{1,0:T(1,128)}, u32[]{:S(2)}) copy-start(s32[1,8]{1,0:T(1,128)} %count.1) | copy-start | bytes 100
  7.5 29.0 %copy-start.8 = (s32[512]{0:T(512)S(1)}, s32[512]{0:T(512)}, u32[]{:S(2)}) copy-start(s32[512]{0:T(512)} %param.15) | copy-start | bytes 6148
  8.7 16.3 %collective-permute-start.4 = (bf16[608,256]{1,0:T(8,128)(2,1)S(1)}, bf16[608,256]{1,0:T(8,128)(2,1)S(1)}, u32[]{:S(2)}, u32[]{:S(2)}) collective-permute-start(bf16[608,256]{1,0:T(8,128)(2,1)S(1)} %get-tuple-element.56.refs_0_), channel_id=1, source_target_pairs={{0,2},{1,3},{2,0},{3,1},{4,6},{5,7},{6,4},{7,5},{8,10},{9,11},{10,... | collective-permute-start | bytes 933896 | tf_op jit(solution)/shard_map/ppermute | solution.py:293
  10.5 14.5 %collective-permute-start.3 = (bf16[608,256]{1,0:T(8,128)(2,1)S(1)}, bf16[608,256]{1,0:T(8,128)(2,1)S(1)}, u32[]{:S(2)}, u32[]{:S(2)}) collective-permute-start(bf16[608,256]{1,0:T(8,128)(2,1)S(1)} %get-tuple-element.56.refs_0_), channel_id=1, source_target_pairs={{0,1},{1,0},{2,3},{3,2},{4,5},{5,4},{6,7},{7,6},{8,9},{9,8},{10,11... | collective-permute-start | bytes 933896 | tf_op jit(solution)/shard_map/ppermute | solution.py:293
  24.9 1.7 %collective-permute-start.5 = (bf16[608,256]{1,0:T(8,128)(2,1)S(1)}, bf16[608,256]{1,0:T(8,128)(2,1)S(1)}, u32[]{:S(2)}, u32[]{:S(2)}) collective-permute-start(bf16[608,256]{1,0:T(8,128)(2,1)S(1)} %collective-permute-done.4.refs_2_), channel_id=1, source_target_pairs={{0,1},{1,0},{2,3},{3,2},{4,5},{5,4},{6,7},{7,6},{8,9},{9,8},{10,11... | collective-permute-start | bytes 933896 | tf_op jit(solution)/shard_map/ppermute | solution.py:293

commit v11 on v9

--- a/solution.py
+++ b/solution.py
@@ -61,7 +61,7 @@
 def call(body, outs, args, scratch=(), copies=0, flops=0, moved=0, grant=0):
     specs = [SMEM if arg.dtype == jnp.int32 and arg.size < 512 else VMEM for arg in args]
     if copies:
-        specs = [spec if spec is SMEM else HBM for spec in specs]
+        specs = [HBM] * len(args)
     room = sum(size_of(shape, dtype) for shape, dtype in [*outs, *scratch])
     room += sum(size_of(arg.shape, arg.dtype) for arg, spec in zip(args, specs) if spec is VMEM)
     return pl.pallas_call(
@@ -70,19 +70,22 @@
         in_specs=specs,
         out_specs=[VMEM] * len(outs),
         scratch_shapes=[pltpu.VMEM(shape, dtype) for shape, dtype in scratch]
-        + ([pltpu.SemaphoreType.DMA((copies,))] if copies else []),
+        + ([pltpu.SemaphoreType.DMA((copies,)), pltpu.SMEM(args[0].shape, jnp.int32)] if copies else []),
         compiler_params=pltpu.CompilerParams(vmem_limit_bytes=grant or min(room + 8 * 2**20, 56 * 2**20)),
         cost_estimate=pl.CostEstimate(flops=flops, bytes_accessed=moved, transcendentals=0),
     )(*args)
 
 
-def prepare_kernel(tile_src, tile_val, a_ref, tiles, dense, sems):
+def prepare_kernel(src_in, tile_val, a_ref, tiles, dense, sems, tile_src):
     blocks, per_block = tile_val.shape[0], tile_val.shape[1]
     own = blocks * BLOCK
+    src_copy = pltpu.make_async_copy(src_in, tile_src, sems.at[blocks])
+    src_copy.start()
     copies = [pltpu.make_async_copy(tile_val.at[b], tiles.at[b], sems.at[b]) for b in range(blocks)]
     for copy in copies:
         copy.start()
     dense[...] = jnp.zeros_like(dense)
+    src_copy.wait()
     for b in range(blocks):
         rows = pl.ds(b * BLOCK, BLOCK)
         copies[b].wait()
@@ -137,10 +140,10 @@
 
 
 def forward_kernel(
-    class_count, grad_scale, groups, ids, a_ref, state, landed, labels, *refs
+    class_count, grad_scale, groups, ids, side, a_ref, state, landed, labels, *refs
 ):
     weights = refs[:groups]
-    turned, mine, agg_mine, loss, slope, packed = refs[groups:]
+    turned, slope, packed, *seconds = refs[groups:]
     halo, cols = landed.shape
     own = state.shape[0] - halo
     units = weights[0].shape[1]
@@ -171,8 +174,7 @@
             held = lax.fori_loop(0, halo // own, one, spread(a_ref[:, : 2 * own], out))
         rounded = held.astype(BF16)
         if k == 0:
-            mine[...] = out
-            agg_mine[...] = rounded
+            mine, agg_mine = out, rounded
         total = total + mm_nt(weights[k][pl.ds(base, pad), :], out) + mm_nt(weights[k][pl.ds(base + pad, pad), :], rounded)
     class_id = lax.broadcasted_iota(jnp.int32, total.shape, 0)
     real = class_id < class_count
@@ -183,7 +185,18 @@
     target = (class_id == labels[...]).astype(F32)
     turned[...] = ((powers / sums - target) * grad_scale).astype(BF16)
     row_loss = jnp.log(sums) - jnp.sum(shifted * target, axis=0, keepdims=True)
-    loss[...] = jnp.broadcast_to(jnp.sum(row_loss, axis=1, keepdims=True), loss.shape)
+    own_grads = mm(turned[...], mine)
+    row = lax.broadcasted_iota(jnp.int32, own_grads.shape, 0)
+    own_grads = jnp.where(row == class_count, jnp.sum(row_loss, axis=1, keepdims=True), own_grads)
+    if len(seconds) == 1:
+        seconds[0][:, :units] = own_grads
+        seconds[0][:, units:] = mm(turned[...], agg_mine)
+    else:
+        keep, give, both = seconds
+        both[0] = own_grads
+        both[1] = mm(turned[...], agg_mine)
+        keep[...] = both[side[0]]
+        give[...] = both[1 - side[0]]
     per_chunk = own // slots
     for c in range(halo // own):
         back = mm(turned[...], a_ref[:, pl.ds(2 * (c + 1) * own, own)]).T.astype(BF16)
@@ -218,29 +231,14 @@
     landed[pl.ds(d * slots + half, half), BLOCK:] = packed[d, slots:, BLOCK // 2 : BLOCK // 2 + tail]
 
 
-def cut(rows, lanes, parts):
-    across = lanes // BLOCK
-    down = parts // across
-    height = rows // down
-    return [(slice(p % down * height, (p % down + 1) * height), slice(p // down * BLOCK, (p // down + 1) * BLOCK)) for p in range(parts)]
-
-
-def backward_kernel(
-    class_count, parts, groups, ids, turned, pick, a_ref, slope, features, state, mine, agg_mine, loss, landed, *refs
-):
+def backward_kernel(parts, groups, ids, turned, pick, a_ref, slope, features, state, landed, *refs):
     weights = refs[:groups]
-    if parts:
-        out, rows, both = refs[groups:]
-    else:
-        out, both, rows = refs[groups:]
-    own, units = mine.shape
+    out, rows = refs[groups:]
+    own = turned.shape[1]
+    units = slope.shape[2]
     pad = turned.shape[0]
     step = features.shape[0]
     base = 2 * step * groups
-    own_grads = mm(turned[...], mine[...])
-    row = lax.broadcasted_iota(jnp.int32, own_grads.shape, 0)
-    both[:, :units] = jnp.where(row == class_count, loss[0:1, 0:1], own_grads)
-    both[:, units:] = mm(turned[...], agg_mine[...])
     for d in range(landed.shape[0]):
         take_message(landed, d, rows)
     high, low = halves(mm(turned[...], a_ref[:, :own]) + mm_tn(rows[...], pick[...]))
@@ -254,34 +252,53 @@
         result = mm(left, (total * slope[k]).astype(BF16))
         if parts:
             for i in range(units // BLOCK):
-                out[group * (units // BLOCK) + i, pl.ds(0, 2 * step), :] = result[:, i * BLOCK : (i + 1) * BLOCK]
+                out[group * (units // BLOCK) + i] = result[:, i * BLOCK : (i + 1) * BLOCK]
         else:
             out[:, pl.ds(pl.multiple_of(group * units, units), units)] = result
-    if parts:
-        for p, (height, lanes) in enumerate(cut(*both.shape, parts)):
-            out[p, pl.ds(2 * step, out.shape[1] - 2 * step), :] = both[height, lanes]
-
-
-def sum_kernel(pieces, out):
-    held = pieces[0]
-    for k in range(1, pieces.shape[0]):
-        held = held + pieces[k]
-    for k in range(pieces.shape[0]):
-        out[k] = held
+
+
+def quarter(p, rows):
+    height = rows // 4
+    return slice(p // 2 * height, (p // 2 + 1) * height), slice(p % 2 * BLOCK, (p % 2 + 1) * BLOCK)
+
+
+def join_kernel(grads, keep, other, out):
+    step = grads.shape[1]
+    height = keep.shape[0] // 4
+    for p in range(grads.shape[0]):
+        at = quarter(p, keep.shape[0])
+        out[p, :step, :] = grads[p]
+        out[p, step : step + height, :] = keep[at] + other[at]
+        out[p, step + height :, :] = jnp.zeros((out.shape[1] - step - height, BLOCK), F32)
+
+
+def sum_kernel(step, height, pieces, out):
+    first = pieces[0, :step, :]
+    second = [pieces[0, step : step + height, :], pieces[1, step : step + height, :]]
+    for p in range(1, pieces.shape[0]):
+        first = first + pieces[p, :step, :]
+        if p > 1:
+            second[p % 2] = second[p % 2] + pieces[p, step : step + height, :]
+    for p in range(pieces.shape[0]):
+        out[p, :step, :] = first
+        out[p, step : step + height, :] = second[0]
+        out[p, step + height :, :] = second[1]
 
 
 def place_kernel(class_count, node_total, pieces, self1, neigh1, self2, neigh2, loss, both):
     step = self1.shape[0]
-    for p, (rows, lanes) in enumerate(cut(*both.shape, pieces.shape[0])):
-        both[rows, lanes] = pieces[p, pl.ds(2 * step, pieces.shape[1] - 2 * step), :]
+    units = self2.shape[1]
+    height = both.shape[1] // 4
     for p in range(pieces.shape[0]):
         at = pl.ds(p * BLOCK, BLOCK)
-        self1[:, at] = pieces[p, pl.ds(0, step), :]
-        neigh1[:, at] = pieces[p, pl.ds(step, step), :]
-    units = self2.shape[1]
-    self2[...] = both[:class_count, :units]
-    neigh2[...] = both[:class_count, units:]
-    loss[...] = both[class_count : class_count + 1, 0:1] / node_total
+        self1[:, at] = pieces[p, :step, :]
+        neigh1[:, at] = pieces[p, step : 2 * step, :]
+        rows, lanes = quarter(p, both.shape[1])
+        both[0, rows, lanes] = pieces[p, 2 * step : 2 * step + height, :]
+        both[1, rows, lanes] = pieces[p, 2 * step + height :, :]
+    self2[...] = both[0, :class_count, :]
+    neigh2[...] = both[1, :class_count, :]
+    loss[...] = both[0, class_count : class_count + 1, 0:1] / node_total
 
 
 def swap(value, count):
@@ -303,11 +320,11 @@
     width = w_self1.shape[1]
     units, classes = w_self2.shape
     pad = -(-(classes + 1) // 16) * 16
-    across = 2 * units // BLOCK
-    parts = nodes if nodes % across == 0 and pad % (8 * (nodes // across)) == 0 and width == nodes * BLOCK else 0
+    parts = nodes if nodes == 8 and units == 2 * BLOCK and width == nodes * BLOCK else 0
     node_total = own * nodes
     grad_scale = 1.0 / math.sqrt(node_total)
     ids = lax.axis_index("feat").astype(jnp.int32).reshape(1)
+    side = (lax.axis_index("node") & 1).astype(jnp.int32).reshape(1)
     blocks = own // BLOCK
     packed_rows = 2 * step * groups + 2 * pad
 
@@ -318,11 +335,11 @@
         [((own, 2 * total_src), BF16)],
         (tile_src, tile_val),
         [(tile_val.shape, BF16), ((own, total_src), F32)],
-        copies=blocks,
+        copies=blocks + 1,
         moved=tile_val.size * 4,
         grant=54 * 2**20 - 4 * own * total_src - 3 * 10**5,
     )
-    a_mat, ids, *turned_all = lax.optimization_barrier((a_mat, ids, *turned_all))
+    a_mat, ids, side, *turned_all = lax.optimization_barrier((a_mat, ids, side, *turned_all))
     pick, full, packed, packed_weights = call(
         functools.partial(pack_kernel, groups),
         [((halo, own), BF16), ((own, cols), BF16), ((halo, cols), BF16), ((packed_rows, units), BF16)],
@@ -340,46 +357,46 @@
         flops=4 * own * total_src * cols,
         moved=4 * own * total_src,
     )
-    packed, ids, *weights = lax.optimization_barrier((packed, ids, *weights))
+    packed, ids, side, *weights = lax.optimization_barrier((packed, ids, side, *weights))
     landed = swap(packed, nodes).reshape(halo, cols)
     message = (nodes, *message_shape(slots, pad))
-    turned_grads, mine, agg_mine, loss, slope, packed = call(
+    second_shape = (pad, 2 * units)
+    turned_grads, slope, packed, *seconds = call(
         functools.partial(forward_kernel, classes, grad_scale, groups),
-        [
-            ((pad, own), BF16),
-            ((own, units), BF16),
-            ((own, units), BF16),
-            ((8, 128), F32),
-            ((groups, own, units), F32),
-            (message, BF16),
-        ],
-        (ids, a_mat, state, landed, labels.reshape(1, own), *weights),
+        [((pad, own), BF16), ((groups, own, units), F32), (message, BF16)]
+        + ([((pad, units), F32)] * 2 if parts else [(second_shape, F32)]),
+        (ids, side, a_mat, state, landed, labels.reshape(1, own), *weights),
+        [((2, pad, units), F32)] if parts else [],
         flops=8 * own * total_src * width,
         moved=16 * own * width,
     )
+    if parts:
+        keep, give = seconds
+        other = lax.ppermute(give, "node", [(i, i ^ 1) for i in range(nodes)])
     landed = swap(packed, nodes)
-    second_shape = (pad, 2 * units)
-    grads_shape = (parts, 2 * step + pad * 2 * units // (BLOCK * parts), BLOCK) if parts else (2 * step, width)
-    grads, *second = call(
-        functools.partial(backward_kernel, classes, parts, groups),
-        [(grads_shape, F32)] + ([] if parts else [(second_shape, F32)]),
-        (ids, turned_grads, pick, a_mat, slope, turned, state, mine, agg_mine, loss, landed, *weights),
-        [((halo, pad), BF16)] + ([(second_shape, F32)] if parts else []),
+    (grads,) = call(
+        functools.partial(backward_kernel, parts, groups),
+        [((parts, 2 * step, BLOCK) if parts else (2 * step, width), F32)],
+        (ids, turned_grads, pick, a_mat, slope, turned, state, landed, *weights),
+        [((halo, pad), BF16)],
         flops=8 * own * pad * width,
         moved=12 * own * width,
     )
     if not parts:
-        grads, second = lax.psum((grads, second[0]), "node")
+        grads, second = lax.psum((grads, seconds[0]), "node")
         loss = second[classes, 0] / node_total
         return (loss, grads[:step], grads[step:], second[:classes, :units].T, second[:classes, units:].T)
+    height = pad // 4
+    grads, other = lax.optimization_barrier((grads, other))
+    (grads,) = call(join_kernel, [((nodes, -(-(2 * step + height) // 8) * 8, BLOCK), F32)], (grads, keep, other))
     grads = swap(grads, nodes)
-    (grads,) = call(sum_kernel, [(grads_shape, F32)], (grads,), moved=2**20)
+    (grads,) = call(functools.partial(sum_kernel, 2 * step, height), [((nodes, 2 * step + 2 * height, BLOCK), F32)], (grads,))
     grads = swap(grads, nodes)
     grad_self1, grad_neigh1, grad_self2, grad_neigh2, loss = call(
         functools.partial(place_kernel, classes, node_total),
         [((step, width), F32)] * 2 + [((classes, units), F32)] * 2 + [((1, 1), F32)],
         (grads,),
-        [(second_shape, F32)],
+        [((2, pad, units), F32)],
     )
     return (loss.reshape(()), grad_self1, grad_neigh1, grad_self2.T, grad_neigh2.T)
 

time: 92.8 us -> 97.8 us (1.054)
  blocking collectives: 69.4 us -> 53.4 us
  local copies, waits for them, and re-layouts: 0.71 us -> 8.88 us
  waiting for transfers between devices: 0.02 us -> 6.18 us
  starting transfers between devices: 6.25 us -> 11.2 us
  Pallas kernels: 15.3 us -> 16.6 us
    all_to_all x5 -> x4, blocking collectives: 69.4 us -> 53.4 us  [swap(): return lax.all_to_all(blocks, 'node', 0, 0, tiled=True)]
    unnamed x18 -> x44, local copies, waits for them, and re-layouts: 0.71 us -> 8.88 us
    all_to_all x0 -> x1, waiting for transfers between devices: none -> 5.8 us  [swap(): return lax.all_to_all(blocks, 'node', 0, 0, tiled=True)]
    all_to_all x0 -> x1, starting transfers between devices: none -> 3.39 us  [swap(): return lax.all_to_all(blocks, 'node', 0, 0, tiled=True)]
    ppermute x0 -> x1, starting transfers between devices: none -> 1.92 us  [shards(): other = lax.ppermute(give, 'node', [(i, i ^ 1) for i in range(nodes)])]
    pallas_call x7 -> x8, Pallas kernels: 15.3 us -> 16.6 us  [call(): pl.pallas_call(body, out_shape=[jax.ShapeDtypeStruct(shape, dtype) for sh...]
  transfers between devices with their start and end apart: 6 -> 8, of which waited for: 0 -> 3; matrix products, arithmetic and copies ran while one was open for 0% -> 0% of each run, Pallas kernels for 5% -> 7%
where the time goes in v11:
time: 97.8 us; the launch traced here: 97.2 us
  blocking collectives  53.4 us (55%)
  Pallas kernels  16.6 us (17%)
  starting transfers between devices  11.2 us (11%)
  local copies, waits for them, and re-layouts  8.88 us (9%)
  waiting for transfers between devices  6.18 us (6%)
    all_to_all x4, blocking collectives, swap(): return lax.all_to_all(blocks, 'node', 0, 0, tiled=True)  53.4 us
    pallas_call x8, Pallas kernels, call(): pl.pallas_call(body, out_shape=[jax.ShapeDtypeStruct(shape, dtype) for sh...  16.6 us
    unnamed x44, local copies, waits for them, and re-layouts  8.88 us
    ppermute x6, starting transfers between devices, gather_shifted(): lax.ppermute(value, 'feat', [(i, (i + k) % count) for i in range(count)])  5.93 us
    all_to_all x1, waiting for transfers between devices, swap(): return lax.all_to_all(blocks, 'node', 0, 0, tiled=True)  5.8 us
    all_to_all x1, starting transfers between devices, swap(): return lax.all_to_all(blocks, 'node', 0, 0, tiled=True)  3.39 us
  transfers between devices with their start and end apart: 8, of which 3 were waited for; matrix products, arithmetic and copies ran while one was open for 0% of the time, Pallas kernels for 7%

profile of v11, /device:TPU:0, one launch (start us, length us, event | category | flops | bytes accessed | tf_op | source)
XLA Modules:
  0.0 97.2 jit_solution(2589166174672863553)
XLA Ops:
  0.6 2.4 %collective-permute-start.2 = (bf16[32,512]{1,0:T(8,128)(2,1)}, bf16[32,512]{1,0:T(8,128)(2,1)S(1)}, u32[]{:S(2)}, u32[]{:S(2)}) collective-permute-start(bf16[32,512]{1,0:T(8,128)(2,1)} %bitcast.15), channel_id=1, source_target_pairs={{0,3},{1,0},{2,1},{3,2},{4,7},{5,4},{6,5},{7,6},{8,11},{9,8},{10,9... | collective-permute-start | bytes 98312 | tf_op jit(solution)/shard_map/ppermute | solution.py:310
  3.9 0.7 copy-done.18
  4.6 2.5 %shard_map.137.a_ref = bf16[512,2048]{1,0:T(8,128)(2,1)S(1)} custom-call(s32[4,16]{1,0:T(4,128)S(1)} %copy-done.18, bf16[4,16,128,128]{3,2,1,0:T(8,128)(2,1)} %tile_val.1), custom_call_target="tpu_custom_call" | custom-call | bytes 4194304 | tf_op jit(solution)/shard_map/pallas_call | solution.py:67
  7.6 1.0 %shard_map.138 = (bf16[512,512]{1,0:T(8,128)(2,1)S(1)}, bf16[512,128]{1,0:T(8,128)(2,1)S(1)}, bf16[512,128]{1,0:T(8,128)(2,1)S(1)}, bf16[608,256]{1,0:T(8,128)(2,1)S(1)}) custom-call(s32[1,8]{1,0:T(1,128)S(1)} %copy-done.19, s32[8,64]{1,0:T(8,128)S(1)} %bitcast.25, bf16[32,1024]{1,0:T(8,128)(2,1)S(1)} %copy-done.15, bf16[32,1024]{1,0:T(8,128)(2,1)S(1)} %copy-done.16, ...), custom_call_target="tpu_custom_call" | custom-call | flops 67108864 | bytes 524288 | tf_op jit(solution)/shard_map/pallas_call | solution.py:67
  8.6 1.3 %collective-permute-start.5 = (bf16[608,256]{1,0:T(8,128)(2,1)S(1)}, bf16[608,256]{1,0:T(8,128)(2,1)S(1)}, u32[]{:S(2)}, u32[]{:S(2)}) collective-permute-start(bf16[608,256]{1,0:T(8,128)(2,1)S(1)} %get-tuple-element.53.refs_0_), channel_id=1, source_target_pairs={{0,3},{1,0},{2,1},{3,2},{4,7},{5,4},{6,5},{7,6},{8,11},{9,8},{10,9... | collective-permute-start | bytes 933896 | tf_op jit(solution)/shard_map/ppermute | solution.py:310
  9.9 1.4 %collective-permute-start.4 = (bf16[608,256]{1,0:T(8,128)(2,1)S(1)}, bf16[608,256]{1,0:T(8,128)(2,1)S(1)}, u32[]{:S(2)}, u32[]{:S(2)}) collective-permute-start(bf16[608,256]{1,0:T(8,128)(2,1)S(1)} %get-tuple-element.53.refs_0_), channel_id=1, source_target_pairs={{0,2},{1,3},{2,0},{3,1},{4,6},{5,7},{6,4},{7,5},{8,10},{9,11},{10,... | collective-permute-start | bytes 933896 | tf_op jit(solution)/shard_map/ppermute | solution.py:310
  11.3 13.5 %all_to_all.25 = bf16[8,64,128]{2,1,0:T(8,128)(2,1)S(1)} all-to-all(bf16[8,64,128]{2,1,0:T(8,128)(2,1)S(1)} %bitcast.20), channel_id=1, replica_groups=mesh['node'=8,'feat'=4] {'node'}, dimensions={0} | all-to-all | bytes 262144 | tf_op jit(solution)/shard_map/all_to_all | solution.py:306
  24.8 1.2 %shard_map.139 = (bf16[1024,256]{1,0:T(8,128)(2,1)S(1)}, bf16[512,128]{1,0:T(8,128)(2,1)S(1)}) custom-call(bf16[512,512]{1,0:T(8,128)(2,1)S(1)} %get-tuple-element.41.pick, bf16[512,2048]{1,0:T(8,128)(2,1)S(1)} %shard_map.137.a_ref, bf16[512,128]{1,0:T(8,128)(2,1)S(1)} %get-tuple-element.43.full, bf16[512,128]{1,0:T(8,128)(2,1)S(1)} %bitcast.14), custom_call_target="tpu_custom_call" | custom-call | flops 268435456 | bytes 2097152 | tf_op jit(solution)/shard_map/pallas_call | solution.py:67
  26.0 12.6 %all_to_all.26 = bf16[8,64,128]{2,1,0:T(8,128)(2,1)S(1)} all-to-all(bf16[8,64,128]{2,1,0:T(8,128)(2,1)S(1)} %bitcast.21), channel_id=1, replica_groups=mesh['node'=8,'feat'=4] {'node'}, dimensions={0} | all-to-all | bytes 262144 | tf_op jit(solution)/shard_map/all_to_all | solution.py:306
  38.7 7.2 %shard_map.140 = (bf16[176,512]{1,0:T(8,128)(2,1)S(1)}, f32[4,512,256]{2,1,0:T(8,128)S(1)}, bf16[8,96,128]{2,1,0:T(8,128)(2,1)}, f32[176,256]{1,0:T(8,128)S(1)}, f32[176,256]{1,0:T(8,128)S(1)}) custom-call(s32[1]{0:T(128)} %bitcast.3.ids, s32[1]{0:T(128)} %bitcast.4.side, bf16[512,2048]{1,0:T(8,128)(2,1)S(1)} %shard_map.137.a_ref, ...), custom_call_target="tpu_custom_call" | custom-call | flops 4294967296 | bytes 8388608 | tf_op jit(solution)/shard_map/pallas_call | solution.py:67
  45.9 1.3 %copy-done = f32[4,512,256]{2,1,0:T(8,128)} copy-done((f32[4,512,256]{2,1,0:T(8,128)}, f32[4,512,256]{2,1,0:T(8,128)S(1)}, u32[]{:S(2)}) %copy-start) | copy-done | bytes 2097176
  48.6 3.4 %all-to-all-start.2 = ((bf16[8,96,128]{2,1,0:T(8,128)(2,1)}), bf16[8,96,128]{2,1,0:T(8,128)(2,1)S(1)}, u32[]{:S(2)}, u32[]{:S(2)}) async-start(bf16[8,96,128]{2,1,0:T(8,128)(2,1)} %get-tuple-element.59), calls=%async_computation.2 | async-start | bytes 393216 | tf_op jit(solution)/shard_map/all_to_all | solution.py:306
  52.0 1.9 %collective-permute-start.6 = (f32[176,256]{1,0:T(8,128)}, f32[176,256]{1,0:T(8,128)}, u32[]{:S(2)}, u32[]{:S(2)}) collective-permute-start(f32[176,256]{1,0:T(8,128)} %copy-done.20), channel_id=1, source_target_pairs={{0,4},{4,0},{8,12},{12,8},{16,20},{20,16},{24,28},{28,24},{1,5},{5... | collective-permute-start | bytes 540680 | tf_op jit(solution)/shard_map/ppermute | solution.py:375
  53.9 5.8 %all-to-all-done.2.landed = bf16[8,96,128]{2,1,0:T(8,128)(2,1)S(1)} async-done(((bf16[8,96,128]{2,1,0:T(8,128)(2,1)}), bf16[8,96,128]{2,1,0:T(8,128)(2,1)S(1)}, u32[]{:S(2)}, u32[]{:S(2)}) %all-to-all-start.2) | async-done | bytes 196640 | tf_op jit(solution)/shard_map/all_to_all | solution.py:306
  59.7 1.6 %copy-done.1 = f32[4,512,256]{2,1,0:T(8,128)S(1)} copy-done((f32[4,512,256]{2,1,0:T(8,128)S(1)}, f32[4,512,256]{2,1,0:T(8,128)}, u32[]{:S(2)}) %copy-start.1) | copy-done | bytes 2097176
  61.3 1.0 copy-done.3
  62.3 1.0 copy-done.5
  63.3 1.0 copy-done.7
  64.2 1.0 copy-done.9
  65.2 2.8 %shard_map.141.grads = f32[8,64,128]{2,1,0:T(8,128)S(1)} custom-call(s32[1]{0:T(128)} %bitcast.3.ids, bf16[176,512]{1,0:T(8,128)(2,1)S(1)} %get-tuple-element.57.turned, bf16[512,512]{1,0:T(8,128)(2,1)S(1)} %get-tuple-element.41.pick, bf16[512,2048]{1,0:T(8,128)(2,1)S(1)} %shard_map.137.a_ref, f32[4,512,256]{2,1,0:T(8,128)S(1)} %copy-done.1, ...), custom_call_target="tpu_custom_call" | custom-call | flops 738197504 | bytes 6291456 | tf_op jit(solution)/shard_map/pallas_call | solution.py:67
  68.0 1.0 shard_map.142
  69.0 12.3 %all_to_all.27.pieces = f32[8,112,128]{2,1,0:T(8,128)S(1)} all-to-all(f32[8,112,128]{2,1,0:T(8,128)S(1)} %shard_map.142), channel_id=1, replica_groups=mesh['node'=8,'feat'=4] {'node'}, dimensions={0} | all-to-all | bytes 917504 | tf_op jit(solution)/shard_map/all_to_all | solution.py:306
  81.3 15.0 %all_to_all.28.pieces = f32[8,152,128]{2,1,0:T(8,128)S(1)} all-to-all(f32[8,152,128]{2,1,0:T(8,128)S(1)} %shard_map.143), channel_id=1, replica_groups=mesh['node'=8,'feat'=4] {'node'}, dimensions={0} | all-to-all | bytes 1245184 | tf_op jit(solution)/shard_map/all_to_all | solution.py:306
  96.3 0.8 shard_map.144
  (48 shorter events, 2.6 us)
Async XLA Ops:
  0.6 6.5 %collective-permute-start.2 = (bf16[32,512]{1,0:T(8,128)(2,1)}, bf16[32,512]{1,0:T(8,128)(2,1)S(1)}, u32[]{:S(2)}, u32[]{:S(2)}) collective-permute-start(bf16[32,512]{1,0:T(8,128)(2,1)} %bitcast.15), channel_id=1, source_target_pairs={{0,3},{1,0},{2,1},{3,2},{4,7},{5,4},{6,5},{7,6},{8,11},{9,8},{10,9... | collective-permute-start | bytes 98312 | tf_op jit(solution)/shard_map/ppermute | solution.py:310
  3.1 4.4 %collective-permute-start.1 = (bf16[32,512]{1,0:T(8,128)(2,1)}, bf16[32,512]{1,0:T(8,128)(2,1)S(1)}, u32[]{:S(2)}, u32[]{:S(2)}) collective-permute-start(bf16[32,512]{1,0:T(8,128)(2,1)} %bitcast.16), channel_id=1, source_target_pairs={{0,2},{1,3},{2,0},{3,1},{4,6},{5,7},{6,4},{7,5},{8,10},{9,11},{10,... | collective-permute-start | bytes 98312 | tf_op jit(solution)/shard_map/ppermute | solution.py:310
  3.7 3.8 %collective-permute-start = (bf16[32,512]{1,0:T(8,128)(2,1)}, bf16[32,512]{1,0:T(8,128)(2,1)S(1)}, u32[]{:S(2)}, u32[]{:S(2)}) collective-permute-start(bf16[32,512]{1,0:T(8,128)(2,1)} %bitcast.17), channel_id=1, source_target_pairs={{0,1},{1,2},{2,3},{3,0},{4,5},{5,6},{6,7},{7,4},{8,9},{9,10},{10,1... | collective-permute-start | bytes 98312 | tf_op jit(solution)/shard_map/ppermute | solution.py:310
  4.6 3.0 %copy-start.12 = (bf16[512,32]{0,1:T(8,128)(2,1)S(1)}, bf16[512,32]{0,1:T(8,128)(2,1)}, u32[]{:S(2)}) copy-start(bf16[512,32]{0,1:T(8,128)(2,1)} %param.10) | copy-start | bytes 98308
  4.6 3.0 %copy-start.13 = (bf16[256,172]{0,1:T(8,128)(2,1)S(1)}, bf16[256,172]{0,1:T(8,128)(2,1)}, u32[]{:S(2)}) copy-start(bf16[256,172]{0,1:T(8,128)(2,1)} %param.18) | copy-start | bytes 264196
  4.6 3.0 %copy-start.14 = (bf16[256,172]{0,1:T(8,128)(2,1)S(1)}, bf16[256,172]{0,1:T(8,128)(2,1)}, u32[]{:S(2)}) copy-start(bf16[256,172]{0,1:T(8,128)(2,1)} %param.19) | copy-start | bytes 264196
  4.6 3.0 %copy-start.15 = (bf16[32,1024]{1,0:T(8,128)(2,1)S(1)}, bf16[32,1024]{1,0:T(8,128)(2,1)}, u32[]{:S(2)}) copy-start(bf16[32,1024]{1,0:T(8,128)(2,1)} %w_self1.1) | copy-start | bytes 196612
  4.6 3.0 %copy-start.16 = (bf16[32,1024]{1,0:T(8,128)(2,1)S(1)}, bf16[32,1024]{1,0:T(8,128)(2,1)}, u32[]{:S(2)}) copy-start(bf16[32,1024]{1,0:T(8,128)(2,1)} %w_neigh1.1) | copy-start | bytes 196612
  4.6 3.0 %copy-start.17 = (s32[1,8,64]{2,1,0:T(8,128)S(1)}, s32[1,8,64]{2,1,0:T(8,128)}, u32[]{:S(2)}) copy-start(s32[1,8,64]{2,1,0:T(8,128)} %param.11) | copy-start | bytes 6148
  4.6 3.0 %copy-start.19 = (s32[1,8]{1,0:T(1,128)S(1)}, s32[1,8]{1,0:T(1,128)}, u32[]{:S(2)}) copy-start(s32[1,8]{1,0:T(1,128)} %count.1) | copy-start | bytes 100
  7.2 31.5 %copy-start.21 = (s32[512]{0:T(512)S(1)}, s32[512]{0:T(512)}, u32[]{:S(2)}) copy-start(s32[512]{0:T(512)} %param.15) | copy-start | bytes 6148
  8.6 37.3 %copy-start.2 = (bf16[608,256]{1,0:T(8,128)(2,1)}, bf16[608,256]{1,0:T(8,128)(2,1)S(1)}, u32[]{:S(2)}) copy-start(bf16[608,256]{1,0:T(8,128)(2,1)S(1)} %get-tuple-element.53.refs_0_) | copy-start | bytes 933892
  8.6 17.4 %collective-permute-start.5 = (bf16[608,256]{1,0:T(8,128)(2,1)S(1)}, bf16[608,256]{1,0:T(8,128)(2,1)S(1)}, u32[]{:S(2)}, u32[]{:S(2)}) collective-permute-start(bf16[608,256]{1,0:T(8,128)(2,1)S(1)} %get-tuple-element.53.refs_0_), channel_id=1, source_target_pairs={{0,3},{1,0},{2,1},{3,2},{4,7},{5,4},{6,5},{7,6},{8,11},{9,8},{10,9... | collective-permute-start | bytes 933896 | tf_op jit(solution)/shard_map/ppermute | solution.py:310
  9.9 16.1 %collective-permute-start.4 = (bf16[608,256]{1,0:T(8,128)(2,1)S(1)}, bf16[608,256]{1,0:T(8,128)(2,1)S(1)}, u32[]{:S(2)}, u32[]{:S(2)}) collective-permute-start(bf16[608,256]{1,0:T(8,128)(2,1)S(1)} %get-tuple-element.53.refs_0_), channel_id=1, source_target_pairs={{0,2},{1,3},{2,0},{3,1},{4,6},{5,7},{6,4},{7,5},{8,10},{9,11},{10,... | collective-permute-start | bytes 933896 | tf_op jit(solution)/shard_map/ppermute | solution.py:310
  11.3 14.7 %collective-permute-start.3 = (bf16[608,256]{1,0:T(8,128)(2,1)S(1)}, bf16[608,256]{1,0:T(8,128)(2,1)S(1)}, u32[]{:S(2)}, u32[]{:S(2)}) collective-permute-start(bf16[608,256]{1,0:T(8,128)(2,1)S(1)} %get-tuple-element.53.refs_0_), channel_id=1, source_target_pairs={{0,1},{1,2},{2,3},{3,0},{4,5},{5,6},{6,7},{7,4},{8,9},{9,10},{10,1... | collective-permute-start | bytes 933896 | tf_op jit(solution)/shard_map/ppermute | solution.py:310
  26.0 19.9 %copy-start.4 = (bf16[608,256]{1,0:T(8,128)(2,1)}, bf16[608,256]{1,0:T(8,128)(2,1)S(1)}, u32[]{:S(2)}) copy-start(bf16[608,256]{1,0:T(8,128)(2,1)S(1)} %collective-permute-done.5.refs_3_) | copy-start | bytes 933892
  26.0 19.9 %copy-start.6 = (bf16[608,256]{1,0:T(8,128)(2,1)}, bf16[608,256]{1,0:T(8,128)(2,1)S(1)}, u32[]{:S(2)}) copy-start(bf16[608,256]{1,0:T(8,128)(2,1)S(1)} %collective-permute-done.4.refs_2_) | copy-start | bytes 933892
  26.0 19.9 %copy-start.8 = (bf16[608,256]{1,0:T(8,128)(2,1)}, bf16[608,256]{1,0:T(8,128)(2,1)S(1)}, u32[]{:S(2)}) copy-start(bf16[608,256]{1,0:T(8,128)(2,1)S(1)} %collective-permute-done.3.refs_1_) | copy-start | bytes 933892
  45.9 1.4 %copy-start = (f32[4,512,256]{2,1,0:T(8,128)}, f32[4,512,256]{2,1,0:T(8,128)S(1)}, u32[]{:S(2)}) copy-start(f32[4,512,256]{2,1,0:T(8,128)S(1)} %get-tuple-element.58.slope) | copy-start | bytes 6291460
  48.6 11.1 %all-to-all-start.2 = ((bf16[8,96,128]{2,1,0:T(8,128)(2,1)}), bf16[8,96,128]{2,1,0:T(8,128)(2,1)S(1)}, u32[]{:S(2)}, u32[]{:S(2)}) async-start(bf16[8,96,128]{2,1,0:T(8,128)(2,1)} %get-tuple-element.59), calls=%async_computation.2 | async-start | bytes 393216 | tf_op jit(solution)/shard_map/all_to_all | solution.py:306
  52.0 16.0 %collective-permute-start.6 = (f32[176,256]{1,0:T(8,128)}, f32[176,256]{1,0:T(8,128)}, u32[]{:S(2)}, u32[]{:S(2)}) collective-permute-start(f32[176,256]{1,0:T(8,128)} %copy-done.20), channel_id=1, source_target_pairs={{0,4},{4,0},{8,12},{12,8},{16,20},{20,16},{24,28},{28,24},{1,5},{5... | collective-permute-start | bytes 540680 | tf_op jit(solution)/shard_map/ppermute | solution.py:375
  59.7 1.6 %copy-start.1 = (f32[4,512,256]{2,1,0:T(8,128)S(1)}, f32[4,512,256]{2,1,0:T(8,128)}, u32[]{:S(2)}) copy-start(f32[4,512,256]{2,1,0:T(8,128)} %copy-done) | copy-start | bytes 6291460
  61.3 1.0 copy-start.3
  65.2 2.8 %copy-start.11 = (f32[176,256]{1,0:T(8,128)S(1)}, f32[176,256]{1,0:T(8,128)}, u32[]{:S(2)}) copy-start(f32[176,256]{1,0:T(8,128)} %copy-done.10) | copy-start | bytes 540676
  (6 other events, 4.9 us)

commit v12 on v11

--- a/solution.py
+++ b/solution.py
@@ -379,8 +379,6 @@
         [((parts, 2 * step, BLOCK) if parts else (2 * step, width), F32)],
         (ids, turned_grads, pick, a_mat, slope, turned, state, landed, *weights),
         [((halo, pad), BF16)],
-        flops=8 * own * pad * width,
-        moved=12 * own * width,
     )
     if not parts:
         grads, second = lax.psum((grads, seconds[0]), "node")

time: 97.8 us -> 97.8 us (level)
  no operation moved by 1% of the time
where the time goes in v12:
time: 97.8 us; the launch traced here: 97.2 us
  blocking collectives  53.4 us (55%)
  Pallas kernels  16.6 us (17%)
  starting transfers between devices  11.2 us (11%)
  local copies, waits for them, and re-layouts  8.88 us (9%)
  waiting for transfers between devices  6.18 us (6%)
    all_to_all x4, blocking collectives, swap(): return lax.all_to_all(blocks, 'node', 0, 0, tiled=True)  53.4 us
    pallas_call x8, Pallas kernels, call(): pl.pallas_call(body, out_shape=[jax.ShapeDtypeStruct(shape, dtype) for sh...  16.6 us
    unnamed x44, local copies, waits for them, and re-layouts  8.88 us
    ppermute x6, starting transfers between devices, gather_shifted(): lax.ppermute(value, 'feat', [(i, (i + k) % count) for i in range(count)])  5.93 us
    all_to_all x1, waiting for transfers between devices, swap(): return lax.all_to_all(blocks, 'node', 0, 0, tiled=True)  5.8 us
    all_to_all x1, starting transfers between devices, swap(): return lax.all_to_all(blocks, 'node', 0, 0, tiled=True)  3.39 us
  transfers between devices with their start and end apart: 8, of which 3 were waited for; matrix products, arithmetic and copies ran while one was open for 0% of the time, Pallas kernels for 7%

profile of v12, /device:TPU:0, one launch (start us, length us, event | category | flops | bytes accessed | tf_op | source)
XLA Modules:
  0.0 97.2 jit_solution(2589166174672863553)
XLA Ops:
  0.6 2.4 %collective-permute-start.2 = (bf16[32,512]{1,0:T(8,128)(2,1)}, bf16[32,512]{1,0:T(8,128)(2,1)S(1)}, u32[]{:S(2)}, u32[]{:S(2)}) collective-permute-start(bf16[32,512]{1,0:T(8,128)(2,1)} %bitcast.15), channel_id=1, source_target_pairs={{0,3},{1,0},{2,1},{3,2},{4,7},{5,4},{6,5},{7,6},{8,11},{9,8},{10,9... | collective-permute-start | bytes 98312 | tf_op jit(solution)/shard_map/ppermute | solution.py:310
  3.9 0.7 copy-done.18
  4.6 2.5 %shard_map.137.a_ref = bf16[512,2048]{1,0:T(8,128)(2,1)S(1)} custom-call(s32[4,16]{1,0:T(4,128)S(1)} %copy-done.18, bf16[4,16,128,128]{3,2,1,0:T(8,128)(2,1)} %tile_val.1), custom_call_target="tpu_custom_call" | custom-call | bytes 4194304 | tf_op jit(solution)/shard_map/pallas_call | solution.py:67
  7.6 1.0 %shard_map.138 = (bf16[512,512]{1,0:T(8,128)(2,1)S(1)}, bf16[512,128]{1,0:T(8,128)(2,1)S(1)}, bf16[512,128]{1,0:T(8,128)(2,1)S(1)}, bf16[608,256]{1,0:T(8,128)(2,1)S(1)}) custom-call(s32[1,8]{1,0:T(1,128)S(1)} %copy-done.19, s32[8,64]{1,0:T(8,128)S(1)} %bitcast.25, bf16[32,1024]{1,0:T(8,128)(2,1)S(1)} %copy-done.15, bf16[32,1024]{1,0:T(8,128)(2,1)S(1)} %copy-done.16, ...), custom_call_target="tpu_custom_call" | custom-call | flops 67108864 | bytes 524288 | tf_op jit(solution)/shard_map/pallas_call | solution.py:67
  8.6 1.3 %collective-permute-start.5 = (bf16[608,256]{1,0:T(8,128)(2,1)S(1)}, bf16[608,256]{1,0:T(8,128)(2,1)S(1)}, u32[]{:S(2)}, u32[]{:S(2)}) collective-permute-start(bf16[608,256]{1,0:T(8,128)(2,1)S(1)} %get-tuple-element.53.refs_0_), channel_id=1, source_target_pairs={{0,3},{1,0},{2,1},{3,2},{4,7},{5,4},{6,5},{7,6},{8,11},{9,8},{10,9... | collective-permute-start | bytes 933896 | tf_op jit(solution)/shard_map/ppermute | solution.py:310
  9.9 1.4 %collective-permute-start.4 = (bf16[608,256]{1,0:T(8,128)(2,1)S(1)}, bf16[608,256]{1,0:T(8,128)(2,1)S(1)}, u32[]{:S(2)}, u32[]{:S(2)}) collective-permute-start(bf16[608,256]{1,0:T(8,128)(2,1)S(1)} %get-tuple-element.53.refs_0_), channel_id=1, source_target_pairs={{0,2},{1,3},{2,0},{3,1},{4,6},{5,7},{6,4},{7,5},{8,10},{9,11},{10,... | collective-permute-start | bytes 933896 | tf_op jit(solution)/shard_map/ppermute | solution.py:310
  11.3 13.5 %all_to_all.25 = bf16[8,64,128]{2,1,0:T(8,128)(2,1)S(1)} all-to-all(bf16[8,64,128]{2,1,0:T(8,128)(2,1)S(1)} %bitcast.20), channel_id=1, replica_groups=mesh['node'=8,'feat'=4] {'node'}, dimensions={0} | all-to-all | bytes 262144 | tf_op jit(solution)/shard_map/all_to_all | solution.py:306
  24.8 1.2 %shard_map.139 = (bf16[1024,256]{1,0:T(8,128)(2,1)S(1)}, bf16[512,128]{1,0:T(8,128)(2,1)S(1)}) custom-call(bf16[512,512]{1,0:T(8,128)(2,1)S(1)} %get-tuple-element.41.pick, bf16[512,2048]{1,0:T(8,128)(2,1)S(1)} %shard_map.137.a_ref, bf16[512,128]{1,0:T(8,128)(2,1)S(1)} %get-tuple-element.43.full, bf16[512,128]{1,0:T(8,128)(2,1)S(1)} %bitcast.14), custom_call_target="tpu_custom_call" | custom-call | flops 268435456 | bytes 2097152 | tf_op jit(solution)/shard_map/pallas_call | solution.py:67
  26.0 12.6 %all_to_all.26 = bf16[8,64,128]{2,1,0:T(8,128)(2,1)S(1)} all-to-all(bf16[8,64,128]{2,1,0:T(8,128)(2,1)S(1)} %bitcast.21), channel_id=1, replica_groups=mesh['node'=8,'feat'=4] {'node'}, dimensions={0} | all-to-all | bytes 262144 | tf_op jit(solution)/shard_map/all_to_all | solution.py:306
  38.7 7.2 %shard_map.140 = (bf16[176,512]{1,0:T(8,128)(2,1)S(1)}, f32[4,512,256]{2,1,0:T(8,128)S(1)}, bf16[8,96,128]{2,1,0:T(8,128)(2,1)}, f32[176,256]{1,0:T(8,128)S(1)}, f32[176,256]{1,0:T(8,128)S(1)}) custom-call(s32[1]{0:T(128)} %bitcast.3.ids, s32[1]{0:T(128)} %bitcast.4.side, bf16[512,2048]{1,0:T(8,128)(2,1)S(1)} %shard_map.137.a_ref, ...), custom_call_target="tpu_custom_call" | custom-call | flops 4294967296 | bytes 8388608 | tf_op jit(solution)/shard_map/pallas_call | solution.py:67
  45.9 1.3 %copy-done = f32[4,512,256]{2,1,0:T(8,128)} copy-done((f32[4,512,256]{2,1,0:T(8,128)}, f32[4,512,256]{2,1,0:T(8,128)S(1)}, u32[]{:S(2)}) %copy-start) | copy-done | bytes 2097176
  48.6 3.4 %all-to-all-start.2 = ((bf16[8,96,128]{2,1,0:T(8,128)(2,1)}), bf16[8,96,128]{2,1,0:T(8,128)(2,1)S(1)}, u32[]{:S(2)}, u32[]{:S(2)}) async-start(bf16[8,96,128]{2,1,0:T(8,128)(2,1)} %get-tuple-element.59), calls=%async_computation.2 | async-start | bytes 393216 | tf_op jit(solution)/shard_map/all_to_all | solution.py:306
  52.0 1.9 %collective-permute-start.6 = (f32[176,256]{1,0:T(8,128)}, f32[176,256]{1,0:T(8,128)}, u32[]{:S(2)}, u32[]{:S(2)}) collective-permute-start(f32[176,256]{1,0:T(8,128)} %copy-done.20), channel_id=1, source_target_pairs={{0,4},{4,0},{8,12},{12,8},{16,20},{20,16},{24,28},{28,24},{1,5},{5... | collective-permute-start | bytes 540680 | tf_op jit(solution)/shard_map/ppermute | solution.py:375
  53.9 5.8 %all-to-all-done.2.landed = bf16[8,96,128]{2,1,0:T(8,128)(2,1)S(1)} async-done(((bf16[8,96,128]{2,1,0:T(8,128)(2,1)}), bf16[8,96,128]{2,1,0:T(8,128)(2,1)S(1)}, u32[]{:S(2)}, u32[]{:S(2)}) %all-to-all-start.2) | async-done | bytes 196640 | tf_op jit(solution)/shard_map/all_to_all | solution.py:306
  59.7 1.6 %copy-done.1 = f32[4,512,256]{2,1,0:T(8,128)S(1)} copy-done((f32[4,512,256]{2,1,0:T(8,128)S(1)}, f32[4,512,256]{2,1,0:T(8,128)}, u32[]{:S(2)}) %copy-start.1) | copy-done | bytes 2097176
  61.3 1.0 copy-done.3
  62.3 1.0 copy-done.5
  63.3 1.0 copy-done.7
  64.2 1.0 copy-done.9
  65.2 2.8 %shard_map.141.grads = f32[8,64,128]{2,1,0:T(8,128)S(1)} custom-call(s32[1]{0:T(128)} %bitcast.3.ids, bf16[176,512]{1,0:T(8,128)(2,1)S(1)} %get-tuple-element.57.turned, bf16[512,512]{1,0:T(8,128)(2,1)S(1)} %get-tuple-element.41.pick, bf16[512,2048]{1,0:T(8,128)(2,1)S(1)} %shard_map.137.a_ref, f32[4,512,256]{2,1,0:T(8,128)S(1)} %copy-done.1, ...), custom_call_target="tpu_custom_call" | custom-call | tf_op jit(solution)/shard_map/pallas_call | solution.py:67
  68.0 1.0 shard_map.142
  69.0 12.3 %all_to_all.27.pieces = f32[8,112,128]{2,1,0:T(8,128)S(1)} all-to-all(f32[8,112,128]{2,1,0:T(8,128)S(1)} %shard_map.142), channel_id=1, replica_groups=mesh['node'=8,'feat'=4] {'node'}, dimensions={0} | all-to-all | bytes 917504 | tf_op jit(solution)/shard_map/all_to_all | solution.py:306
  81.3 15.0 %all_to_all.28.pieces = f32[8,152,128]{2,1,0:T(8,128)S(1)} all-to-all(f32[8,152,128]{2,1,0:T(8,128)S(1)} %shard_map.143), channel_id=1, replica_groups=mesh['node'=8,'feat'=4] {'node'}, dimensions={0} | all-to-all | bytes 1245184 | tf_op jit(solution)/shard_map/all_to_all | solution.py:306
  96.3 0.8 shard_map.144
  (48 shorter events, 2.6 us)
Async XLA Ops:
  0.6 6.5 %collective-permute-start.2 = (bf16[32,512]{1,0:T(8,128)(2,1)}, bf16[32,512]{1,0:T(8,128)(2,1)S(1)}, u32[]{:S(2)}, u32[]{:S(2)}) collective-permute-start(bf16[32,512]{1,0:T(8,128)(2,1)} %bitcast.15), channel_id=1, source_target_pairs={{0,3},{1,0},{2,1},{3,2},{4,7},{5,4},{6,5},{7,6},{8,11},{9,8},{10,9... | collective-permute-start | bytes 98312 | tf_op jit(solution)/shard_map/ppermute | solution.py:310
  3.1 4.4 %collective-permute-start.1 = (bf16[32,512]{1,0:T(8,128)(2,1)}, bf16[32,512]{1,0:T(8,128)(2,1)S(1)}, u32[]{:S(2)}, u32[]{:S(2)}) collective-permute-start(bf16[32,512]{1,0:T(8,128)(2,1)} %bitcast.16), channel_id=1, source_target_pairs={{0,2},{1,3},{2,0},{3,1},{4,6},{5,7},{6,4},{7,5},{8,10},{9,11},{10,... | collective-permute-start | bytes 98312 | tf_op jit(solution)/shard_map/ppermute | solution.py:310
  3.7 3.8 %collective-permute-start = (bf16[32,512]{1,0:T(8,128)(2,1)}, bf16[32,512]{1,0:T(8,128)(2,1)S(1)}, u32[]{:S(2)}, u32[]{:S(2)}) collective-permute-start(bf16[32,512]{1,0:T(8,128)(2,1)} %bitcast.17), channel_id=1, source_target_pairs={{0,1},{1,2},{2,3},{3,0},{4,5},{5,6},{6,7},{7,4},{8,9},{9,10},{10,1... | collective-permute-start | bytes 98312 | tf_op jit(solution)/shard_map/ppermute | solution.py:310
  4.6 3.0 %copy-start.12 = (bf16[512,32]{0,1:T(8,128)(2,1)S(1)}, bf16[512,32]{0,1:T(8,128)(2,1)}, u32[]{:S(2)}) copy-start(bf16[512,32]{0,1:T(8,128)(2,1)} %param.10) | copy-start | bytes 98308
  4.6 3.0 %copy-start.13 = (bf16[256,172]{0,1:T(8,128)(2,1)S(1)}, bf16[256,172]{0,1:T(8,128)(2,1)}, u32[]{:S(2)}) copy-start(bf16[256,172]{0,1:T(8,128)(2,1)} %param.18) | copy-start | bytes 264196
  4.6 3.0 %copy-start.14 = (bf16[256,172]{0,1:T(8,128)(2,1)S(1)}, bf16[256,172]{0,1:T(8,128)(2,1)}, u32[]{:S(2)}) copy-start(bf16[256,172]{0,1:T(8,128)(2,1)} %param.19) | copy-start | bytes 264196
  4.6 3.0 %copy-start.15 = (bf16[32,1024]{1,0:T(8,128)(2,1)S(1)}, bf16[32,1024]{1,0:T(8,128)(2,1)}, u32[]{:S(2)}) copy-start(bf16[32,1024]{1,0:T(8,128)(2,1)} %w_self1.1) | copy-start | bytes 196612
  4.6 3.0 %copy-start.16 = (bf16[32,1024]{1,0:T(8,128)(2,1)S(1)}, bf16[32,1024]{1,0:T(8,128)(2,1)}, u32[]{:S(2)}) copy-start(bf16[32,1024]{1,0:T(8,128)(2,1)} %w_neigh1.1) | copy-start | bytes 196612
  4.6 3.0 %copy-start.17 = (s32[1,8,64]{2,1,0:T(8,128)S(1)}, s32[1,8,64]{2,1,0:T(8,128)}, u32[]{:S(2)}) copy-start(s32[1,8,64]{2,1,0:T(8,128)} %param.11) | copy-start | bytes 6148
  4.6 3.0 %copy-start.19 = (s32[1,8]{1,0:T(1,128)S(1)}, s32[1,8]{1,0:T(1,128)}, u32[]{:S(2)}) copy-start(s32[1,8]{1,0:T(1,128)} %count.1) | copy-start | bytes 100
  7.1 31.5 %copy-start.21 = (s32[512]{0:T(512)S(1)}, s32[512]{0:T(512)}, u32[]{:S(2)}) copy-start(s32[512]{0:T(512)} %param.15) | copy-start | bytes 6148
  8.6 37.3 %copy-start.2 = (bf16[608,256]{1,0:T(8,128)(2,1)}, bf16[608,256]{1,0:T(8,128)(2,1)S(1)}, u32[]{:S(2)}) copy-start(bf16[608,256]{1,0:T(8,128)(2,1)S(1)} %get-tuple-element.53.refs_0_) | copy-start | bytes 933892
  8.6 17.4 %collective-permute-start.5 = (bf16[608,256]{1,0:T(8,128)(2,1)S(1)}, bf16[608,256]{1,0:T(8,128)(2,1)S(1)}, u32[]{:S(2)}, u32[]{:S(2)}) collective-permute-start(bf16[608,256]{1,0:T(8,128)(2,1)S(1)} %get-tuple-element.53.refs_0_), channel_id=1, source_target_pairs={{0,3},{1,0},{2,1},{3,2},{4,7},{5,4},{6,5},{7,6},{8,11},{9,8},{10,9... | collective-permute-start | bytes 933896 | tf_op jit(solution)/shard_map/ppermute | solution.py:310
  9.9 16.1 %collective-permute-start.4 = (bf16[608,256]{1,0:T(8,128)(2,1)S(1)}, bf16[608,256]{1,0:T(8,128)(2,1)S(1)}, u32[]{:S(2)}, u32[]{:S(2)}) collective-permute-start(bf16[608,256]{1,0:T(8,128)(2,1)S(1)} %get-tuple-element.53.refs_0_), channel_id=1, source_target_pairs={{0,2},{1,3},{2,0},{3,1},{4,6},{5,7},{6,4},{7,5},{8,10},{9,11},{10,... | collective-permute-start | bytes 933896 | tf_op jit(solution)/shard_map/ppermute | solution.py:310
  11.3 14.7 %collective-permute-start.3 = (bf16[608,256]{1,0:T(8,128)(2,1)S(1)}, bf16[608,256]{1,0:T(8,128)(2,1)S(1)}, u32[]{:S(2)}, u32[]{:S(2)}) collective-permute-start(bf16[608,256]{1,0:T(8,128)(2,1)S(1)} %get-tuple-element.53.refs_0_), channel_id=1, source_target_pairs={{0,1},{1,2},{2,3},{3,0},{4,5},{5,6},{6,7},{7,4},{8,9},{9,10},{10,1... | collective-permute-start | bytes 933896 | tf_op jit(solution)/shard_map/ppermute | solution.py:310
  26.0 19.9 %copy-start.4 = (bf16[608,256]{1,0:T(8,128)(2,1)}, bf16[608,256]{1,0:T(8,128)(2,1)S(1)}, u32[]{:S(2)}) copy-start(bf16[608,256]{1,0:T(8,128)(2,1)S(1)} %collective-permute-done.5.refs_3_) | copy-start | bytes 933892
  26.0 19.9 %copy-start.6 = (bf16[608,256]{1,0:T(8,128)(2,1)}, bf16[608,256]{1,0:T(8,128)(2,1)S(1)}, u32[]{:S(2)}) copy-start(bf16[608,256]{1,0:T(8,128)(2,1)S(1)} %collective-permute-done.4.refs_2_) | copy-start | bytes 933892
  26.0 19.9 %copy-start.8 = (bf16[608,256]{1,0:T(8,128)(2,1)}, bf16[608,256]{1,0:T(8,128)(2,1)S(1)}, u32[]{:S(2)}) copy-start(bf16[608,256]{1,0:T(8,128)(2,1)S(1)} %collective-permute-done.3.refs_1_) | copy-start | bytes 933892
  45.9 1.4 %copy-start = (f32[4,512,256]{2,1,0:T(8,128)}, f32[4,512,256]{2,1,0:T(8,128)S(1)}, u32[]{:S(2)}) copy-start(f32[4,512,256]{2,1,0:T(8,128)S(1)} %get-tuple-element.58.slope) | copy-start | bytes 6291460
  48.6 11.1 %all-to-all-start.2 = ((bf16[8,96,128]{2,1,0:T(8,128)(2,1)}), bf16[8,96,128]{2,1,0:T(8,128)(2,1)S(1)}, u32[]{:S(2)}, u32[]{:S(2)}) async-start(bf16[8,96,128]{2,1,0:T(8,128)(2,1)} %get-tuple-element.59), calls=%async_computation.2 | async-start | bytes 393216 | tf_op jit(solution)/shard_map/all_to_all | solution.py:306
  52.0 16.0 %collective-permute-start.6 = (f32[176,256]{1,0:T(8,128)}, f32[176,256]{1,0:T(8,128)}, u32[]{:S(2)}, u32[]{:S(2)}) collective-permute-start(f32[176,256]{1,0:T(8,128)} %copy-done.20), channel_id=1, source_target_pairs={{0,4},{4,0},{8,12},{12,8},{16,20},{20,16},{24,28},{28,24},{1,5},{5... | collective-permute-start | bytes 540680 | tf_op jit(solution)/shard_map/ppermute | solution.py:375
  59.7 1.6 %copy-start.1 = (f32[4,512,256]{2,1,0:T(8,128)S(1)}, f32[4,512,256]{2,1,0:T(8,128)}, u32[]{:S(2)}) copy-start(f32[4,512,256]{2,1,0:T(8,128)} %copy-done) | copy-start | bytes 6291460
  62.3 1.0 copy-start.5
  65.2 2.8 %copy-start.11 = (f32[176,256]{1,0:T(8,128)S(1)}, f32[176,256]{1,0:T(8,128)}, u32[]{:S(2)}) copy-start(f32[176,256]{1,0:T(8,128)} %copy-done.10) | copy-start | bytes 540676
  (6 other events, 4.9 us)

commit v13 on v12

--- a/solution.py
+++ b/solution.py
@@ -140,10 +140,10 @@
 
 
 def forward_kernel(
-    class_count, grad_scale, groups, ids, side, a_ref, state, landed, labels, *refs
+    class_count, grad_scale, groups, ids, a_ref, state, landed, labels, *refs
 ):
     weights = refs[:groups]
-    turned, slope, packed, *seconds = refs[groups:]
+    turned, slope, packed, second = refs[groups:]
     halo, cols = landed.shape
     own = state.shape[0] - halo
     units = weights[0].shape[1]
@@ -188,15 +188,8 @@
     own_grads = mm(turned[...], mine)
     row = lax.broadcasted_iota(jnp.int32, own_grads.shape, 0)
     own_grads = jnp.where(row == class_count, jnp.sum(row_loss, axis=1, keepdims=True), own_grads)
-    if len(seconds) == 1:
-        seconds[0][:, :units] = own_grads
-        seconds[0][:, units:] = mm(turned[...], agg_mine)
-    else:
-        keep, give, both = seconds
-        both[0] = own_grads
-        both[1] = mm(turned[...], agg_mine)
-        keep[...] = both[side[0]]
-        give[...] = both[1 - side[0]]
+    second[0] = own_grads
+    second[1] = mm(turned[...], agg_mine)
     per_chunk = own // slots
     for c in range(halo // own):
         back = mm(turned[...], a_ref[:, pl.ds(2 * (c + 1) * own, own)]).T.astype(BF16)
@@ -262,13 +255,13 @@
     return slice(p // 2 * height, (p // 2 + 1) * height), slice(p % 2 * BLOCK, (p % 2 + 1) * BLOCK)
 
 
-def join_kernel(grads, keep, other, out):
+def join_kernel(side, grads, second, other, out, total):
     step = grads.shape[1]
-    height = keep.shape[0] // 4
+    height = total.shape[0] // 4
+    total[...] = second[side[0]] + other[side[0]]
     for p in range(grads.shape[0]):
-        at = quarter(p, keep.shape[0])
         out[p, :step, :] = grads[p]
-        out[p, step : step + height, :] = keep[at] + other[at]
+        out[p, step : step + height, :] = total[quarter(p, total.shape[0])]
         out[p, step + height :, :] = jnp.zeros((out.shape[1] - step - height, BLOCK), F32)
 
 
@@ -360,19 +353,15 @@
     packed, ids, side, *weights = lax.optimization_barrier((packed, ids, side, *weights))
     landed = swap(packed, nodes).reshape(halo, cols)
     message = (nodes, *message_shape(slots, pad))
-    second_shape = (pad, 2 * units)
-    turned_grads, slope, packed, *seconds = call(
+    turned_grads, slope, packed, second = call(
         functools.partial(forward_kernel, classes, grad_scale, groups),
-        [((pad, own), BF16), ((groups, own, units), F32), (message, BF16)]
-        + ([((pad, units), F32)] * 2 if parts else [(second_shape, F32)]),
-        (ids, side, a_mat, state, landed, labels.reshape(1, own), *weights),
-        [((2, pad, units), F32)] if parts else [],
+        [((pad, own), BF16), ((groups, own, units), F32), (message, BF16), ((2, pad, units), F32)],
+        (ids, a_mat, state, landed, labels.reshape(1, own), *weights),
         flops=8 * own * total_src * width,
         moved=16 * own * width,
     )
     if parts:
-        keep, give = seconds
-        other = lax.ppermute(give, "node", [(i, i ^ 1) for i in range(nodes)])
+        other = lax.ppermute(second, "node", [(i, i ^ 1) for i in range(nodes)])
     landed = swap(packed, nodes)
     (grads,) = call(
         functools.partial(backward_kernel, parts, groups),
@@ -381,12 +370,17 @@
         [((halo, pad), BF16)],
     )
     if not parts:
-        grads, second = lax.psum((grads, seconds[0]), "node")
-        loss = second[classes, 0] / node_total
-        return (loss, grads[:step], grads[step:], second[:classes, :units].T, second[:classes, units:].T)
+        grads, second = lax.psum((grads, second), "node")
+        loss = second[0, classes, 0] / node_total
+        return (loss, grads[:step], grads[step:], second[0, :classes].T, second[1, :classes].T)
     height = pad // 4
     grads, other = lax.optimization_barrier((grads, other))
-    (grads,) = call(join_kernel, [((nodes, -(-(2 * step + height) // 8) * 8, BLOCK), F32)], (grads, keep, other))
+    (grads,) = call(
+        join_kernel,
+        [((nodes, -(-(2 * step + height) // 8) * 8, BLOCK), F32)],
+        (side, grads, second, other),
+        [((pad, units), F32)],
+    )
     grads = swap(grads, nodes)
     (grads,) = call(functools.partial(sum_kernel, 2 * step, height), [((nodes, 2 * step + 2 * height, BLOCK), F32)], (grads,))
     grads = swap(grads, nodes)

time: 97.8 us -> 87.5 us (0.89)
  blocking collectives: 53.4 us -> 64.1 us
  local copies, waits for them, and re-layouts: 8.88 us -> 0.71 us
  waiting for transfers between devices: 6.18 us -> 0.38 us
  starting transfers between devices: 11.2 us -> 6.2 us
  Pallas kernels: 16.6 us -> 15 us
    all_to_all x4 -> x5, blocking collectives: 53.4 us -> 64.1 us  [swap(): return lax.all_to_all(blocks, 'node', 0, 0, tiled=True)]
    unnamed x44 -> x18, local copies, waits for them, and re-layouts: 8.88 us -> 0.71 us
    all_to_all x1 -> x0, waiting for transfers between devices: 5.8 us -> none  [swap(): return lax.all_to_all(blocks, 'node', 0, 0, tiled=True)]
    all_to_all x1 -> x0, starting transfers between devices: 3.39 us -> none  [swap(): return lax.all_to_all(blocks, 'node', 0, 0, tiled=True)]
    ppermute x1, starting transfers between devices: 1.92 us -> 0.28 us  [shards(): other = lax.ppermute(second, 'node', [(i, i ^ 1) for i in range(nodes)])]
    pallas_call x8, Pallas kernels: 16.6 us -> 15 us  [call(): pl.pallas_call(body, out_shape=[jax.ShapeDtypeStruct(shape, dtype) for sh...]
  transfers between devices with their start and end apart: 8 -> 7, of which waited for: 3 -> 2; matrix products, arithmetic and copies ran while one was open for 0% -> 0% of each run, Pallas kernels for 7% -> 7%
where the time goes in v13:
time: 87.5 us; the launch traced here: 87.2 us
  blocking collectives  64.1 us (73%)
  Pallas kernels  15 us (17%)
  starting transfers between devices  6.2 us (7%)
    all_to_all x5, blocking collectives, swap(): return lax.all_to_all(blocks, 'node', 0, 0, tiled=True)  64.1 us
    pallas_call x8, Pallas kernels, call(): pl.pallas_call(body, out_shape=[jax.ShapeDtypeStruct(shape, dtype) for sh...  15 us
    ppermute x6, starting transfers between devices, gather_shifted(): lax.ppermute(value, 'feat', [(i, (i + k) % count) for i in range(count)])  5.92 us
  transfers between devices with their start and end apart: 7, of which 2 were waited for; matrix products, arithmetic and copies ran while one was open for 0% of the time, Pallas kernels for 7%

profile of v13, /device:TPU:0, one launch (start us, length us, event | category | flops | bytes accessed | tf_op | source)
XLA Modules:
  0.0 87.2 jit_solution(3195589639841887065)
XLA Ops:
  0.6 2.4 %collective-permute-start.2 = (bf16[32,512]{1,0:T(8,128)(2,1)}, bf16[32,512]{1,0:T(8,128)(2,1)S(1)}, u32[]{:S(2)}, u32[]{:S(2)}) collective-permute-start(bf16[32,512]{1,0:T(8,128)(2,1)} %bitcast.15), channel_id=1, source_target_pairs={{0,3},{1,0},{2,1},{3,2},{4,7},{5,4},{6,5},{7,6},{8,11},{9,8},{10,9... | collective-permute-start | bytes 98312 | tf_op jit(solution)/shard_map/ppermute | solution.py:303
  3.1 0.6 collective-permute-start.1
  3.7 0.2 collective-permute-start
  3.9 0.7 copy-done.6
  4.6 2.5 %shard_map.137.a_ref = bf16[512,2048]{1,0:T(8,128)(2,1)S(1)} custom-call(s32[4,16]{1,0:T(4,128)S(1)} %copy-done.6, bf16[4,16,128,128]{3,2,1,0:T(8,128)(2,1)} %tile_val.1), custom_call_target="tpu_custom_call" | custom-call | bytes 4194304 | tf_op jit(solution)/shard_map/pallas_call | solution.py:67
  7.1 0.0 copy-start.8
  7.2 0.3 collective-permute-done.1.refs_2_
  7.5 0.1 collective-permute-done.refs_1_
  7.6 1.0 %shard_map.138 = (bf16[512,512]{1,0:T(8,128)(2,1)S(1)}, bf16[512,128]{1,0:T(8,128)(2,1)S(1)}, bf16[512,128]{1,0:T(8,128)(2,1)S(1)}, bf16[608,256]{1,0:T(8,128)(2,1)S(1)}) custom-call(s32[1,8]{1,0:T(1,128)S(1)} %copy-done.7, s32[8,64]{1,0:T(8,128)S(1)} %bitcast.25, bf16[32,1024]{1,0:T(8,128)(2,1)S(1)} %copy-done.3, bf16[32,1024]{1,0:T(8,128)(2,1)S(1)} %copy-done.4, ...), custom_call_target="tpu_custom_call" | custom-call | flops 67108864 | bytes 524288 | tf_op jit(solution)/shard_map/pallas_call | solution.py:67
  8.6 1.3 %collective-permute-start.5 = (bf16[608,256]{1,0:T(8,128)(2,1)S(1)}, bf16[608,256]{1,0:T(8,128)(2,1)S(1)}, u32[]{:S(2)}, u32[]{:S(2)}) collective-permute-start(bf16[608,256]{1,0:T(8,128)(2,1)S(1)} %get-tuple-element.52.refs_0_), channel_id=1, source_target_pairs={{0,3},{1,0},{2,1},{3,2},{4,7},{5,4},{6,5},{7,6},{8,11},{9,8},{10,9... | collective-permute-start | bytes 933896 | tf_op jit(solution)/shard_map/ppermute | solution.py:303
  9.9 1.4 %collective-permute-start.4 = (bf16[608,256]{1,0:T(8,128)(2,1)S(1)}, bf16[608,256]{1,0:T(8,128)(2,1)S(1)}, u32[]{:S(2)}, u32[]{:S(2)}) collective-permute-start(bf16[608,256]{1,0:T(8,128)(2,1)S(1)} %get-tuple-element.52.refs_0_), channel_id=1, source_target_pairs={{0,2},{1,3},{2,0},{3,1},{4,6},{5,7},{6,4},{7,5},{8,10},{9,11},{10,... | collective-permute-start | bytes 933896 | tf_op jit(solution)/shard_map/ppermute | solution.py:303
  11.3 0.0 collective-permute-start.3
  11.3 13.5 %all_to_all.25 = bf16[8,64,128]{2,1,0:T(8,128)(2,1)S(1)} all-to-all(bf16[8,64,128]{2,1,0:T(8,128)(2,1)S(1)} %bitcast.20), channel_id=1, replica_groups=mesh['node'=8,'feat'=4] {'node'}, dimensions={0} | all-to-all | bytes 262144 | tf_op jit(solution)/shard_map/all_to_all | solution.py:299
  24.8 1.2 %shard_map.139 = (bf16[1024,256]{1,0:T(8,128)(2,1)S(1)}, bf16[512,128]{1,0:T(8,128)(2,1)S(1)}) custom-call(bf16[512,512]{1,0:T(8,128)(2,1)S(1)} %get-tuple-element.40.pick, bf16[512,2048]{1,0:T(8,128)(2,1)S(1)} %shard_map.137.a_ref, bf16[512,128]{1,0:T(8,128)(2,1)S(1)} %get-tuple-element.42.full, bf16[512,128]{1,0:T(8,128)(2,1)S(1)} %bitcast.14), custom_call_target="tpu_custom_call" | custom-call | flops 268435456 | bytes 2097152 | tf_op jit(solution)/shard_map/pallas_call | solution.py:67
  26.0 12.6 %all_to_all.26 = bf16[8,64,128]{2,1,0:T(8,128)(2,1)S(1)} all-to-all(bf16[8,64,128]{2,1,0:T(8,128)(2,1)S(1)} %bitcast.21), channel_id=1, replica_groups=mesh['node'=8,'feat'=4] {'node'}, dimensions={0} | all-to-all | bytes 262144 | tf_op jit(solution)/shard_map/all_to_all | solution.py:299
  38.6 6.6 %shard_map.140 = (bf16[176,512]{1,0:T(8,128)(2,1)S(1)}, f32[4,512,256]{2,1,0:T(8,128)S(1)}, bf16[8,96,128]{2,1,0:T(8,128)(2,1)S(1)}, f32[2,176,256]{2,1,0:T(8,128)S(1)}) custom-call(s32[1]{0:T(128)} %bitcast.3.ids, bf16[512,2048]{1,0:T(8,128)(2,1)S(1)} %shard_map.137.a_ref, bf16[1024,256]{1,0:T(8,128)(2,1)S(1)} %get-tuple-element.50.state, ...), custom_call_target="tpu_custom_call" | custom-call | flops 4294967296 | bytes 8388608 | tf_op jit(solution)/shard_map/pallas_call | solution.py:67
  45.2 0.3 collective-permute-start.6
  45.5 10.7 %all_to_all.27.landed = bf16[8,96,128]{2,1,0:T(8,128)(2,1)S(1)} all-to-all(bf16[8,96,128]{2,1,0:T(8,128)(2,1)S(1)} %get-tuple-element.58), channel_id=1, replica_groups=mesh['node'=8,'feat'=4] {'node'}, dimensions={0} | all-to-all | bytes 393216 | tf_op jit(solution)/shard_map/all_to_all | solution.py:299
  56.1 2.8 %shard_map.141.grads = f32[8,64,128]{2,1,0:T(8,128)S(1)} custom-call(s32[1]{0:T(128)} %bitcast.3.ids, bf16[176,512]{1,0:T(8,128)(2,1)S(1)} %get-tuple-element.56.turned, bf16[512,512]{1,0:T(8,128)(2,1)S(1)} %get-tuple-element.40.pick, bf16[512,2048]{1,0:T(8,128)(2,1)S(1)} %shard_map.137.a_ref, f32[4,512,256]{2,1,0:T(8,128)S(1)} %get-tuple-element.57.slope, ...), custom_call_target="tpu_custom_call" | custom-call | tf_op jit(solution)/shard_map/pallas_call | solution.py:67
  59.0 0.1 shard_map.142
  59.0 12.4 %all_to_all.28.pieces = f32[8,112,128]{2,1,0:T(8,128)S(1)} all-to-all(f32[8,112,128]{2,1,0:T(8,128)S(1)} %shard_map.142), channel_id=1, replica_groups=mesh['node'=8,'feat'=4] {'node'}, dimensions={0} | all-to-all | bytes 917504 | tf_op jit(solution)/shard_map/all_to_all | solution.py:299
  71.4 0.1 shard_map.143
  71.5 14.9 %all_to_all.29.pieces = f32[8,152,128]{2,1,0:T(8,128)S(1)} all-to-all(f32[8,152,128]{2,1,0:T(8,128)S(1)} %shard_map.143), channel_id=1, replica_groups=mesh['node'=8,'feat'=4] {'node'}, dimensions={0} | all-to-all | bytes 1245184 | tf_op jit(solution)/shard_map/all_to_all | solution.py:299
  86.4 0.8 shard_map.144
  (21 shorter events, 0.0 us)
Async XLA Ops:
  0.6 6.5 %collective-permute-start.2 = (bf16[32,512]{1,0:T(8,128)(2,1)}, bf16[32,512]{1,0:T(8,128)(2,1)S(1)}, u32[]{:S(2)}, u32[]{:S(2)}) collective-permute-start(bf16[32,512]{1,0:T(8,128)(2,1)} %bitcast.15), channel_id=1, source_target_pairs={{0,3},{1,0},{2,1},{3,2},{4,7},{5,4},{6,5},{7,6},{8,11},{9,8},{10,9... | collective-permute-start | bytes 98312 | tf_op jit(solution)/shard_map/ppermute | solution.py:303
  3.1 4.4 %collective-permute-start.1 = (bf16[32,512]{1,0:T(8,128)(2,1)}, bf16[32,512]{1,0:T(8,128)(2,1)S(1)}, u32[]{:S(2)}, u32[]{:S(2)}) collective-permute-start(bf16[32,512]{1,0:T(8,128)(2,1)} %bitcast.16), channel_id=1, source_target_pairs={{0,2},{1,3},{2,0},{3,1},{4,6},{5,7},{6,4},{7,5},{8,10},{9,11},{10,... | collective-permute-start | bytes 98312 | tf_op jit(solution)/shard_map/ppermute | solution.py:303
  3.7 3.8 %collective-permute-start = (bf16[32,512]{1,0:T(8,128)(2,1)}, bf16[32,512]{1,0:T(8,128)(2,1)S(1)}, u32[]{:S(2)}, u32[]{:S(2)}) collective-permute-start(bf16[32,512]{1,0:T(8,128)(2,1)} %bitcast.17), channel_id=1, source_target_pairs={{0,1},{1,2},{2,3},{3,0},{4,5},{5,6},{6,7},{7,4},{8,9},{9,10},{10,1... | collective-permute-start | bytes 98312 | tf_op jit(solution)/shard_map/ppermute | solution.py:303
  3.9 0.7 copy-start.6
  4.6 3.0 %copy-start = (bf16[512,32]{0,1:T(8,128)(2,1)S(1)}, bf16[512,32]{0,1:T(8,128)(2,1)}, u32[]{:S(2)}) copy-start(bf16[512,32]{0,1:T(8,128)(2,1)} %param.10) | copy-start | bytes 98308
  4.6 3.0 %copy-start.1 = (bf16[256,172]{0,1:T(8,128)(2,1)S(1)}, bf16[256,172]{0,1:T(8,128)(2,1)}, u32[]{:S(2)}) copy-start(bf16[256,172]{0,1:T(8,128)(2,1)} %param.18) | copy-start | bytes 264196
  4.6 3.0 %copy-start.2 = (bf16[256,172]{0,1:T(8,128)(2,1)S(1)}, bf16[256,172]{0,1:T(8,128)(2,1)}, u32[]{:S(2)}) copy-start(bf16[256,172]{0,1:T(8,128)(2,1)} %param.19) | copy-start | bytes 264196
  4.6 3.0 %copy-start.3 = (bf16[32,1024]{1,0:T(8,128)(2,1)S(1)}, bf16[32,1024]{1,0:T(8,128)(2,1)}, u32[]{:S(2)}) copy-start(bf16[32,1024]{1,0:T(8,128)(2,1)} %w_self1.1) | copy-start | bytes 196612
  4.6 3.0 %copy-start.4 = (bf16[32,1024]{1,0:T(8,128)(2,1)S(1)}, bf16[32,1024]{1,0:T(8,128)(2,1)}, u32[]{:S(2)}) copy-start(bf16[32,1024]{1,0:T(8,128)(2,1)} %w_neigh1.1) | copy-start | bytes 196612
  4.6 3.0 %copy-start.5 = (s32[1,8,64]{2,1,0:T(8,128)S(1)}, s32[1,8,64]{2,1,0:T(8,128)}, u32[]{:S(2)}) copy-start(s32[1,8,64]{2,1,0:T(8,128)} %param.11) | copy-start | bytes 6148
  4.6 3.0 %copy-start.7 = (s32[1,8]{1,0:T(1,128)S(1)}, s32[1,8]{1,0:T(1,128)}, u32[]{:S(2)}) copy-start(s32[1,8]{1,0:T(1,128)} %count.1) | copy-start | bytes 100
  7.1 31.5 %copy-start.8 = (s32[512]{0:T(512)S(1)}, s32[512]{0:T(512)}, u32[]{:S(2)}) copy-start(s32[512]{0:T(512)} %param.15) | copy-start | bytes 6148
  8.6 17.4 %collective-permute-start.5 = (bf16[608,256]{1,0:T(8,128)(2,1)S(1)}, bf16[608,256]{1,0:T(8,128)(2,1)S(1)}, u32[]{:S(2)}, u32[]{:S(2)}) collective-permute-start(bf16[608,256]{1,0:T(8,128)(2,1)S(1)} %get-tuple-element.52.refs_0_), channel_id=1, source_target_pairs={{0,3},{1,0},{2,1},{3,2},{4,7},{5,4},{6,5},{7,6},{8,11},{9,8},{10,9... | collective-permute-start | bytes 933896 | tf_op jit(solution)/shard_map/ppermute | solution.py:303
  9.9 16.1 %collective-permute-start.4 = (bf16[608,256]{1,0:T(8,128)(2,1)S(1)}, bf16[608,256]{1,0:T(8,128)(2,1)S(1)}, u32[]{:S(2)}, u32[]{:S(2)}) collective-permute-start(bf16[608,256]{1,0:T(8,128)(2,1)S(1)} %get-tuple-element.52.refs_0_), channel_id=1, source_target_pairs={{0,2},{1,3},{2,0},{3,1},{4,6},{5,7},{6,4},{7,5},{8,10},{9,11},{10,... | collective-permute-start | bytes 933896 | tf_op jit(solution)/shard_map/ppermute | solution.py:303
  11.3 14.7 %collective-permute-start.3 = (bf16[608,256]{1,0:T(8,128)(2,1)S(1)}, bf16[608,256]{1,0:T(8,128)(2,1)S(1)}, u32[]{:S(2)}, u32[]{:S(2)}) collective-permute-start(bf16[608,256]{1,0:T(8,128)(2,1)S(1)} %get-tuple-element.52.refs_0_), channel_id=1, source_target_pairs={{0,1},{1,2},{2,3},{3,0},{4,5},{5,6},{6,7},{7,4},{8,9},{9,10},{10,1... | collective-permute-start | bytes 933896 | tf_op jit(solution)/shard_map/ppermute | solution.py:303
  45.2 13.8 %collective-permute-start.6 = (f32[2,176,256]{2,1,0:T(8,128)S(1)}, f32[2,176,256]{2,1,0:T(8,128)S(1)}, u32[]{:S(2)}, u32[]{:S(2)}) collective-permute-start(f32[2,176,256]{2,1,0:T(8,128)S(1)} %get-tuple-element.59.second), channel_id=1, source_target_pairs={{0,4},{4,0},{8,12},{12,8},{16,20},{20,16},{24,28},{28,24},{1,5},{5... | collective-permute-start | bytes 1081352 | tf_op jit(solution)/shard_map/ppermute | solution.py:364

commit v14 on v13

--- a/solution.py
+++ b/solution.py
@@ -18,10 +18,6 @@
 
 def mm(a, b):
     return lax.dot_general(a, b, (((1,), (0,)), ((), ())), preferred_element_type=F32)
-
-
-def mm_nt(a, b):
-    return lax.dot_general(a, b, (((1,), (1,)), ((), ())), preferred_element_type=F32)
 
 
 def mm_tn(a, b):
@@ -152,7 +148,7 @@
     pad = turned.shape[0]
     slots = halo // packed.shape[0]
     near = state[:own, :]
-    total = jnp.zeros((pad, own), F32)
+    total = jnp.zeros((own, pad), F32)
     for k in range(groups):
         group = lax.rem(ids[0] + groups - k, groups)
         begin = [pl.multiple_of(2 * step * group + part * step, step) for part in (0, 1)]
@@ -175,7 +171,9 @@
         rounded = held.astype(BF16)
         if k == 0:
             mine, agg_mine = out, rounded
-        total = total + mm_nt(weights[k][pl.ds(base, pad), :], out) + mm_nt(weights[k][pl.ds(base + pad, pad), :], rounded)
+        w_self, w_neigh = weights[k][pl.ds(base, pad), :].T, weights[k][pl.ds(base + pad, pad), :].T
+        total = total + mm(jnp.concatenate([out, rounded], axis=1), jnp.concatenate([w_self, w_neigh], axis=0))
+    total = total.T
     class_id = lax.broadcasted_iota(jnp.int32, total.shape, 0)
     real = class_id < class_count
     top = jnp.max(jnp.where(real, total, -jnp.inf), axis=0, keepdims=True)

time: 87.5 us -> 86.2 us (0.985)
  Pallas kernels: 15 us -> 13.7 us
    pallas_call x8, Pallas kernels: 15 us -> 13.7 us  [call(): pl.pallas_call(body, out_shape=[jax.ShapeDtypeStruct(shape, dtype) for sh...]
  transfers between devices with their start and end apart: 7 -> 7, of which waited for: 2 -> 2; matrix products, arithmetic and copies ran while one was open for 0% -> 0% of each run, Pallas kernels for 7% -> 8%
where the time goes in v14:
time: 86.2 us; the launch traced here: 85.9 us
  blocking collectives  64.1 us (74%)
  Pallas kernels  13.7 us (16%)
  starting transfers between devices  6.2 us (7%)
    all_to_all x5, blocking collectives, swap(): return lax.all_to_all(blocks, 'node', 0, 0, tiled=True)  64.1 us
    pallas_call x8, Pallas kernels, call(): pl.pallas_call(body, out_shape=[jax.ShapeDtypeStruct(shape, dtype) for sh...  13.7 us
    ppermute x6, starting transfers between devices, gather_shifted(): lax.ppermute(value, 'feat', [(i, (i + k) % count) for i in range(count)])  5.92 us
  transfers between devices with their start and end apart: 7, of which 2 were waited for; matrix products, arithmetic and copies ran while one was open for 0% of the time, Pallas kernels for 8%

profile of v14, /device:TPU:0, one launch (start us, length us, event | category | flops | bytes accessed | tf_op | source)
XLA Modules:
  0.0 85.9 jit_solution(2641550592164936276)
XLA Ops:
  0.6 2.4 %collective-permute-start.2 = (bf16[32,512]{1,0:T(8,128)(2,1)}, bf16[32,512]{1,0:T(8,128)(2,1)S(1)}, u32[]{:S(2)}, u32[]{:S(2)}) collective-permute-start(bf16[32,512]{1,0:T(8,128)(2,1)} %bitcast.15), channel_id=1, source_target_pairs={{0,3},{1,0},{2,1},{3,2},{4,7},{5,4},{6,5},{7,6},{8,11},{9,8},{10,9... | collective-permute-start | bytes 98312 | tf_op jit(solution)/shard_map/ppermute | solution.py:301
  3.1 0.6 collective-permute-start.1
  3.7 0.2 collective-permute-start
  3.9 0.7 copy-done.6
  4.6 2.5 %shard_map.137.a_ref = bf16[512,2048]{1,0:T(8,128)(2,1)S(1)} custom-call(s32[4,16]{1,0:T(4,128)S(1)} %copy-done.6, bf16[4,16,128,128]{3,2,1,0:T(8,128)(2,1)} %tile_val.1), custom_call_target="tpu_custom_call" | custom-call | bytes 4194304 | tf_op jit(solution)/shard_map/pallas_call | solution.py:63
  7.1 0.0 copy-start.8
  7.2 0.0 collective-permute-done.2.refs_3_
  7.2 0.3 collective-permute-done.1.refs_2_
  7.5 0.1 collective-permute-done.refs_1_
  7.6 1.0 %shard_map.138 = (bf16[512,512]{1,0:T(8,128)(2,1)S(1)}, bf16[512,128]{1,0:T(8,128)(2,1)S(1)}, bf16[512,128]{1,0:T(8,128)(2,1)S(1)}, bf16[608,256]{1,0:T(8,128)(2,1)S(1)}) custom-call(s32[1,8]{1,0:T(1,128)S(1)} %copy-done.7, s32[8,64]{1,0:T(8,128)S(1)} %bitcast.25, bf16[32,1024]{1,0:T(8,128)(2,1)S(1)} %copy-done.3, bf16[32,1024]{1,0:T(8,128)(2,1)S(1)} %copy-done.4, ...), custom_call_target="tpu_custom_call" | custom-call | flops 67108864 | bytes 524288 | tf_op jit(solution)/shard_map/pallas_call | solution.py:63
  8.6 1.3 %collective-permute-start.5 = (bf16[608,256]{1,0:T(8,128)(2,1)S(1)}, bf16[608,256]{1,0:T(8,128)(2,1)S(1)}, u32[]{:S(2)}, u32[]{:S(2)}) collective-permute-start(bf16[608,256]{1,0:T(8,128)(2,1)S(1)} %get-tuple-element.52.refs_0_), channel_id=1, source_target_pairs={{0,3},{1,0},{2,1},{3,2},{4,7},{5,4},{6,5},{7,6},{8,11},{9,8},{10,9... | collective-permute-start | bytes 933896 | tf_op jit(solution)/shard_map/ppermute | solution.py:301
  9.9 1.4 %collective-permute-start.4 = (bf16[608,256]{1,0:T(8,128)(2,1)S(1)}, bf16[608,256]{1,0:T(8,128)(2,1)S(1)}, u32[]{:S(2)}, u32[]{:S(2)}) collective-permute-start(bf16[608,256]{1,0:T(8,128)(2,1)S(1)} %get-tuple-element.52.refs_0_), channel_id=1, source_target_pairs={{0,2},{1,3},{2,0},{3,1},{4,6},{5,7},{6,4},{7,5},{8,10},{9,11},{10,... | collective-permute-start | bytes 933896 | tf_op jit(solution)/shard_map/ppermute | solution.py:301
  11.3 13.5 %all_to_all.25 = bf16[8,64,128]{2,1,0:T(8,128)(2,1)S(1)} all-to-all(bf16[8,64,128]{2,1,0:T(8,128)(2,1)S(1)} %bitcast.20), channel_id=1, replica_groups=mesh['node'=8,'feat'=4] {'node'}, dimensions={0} | all-to-all | bytes 262144 | tf_op jit(solution)/shard_map/all_to_all | solution.py:297
  24.8 1.2 %shard_map.139 = (bf16[1024,256]{1,0:T(8,128)(2,1)S(1)}, bf16[512,128]{1,0:T(8,128)(2,1)S(1)}) custom-call(bf16[512,512]{1,0:T(8,128)(2,1)S(1)} %get-tuple-element.40.pick, bf16[512,2048]{1,0:T(8,128)(2,1)S(1)} %shard_map.137.a_ref, bf16[512,128]{1,0:T(8,128)(2,1)S(1)} %get-tuple-element.42.full, bf16[512,128]{1,0:T(8,128)(2,1)S(1)} %bitcast.14), custom_call_target="tpu_custom_call" | custom-call | flops 268435456 | bytes 2097152 | tf_op jit(solution)/shard_map/pallas_call | solution.py:63
  26.0 12.6 %all_to_all.26 = bf16[8,64,128]{2,1,0:T(8,128)(2,1)S(1)} all-to-all(bf16[8,64,128]{2,1,0:T(8,128)(2,1)S(1)} %bitcast.21), channel_id=1, replica_groups=mesh['node'=8,'feat'=4] {'node'}, dimensions={0} | all-to-all | bytes 262144 | tf_op jit(solution)/shard_map/all_to_all | solution.py:297
  38.6 5.2 %shard_map.140 = (bf16[176,512]{1,0:T(8,128)(2,1)S(1)}, f32[4,512,256]{2,1,0:T(8,128)S(1)}, bf16[8,96,128]{2,1,0:T(8,128)(2,1)S(1)}, f32[2,176,256]{2,1,0:T(8,128)S(1)}) custom-call(s32[1]{0:T(128)} %bitcast.3.ids, bf16[512,2048]{1,0:T(8,128)(2,1)S(1)} %shard_map.137.a_ref, bf16[1024,256]{1,0:T(8,128)(2,1)S(1)} %get-tuple-element.50.state, ...), custom_call_target="tpu_custom_call" | custom-call | flops 4294967296 | bytes 8388608 | tf_op jit(solution)/shard_map/pallas_call | solution.py:63
  43.9 0.3 collective-permute-start.6
  44.2 10.7 %all_to_all.27.landed = bf16[8,96,128]{2,1,0:T(8,128)(2,1)S(1)} all-to-all(bf16[8,96,128]{2,1,0:T(8,128)(2,1)S(1)} %get-tuple-element.58), channel_id=1, replica_groups=mesh['node'=8,'feat'=4] {'node'}, dimensions={0} | all-to-all | bytes 393216 | tf_op jit(solution)/shard_map/all_to_all | solution.py:297
  54.8 2.8 %shard_map.141.grads = f32[8,64,128]{2,1,0:T(8,128)S(1)} custom-call(s32[1]{0:T(128)} %bitcast.3.ids, bf16[176,512]{1,0:T(8,128)(2,1)S(1)} %get-tuple-element.56.turned, bf16[512,512]{1,0:T(8,128)(2,1)S(1)} %get-tuple-element.40.pick, bf16[512,2048]{1,0:T(8,128)(2,1)S(1)} %shard_map.137.a_ref, f32[4,512,256]{2,1,0:T(8,128)S(1)} %get-tuple-element.57.slope, ...), custom_call_target="tpu_custom_call" | custom-call | tf_op jit(solution)/shard_map/pallas_call | solution.py:63
  57.7 0.1 shard_map.142
  57.7 12.4 %all_to_all.28.pieces = f32[8,112,128]{2,1,0:T(8,128)S(1)} all-to-all(f32[8,112,128]{2,1,0:T(8,128)S(1)} %shard_map.142), channel_id=1, replica_groups=mesh['node'=8,'feat'=4] {'node'}, dimensions={0} | all-to-all | bytes 917504 | tf_op jit(solution)/shard_map/all_to_all | solution.py:297
  70.1 0.1 shard_map.143
  70.2 14.9 %all_to_all.29.pieces = f32[8,152,128]{2,1,0:T(8,128)S(1)} all-to-all(f32[8,152,128]{2,1,0:T(8,128)S(1)} %shard_map.143), channel_id=1, replica_groups=mesh['node'=8,'feat'=4] {'node'}, dimensions={0} | all-to-all | bytes 1245184 | tf_op jit(solution)/shard_map/all_to_all | solution.py:297
  85.1 0.8 shard_map.144
  (21 shorter events, 0.0 us)
Async XLA Ops:
  0.6 6.5 %collective-permute-start.2 = (bf16[32,512]{1,0:T(8,128)(2,1)}, bf16[32,512]{1,0:T(8,128)(2,1)S(1)}, u32[]{:S(2)}, u32[]{:S(2)}) collective-permute-start(bf16[32,512]{1,0:T(8,128)(2,1)} %bitcast.15), channel_id=1, source_target_pairs={{0,3},{1,0},{2,1},{3,2},{4,7},{5,4},{6,5},{7,6},{8,11},{9,8},{10,9... | collective-permute-start | bytes 98312 | tf_op jit(solution)/shard_map/ppermute | solution.py:301
  3.1 4.4 %collective-permute-start.1 = (bf16[32,512]{1,0:T(8,128)(2,1)}, bf16[32,512]{1,0:T(8,128)(2,1)S(1)}, u32[]{:S(2)}, u32[]{:S(2)}) collective-permute-start(bf16[32,512]{1,0:T(8,128)(2,1)} %bitcast.16), channel_id=1, source_target_pairs={{0,2},{1,3},{2,0},{3,1},{4,6},{5,7},{6,4},{7,5},{8,10},{9,11},{10,... | collective-permute-start | bytes 98312 | tf_op jit(solution)/shard_map/ppermute | solution.py:301
  3.7 3.8 %collective-permute-start = (bf16[32,512]{1,0:T(8,128)(2,1)}, bf16[32,512]{1,0:T(8,128)(2,1)S(1)}, u32[]{:S(2)}, u32[]{:S(2)}) collective-permute-start(bf16[32,512]{1,0:T(8,128)(2,1)} %bitcast.17), channel_id=1, source_target_pairs={{0,1},{1,2},{2,3},{3,0},{4,5},{5,6},{6,7},{7,4},{8,9},{9,10},{10,1... | collective-permute-start | bytes 98312 | tf_op jit(solution)/shard_map/ppermute | solution.py:301
  3.9 0.7 copy-start.6
  4.6 3.0 %copy-start = (bf16[512,32]{0,1:T(8,128)(2,1)S(1)}, bf16[512,32]{0,1:T(8,128)(2,1)}, u32[]{:S(2)}) copy-start(bf16[512,32]{0,1:T(8,128)(2,1)} %param.10) | copy-start | bytes 98308
  4.6 3.0 %copy-start.1 = (bf16[256,172]{0,1:T(8,128)(2,1)S(1)}, bf16[256,172]{0,1:T(8,128)(2,1)}, u32[]{:S(2)}) copy-start(bf16[256,172]{0,1:T(8,128)(2,1)} %param.18) | copy-start | bytes 264196
  4.6 3.0 %copy-start.2 = (bf16[256,172]{0,1:T(8,128)(2,1)S(1)}, bf16[256,172]{0,1:T(8,128)(2,1)}, u32[]{:S(2)}) copy-start(bf16[256,172]{0,1:T(8,128)(2,1)} %param.19) | copy-start | bytes 264196
  4.6 3.0 %copy-start.3 = (bf16[32,1024]{1,0:T(8,128)(2,1)S(1)}, bf16[32,1024]{1,0:T(8,128)(2,1)}, u32[]{:S(2)}) copy-start(bf16[32,1024]{1,0:T(8,128)(2,1)} %w_self1.1) | copy-start | bytes 196612
  4.6 3.0 %copy-start.4 = (bf16[32,1024]{1,0:T(8,128)(2,1)S(1)}, bf16[32,1024]{1,0:T(8,128)(2,1)}, u32[]{:S(2)}) copy-start(bf16[32,1024]{1,0:T(8,128)(2,1)} %w_neigh1.1) | copy-start | bytes 196612
  4.6 3.0 %copy-start.5 = (s32[1,8,64]{2,1,0:T(8,128)S(1)}, s32[1,8,64]{2,1,0:T(8,128)}, u32[]{:S(2)}) copy-start(s32[1,8,64]{2,1,0:T(8,128)} %param.11) | copy-start | bytes 6148
  4.6 3.0 %copy-start.7 = (s32[1,8]{1,0:T(1,128)S(1)}, s32[1,8]{1,0:T(1,128)}, u32[]{:S(2)}) copy-start(s32[1,8]{1,0:T(1,128)} %count.1) | copy-start | bytes 100
  7.1 31.5 %copy-start.8 = (s32[512]{0:T(512)S(1)}, s32[512]{0:T(512)}, u32[]{:S(2)}) copy-start(s32[512]{0:T(512)} %param.15) | copy-start | bytes 6148
  8.6 17.4 %collective-permute-start.5 = (bf16[608,256]{1,0:T(8,128)(2,1)S(1)}, bf16[608,256]{1,0:T(8,128)(2,1)S(1)}, u32[]{:S(2)}, u32[]{:S(2)}) collective-permute-start(bf16[608,256]{1,0:T(8,128)(2,1)S(1)} %get-tuple-element.52.refs_0_), channel_id=1, source_target_pairs={{0,3},{1,0},{2,1},{3,2},{4,7},{5,4},{6,5},{7,6},{8,11},{9,8},{10,9... | collective-permute-start | bytes 933896 | tf_op jit(solution)/shard_map/ppermute | solution.py:301
  9.9 16.1 %collective-permute-start.4 = (bf16[608,256]{1,0:T(8,128)(2,1)S(1)}, bf16[608,256]{1,0:T(8,128)(2,1)S(1)}, u32[]{:S(2)}, u32[]{:S(2)}) collective-permute-start(bf16[608,256]{1,0:T(8,128)(2,1)S(1)} %get-tuple-element.52.refs_0_), channel_id=1, source_target_pairs={{0,2},{1,3},{2,0},{3,1},{4,6},{5,7},{6,4},{7,5},{8,10},{9,11},{10,... | collective-permute-start | bytes 933896 | tf_op jit(solution)/shard_map/ppermute | solution.py:301
  11.3 14.7 %collective-permute-start.3 = (bf16[608,256]{1,0:T(8,128)(2,1)S(1)}, bf16[608,256]{1,0:T(8,128)(2,1)S(1)}, u32[]{:S(2)}, u32[]{:S(2)}) collective-permute-start(bf16[608,256]{1,0:T(8,128)(2,1)S(1)} %get-tuple-element.52.refs_0_), channel_id=1, source_target_pairs={{0,1},{1,2},{2,3},{3,0},{4,5},{5,6},{6,7},{7,4},{8,9},{9,10},{10,1... | collective-permute-start | bytes 933896 | tf_op jit(solution)/shard_map/ppermute | solution.py:301
  43.9 13.8 %collective-permute-start.6 = (f32[2,176,256]{2,1,0:T(8,128)S(1)}, f32[2,176,256]{2,1,0:T(8,128)S(1)}, u32[]{:S(2)}, u32[]{:S(2)}) collective-permute-start(f32[2,176,256]{2,1,0:T(8,128)S(1)} %get-tuple-element.59.second), channel_id=1, source_target_pairs={{0,4},{4,0},{8,12},{12,8},{16,20},{20,16},{24,28},{28,24},{1,5},{5... | collective-permute-start | bytes 1081352 | tf_op jit(solution)/shard_map/ppermute | solution.py:362

commit v15 on v14

--- a/solution.py
+++ b/solution.py
@@ -30,12 +30,9 @@
 
 
 def spread(a, rows):
-    own = a.shape[0]
-    parts = []
-    for c in range(rows.shape[0] // own):
-        part = rows[c * own : (c + 1) * own]
-        parts += [part, part]
-    return mm(a, jnp.concatenate(parts, axis=0))
+    both = mm(a, rows)
+    half = both.shape[0] // 2
+    return both[:half] + both[half:]
 
 
 def activate(v, with_slope):
@@ -92,10 +89,9 @@
             return 0
 
         lax.fori_loop(0, per_block, add, 0)
-        for c in range(dense.shape[1] // own):
-            high, low = halves(dense[rows, pl.ds(c * own, own)])
-            a_ref[rows, pl.ds(2 * c * own, own)] = high
-            a_ref[rows, pl.ds((2 * c + 1) * own, own)] = low
+        high, low = halves(dense[rows, :])
+        a_ref[rows, :] = high
+        a_ref[pl.ds(own + b * BLOCK, BLOCK), :] = low
 
 
 def pack_kernel(groups, count, send_rows, w_self1, w_neigh1, w_self2, w_neigh2, *refs):
@@ -126,7 +122,7 @@
 
 def first_kernel(pick, a_ref, full, source, state, packed):
     own, cols = full.shape
-    total = spread(a_ref[:, : 2 * own], full[...]) + spread(a_ref[:, 2 * own :], source[...])
+    total = spread(a_ref[:, :own], full[...]) + spread(a_ref[:, own:], source[...])
     agg = total.astype(BF16)
     packed[...] = mm(pick[...], agg).astype(BF16)
     state[:own, :cols] = full[...]
@@ -162,12 +158,12 @@
 
             def one(r, held, w_one=w_one):
                 rows = pl.ds(pl.multiple_of(r * own, own), own)
-                srcs = pl.ds(pl.multiple_of(2 * (r + 1) * own, own), 2 * own)
+                srcs = pl.ds(pl.multiple_of((r + 1) * own, own), own)
                 lower = pl.ds(pl.multiple_of((r + 1) * own, own), own)
                 both = jnp.concatenate([state[lower, :cols], landed[rows, :]], axis=1)
                 return held + spread(a_ref[:, srcs], activate(mm(both, w_one), False))
 
-            held = lax.fori_loop(0, halo // own, one, spread(a_ref[:, : 2 * own], out))
+            held = lax.fori_loop(0, halo // own, one, spread(a_ref[:, :own], out))
         rounded = held.astype(BF16)
         if k == 0:
             mine, agg_mine = out, rounded
@@ -190,7 +186,7 @@
     second[1] = mm(turned[...], agg_mine)
     per_chunk = own // slots
     for c in range(halo // own):
-        back = mm(turned[...], a_ref[:, pl.ds(2 * (c + 1) * own, own)]).T.astype(BF16)
+        back = mm(turned[...], a_ref[:own, pl.ds((c + 1) * own, own)]).T.astype(BF16)
         for d in range(per_chunk):
             put_message(packed, c * per_chunk + d, back[d * slots : (d + 1) * slots])
 
@@ -232,7 +228,7 @@
     base = 2 * step * groups
     for d in range(landed.shape[0]):
         take_message(landed, d, rows)
-    high, low = halves(mm(turned[...], a_ref[:, :own]) + mm_tn(rows[...], pick[...]))
+    high, low = halves(mm(turned[...], a_ref[:own, :own]) + mm_tn(rows[...], pick[...]))
     wide = jnp.concatenate([turned[...], high, low], axis=0).T
     cols = state.shape[1] // 2
     left = jnp.concatenate([features[...], state[:own, cols:].T[:step]], axis=0)
@@ -323,7 +319,7 @@
     turned_all = gather_shifted(turned, groups)
     (a_mat,) = call(
         prepare_kernel,
-        [((own, 2 * total_src), BF16)],
+        [((2 * own, total_src), BF16)],
         (tile_src, tile_val),
         [(tile_val.shape, BF16), ((own, total_src), F32)],
         copies=blocks + 1,

time: 86.2 us -> 86.2 us (level)
  no operation moved by 1% of the time
where the time goes in v15:
time: 86.2 us; the launch traced here: 85.9 us
  blocking collectives  64.1 us (74%)
  Pallas kernels  13.7 us (16%)
  starting transfers between devices  6.23 us (7%)
    all_to_all x5, blocking collectives, swap(): return lax.all_to_all(blocks, 'node', 0, 0, tiled=True)  64.1 us
    pallas_call x8, Pallas kernels, call(): pl.pallas_call(body, out_shape=[jax.ShapeDtypeStruct(shape, dtype) for sh...  13.7 us
    ppermute x6, starting transfers between devices, gather_shifted(): lax.ppermute(value, 'feat', [(i, (i + k) % count) for i in range(count)])  5.96 us
  transfers between devices with their start and end apart: 7, of which 2 were waited for; matrix products, arithmetic and copies ran while one was open for 0% of the time, Pallas kernels for 8%

profile of v15, /device:TPU:0, one launch (start us, length us, event | category | flops | bytes accessed | tf_op | source)
XLA Modules:
  0.0 85.9 jit_solution(3046387187806604689)
XLA Ops:
  0.6 2.4 %collective-permute-start.2 = (bf16[32,512]{1,0:T(8,128)(2,1)}, bf16[32,512]{1,0:T(8,128)(2,1)S(1)}, u32[]{:S(2)}, u32[]{:S(2)}) collective-permute-start(bf16[32,512]{1,0:T(8,128)(2,1)} %bitcast.15), channel_id=1, source_target_pairs={{0,3},{1,0},{2,1},{3,2},{4,7},{5,4},{6,5},{7,6},{8,11},{9,8},{10,9... | collective-permute-start | bytes 98312 | tf_op jit(solution)/shard_map/ppermute | solution.py:297
  3.1 0.6 collective-permute-start.1
  3.7 0.2 collective-permute-start
  3.9 0.7 copy-done.6
  4.6 2.6 %shard_map.137.a_ref = bf16[1024,1024]{1,0:T(8,128)(2,1)S(1)} custom-call(s32[4,16]{1,0:T(4,128)S(1)} %copy-done.6, bf16[4,16,128,128]{3,2,1,0:T(8,128)(2,1)} %tile_val.1), custom_call_target="tpu_custom_call" | custom-call | bytes 4194304 | tf_op jit(solution)/shard_map/pallas_call | solution.py:60
  7.2 0.0 copy-start.8
  7.2 0.3 collective-permute-done.1.refs_2_
  7.5 0.1 collective-permute-done.refs_1_
  7.6 1.0 %shard_map.138 = (bf16[512,512]{1,0:T(8,128)(2,1)S(1)}, bf16[512,128]{1,0:T(8,128)(2,1)S(1)}, bf16[512,128]{1,0:T(8,128)(2,1)S(1)}, bf16[608,256]{1,0:T(8,128)(2,1)S(1)}) custom-call(s32[1,8]{1,0:T(1,128)S(1)} %copy-done.7, s32[8,64]{1,0:T(8,128)S(1)} %bitcast.25, bf16[32,1024]{1,0:T(8,128)(2,1)S(1)} %copy-done.3, bf16[32,1024]{1,0:T(8,128)(2,1)S(1)} %copy-done.4, ...), custom_call_target="tpu_custom_call" | custom-call | flops 67108864 | bytes 524288 | tf_op jit(solution)/shard_map/pallas_call | solution.py:60
  8.6 1.3 %collective-permute-start.5 = (bf16[608,256]{1,0:T(8,128)(2,1)S(1)}, bf16[608,256]{1,0:T(8,128)(2,1)S(1)}, u32[]{:S(2)}, u32[]{:S(2)}) collective-permute-start(bf16[608,256]{1,0:T(8,128)(2,1)S(1)} %get-tuple-element.52.refs_0_), channel_id=1, source_target_pairs={{0,3},{1,0},{2,1},{3,2},{4,7},{5,4},{6,5},{7,6},{8,11},{9,8},{10,9... | collective-permute-start | bytes 933896 | tf_op jit(solution)/shard_map/ppermute | solution.py:297
  9.9 1.4 %collective-permute-start.4 = (bf16[608,256]{1,0:T(8,128)(2,1)S(1)}, bf16[608,256]{1,0:T(8,128)(2,1)S(1)}, u32[]{:S(2)}, u32[]{:S(2)}) collective-permute-start(bf16[608,256]{1,0:T(8,128)(2,1)S(1)} %get-tuple-element.52.refs_0_), channel_id=1, source_target_pairs={{0,2},{1,3},{2,0},{3,1},{4,6},{5,7},{6,4},{7,5},{8,10},{9,11},{10,... | collective-permute-start | bytes 933896 | tf_op jit(solution)/shard_map/ppermute | solution.py:297
  11.3 0.0 collective-permute-start.3
  11.3 13.5 %all_to_all.25 = bf16[8,64,128]{2,1,0:T(8,128)(2,1)S(1)} all-to-all(bf16[8,64,128]{2,1,0:T(8,128)(2,1)S(1)} %bitcast.20), channel_id=1, replica_groups=mesh['node'=8,'feat'=4] {'node'}, dimensions={0} | all-to-all | bytes 262144 | tf_op jit(solution)/shard_map/all_to_all | solution.py:293
  24.8 1.2 %shard_map.139 = (bf16[1024,256]{1,0:T(8,128)(2,1)S(1)}, bf16[512,128]{1,0:T(8,128)(2,1)S(1)}) custom-call(bf16[512,512]{1,0:T(8,128)(2,1)S(1)} %get-tuple-element.40.pick, bf16[1024,1024]{1,0:T(8,128)(2,1)S(1)} %shard_map.137.a_ref, bf16[512,128]{1,0:T(8,128)(2,1)S(1)} %get-tuple-element.42.full, bf16[512,128]{1,0:T(8,128)(2,1)S(1)} %bitcast.14), custom_call_target="tpu_custom_call" | custom-call | flops 268435456 | bytes 2097152 | tf_op jit(solution)/shard_map/pallas_call | solution.py:60
  26.0 12.6 %all_to_all.26 = bf16[8,64,128]{2,1,0:T(8,128)(2,1)S(1)} all-to-all(bf16[8,64,128]{2,1,0:T(8,128)(2,1)S(1)} %bitcast.21), channel_id=1, replica_groups=mesh['node'=8,'feat'=4] {'node'}, dimensions={0} | all-to-all | bytes 262144 | tf_op jit(solution)/shard_map/all_to_all | solution.py:293
  38.7 5.2 %shard_map.140 = (bf16[176,512]{1,0:T(8,128)(2,1)S(1)}, f32[4,512,256]{2,1,0:T(8,128)S(1)}, bf16[8,96,128]{2,1,0:T(8,128)(2,1)S(1)}, f32[2,176,256]{2,1,0:T(8,128)S(1)}) custom-call(s32[1]{0:T(128)} %bitcast.3.ids, bf16[1024,1024]{1,0:T(8,128)(2,1)S(1)} %shard_map.137.a_ref, bf16[1024,256]{1,0:T(8,128)(2,1)S(1)} %get-tuple-element.50.state, ...), custom_call_target="tpu_custom_call" | custom-call | flops 4294967296 | bytes 8388608 | tf_op jit(solution)/shard_map/pallas_call | solution.py:60
  43.9 0.3 collective-permute-start.6
  44.2 10.7 %all_to_all.27.landed = bf16[8,96,128]{2,1,0:T(8,128)(2,1)S(1)} all-to-all(bf16[8,96,128]{2,1,0:T(8,128)(2,1)S(1)} %get-tuple-element.58), channel_id=1, replica_groups=mesh['node'=8,'feat'=4] {'node'}, dimensions={0} | all-to-all | bytes 393216 | tf_op jit(solution)/shard_map/all_to_all | solution.py:293
  54.8 2.8 %shard_map.141.grads = f32[8,64,128]{2,1,0:T(8,128)S(1)} custom-call(s32[1]{0:T(128)} %bitcast.3.ids, bf16[176,512]{1,0:T(8,128)(2,1)S(1)} %get-tuple-element.56.turned, bf16[512,512]{1,0:T(8,128)(2,1)S(1)} %get-tuple-element.40.pick, bf16[1024,1024]{1,0:T(8,128)(2,1)S(1)} %shard_map.137.a_ref, f32[4,512,256]{2,1,0:T(8,128)S(1)} %get-tuple-element.57.slope, ...), custom_call_target="tpu_custom_call" | custom-call | tf_op jit(solution)/shard_map/pallas_call | solution.py:60
  57.7 0.1 shard_map.142
  57.7 12.4 %all_to_all.28.pieces = f32[8,112,128]{2,1,0:T(8,128)S(1)} all-to-all(f32[8,112,128]{2,1,0:T(8,128)S(1)} %shard_map.142), channel_id=1, replica_groups=mesh['node'=8,'feat'=4] {'node'}, dimensions={0} | all-to-all | bytes 917504 | tf_op jit(solution)/shard_map/all_to_all | solution.py:293
  70.2 0.1 shard_map.143
  70.2 14.9 %all_to_all.29.pieces = f32[8,152,128]{2,1,0:T(8,128)S(1)} all-to-all(f32[8,152,128]{2,1,0:T(8,128)S(1)} %shard_map.143), channel_id=1, replica_groups=mesh['node'=8,'feat'=4] {'node'}, dimensions={0} | all-to-all | bytes 1245184 | tf_op jit(solution)/shard_map/all_to_all | solution.py:293
  85.1 0.8 shard_map.144
  (21 shorter events, 0.0 us)
Async XLA Ops:
  0.6 6.6 %collective-permute-start.2 = (bf16[32,512]{1,0:T(8,128)(2,1)}, bf16[32,512]{1,0:T(8,128)(2,1)S(1)}, u32[]{:S(2)}, u32[]{:S(2)}) collective-permute-start(bf16[32,512]{1,0:T(8,128)(2,1)} %bitcast.15), channel_id=1, source_target_pairs={{0,3},{1,0},{2,1},{3,2},{4,7},{5,4},{6,5},{7,6},{8,11},{9,8},{10,9... | collective-permute-start | bytes 98312 | tf_op jit(solution)/shard_map/ppermute | solution.py:297
  3.1 4.4 %collective-permute-start.1 = (bf16[32,512]{1,0:T(8,128)(2,1)}, bf16[32,512]{1,0:T(8,128)(2,1)S(1)}, u32[]{:S(2)}, u32[]{:S(2)}) collective-permute-start(bf16[32,512]{1,0:T(8,128)(2,1)} %bitcast.16), channel_id=1, source_target_pairs={{0,2},{1,3},{2,0},{3,1},{4,6},{5,7},{6,4},{7,5},{8,10},{9,11},{10,... | collective-permute-start | bytes 98312 | tf_op jit(solution)/shard_map/ppermute | solution.py:297
  3.7 3.8 %collective-permute-start = (bf16[32,512]{1,0:T(8,128)(2,1)}, bf16[32,512]{1,0:T(8,128)(2,1)S(1)}, u32[]{:S(2)}, u32[]{:S(2)}) collective-permute-start(bf16[32,512]{1,0:T(8,128)(2,1)} %bitcast.17), channel_id=1, source_target_pairs={{0,1},{1,2},{2,3},{3,0},{4,5},{5,6},{6,7},{7,4},{8,9},{9,10},{10,1... | collective-permute-start | bytes 98312 | tf_op jit(solution)/shard_map/ppermute | solution.py:297
  3.9 0.7 copy-start.6
  4.6 3.0 %copy-start = (bf16[512,32]{0,1:T(8,128)(2,1)S(1)}, bf16[512,32]{0,1:T(8,128)(2,1)}, u32[]{:S(2)}) copy-start(bf16[512,32]{0,1:T(8,128)(2,1)} %param.10) | copy-start | bytes 98308
  4.6 3.0 %copy-start.1 = (bf16[256,172]{0,1:T(8,128)(2,1)S(1)}, bf16[256,172]{0,1:T(8,128)(2,1)}, u32[]{:S(2)}) copy-start(bf16[256,172]{0,1:T(8,128)(2,1)} %param.18) | copy-start | bytes 264196
  4.6 3.0 %copy-start.2 = (bf16[256,172]{0,1:T(8,128)(2,1)S(1)}, bf16[256,172]{0,1:T(8,128)(2,1)}, u32[]{:S(2)}) copy-start(bf16[256,172]{0,1:T(8,128)(2,1)} %param.19) | copy-start | bytes 264196
  4.6 3.0 %copy-start.3 = (bf16[32,1024]{1,0:T(8,128)(2,1)S(1)}, bf16[32,1024]{1,0:T(8,128)(2,1)}, u32[]{:S(2)}) copy-start(bf16[32,1024]{1,0:T(8,128)(2,1)} %w_self1.1) | copy-start | bytes 196612
  4.6 3.0 %copy-start.4 = (bf16[32,1024]{1,0:T(8,128)(2,1)S(1)}, bf16[32,1024]{1,0:T(8,128)(2,1)}, u32[]{:S(2)}) copy-start(bf16[32,1024]{1,0:T(8,128)(2,1)} %w_neigh1.1) | copy-start | bytes 196612
  4.6 3.0 %copy-start.5 = (s32[1,8,64]{2,1,0:T(8,128)S(1)}, s32[1,8,64]{2,1,0:T(8,128)}, u32[]{:S(2)}) copy-start(s32[1,8,64]{2,1,0:T(8,128)} %param.11) | copy-start | bytes 6148
  4.6 3.0 %copy-start.7 = (s32[1,8]{1,0:T(1,128)S(1)}, s32[1,8]{1,0:T(1,128)}, u32[]{:S(2)}) copy-start(s32[1,8]{1,0:T(1,128)} %count.1) | copy-start | bytes 100
  7.2 31.5 %copy-start.8 = (s32[512]{0:T(512)S(1)}, s32[512]{0:T(512)}, u32[]{:S(2)}) copy-start(s32[512]{0:T(512)} %param.15) | copy-start | bytes 6148
  8.6 17.4 %collective-permute-start.5 = (bf16[608,256]{1,0:T(8,128)(2,1)S(1)}, bf16[608,256]{1,0:T(8,128)(2,1)S(1)}, u32[]{:S(2)}, u32[]{:S(2)}) collective-permute-start(bf16[608,256]{1,0:T(8,128)(2,1)S(1)} %get-tuple-element.52.refs_0_), channel_id=1, source_target_pairs={{0,3},{1,0},{2,1},{3,2},{4,7},{5,4},{6,5},{7,6},{8,11},{9,8},{10,9... | collective-permute-start | bytes 933896 | tf_op jit(solution)/shard_map/ppermute | solution.py:297
  9.9 16.1 %collective-permute-start.4 = (bf16[608,256]{1,0:T(8,128)(2,1)S(1)}, bf16[608,256]{1,0:T(8,128)(2,1)S(1)}, u32[]{:S(2)}, u32[]{:S(2)}) collective-permute-start(bf16[608,256]{1,0:T(8,128)(2,1)S(1)} %get-tuple-element.52.refs_0_), channel_id=1, source_target_pairs={{0,2},{1,3},{2,0},{3,1},{4,6},{5,7},{6,4},{7,5},{8,10},{9,11},{10,... | collective-permute-start | bytes 933896 | tf_op jit(solution)/shard_map/ppermute | solution.py:297
  11.3 14.7 %collective-permute-start.3 = (bf16[608,256]{1,0:T(8,128)(2,1)S(1)}, bf16[608,256]{1,0:T(8,128)(2,1)S(1)}, u32[]{:S(2)}, u32[]{:S(2)}) collective-permute-start(bf16[608,256]{1,0:T(8,128)(2,1)S(1)} %get-tuple-element.52.refs_0_), channel_id=1, source_target_pairs={{0,1},{1,2},{2,3},{3,0},{4,5},{5,6},{6,7},{7,4},{8,9},{9,10},{10,1... | collective-permute-start | bytes 933896 | tf_op jit(solution)/shard_map/ppermute | solution.py:297
  43.9 13.8 %collective-permute-start.6 = (f32[2,176,256]{2,1,0:T(8,128)S(1)}, f32[2,176,256]{2,1,0:T(8,128)S(1)}, u32[]{:S(2)}, u32[]{:S(2)}) collective-permute-start(f32[2,176,256]{2,1,0:T(8,128)S(1)} %get-tuple-element.59.second), channel_id=1, source_target_pairs={{0,4},{4,0},{8,12},{12,8},{16,20},{20,16},{24,28},{28,24},{1,5},{5... | collective-permute-start | bytes 1081352 | tf_op jit(solution)/shard_map/ppermute | solution.py:358

commit v16 on v14

--- a/solution.py
+++ b/solution.py
@@ -18,6 +18,10 @@
 
 def mm(a, b):
     return lax.dot_general(a, b, (((1,), (0,)), ((), ())), preferred_element_type=F32)
+
+
+def mm_nt(a, b):
+    return lax.dot_general(a, b, (((1,), (1,)), ((), ())), preferred_element_type=F32)
 
 
 def mm_tn(a, b):
@@ -171,8 +175,8 @@
         rounded = held.astype(BF16)
         if k == 0:
             mine, agg_mine = out, rounded
-        w_self, w_neigh = weights[k][pl.ds(base, pad), :].T, weights[k][pl.ds(base + pad, pad), :].T
-        total = total + mm(jnp.concatenate([out, rounded], axis=1), jnp.concatenate([w_self, w_neigh], axis=0))
+        w_pair = jnp.concatenate([weights[k][pl.ds(base, pad), :], weights[k][pl.ds(base + pad, pad), :]], axis=1)
+        total = total + mm_nt(jnp.concatenate([out, rounded], axis=1), w_pair)
     total = total.T
     class_id = lax.broadcasted_iota(jnp.int32, total.shape, 0)
     real = class_id < class_count
@@ -190,7 +194,7 @@
     second[1] = mm(turned[...], agg_mine)
     per_chunk = own // slots
     for c in range(halo // own):
-        back = mm(turned[...], a_ref[:, pl.ds(2 * (c + 1) * own, own)]).T.astype(BF16)
+        back = mm(turned[...], a_ref[:, pl.ds(2 * (c + 1) * own, own)]).astype(BF16).T
         for d in range(per_chunk):
             put_message(packed, c * per_chunk + d, back[d * slots : (d + 1) * slots])
 

time: 86.2 us -> 86.2 us (level)
  no operation moved by 1% of the time
where the time goes in v16:
time: 86.2 us; the launch traced here: 85.9 us
  blocking collectives  64.1 us (74%)
  Pallas kernels  13.7 us (16%)
  starting transfers between devices  6.21 us (7%)
    all_to_all x5, blocking collectives, swap(): return lax.all_to_all(blocks, 'node', 0, 0, tiled=True)  64.1 us
    pallas_call x8, Pallas kernels, call(): pl.pallas_call(body, out_shape=[jax.ShapeDtypeStruct(shape, dtype) for sh...  13.7 us
    ppermute x6, starting transfers between devices, gather_shifted(): lax.ppermute(value, 'feat', [(i, (i + k) % count) for i in range(count)])  5.92 us
  transfers between devices with their start and end apart: 7, of which 2 were waited for; matrix products, arithmetic and copies ran while one was open for 0% of the time, Pallas kernels for 8%

profile of v16, /device:TPU:0, one launch (start us, length us, event | category | flops | bytes accessed | tf_op | source)
XLA Modules:
  0.0 85.9 jit_solution(357492616411894288)
XLA Ops:
  0.6 2.4 %collective-permute-start.2 = (bf16[32,512]{1,0:T(8,128)(2,1)}, bf16[32,512]{1,0:T(8,128)(2,1)S(1)}, u32[]{:S(2)}, u32[]{:S(2)}) collective-permute-start(bf16[32,512]{1,0:T(8,128)(2,1)} %bitcast.15), channel_id=1, source_target_pairs={{0,3},{1,0},{2,1},{3,2},{4,7},{5,4},{6,5},{7,6},{8,11},{9,8},{10,9... | collective-permute-start | bytes 98312 | tf_op jit(solution)/shard_map/ppermute | solution.py:305
  3.1 0.6 collective-permute-start.1
  3.7 0.2 collective-permute-start
  3.9 0.7 copy-done.6
  4.6 2.5 %shard_map.137.a_ref = bf16[512,2048]{1,0:T(8,128)(2,1)S(1)} custom-call(s32[4,16]{1,0:T(4,128)S(1)} %copy-done.6, bf16[4,16,128,128]{3,2,1,0:T(8,128)(2,1)} %tile_val.1), custom_call_target="tpu_custom_call" | custom-call | bytes 4194304 | tf_op jit(solution)/shard_map/pallas_call | solution.py:67
  7.1 0.0 copy-start.8
  7.2 0.0 collective-permute-done.2.refs_3_
  7.2 0.3 collective-permute-done.1.refs_2_
  7.5 0.1 collective-permute-done.refs_1_
  7.6 1.0 %shard_map.138 = (bf16[512,512]{1,0:T(8,128)(2,1)S(1)}, bf16[512,128]{1,0:T(8,128)(2,1)S(1)}, bf16[512,128]{1,0:T(8,128)(2,1)S(1)}, bf16[608,256]{1,0:T(8,128)(2,1)S(1)}) custom-call(s32[1,8]{1,0:T(1,128)S(1)} %copy-done.7, s32[8,64]{1,0:T(8,128)S(1)} %bitcast.25, bf16[32,1024]{1,0:T(8,128)(2,1)S(1)} %copy-done.3, bf16[32,1024]{1,0:T(8,128)(2,1)S(1)} %copy-done.4, ...), custom_call_target="tpu_custom_call" | custom-call | flops 67108864 | bytes 524288 | tf_op jit(solution)/shard_map/pallas_call | solution.py:67
  8.6 1.3 %collective-permute-start.5 = (bf16[608,256]{1,0:T(8,128)(2,1)S(1)}, bf16[608,256]{1,0:T(8,128)(2,1)S(1)}, u32[]{:S(2)}, u32[]{:S(2)}) collective-permute-start(bf16[608,256]{1,0:T(8,128)(2,1)S(1)} %get-tuple-element.52.refs_0_), channel_id=1, source_target_pairs={{0,3},{1,0},{2,1},{3,2},{4,7},{5,4},{6,5},{7,6},{8,11},{9,8},{10,9... | collective-permute-start | bytes 933896 | tf_op jit(solution)/shard_map/ppermute | solution.py:305
  9.9 1.4 %collective-permute-start.4 = (bf16[608,256]{1,0:T(8,128)(2,1)S(1)}, bf16[608,256]{1,0:T(8,128)(2,1)S(1)}, u32[]{:S(2)}, u32[]{:S(2)}) collective-permute-start(bf16[608,256]{1,0:T(8,128)(2,1)S(1)} %get-tuple-element.52.refs_0_), channel_id=1, source_target_pairs={{0,2},{1,3},{2,0},{3,1},{4,6},{5,7},{6,4},{7,5},{8,10},{9,11},{10,... | collective-permute-start | bytes 933896 | tf_op jit(solution)/shard_map/ppermute | solution.py:305
  11.3 13.5 %all_to_all.25 = bf16[8,64,128]{2,1,0:T(8,128)(2,1)S(1)} all-to-all(bf16[8,64,128]{2,1,0:T(8,128)(2,1)S(1)} %bitcast.20), channel_id=1, replica_groups=mesh['node'=8,'feat'=4] {'node'}, dimensions={0} | all-to-all | bytes 262144 | tf_op jit(solution)/shard_map/all_to_all | solution.py:301
  24.8 1.2 %shard_map.139 = (bf16[1024,256]{1,0:T(8,128)(2,1)S(1)}, bf16[512,128]{1,0:T(8,128)(2,1)S(1)}) custom-call(bf16[512,512]{1,0:T(8,128)(2,1)S(1)} %get-tuple-element.40.pick, bf16[512,2048]{1,0:T(8,128)(2,1)S(1)} %shard_map.137.a_ref, bf16[512,128]{1,0:T(8,128)(2,1)S(1)} %get-tuple-element.42.full, bf16[512,128]{1,0:T(8,128)(2,1)S(1)} %bitcast.14), custom_call_target="tpu_custom_call" | custom-call | flops 268435456 | bytes 2097152 | tf_op jit(solution)/shard_map/pallas_call | solution.py:67
  26.0 12.6 %all_to_all.26 = bf16[8,64,128]{2,1,0:T(8,128)(2,1)S(1)} all-to-all(bf16[8,64,128]{2,1,0:T(8,128)(2,1)S(1)} %bitcast.21), channel_id=1, replica_groups=mesh['node'=8,'feat'=4] {'node'}, dimensions={0} | all-to-all | bytes 262144 | tf_op jit(solution)/shard_map/all_to_all | solution.py:301
  38.6 5.3 %shard_map.140 = (bf16[176,512]{1,0:T(8,128)(2,1)S(1)}, f32[4,512,256]{2,1,0:T(8,128)S(1)}, bf16[8,96,128]{2,1,0:T(8,128)(2,1)S(1)}, f32[2,176,256]{2,1,0:T(8,128)S(1)}) custom-call(s32[1]{0:T(128)} %bitcast.3.ids, bf16[512,2048]{1,0:T(8,128)(2,1)S(1)} %shard_map.137.a_ref, bf16[1024,256]{1,0:T(8,128)(2,1)S(1)} %get-tuple-element.50.state, ...), custom_call_target="tpu_custom_call" | custom-call | flops 4294967296 | bytes 8388608 | tf_op jit(solution)/shard_map/pallas_call | solution.py:67
  43.9 0.3 collective-permute-start.6
  44.2 10.6 %all_to_all.27.landed = bf16[8,96,128]{2,1,0:T(8,128)(2,1)S(1)} all-to-all(bf16[8,96,128]{2,1,0:T(8,128)(2,1)S(1)} %get-tuple-element.58), channel_id=1, replica_groups=mesh['node'=8,'feat'=4] {'node'}, dimensions={0} | all-to-all | bytes 393216 | tf_op jit(solution)/shard_map/all_to_all | solution.py:301
  54.8 2.8 %shard_map.141.grads = f32[8,64,128]{2,1,0:T(8,128)S(1)} custom-call(s32[1]{0:T(128)} %bitcast.3.ids, bf16[176,512]{1,0:T(8,128)(2,1)S(1)} %get-tuple-element.56.turned, bf16[512,512]{1,0:T(8,128)(2,1)S(1)} %get-tuple-element.40.pick, bf16[512,2048]{1,0:T(8,128)(2,1)S(1)} %shard_map.137.a_ref, f32[4,512,256]{2,1,0:T(8,128)S(1)} %get-tuple-element.57.slope, ...), custom_call_target="tpu_custom_call" | custom-call | tf_op jit(solution)/shard_map/pallas_call | solution.py:67
  57.7 0.1 shard_map.142
  57.7 12.4 %all_to_all.28.pieces = f32[8,112,128]{2,1,0:T(8,128)S(1)} all-to-all(f32[8,112,128]{2,1,0:T(8,128)S(1)} %shard_map.142), channel_id=1, replica_groups=mesh['node'=8,'feat'=4] {'node'}, dimensions={0} | all-to-all | bytes 917504 | tf_op jit(solution)/shard_map/all_to_all | solution.py:301
  70.2 0.1 shard_map.143
  70.2 14.9 %all_to_all.29.pieces = f32[8,152,128]{2,1,0:T(8,128)S(1)} all-to-all(f32[8,152,128]{2,1,0:T(8,128)S(1)} %shard_map.143), channel_id=1, replica_groups=mesh['node'=8,'feat'=4] {'node'}, dimensions={0} | all-to-all | bytes 1245184 | tf_op jit(solution)/shard_map/all_to_all | solution.py:301
  85.1 0.8 shard_map.144
  (21 shorter events, 0.0 us)
Async XLA Ops:
  0.6 6.5 %collective-permute-start.2 = (bf16[32,512]{1,0:T(8,128)(2,1)}, bf16[32,512]{1,0:T(8,128)(2,1)S(1)}, u32[]{:S(2)}, u32[]{:S(2)}) collective-permute-start(bf16[32,512]{1,0:T(8,128)(2,1)} %bitcast.15), channel_id=1, source_target_pairs={{0,3},{1,0},{2,1},{3,2},{4,7},{5,4},{6,5},{7,6},{8,11},{9,8},{10,9... | collective-permute-start | bytes 98312 | tf_op jit(solution)/shard_map/ppermute | solution.py:305
  3.1 4.4 %collective-permute-start.1 = (bf16[32,512]{1,0:T(8,128)(2,1)}, bf16[32,512]{1,0:T(8,128)(2,1)S(1)}, u32[]{:S(2)}, u32[]{:S(2)}) collective-permute-start(bf16[32,512]{1,0:T(8,128)(2,1)} %bitcast.16), channel_id=1, source_target_pairs={{0,2},{1,3},{2,0},{3,1},{4,6},{5,7},{6,4},{7,5},{8,10},{9,11},{10,... | collective-permute-start | bytes 98312 | tf_op jit(solution)/shard_map/ppermute | solution.py:305
  3.7 3.8 %collective-permute-start = (bf16[32,512]{1,0:T(8,128)(2,1)}, bf16[32,512]{1,0:T(8,128)(2,1)S(1)}, u32[]{:S(2)}, u32[]{:S(2)}) collective-permute-start(bf16[32,512]{1,0:T(8,128)(2,1)} %bitcast.17), channel_id=1, source_target_pairs={{0,1},{1,2},{2,3},{3,0},{4,5},{5,6},{6,7},{7,4},{8,9},{9,10},{10,1... | collective-permute-start | bytes 98312 | tf_op jit(solution)/shard_map/ppermute | solution.py:305
  3.9 0.7 copy-start.6
  4.6 3.0 %copy-start = (bf16[512,32]{0,1:T(8,128)(2,1)S(1)}, bf16[512,32]{0,1:T(8,128)(2,1)}, u32[]{:S(2)}) copy-start(bf16[512,32]{0,1:T(8,128)(2,1)} %param.10) | copy-start | bytes 98308
  4.6 3.0 %copy-start.1 = (bf16[256,172]{0,1:T(8,128)(2,1)S(1)}, bf16[256,172]{0,1:T(8,128)(2,1)}, u32[]{:S(2)}) copy-start(bf16[256,172]{0,1:T(8,128)(2,1)} %param.18) | copy-start | bytes 264196
  4.6 3.0 %copy-start.2 = (bf16[256,172]{0,1:T(8,128)(2,1)S(1)}, bf16[256,172]{0,1:T(8,128)(2,1)}, u32[]{:S(2)}) copy-start(bf16[256,172]{0,1:T(8,128)(2,1)} %param.19) | copy-start | bytes 264196
  4.6 3.0 %copy-start.3 = (bf16[32,1024]{1,0:T(8,128)(2,1)S(1)}, bf16[32,1024]{1,0:T(8,128)(2,1)}, u32[]{:S(2)}) copy-start(bf16[32,1024]{1,0:T(8,128)(2,1)} %w_self1.1) | copy-start | bytes 196612
  4.6 3.0 %copy-start.4 = (bf16[32,1024]{1,0:T(8,128)(2,1)S(1)}, bf16[32,1024]{1,0:T(8,128)(2,1)}, u32[]{:S(2)}) copy-start(bf16[32,1024]{1,0:T(8,128)(2,1)} %w_neigh1.1) | copy-start | bytes 196612
  4.6 3.0 %copy-start.5 = (s32[1,8,64]{2,1,0:T(8,128)S(1)}, s32[1,8,64]{2,1,0:T(8,128)}, u32[]{:S(2)}) copy-start(s32[1,8,64]{2,1,0:T(8,128)} %param.11) | copy-start | bytes 6148
  4.6 3.0 %copy-start.7 = (s32[1,8]{1,0:T(1,128)S(1)}, s32[1,8]{1,0:T(1,128)}, u32[]{:S(2)}) copy-start(s32[1,8]{1,0:T(1,128)} %count.1) | copy-start | bytes 100
  7.1 31.5 %copy-start.8 = (s32[512]{0:T(512)S(1)}, s32[512]{0:T(512)}, u32[]{:S(2)}) copy-start(s32[512]{0:T(512)} %param.15) | copy-start | bytes 6148
  8.6 17.4 %collective-permute-start.5 = (bf16[608,256]{1,0:T(8,128)(2,1)S(1)}, bf16[608,256]{1,0:T(8,128)(2,1)S(1)}, u32[]{:S(2)}, u32[]{:S(2)}) collective-permute-start(bf16[608,256]{1,0:T(8,128)(2,1)S(1)} %get-tuple-element.52.refs_0_), channel_id=1, source_target_pairs={{0,3},{1,0},{2,1},{3,2},{4,7},{5,4},{6,5},{7,6},{8,11},{9,8},{10,9... | collective-permute-start | bytes 933896 | tf_op jit(solution)/shard_map/ppermute | solution.py:305
  9.9 16.1 %collective-permute-start.4 = (bf16[608,256]{1,0:T(8,128)(2,1)S(1)}, bf16[608,256]{1,0:T(8,128)(2,1)S(1)}, u32[]{:S(2)}, u32[]{:S(2)}) collective-permute-start(bf16[608,256]{1,0:T(8,128)(2,1)S(1)} %get-tuple-element.52.refs_0_), channel_id=1, source_target_pairs={{0,2},{1,3},{2,0},{3,1},{4,6},{5,7},{6,4},{7,5},{8,10},{9,11},{10,... | collective-permute-start | bytes 933896 | tf_op jit(solution)/shard_map/ppermute | solution.py:305
  11.3 14.7 %collective-permute-start.3 = (bf16[608,256]{1,0:T(8,128)(2,1)S(1)}, bf16[608,256]{1,0:T(8,128)(2,1)S(1)}, u32[]{:S(2)}, u32[]{:S(2)}) collective-permute-start(bf16[608,256]{1,0:T(8,128)(2,1)S(1)} %get-tuple-element.52.refs_0_), channel_id=1, source_target_pairs={{0,1},{1,2},{2,3},{3,0},{4,5},{5,6},{6,7},{7,4},{8,9},{9,10},{10,1... | collective-permute-start | bytes 933896 | tf_op jit(solution)/shard_map/ppermute | solution.py:305
  43.9 13.8 %collective-permute-start.6 = (f32[2,176,256]{2,1,0:T(8,128)S(1)}, f32[2,176,256]{2,1,0:T(8,128)S(1)}, u32[]{:S(2)}, u32[]{:S(2)}) collective-permute-start(f32[2,176,256]{2,1,0:T(8,128)S(1)} %get-tuple-element.59.second), channel_id=1, source_target_pairs={{0,4},{4,0},{8,12},{12,8},{16,20},{20,16},{24,28},{28,24},{1,5},{5... | collective-permute-start | bytes 1081352 | tf_op jit(solution)/shard_map/ppermute | solution.py:366

commit v17 on v14

--- a/solution.py
+++ b/solution.py
@@ -98,7 +98,7 @@
             a_ref[rows, pl.ds((2 * c + 1) * own, own)] = low
 
 
-def pack_kernel(groups, count, send_rows, w_self1, w_neigh1, w_self2, w_neigh2, *refs):
+def pack_kernel(groups, ids, count, send_rows, w_self1, w_neigh1, w_self2, w_neigh2, *refs):
     pieces, (pick, full, packed, weights), (turned,) = refs[:groups], refs[groups : groups + 4], refs[groups + 4 :]
     step, own = pieces[0].shape
     classes, units = w_self2.shape
@@ -118,8 +118,10 @@
     for d in range(dests):
         hit = (columns[:, d : d + 1] == row_id) & (slot_id < count[0, d])
         pick[pl.ds(d * slots, slots), :] = jnp.where(hit, 1.0, 0.0).astype(BF16)
-    for k, piece in enumerate(pieces):
-        turned[pl.ds(k * step, step), :] = piece[...]
+    turned[:step] = pieces[0][...]
+    for k in range(1, groups):
+        place = lax.rem(ids[0] + groups - jnp.bitwise_xor(ids[0], k), groups)
+        turned[pl.ds(pl.multiple_of(place * step, step), step), :] = pieces[k][...]
     full[...] = turned[...].T
     packed[...] = mm(pick[...], full[...]).astype(BF16)
 
@@ -320,7 +322,7 @@
     packed_rows = 2 * step * groups + 2 * pad
 
     turned = features.T
-    turned_all = gather_shifted(turned, groups)
+    turned_all = [turned] + [lax.ppermute(turned, "feat", [(i, i ^ k) for i in range(groups)]) for k in range(1, groups)]
     (a_mat,) = call(
         prepare_kernel,
         [((own, 2 * total_src), BF16)],
@@ -334,7 +336,7 @@
     pick, full, packed, packed_weights = call(
         functools.partial(pack_kernel, groups),
         [((halo, own), BF16), ((own, cols), BF16), ((halo, cols), BF16), ((packed_rows, units), BF16)],
-        (send_count, send_rows[0], w_self1, w_neigh1, w_self2.T, w_neigh2.T, *turned_all),
+        (ids, send_count, send_rows[0], w_self1, w_neigh1, w_self2.T, w_neigh2.T, *turned_all),
         [((cols, own), BF16)],
         flops=2 * halo * own * cols,
         moved=halo * own * 2,

time: 86.2 us -> 85.9 us (level)
    ppermute x6 -> x3, starting transfers between devices: 5.92 us -> 1.98 us  [gather_shifted(): lax.ppermute(value, 'feat', [(i, (i + k) % count) for i in range(count)])]
    ppermute x0 -> x3, starting transfers between devices: none -> 3.12 us  [shards(): lax.ppermute(turned, 'feat', [(i, i ^ k) for i in range(groups)])]
  transfers between devices with their start and end apart: 7 -> 7, of which waited for: 2 -> 1; matrix products, arithmetic and copies ran while one was open for 0% -> 0% of each run, Pallas kernels for 8% -> 8%
where the time goes in v17:
time: 85.9 us; the launch traced here: 85.6 us
  blocking collectives  64.7 us (75%)
  Pallas kernels  13.7 us (16%)
  starting transfers between devices  5.41 us (6%)
    all_to_all x5, blocking collectives, swap(): return lax.all_to_all(blocks, 'node', 0, 0, tiled=True)  64.7 us
    pallas_call x8, Pallas kernels, call(): pl.pallas_call(body, out_shape=[jax.ShapeDtypeStruct(shape, dtype) for sh...  13.7 us
    ppermute x3, starting transfers between devices, shards(): lax.ppermute(turned, 'feat', [(i, i ^ k) for i in range(groups)])  3.12 us
    ppermute x3, starting transfers between devices, gather_shifted(): lax.ppermute(value, 'feat', [(i, (i + k) % count) for i in range(count)])  1.98 us
  transfers between devices with their start and end apart: 7, of which 1 were waited for; matrix products, arithmetic and copies ran while one was open for 0% of the time, Pallas kernels for 8%

profile of v17, /device:TPU:0, one launch (start us, length us, event | category | flops | bytes accessed | tf_op | source)
XLA Modules:
  0.0 85.6 jit_solution(3505409572114539354)
XLA Ops:
  0.6 2.4 %collective-permute-start.2 = (bf16[32,512]{1,0:T(8,128)(2,1)}, bf16[32,512]{1,0:T(8,128)(2,1)S(1)}, u32[]{:S(2)}, u32[]{:S(2)}) collective-permute-start(bf16[32,512]{1,0:T(8,128)(2,1)} %bitcast.15), channel_id=1, source_target_pairs={{0,3},{1,2},{2,1},{3,0},{4,7},{5,6},{6,5},{7,4},{8,11},{9,10},{10,... | collective-permute-start | bytes 98312 | tf_op jit(solution)/shard_map/ppermute | solution.py:325
  3.1 0.6 collective-permute-start.1
  3.7 0.0 collective-permute-start
  3.8 0.7 copy-done.6
  4.5 2.5 %shard_map.137.a_ref = bf16[512,2048]{1,0:T(8,128)(2,1)S(1)} custom-call(s32[4,16]{1,0:T(4,128)S(1)} %copy-done.6, bf16[4,16,128,128]{3,2,1,0:T(8,128)(2,1)} %tile_val.1), custom_call_target="tpu_custom_call" | custom-call | bytes 4194304 | tf_op jit(solution)/shard_map/pallas_call | solution.py:63
  7.0 0.0 copy-start.8
  7.0 0.0 collective-permute-done.2.refs_3_
  7.1 0.2 collective-permute-done.1.refs_2_
  7.3 0.0 collective-permute-done.refs_1_
  7.3 1.0 %shard_map.138 = (bf16[512,512]{1,0:T(8,128)(2,1)S(1)}, bf16[512,128]{1,0:T(8,128)(2,1)S(1)}, bf16[512,128]{1,0:T(8,128)(2,1)S(1)}, bf16[608,256]{1,0:T(8,128)(2,1)S(1)}) custom-call(s32[1]{0:T(128)} %bitcast.ids, s32[1,8]{1,0:T(1,128)S(1)} %copy-done.7, s32[8,64]{1,0:T(8,128)S(1)} %bitcast.25, bf16[32,1024]{1,0:T(8,128)(2,1)S(1)} %copy-done.3, ...), custom_call_target="tpu_custom_call" | custom-call | flops 67108864 | bytes 524288 | tf_op jit(solution)/shard_map/pallas_call | solution.py:63
  8.3 1.3 %collective-permute-start.5 = (bf16[608,256]{1,0:T(8,128)(2,1)S(1)}, bf16[608,256]{1,0:T(8,128)(2,1)S(1)}, u32[]{:S(2)}, u32[]{:S(2)}) collective-permute-start(bf16[608,256]{1,0:T(8,128)(2,1)S(1)} %get-tuple-element.52.refs_0_), channel_id=1, source_target_pairs={{0,3},{1,0},{2,1},{3,2},{4,7},{5,4},{6,5},{7,6},{8,11},{9,8},{10,9... | collective-permute-start | bytes 933896 | tf_op jit(solution)/shard_map/ppermute | solution.py:303
  9.7 0.6 collective-permute-start.4
  10.3 13.6 %all_to_all.25 = bf16[8,64,128]{2,1,0:T(8,128)(2,1)S(1)} all-to-all(bf16[8,64,128]{2,1,0:T(8,128)(2,1)S(1)} %bitcast.20), channel_id=1, replica_groups=mesh['node'=8,'feat'=4] {'node'}, dimensions={0} | all-to-all | bytes 262144 | tf_op jit(solution)/shard_map/all_to_all | solution.py:299
  23.9 1.2 %shard_map.139 = (bf16[1024,256]{1,0:T(8,128)(2,1)S(1)}, bf16[512,128]{1,0:T(8,128)(2,1)S(1)}) custom-call(bf16[512,512]{1,0:T(8,128)(2,1)S(1)} %get-tuple-element.41.pick, bf16[512,2048]{1,0:T(8,128)(2,1)S(1)} %shard_map.137.a_ref, bf16[512,128]{1,0:T(8,128)(2,1)S(1)} %get-tuple-element.43.full, bf16[512,128]{1,0:T(8,128)(2,1)S(1)} %bitcast.14), custom_call_target="tpu_custom_call" | custom-call | flops 268435456 | bytes 2097152 | tf_op jit(solution)/shard_map/pallas_call | solution.py:63
  25.1 0.0 collective-permute-done.5.refs_3_
  25.1 12.8 %all_to_all.26 = bf16[8,64,128]{2,1,0:T(8,128)(2,1)S(1)} all-to-all(bf16[8,64,128]{2,1,0:T(8,128)(2,1)S(1)} %bitcast.21), channel_id=1, replica_groups=mesh['node'=8,'feat'=4] {'node'}, dimensions={0} | all-to-all | bytes 262144 | tf_op jit(solution)/shard_map/all_to_all | solution.py:299
  37.9 5.3 %shard_map.140 = (bf16[176,512]{1,0:T(8,128)(2,1)S(1)}, f32[4,512,256]{2,1,0:T(8,128)S(1)}, bf16[8,96,128]{2,1,0:T(8,128)(2,1)S(1)}, f32[2,176,256]{2,1,0:T(8,128)S(1)}) custom-call(s32[1]{0:T(128)} %bitcast.ids, bf16[512,2048]{1,0:T(8,128)(2,1)S(1)} %shard_map.137.a_ref, bf16[1024,256]{1,0:T(8,128)(2,1)S(1)} %get-tuple-element.50.state, ...), custom_call_target="tpu_custom_call" | custom-call | flops 4294967296 | bytes 8388608 | tf_op jit(solution)/shard_map/pallas_call | solution.py:63
  43.1 0.3 collective-permute-start.6
  43.5 10.6 %all_to_all.27.landed = bf16[8,96,128]{2,1,0:T(8,128)(2,1)S(1)} all-to-all(bf16[8,96,128]{2,1,0:T(8,128)(2,1)S(1)} %get-tuple-element.58), channel_id=1, replica_groups=mesh['node'=8,'feat'=4] {'node'}, dimensions={0} | all-to-all | bytes 393216 | tf_op jit(solution)/shard_map/all_to_all | solution.py:299
  54.1 2.8 %shard_map.141.grads = f32[8,64,128]{2,1,0:T(8,128)S(1)} custom-call(s32[1]{0:T(128)} %bitcast.ids, bf16[176,512]{1,0:T(8,128)(2,1)S(1)} %get-tuple-element.56.turned, bf16[512,512]{1,0:T(8,128)(2,1)S(1)} %get-tuple-element.41.pick, bf16[512,2048]{1,0:T(8,128)(2,1)S(1)} %shard_map.137.a_ref, f32[4,512,256]{2,1,0:T(8,128)S(1)} %get-tuple-element.57.slope, ...), custom_call_target="tpu_custom_call" | custom-call | tf_op jit(solution)/shard_map/pallas_call | solution.py:63
  57.0 12.3 %all_to_all.28.pieces = f32[8,112,128]{2,1,0:T(8,128)S(1)} all-to-all(f32[8,112,128]{2,1,0:T(8,128)S(1)} %shard_map.142), channel_id=1, replica_groups=mesh['node'=8,'feat'=4] {'node'}, dimensions={0} | all-to-all | bytes 917504 | tf_op jit(solution)/shard_map/all_to_all | solution.py:299
  69.3 0.1 shard_map.143
  69.3 15.4 %all_to_all.29.pieces = f32[8,152,128]{2,1,0:T(8,128)S(1)} all-to-all(f32[8,152,128]{2,1,0:T(8,128)S(1)} %shard_map.143), channel_id=1, replica_groups=mesh['node'=8,'feat'=4] {'node'}, dimensions={0} | all-to-all | bytes 1245184 | tf_op jit(solution)/shard_map/all_to_all | solution.py:299
  84.7 0.8 shard_map.144
  (21 shorter events, 0.1 us)
Async XLA Ops:
  0.6 6.4 %collective-permute-start.2 = (bf16[32,512]{1,0:T(8,128)(2,1)}, bf16[32,512]{1,0:T(8,128)(2,1)S(1)}, u32[]{:S(2)}, u32[]{:S(2)}) collective-permute-start(bf16[32,512]{1,0:T(8,128)(2,1)} %bitcast.15), channel_id=1, source_target_pairs={{0,3},{1,2},{2,1},{3,0},{4,7},{5,6},{6,5},{7,4},{8,11},{9,10},{10,... | collective-permute-start | bytes 98312 | tf_op jit(solution)/shard_map/ppermute | solution.py:325
  3.1 4.2 %collective-permute-start.1 = (bf16[32,512]{1,0:T(8,128)(2,1)}, bf16[32,512]{1,0:T(8,128)(2,1)S(1)}, u32[]{:S(2)}, u32[]{:S(2)}) collective-permute-start(bf16[32,512]{1,0:T(8,128)(2,1)} %bitcast.16), channel_id=1, source_target_pairs={{0,2},{1,3},{2,0},{3,1},{4,6},{5,7},{6,4},{7,5},{8,10},{9,11},{10,... | collective-permute-start | bytes 98312 | tf_op jit(solution)/shard_map/ppermute | solution.py:325
  3.7 3.5 %collective-permute-start = (bf16[32,512]{1,0:T(8,128)(2,1)}, bf16[32,512]{1,0:T(8,128)(2,1)S(1)}, u32[]{:S(2)}, u32[]{:S(2)}) collective-permute-start(bf16[32,512]{1,0:T(8,128)(2,1)} %bitcast.17), channel_id=1, source_target_pairs={{0,1},{1,0},{2,3},{3,2},{4,5},{5,4},{6,7},{7,6},{8,9},{9,8},{10,11... | collective-permute-start | bytes 98312 | tf_op jit(solution)/shard_map/ppermute | solution.py:325
  3.8 0.7 copy-start.6
  4.4 2.8 %copy-start = (bf16[512,32]{0,1:T(8,128)(2,1)S(1)}, bf16[512,32]{0,1:T(8,128)(2,1)}, u32[]{:S(2)}) copy-start(bf16[512,32]{0,1:T(8,128)(2,1)} %param.10) | copy-start | bytes 98308
  4.4 2.8 %copy-start.1 = (bf16[256,172]{0,1:T(8,128)(2,1)S(1)}, bf16[256,172]{0,1:T(8,128)(2,1)}, u32[]{:S(2)}) copy-start(bf16[256,172]{0,1:T(8,128)(2,1)} %param.18) | copy-start | bytes 264196
  4.4 2.8 %copy-start.2 = (bf16[256,172]{0,1:T(8,128)(2,1)S(1)}, bf16[256,172]{0,1:T(8,128)(2,1)}, u32[]{:S(2)}) copy-start(bf16[256,172]{0,1:T(8,128)(2,1)} %param.19) | copy-start | bytes 264196
  4.4 2.8 %copy-start.3 = (bf16[32,1024]{1,0:T(8,128)(2,1)S(1)}, bf16[32,1024]{1,0:T(8,128)(2,1)}, u32[]{:S(2)}) copy-start(bf16[32,1024]{1,0:T(8,128)(2,1)} %w_self1.1) | copy-start | bytes 196612
  4.5 2.8 %copy-start.4 = (bf16[32,1024]{1,0:T(8,128)(2,1)S(1)}, bf16[32,1024]{1,0:T(8,128)(2,1)}, u32[]{:S(2)}) copy-start(bf16[32,1024]{1,0:T(8,128)(2,1)} %w_neigh1.1) | copy-start | bytes 196612
  4.5 2.8 %copy-start.5 = (s32[1,8,64]{2,1,0:T(8,128)S(1)}, s32[1,8,64]{2,1,0:T(8,128)}, u32[]{:S(2)}) copy-start(s32[1,8,64]{2,1,0:T(8,128)} %param.11) | copy-start | bytes 6148
  4.5 2.8 %copy-start.7 = (s32[1,8]{1,0:T(1,128)S(1)}, s32[1,8]{1,0:T(1,128)}, u32[]{:S(2)}) copy-start(s32[1,8]{1,0:T(1,128)} %count.1) | copy-start | bytes 100
  7.0 30.8 %copy-start.8 = (s32[512]{0:T(512)S(1)}, s32[512]{0:T(512)}, u32[]{:S(2)}) copy-start(s32[512]{0:T(512)} %param.15) | copy-start | bytes 6148
  8.3 16.7 %collective-permute-start.5 = (bf16[608,256]{1,0:T(8,128)(2,1)S(1)}, bf16[608,256]{1,0:T(8,128)(2,1)S(1)}, u32[]{:S(2)}, u32[]{:S(2)}) collective-permute-start(bf16[608,256]{1,0:T(8,128)(2,1)S(1)} %get-tuple-element.52.refs_0_), channel_id=1, source_target_pairs={{0,3},{1,0},{2,1},{3,2},{4,7},{5,4},{6,5},{7,6},{8,11},{9,8},{10,9... | collective-permute-start | bytes 933896 | tf_op jit(solution)/shard_map/ppermute | solution.py:303
  9.7 15.4 %collective-permute-start.4 = (bf16[608,256]{1,0:T(8,128)(2,1)S(1)}, bf16[608,256]{1,0:T(8,128)(2,1)S(1)}, u32[]{:S(2)}, u32[]{:S(2)}) collective-permute-start(bf16[608,256]{1,0:T(8,128)(2,1)S(1)} %get-tuple-element.52.refs_0_), channel_id=1, source_target_pairs={{0,2},{1,3},{2,0},{3,1},{4,6},{5,7},{6,4},{7,5},{8,10},{9,11},{10,... | collective-permute-start | bytes 933896 | tf_op jit(solution)/shard_map/ppermute | solution.py:303
  10.3 14.8 %collective-permute-start.3 = (bf16[608,256]{1,0:T(8,128)(2,1)S(1)}, bf16[608,256]{1,0:T(8,128)(2,1)S(1)}, u32[]{:S(2)}, u32[]{:S(2)}) collective-permute-start(bf16[608,256]{1,0:T(8,128)(2,1)S(1)} %get-tuple-element.52.refs_0_), channel_id=1, source_target_pairs={{0,1},{1,2},{2,3},{3,0},{4,5},{5,6},{6,7},{7,4},{8,9},{9,10},{10,1... | collective-permute-start | bytes 933896 | tf_op jit(solution)/shard_map/ppermute | solution.py:303
  43.1 13.8 %collective-permute-start.6 = (f32[2,176,256]{2,1,0:T(8,128)S(1)}, f32[2,176,256]{2,1,0:T(8,128)S(1)}, u32[]{:S(2)}, u32[]{:S(2)}) collective-permute-start(f32[2,176,256]{2,1,0:T(8,128)S(1)} %get-tuple-element.59.second), channel_id=1, source_target_pairs={{0,4},{4,0},{8,12},{12,8},{16,20},{20,16},{24,28},{28,24},{1,5},{5... | collective-permute-start | bytes 1081352 | tf_op jit(solution)/shard_map/ppermute | solution.py:364

commit v18 on v17

--- a/solution.py
+++ b/solution.py
@@ -98,10 +98,10 @@
             a_ref[rows, pl.ds((2 * c + 1) * own, own)] = low
 
 
-def pack_kernel(groups, ids, count, send_rows, w_self1, w_neigh1, w_self2, w_neigh2, *refs):
-    pieces, (pick, full, packed, weights), (turned,) = refs[:groups], refs[groups : groups + 4], refs[groups + 4 :]
-    step, own = pieces[0].shape
-    classes, units = w_self2.shape
+def weights_kernel(w_self1, w_neigh1, w_self2, w_neigh2, weights):
+    step, units = w_self1.shape[0], weights.shape[1]
+    groups = w_self1.shape[1] // units
+    classes = w_self2.shape[0]
     base = 2 * step * groups
     pad = (weights.shape[0] - base) // 2
     for j in range(groups):
@@ -111,6 +111,11 @@
     weights[pl.ds(base, 2 * pad), :] = jnp.zeros((2 * pad, units), BF16)
     weights[pl.ds(base, classes), :] = w_self2[...]
     weights[pl.ds(base + pad, classes), :] = w_neigh2[...]
+
+
+def pack_kernel(groups, ids, count, send_rows, *refs):
+    pieces, (pick, full, packed), (turned,) = refs[:groups], refs[groups : groups + 3], refs[groups + 3 :]
+    step, own = pieces[0].shape
     dests, slots = send_rows.shape
     columns = send_rows[...].astype(F32).T
     row_id = lax.broadcasted_iota(jnp.int32, (slots, own), 1).astype(F32)
@@ -332,16 +337,18 @@
         moved=tile_val.size * 4,
         grant=54 * 2**20 - 4 * own * total_src - 3 * 10**5,
     )
-    a_mat, ids, side, *turned_all = lax.optimization_barrier((a_mat, ids, side, *turned_all))
-    pick, full, packed, packed_weights = call(
+    a_mat, *pairs = lax.optimization_barrier((a_mat, w_self1, w_neigh1, w_self2.T, w_neigh2.T))
+    (packed_weights,) = call(weights_kernel, [((packed_rows, units), BF16)], pairs)
+    packed_weights, ids, *turned_all = lax.optimization_barrier((packed_weights, ids, *turned_all))
+    weights = gather_shifted(packed_weights, groups)
+    pick, full, packed = call(
         functools.partial(pack_kernel, groups),
-        [((halo, own), BF16), ((own, cols), BF16), ((halo, cols), BF16), ((packed_rows, units), BF16)],
-        (ids, send_count, send_rows[0], w_self1, w_neigh1, w_self2.T, w_neigh2.T, *turned_all),
+        [((halo, own), BF16), ((own, cols), BF16), ((halo, cols), BF16)],
+        (ids, send_count, send_rows[0], *turned_all),
         [((cols, own), BF16)],
         flops=2 * halo * own * cols,
         moved=halo * own * 2,
     )
-    weights = gather_shifted(packed_weights, groups)
     source = swap(packed, nodes).reshape(halo, cols)
     state, packed = call(
         first_kernel,

time: 85.9 us -> 90.3 us (1.051)
  blocking collectives: 64.7 us -> 52.5 us
  waiting for transfers between devices: 0.22 us -> 8.13 us
  starting transfers between devices: 5.41 us -> 11.3 us
  Pallas kernels: 13.7 us -> 15.8 us
    all_to_all x5 -> x4, blocking collectives: 64.7 us -> 52.5 us  [swap(): return lax.all_to_all(blocks, 'node', 0, 0, tiled=True)]
    all_to_all x0 -> x1, waiting for transfers between devices: none -> 7.98 us  [swap(): return lax.all_to_all(blocks, 'node', 0, 0, tiled=True)]
    all_to_all x0 -> x1, starting transfers between devices: none -> 5.84 us  [swap(): return lax.all_to_all(blocks, 'node', 0, 0, tiled=True)]
    pallas_call x8 -> x9, Pallas kernels: 13.7 us -> 15.8 us  [call(): pl.pallas_call(body, out_shape=[jax.ShapeDtypeStruct(shape, dtype) for sh...]
  transfers between devices with their start and end apart: 7 -> 8, of which waited for: 1 -> 2; matrix products, arithmetic and copies ran while one was open for 0% -> 0% of each run, Pallas kernels for 8% -> 10%
where the time goes in v18:
time: 90.3 us; the launch traced here: 89.9 us
  blocking collectives  52.5 us (58%)
  Pallas kernels  15.8 us (17%)
  starting transfers between devices  11.3 us (13%)
  waiting for transfers between devices  8.13 us (9%)
  local copies, waits for them, and re-layouts  1.36 us (2%)
    all_to_all x4, blocking collectives, swap(): return lax.all_to_all(blocks, 'node', 0, 0, tiled=True)  52.5 us
    pallas_call x9, Pallas kernels, call(): pl.pallas_call(body, out_shape=[jax.ShapeDtypeStruct(shape, dtype) for sh...  15.8 us
    all_to_all x1, waiting for transfers between devices, swap(): return lax.all_to_all(blocks, 'node', 0, 0, tiled=True)  7.98 us
    all_to_all x1, starting transfers between devices, swap(): return lax.all_to_all(blocks, 'node', 0, 0, tiled=True)  5.84 us
    ppermute x3, starting transfers between devices, shards(): lax.ppermute(turned, 'feat', [(i, i ^ k) for i in range(groups)])  3.12 us
    ppermute x3, starting transfers between devices, gather_shifted(): lax.ppermute(value, 'feat', [(i, (i + k) % count) for i in range(count)])  2.04 us
  transfers between devices with their start and end apart: 8, of which 2 were waited for; matrix products, arithmetic and copies ran while one was open for 0% of the time, Pallas kernels for 10%

profile of v18, /device:TPU:0, one launch (start us, length us, event | category | flops | bytes accessed | tf_op | source)
XLA Modules:
  0.0 89.9 jit_solution(8296669159208931789)
XLA Ops:
  0.6 2.4 %collective-permute-start.2 = (bf16[32,512]{1,0:T(8,128)(2,1)}, bf16[32,512]{1,0:T(8,128)(2,1)S(1)}, u32[]{:S(2)}, u32[]{:S(2)}) collective-permute-start(bf16[32,512]{1,0:T(8,128)(2,1)} %bitcast.20), channel_id=1, source_target_pairs={{0,3},{1,2},{2,1},{3,0},{4,7},{5,6},{6,5},{7,4},{8,11},{9,10},{10,... | collective-permute-start | bytes 98312 | tf_op jit(solution)/shard_map/ppermute | solution.py:330
  3.1 0.6 collective-permute-start.1
  3.7 0.0 collective-permute-start
  3.8 0.7 copy-done.6
  4.5 2.5 %shard_map.137.a_ref = bf16[512,2048]{1,0:T(8,128)(2,1)S(1)} custom-call(s32[4,16]{1,0:T(4,128)S(1)} %copy-done.6, bf16[4,16,128,128]{3,2,1,0:T(8,128)(2,1)} %tile_val.1), custom_call_target="tpu_custom_call" | custom-call | bytes 4194304 | tf_op jit(solution)/shard_map/pallas_call | solution.py:63
  7.1 0.0 copy-start.8
  7.1 0.1 collective-permute-done.1.refs_2_
  7.3 1.4 %collective-permute-start.5 = (bf16[608,256]{1,0:T(8,128)(2,1)S(1)}, bf16[608,256]{1,0:T(8,128)(2,1)S(1)}, u32[]{:S(2)}, u32[]{:S(2)}) collective-permute-start(bf16[608,256]{1,0:T(8,128)(2,1)S(1)} %shard_map.138.refs_0_), channel_id=1, source_target_pairs={{0,3},{1,0},{2,1},{3,2},{4,7},{5,4},{6,5},{7,6},{8,11},{9,8},{10,9... | collective-permute-start | bytes 933896 | tf_op jit(solution)/shard_map/ppermute | solution.py:308
  8.7 0.6 collective-permute-start.4
  9.3 1.0 %shard_map.139 = (bf16[512,512]{1,0:T(8,128)(2,1)S(1)}, bf16[512,128]{1,0:T(8,128)(2,1)S(1)}, bf16[512,128]{1,0:T(8,128)(2,1)S(1)}) custom-call(s32[1]{0:T(128)} %bitcast.2.ids, s32[1,8]{1,0:T(1,128)S(1)} %copy-done.9, s32[8,64]{1,0:T(8,128)S(1)} %bitcast.25, bf16[32,512]{1,0:T(8,128)(2,1)S(1)} %bitcast.23, ...), custom_call_target="tpu_custom_call" | custom-call | flops 67108864 | bytes 524288 | tf_op jit(solution)/shard_map/pallas_call | solution.py:63
  10.3 0.0 copy-start
  10.3 0.6 copy-done
  11.0 5.8 %all-to-all-start = ((bf16[8,64,128]{2,1,0:T(8,128)(2,1)}), bf16[8,64,128]{2,1,0:T(8,128)(2,1)S(1)}, u32[]{:S(2)}, u32[]{:S(2)}) async-start(bf16[8,64,128]{2,1,0:T(8,128)(2,1)} %bitcast.15), calls=%async_computation | async-start | bytes 262144 | tf_op jit(solution)/shard_map/all_to_all | solution.py:304
  16.8 8.0 %all-to-all-done = bf16[8,64,128]{2,1,0:T(8,128)(2,1)S(1)} async-done(((bf16[8,64,128]{2,1,0:T(8,128)(2,1)}), bf16[8,64,128]{2,1,0:T(8,128)(2,1)S(1)}, u32[]{:S(2)}, u32[]{:S(2)}) %all-to-all-start) | async-done | bytes 131104 | tf_op jit(solution)/shard_map/all_to_all | solution.py:304
  24.8 1.2 %shard_map.140 = (bf16[1024,256]{1,0:T(8,128)(2,1)S(1)}, bf16[512,128]{1,0:T(8,128)(2,1)S(1)}) custom-call(bf16[512,512]{1,0:T(8,128)(2,1)S(1)} %get-tuple-element.48.pick, bf16[512,2048]{1,0:T(8,128)(2,1)S(1)} %shard_map.137.a_ref, bf16[512,128]{1,0:T(8,128)(2,1)S(1)} %get-tuple-element.50.full, bf16[512,128]{1,0:T(8,128)(2,1)S(1)} %bitcast.14), custom_call_target="tpu_custom_call" | custom-call | flops 268435456 | bytes 2097152 | tf_op jit(solution)/shard_map/pallas_call | solution.py:63
  26.0 11.0 %all_to_all.25 = bf16[8,64,128]{2,1,0:T(8,128)(2,1)S(1)} all-to-all(bf16[8,64,128]{2,1,0:T(8,128)(2,1)S(1)} %bitcast.16), channel_id=1, replica_groups=mesh['node'=8,'feat'=4] {'node'}, dimensions={0} | all-to-all | bytes 262144 | tf_op jit(solution)/shard_map/all_to_all | solution.py:304
  37.0 6.3 %shard_map.141 = (bf16[176,512]{1,0:T(8,128)(2,1)S(1)}, f32[4,512,256]{2,1,0:T(8,128)S(1)}, bf16[8,96,128]{2,1,0:T(8,128)(2,1)S(1)}, f32[2,176,256]{2,1,0:T(8,128)S(1)}) custom-call(s32[1]{0:T(128)} %bitcast.2.ids, bf16[512,2048]{1,0:T(8,128)(2,1)S(1)} %shard_map.137.a_ref, bf16[1024,256]{1,0:T(8,128)(2,1)S(1)} %get-tuple-element.56.state, ...), custom_call_target="tpu_custom_call" | custom-call | flops 4294967296 | bytes 8388608 | tf_op jit(solution)/shard_map/pallas_call | solution.py:63
  43.3 0.3 collective-permute-start.6
  43.5 10.7 %all_to_all.26.landed = bf16[8,96,128]{2,1,0:T(8,128)(2,1)S(1)} all-to-all(bf16[8,96,128]{2,1,0:T(8,128)(2,1)S(1)} %get-tuple-element.64), channel_id=1, replica_groups=mesh['node'=8,'feat'=4] {'node'}, dimensions={0} | all-to-all | bytes 393216 | tf_op jit(solution)/shard_map/all_to_all | solution.py:304
  54.2 3.9 %shard_map.142.grads = f32[8,64,128]{2,1,0:T(8,128)S(1)} custom-call(s32[1]{0:T(128)} %bitcast.2.ids, bf16[176,512]{1,0:T(8,128)(2,1)S(1)} %get-tuple-element.62.turned, bf16[512,512]{1,0:T(8,128)(2,1)S(1)} %get-tuple-element.48.pick, bf16[512,2048]{1,0:T(8,128)(2,1)S(1)} %shard_map.137.a_ref, f32[4,512,256]{2,1,0:T(8,128)S(1)} %get-tuple-element.63.slope, ...), custom_call_target="tpu_custom_call" | custom-call | tf_op jit(solution)/shard_map/pallas_call | solution.py:63
  58.1 12.7 %all_to_all.27.pieces = f32[8,112,128]{2,1,0:T(8,128)S(1)} all-to-all(f32[8,112,128]{2,1,0:T(8,128)S(1)} %shard_map.143), channel_id=1, replica_groups=mesh['node'=8,'feat'=4] {'node'}, dimensions={0} | all-to-all | bytes 917504 | tf_op jit(solution)/shard_map/all_to_all | solution.py:304
  70.8 0.1 shard_map.144
  70.9 18.2 %all_to_all.28.pieces = f32[8,152,128]{2,1,0:T(8,128)S(1)} all-to-all(f32[8,152,128]{2,1,0:T(8,128)S(1)} %shard_map.144), channel_id=1, replica_groups=mesh['node'=8,'feat'=4] {'node'}, dimensions={0} | all-to-all | bytes 1245184 | tf_op jit(solution)/shard_map/all_to_all | solution.py:304
  89.1 0.8 shard_map.145
  (25 shorter events, 0.1 us)
Async XLA Ops:
  0.6 6.5 %collective-permute-start.2 = (bf16[32,512]{1,0:T(8,128)(2,1)}, bf16[32,512]{1,0:T(8,128)(2,1)S(1)}, u32[]{:S(2)}, u32[]{:S(2)}) collective-permute-start(bf16[32,512]{1,0:T(8,128)(2,1)} %bitcast.20), channel_id=1, source_target_pairs={{0,3},{1,2},{2,1},{3,0},{4,7},{5,6},{6,5},{7,4},{8,11},{9,10},{10,... | collective-permute-start | bytes 98312 | tf_op jit(solution)/shard_map/ppermute | solution.py:330
  3.1 4.2 %collective-permute-start.1 = (bf16[32,512]{1,0:T(8,128)(2,1)}, bf16[32,512]{1,0:T(8,128)(2,1)S(1)}, u32[]{:S(2)}, u32[]{:S(2)}) collective-permute-start(bf16[32,512]{1,0:T(8,128)(2,1)} %bitcast.21), channel_id=1, source_target_pairs={{0,2},{1,3},{2,0},{3,1},{4,6},{5,7},{6,4},{7,5},{8,10},{9,11},{10,... | collective-permute-start | bytes 98312 | tf_op jit(solution)/shard_map/ppermute | solution.py:330
  3.7 3.5 %collective-permute-start = (bf16[32,512]{1,0:T(8,128)(2,1)}, bf16[32,512]{1,0:T(8,128)(2,1)S(1)}, u32[]{:S(2)}, u32[]{:S(2)}) collective-permute-start(bf16[32,512]{1,0:T(8,128)(2,1)} %bitcast.22), channel_id=1, source_target_pairs={{0,1},{1,0},{2,3},{3,2},{4,5},{5,4},{6,7},{7,6},{8,9},{9,8},{10,11... | collective-permute-start | bytes 98312 | tf_op jit(solution)/shard_map/ppermute | solution.py:330
  3.8 0.7 copy-start.6
  4.4 2.6 %copy-start.1 = (bf16[256,172]{0,1:T(8,128)(2,1)S(1)}, bf16[256,172]{0,1:T(8,128)(2,1)}, u32[]{:S(2)}) copy-start(bf16[256,172]{0,1:T(8,128)(2,1)} %param.18) | copy-start | bytes 264196
  4.4 2.6 %copy-start.2 = (bf16[256,172]{0,1:T(8,128)(2,1)S(1)}, bf16[256,172]{0,1:T(8,128)(2,1)}, u32[]{:S(2)}) copy-start(bf16[256,172]{0,1:T(8,128)(2,1)} %param.19) | copy-start | bytes 264196
  4.4 2.6 %copy-start.3 = (bf16[32,1024]{1,0:T(8,128)(2,1)S(1)}, bf16[32,1024]{1,0:T(8,128)(2,1)}, u32[]{:S(2)}) copy-start(bf16[32,1024]{1,0:T(8,128)(2,1)} %w_self1) | copy-start | bytes 196612
  4.4 2.6 %copy-start.4 = (bf16[32,1024]{1,0:T(8,128)(2,1)S(1)}, bf16[32,1024]{1,0:T(8,128)(2,1)}, u32[]{:S(2)}) copy-start(bf16[32,1024]{1,0:T(8,128)(2,1)} %w_neigh1) | copy-start | bytes 196612
  4.5 4.9 %copy-start.5 = (bf16[512,32]{0,1:T(8,128)(2,1)S(1)}, bf16[512,32]{0,1:T(8,128)(2,1)}, u32[]{:S(2)}) copy-start(bf16[512,32]{0,1:T(8,128)(2,1)} %param.10) | copy-start | bytes 98308
  4.5 4.9 %copy-start.7 = (s32[1,8,64]{2,1,0:T(8,128)S(1)}, s32[1,8,64]{2,1,0:T(8,128)}, u32[]{:S(2)}) copy-start(s32[1,8,64]{2,1,0:T(8,128)} %param.11) | copy-start | bytes 6148
  4.5 4.8 %copy-start.9 = (s32[1,8]{1,0:T(1,128)S(1)}, s32[1,8]{1,0:T(1,128)}, u32[]{:S(2)}) copy-start(s32[1,8]{1,0:T(1,128)} %count.1) | copy-start | bytes 100
  7.1 29.9 %copy-start.8 = (s32[512]{0:T(512)S(1)}, s32[512]{0:T(512)}, u32[]{:S(2)}) copy-start(s32[512]{0:T(512)} %param.15) | copy-start | bytes 6148
  7.3 18.7 %collective-permute-start.5 = (bf16[608,256]{1,0:T(8,128)(2,1)S(1)}, bf16[608,256]{1,0:T(8,128)(2,1)S(1)}, u32[]{:S(2)}, u32[]{:S(2)}) collective-permute-start(bf16[608,256]{1,0:T(8,128)(2,1)S(1)} %shard_map.138.refs_0_), channel_id=1, source_target_pairs={{0,3},{1,0},{2,1},{3,2},{4,7},{5,4},{6,5},{7,6},{8,11},{9,8},{10,9... | collective-permute-start | bytes 933896 | tf_op jit(solution)/shard_map/ppermute | solution.py:308
  8.7 17.3 %collective-permute-start.4 = (bf16[608,256]{1,0:T(8,128)(2,1)S(1)}, bf16[608,256]{1,0:T(8,128)(2,1)}, u32[]{:S(2)}, u32[]{:S(2)}) collective-permute-start(bf16[608,256]{1,0:T(8,128)(2,1)S(1)} %shard_map.138.refs_0_), channel_id=1, source_target_pairs={{0,2},{1,3},{2,0},{3,1},{4,6},{5,7},{6,4},{7,5},{8,10},{9,11},{10,... | collective-permute-start | bytes 933896 | tf_op jit(solution)/shard_map/ppermute | solution.py:308
  9.3 16.7 %collective-permute-start.3 = (bf16[608,256]{1,0:T(8,128)(2,1)S(1)}, bf16[608,256]{1,0:T(8,128)(2,1)}, u32[]{:S(2)}, u32[]{:S(2)}) collective-permute-start(bf16[608,256]{1,0:T(8,128)(2,1)S(1)} %shard_map.138.refs_0_), channel_id=1, source_target_pairs={{0,1},{1,2},{2,3},{3,0},{4,5},{5,6},{6,7},{7,4},{8,9},{9,10},{10,1... | collective-permute-start | bytes 933896 | tf_op jit(solution)/shard_map/ppermute | solution.py:308
  10.3 0.7 copy-start
  11.0 13.8 %all-to-all-start = ((bf16[8,64,128]{2,1,0:T(8,128)(2,1)}), bf16[8,64,128]{2,1,0:T(8,128)(2,1)S(1)}, u32[]{:S(2)}, u32[]{:S(2)}) async-start(bf16[8,64,128]{2,1,0:T(8,128)(2,1)} %bitcast.15), calls=%async_computation | async-start | bytes 262144 | tf_op jit(solution)/shard_map/all_to_all | solution.py:304
  43.3 14.8 %collective-permute-start.6 = (f32[2,176,256]{2,1,0:T(8,128)S(1)}, f32[2,176,256]{2,1,0:T(8,128)S(1)}, u32[]{:S(2)}, u32[]{:S(2)}) collective-permute-start(f32[2,176,256]{2,1,0:T(8,128)S(1)} %get-tuple-element.65.second), channel_id=1, source_target_pairs={{0,4},{4,0},{8,12},{12,8},{16,20},{20,16},{24,28},{28,24},{1,5},{5... | collective-permute-start | bytes 1081352 | tf_op jit(solution)/shard_map/ppermute | solution.py:371

commit v19 on v18

--- a/solution.py
+++ b/solution.py
@@ -339,7 +339,7 @@
     )
     a_mat, *pairs = lax.optimization_barrier((a_mat, w_self1, w_neigh1, w_self2.T, w_neigh2.T))
     (packed_weights,) = call(weights_kernel, [((packed_rows, units), BF16)], pairs)
-    packed_weights, ids, *turned_all = lax.optimization_barrier((packed_weights, ids, *turned_all))
+    packed_weights, ids, side, *turned_all = lax.optimization_barrier((packed_weights, ids, side, *turned_all))
     weights = gather_shifted(packed_weights, groups)
     pick, full, packed = call(
         functools.partial(pack_kernel, groups),

time: 90.3 us -> 84.9 us (0.940)
  blocking collectives: 52.5 us -> 63.7 us
  waiting for transfers between devices: 8.13 us -> 0.14 us
  starting transfers between devices: 11.3 us -> 5.45 us
  Pallas kernels: 15.8 us -> 13.7 us
    all_to_all x4 -> x5, blocking collectives: 52.5 us -> 63.7 us  [swap(): return lax.all_to_all(blocks, 'node', 0, 0, tiled=True)]
    all_to_all x1 -> x0, waiting for transfers between devices: 7.98 us -> none  [swap(): return lax.all_to_all(blocks, 'node', 0, 0, tiled=True)]
    all_to_all x1 -> x0, starting transfers between devices: 5.84 us -> none  [swap(): return lax.all_to_all(blocks, 'node', 0, 0, tiled=True)]
    pallas_call x9, Pallas kernels: 15.8 us -> 13.7 us  [call(): pl.pallas_call(body, out_shape=[jax.ShapeDtypeStruct(shape, dtype) for sh...]
  transfers between devices with their start and end apart: 8 -> 7, of which waited for: 2 -> 1; matrix products, arithmetic and copies ran while one was open for 0% -> 0% of each run, Pallas kernels for 10% -> 9%
where the time goes in v19:
time: 84.9 us; the launch traced here: 84.5 us
  blocking collectives  63.7 us (75%)
  Pallas kernels  13.7 us (16%)
  starting transfers between devices  5.45 us (6%)
    all_to_all x5, blocking collectives, swap(): return lax.all_to_all(blocks, 'node', 0, 0, tiled=True)  63.7 us
    pallas_call x9, Pallas kernels, call(): pl.pallas_call(body, out_shape=[jax.ShapeDtypeStruct(shape, dtype) for sh...  13.7 us
    ppermute x3, starting transfers between devices, shards(): lax.ppermute(turned, 'feat', [(i, i ^ k) for i in range(groups)])  3.12 us
    ppermute x3, starting transfers between devices, gather_shifted(): lax.ppermute(value, 'feat', [(i, (i + k) % count) for i in range(count)])  2.05 us
  transfers between devices with their start and end apart: 7, of which 1 were waited for; matrix products, arithmetic and copies ran while one was open for 0% of the time, Pallas kernels for 9%

profile of v19, /device:TPU:0, one launch (start us, length us, event | category | flops | bytes accessed | tf_op | source)
XLA Modules:
  0.0 84.5 jit_solution(10312837210361714215)
XLA Ops:
  0.6 2.4 %collective-permute-start.2 = (bf16[32,512]{1,0:T(8,128)(2,1)}, bf16[32,512]{1,0:T(8,128)(2,1)S(1)}, u32[]{:S(2)}, u32[]{:S(2)}) collective-permute-start(bf16[32,512]{1,0:T(8,128)(2,1)} %bitcast.20), channel_id=1, source_target_pairs={{0,3},{1,2},{2,1},{3,0},{4,7},{5,6},{6,5},{7,4},{8,11},{9,10},{10,... | collective-permute-start | bytes 98312 | tf_op jit(solution)/shard_map/ppermute | solution.py:330
  3.1 0.6 collective-permute-start.1
  3.7 0.0 collective-permute-start
  3.8 0.7 copy-done.5
  4.5 2.5 %shard_map.137.a_ref = bf16[512,2048]{1,0:T(8,128)(2,1)S(1)} custom-call(s32[4,16]{1,0:T(4,128)S(1)} %copy-done.5, bf16[4,16,128,128]{3,2,1,0:T(8,128)(2,1)} %tile_val.1), custom_call_target="tpu_custom_call" | custom-call | bytes 4194304 | tf_op jit(solution)/shard_map/pallas_call | solution.py:63
  7.1 0.0 copy-start.7
  7.1 0.0 collective-permute-done.2.refs_3_
  7.1 0.1 collective-permute-done.1.refs_2_
  7.3 1.4 %collective-permute-start.5 = (bf16[608,256]{1,0:T(8,128)(2,1)S(1)}, bf16[608,256]{1,0:T(8,128)(2,1)S(1)}, u32[]{:S(2)}, u32[]{:S(2)}) collective-permute-start(bf16[608,256]{1,0:T(8,128)(2,1)S(1)} %shard_map.138.refs_0_), channel_id=1, source_target_pairs={{0,3},{1,0},{2,1},{3,2},{4,7},{5,4},{6,5},{7,6},{8,11},{9,8},{10,9... | collective-permute-start | bytes 933896 | tf_op jit(solution)/shard_map/ppermute | solution.py:308
  8.7 0.6 collective-permute-start.4
  9.3 1.0 %shard_map.139 = (bf16[512,512]{1,0:T(8,128)(2,1)S(1)}, bf16[512,128]{1,0:T(8,128)(2,1)S(1)}, bf16[512,128]{1,0:T(8,128)(2,1)S(1)}) custom-call(s32[1]{0:T(128)} %bitcast.2.ids, s32[1,8]{1,0:T(1,128)S(1)} %copy-done.8, s32[8,64]{1,0:T(8,128)S(1)} %bitcast.25, bf16[32,512]{1,0:T(8,128)(2,1)S(1)} %bitcast.23, ...), custom_call_target="tpu_custom_call" | custom-call | flops 67108864 | bytes 524288 | tf_op jit(solution)/shard_map/pallas_call | solution.py:63
  10.3 13.6 %all_to_all.25 = bf16[8,64,128]{2,1,0:T(8,128)(2,1)S(1)} all-to-all(bf16[8,64,128]{2,1,0:T(8,128)(2,1)S(1)} %bitcast.16), channel_id=1, replica_groups=mesh['node'=8,'feat'=4] {'node'}, dimensions={0} | all-to-all | bytes 262144 | tf_op jit(solution)/shard_map/all_to_all | solution.py:304
  24.0 1.2 %shard_map.140 = (bf16[1024,256]{1,0:T(8,128)(2,1)S(1)}, bf16[512,128]{1,0:T(8,128)(2,1)S(1)}) custom-call(bf16[512,512]{1,0:T(8,128)(2,1)S(1)} %get-tuple-element.49.pick, bf16[512,2048]{1,0:T(8,128)(2,1)S(1)} %shard_map.137.a_ref, bf16[512,128]{1,0:T(8,128)(2,1)S(1)} %get-tuple-element.51.full, bf16[512,128]{1,0:T(8,128)(2,1)S(1)} %bitcast.14), custom_call_target="tpu_custom_call" | custom-call | flops 268435456 | bytes 2097152 | tf_op jit(solution)/shard_map/pallas_call | solution.py:63
  25.1 0.0 collective-permute-done.5.refs_3_
  25.2 11.7 %all_to_all.26 = bf16[8,64,128]{2,1,0:T(8,128)(2,1)S(1)} all-to-all(bf16[8,64,128]{2,1,0:T(8,128)(2,1)S(1)} %bitcast.15), channel_id=1, replica_groups=mesh['node'=8,'feat'=4] {'node'}, dimensions={0} | all-to-all | bytes 262144 | tf_op jit(solution)/shard_map/all_to_all | solution.py:304
  36.9 5.3 %shard_map.141 = (bf16[176,512]{1,0:T(8,128)(2,1)S(1)}, f32[4,512,256]{2,1,0:T(8,128)S(1)}, bf16[8,96,128]{2,1,0:T(8,128)(2,1)S(1)}, f32[2,176,256]{2,1,0:T(8,128)S(1)}) custom-call(s32[1]{0:T(128)} %bitcast.2.ids, bf16[512,2048]{1,0:T(8,128)(2,1)S(1)} %shard_map.137.a_ref, bf16[1024,256]{1,0:T(8,128)(2,1)S(1)} %get-tuple-element.58.state, ...), custom_call_target="tpu_custom_call" | custom-call | flops 4294967296 | bytes 8388608 | tf_op jit(solution)/shard_map/pallas_call | solution.py:63
  42.1 0.3 collective-permute-start.6
  42.4 10.7 %all_to_all.27.landed = bf16[8,96,128]{2,1,0:T(8,128)(2,1)S(1)} all-to-all(bf16[8,96,128]{2,1,0:T(8,128)(2,1)S(1)} %get-tuple-element.66), channel_id=1, replica_groups=mesh['node'=8,'feat'=4] {'node'}, dimensions={0} | all-to-all | bytes 393216 | tf_op jit(solution)/shard_map/all_to_all | solution.py:304
  53.1 2.8 %shard_map.142.grads = f32[8,64,128]{2,1,0:T(8,128)S(1)} custom-call(s32[1]{0:T(128)} %bitcast.2.ids, bf16[176,512]{1,0:T(8,128)(2,1)S(1)} %get-tuple-element.64.turned, bf16[512,512]{1,0:T(8,128)(2,1)S(1)} %get-tuple-element.49.pick, bf16[512,2048]{1,0:T(8,128)(2,1)S(1)} %shard_map.137.a_ref, f32[4,512,256]{2,1,0:T(8,128)S(1)} %get-tuple-element.65.slope, ...), custom_call_target="tpu_custom_call" | custom-call | tf_op jit(solution)/shard_map/pallas_call | solution.py:63
  55.9 0.1 shard_map.143
  56.0 12.3 %all_to_all.28.pieces = f32[8,112,128]{2,1,0:T(8,128)S(1)} all-to-all(f32[8,112,128]{2,1,0:T(8,128)S(1)} %shard_map.143), channel_id=1, replica_groups=mesh['node'=8,'feat'=4] {'node'}, dimensions={0} | all-to-all | bytes 917504 | tf_op jit(solution)/shard_map/all_to_all | solution.py:304
  68.3 0.1 shard_map.144
  68.3 15.4 %all_to_all.29.pieces = f32[8,152,128]{2,1,0:T(8,128)S(1)} all-to-all(f32[8,152,128]{2,1,0:T(8,128)S(1)} %shard_map.144), channel_id=1, replica_groups=mesh['node'=8,'feat'=4] {'node'}, dimensions={0} | all-to-all | bytes 1245184 | tf_op jit(solution)/shard_map/all_to_all | solution.py:304
  83.7 0.8 shard_map.145
  (22 shorter events, 0.1 us)
Async XLA Ops:
  0.6 6.5 %collective-permute-start.2 = (bf16[32,512]{1,0:T(8,128)(2,1)}, bf16[32,512]{1,0:T(8,128)(2,1)S(1)}, u32[]{:S(2)}, u32[]{:S(2)}) collective-permute-start(bf16[32,512]{1,0:T(8,128)(2,1)} %bitcast.20), channel_id=1, source_target_pairs={{0,3},{1,2},{2,1},{3,0},{4,7},{5,6},{6,5},{7,4},{8,11},{9,10},{10,... | collective-permute-start | bytes 98312 | tf_op jit(solution)/shard_map/ppermute | solution.py:330
  3.1 4.2 %collective-permute-start.1 = (bf16[32,512]{1,0:T(8,128)(2,1)}, bf16[32,512]{1,0:T(8,128)(2,1)S(1)}, u32[]{:S(2)}, u32[]{:S(2)}) collective-permute-start(bf16[32,512]{1,0:T(8,128)(2,1)} %bitcast.21), channel_id=1, source_target_pairs={{0,2},{1,3},{2,0},{3,1},{4,6},{5,7},{6,4},{7,5},{8,10},{9,11},{10,... | collective-permute-start | bytes 98312 | tf_op jit(solution)/shard_map/ppermute | solution.py:330
  3.7 3.5 %collective-permute-start = (bf16[32,512]{1,0:T(8,128)(2,1)}, bf16[32,512]{1,0:T(8,128)(2,1)S(1)}, u32[]{:S(2)}, u32[]{:S(2)}) collective-permute-start(bf16[32,512]{1,0:T(8,128)(2,1)} %bitcast.22), channel_id=1, source_target_pairs={{0,1},{1,0},{2,3},{3,2},{4,5},{5,4},{6,7},{7,6},{8,9},{9,8},{10,11... | collective-permute-start | bytes 98312 | tf_op jit(solution)/shard_map/ppermute | solution.py:330
  3.8 0.7 copy-start.5
  4.4 2.6 %copy-start = (bf16[256,172]{0,1:T(8,128)(2,1)S(1)}, bf16[256,172]{0,1:T(8,128)(2,1)}, u32[]{:S(2)}) copy-start(bf16[256,172]{0,1:T(8,128)(2,1)} %param.18) | copy-start | bytes 264196
  4.4 2.6 %copy-start.1 = (bf16[256,172]{0,1:T(8,128)(2,1)S(1)}, bf16[256,172]{0,1:T(8,128)(2,1)}, u32[]{:S(2)}) copy-start(bf16[256,172]{0,1:T(8,128)(2,1)} %param.19) | copy-start | bytes 264196
  4.4 2.6 %copy-start.2 = (bf16[32,1024]{1,0:T(8,128)(2,1)S(1)}, bf16[32,1024]{1,0:T(8,128)(2,1)}, u32[]{:S(2)}) copy-start(bf16[32,1024]{1,0:T(8,128)(2,1)} %w_self1) | copy-start | bytes 196612
  4.4 2.6 %copy-start.3 = (bf16[32,1024]{1,0:T(8,128)(2,1)S(1)}, bf16[32,1024]{1,0:T(8,128)(2,1)}, u32[]{:S(2)}) copy-start(bf16[32,1024]{1,0:T(8,128)(2,1)} %w_neigh1) | copy-start | bytes 196612
  4.5 4.9 %copy-start.4 = (bf16[512,32]{0,1:T(8,128)(2,1)S(1)}, bf16[512,32]{0,1:T(8,128)(2,1)}, u32[]{:S(2)}) copy-start(bf16[512,32]{0,1:T(8,128)(2,1)} %param.10) | copy-start | bytes 98308
  4.5 4.9 %copy-start.6 = (s32[1,8,64]{2,1,0:T(8,128)S(1)}, s32[1,8,64]{2,1,0:T(8,128)}, u32[]{:S(2)}) copy-start(s32[1,8,64]{2,1,0:T(8,128)} %param.11) | copy-start | bytes 6148
  4.5 4.9 %copy-start.8 = (s32[1,8]{1,0:T(1,128)S(1)}, s32[1,8]{1,0:T(1,128)}, u32[]{:S(2)}) copy-start(s32[1,8]{1,0:T(1,128)} %count.1) | copy-start | bytes 100
  7.1 29.8 %copy-start.7 = (s32[512]{0:T(512)S(1)}, s32[512]{0:T(512)}, u32[]{:S(2)}) copy-start(s32[512]{0:T(512)} %param.15) | copy-start | bytes 6148
  7.3 17.9 %collective-permute-start.5 = (bf16[608,256]{1,0:T(8,128)(2,1)S(1)}, bf16[608,256]{1,0:T(8,128)(2,1)S(1)}, u32[]{:S(2)}, u32[]{:S(2)}) collective-permute-start(bf16[608,256]{1,0:T(8,128)(2,1)S(1)} %shard_map.138.refs_0_), channel_id=1, source_target_pairs={{0,3},{1,0},{2,1},{3,2},{4,7},{5,4},{6,5},{7,6},{8,11},{9,8},{10,9... | collective-permute-start | bytes 933896 | tf_op jit(solution)/shard_map/ppermute | solution.py:308
  8.7 16.5 %collective-permute-start.4 = (bf16[608,256]{1,0:T(8,128)(2,1)S(1)}, bf16[608,256]{1,0:T(8,128)(2,1)S(1)}, u32[]{:S(2)}, u32[]{:S(2)}) collective-permute-start(bf16[608,256]{1,0:T(8,128)(2,1)S(1)} %shard_map.138.refs_0_), channel_id=1, source_target_pairs={{0,2},{1,3},{2,0},{3,1},{4,6},{5,7},{6,4},{7,5},{8,10},{9,11},{10,... | collective-permute-start | bytes 933896 | tf_op jit(solution)/shard_map/ppermute | solution.py:308
  9.3 15.8 %collective-permute-start.3 = (bf16[608,256]{1,0:T(8,128)(2,1)S(1)}, bf16[608,256]{1,0:T(8,128)(2,1)S(1)}, u32[]{:S(2)}, u32[]{:S(2)}) collective-permute-start(bf16[608,256]{1,0:T(8,128)(2,1)S(1)} %shard_map.138.refs_0_), channel_id=1, source_target_pairs={{0,1},{1,2},{2,3},{3,0},{4,5},{5,6},{6,7},{7,4},{8,9},{9,10},{10,1... | collective-permute-start | bytes 933896 | tf_op jit(solution)/shard_map/ppermute | solution.py:308
  42.1 13.8 %collective-permute-start.6 = (f32[2,176,256]{2,1,0:T(8,128)S(1)}, f32[2,176,256]{2,1,0:T(8,128)S(1)}, u32[]{:S(2)}, u32[]{:S(2)}) collective-permute-start(f32[2,176,256]{2,1,0:T(8,128)S(1)} %get-tuple-element.67.second), channel_id=1, source_target_pairs={{0,4},{4,0},{8,12},{12,8},{16,20},{20,16},{24,28},{28,24},{1,5},{5... | collective-permute-start | bytes 1081352 | tf_op jit(solution)/shard_map/ppermute | solution.py:371

commit v20 on v19

--- a/solution.py
+++ b/solution.py
@@ -131,7 +131,7 @@
     packed[...] = mm(pick[...], full[...]).astype(BF16)
 
 
-def first_kernel(pick, a_ref, full, source, state, packed):
+def first_kernel(pick, a_ref, full, source, features, state, packed, left):
     own, cols = full.shape
     total = spread(a_ref[:, : 2 * own], full[...]) + spread(a_ref[:, 2 * own :], source[...])
     agg = total.astype(BF16)
@@ -140,6 +140,9 @@
     state[:own, cols:] = agg
     state[own:, :cols] = source[...]
     state[own:, cols:] = jnp.zeros_like(source)
+    step = features.shape[0]
+    left[:step] = features[...]
+    left[step:] = agg.T[:step]
 
 
 def forward_kernel(
@@ -229,25 +232,23 @@
     landed[pl.ds(d * slots + half, half), BLOCK:] = packed[d, slots:, BLOCK // 2 : BLOCK // 2 + tail]
 
 
-def backward_kernel(parts, groups, ids, turned, pick, a_ref, slope, features, state, landed, *refs):
+def backward_kernel(parts, groups, ids, turned, pick, a_ref, slope, left, landed, *refs):
     weights = refs[:groups]
     out, rows = refs[groups:]
     own = turned.shape[1]
     units = slope.shape[2]
     pad = turned.shape[0]
-    step = features.shape[0]
+    step = left.shape[0] // 2
     base = 2 * step * groups
     for d in range(landed.shape[0]):
         take_message(landed, d, rows)
     high, low = halves(mm(turned[...], a_ref[:, :own]) + mm_tn(rows[...], pick[...]))
     wide = jnp.concatenate([turned[...], high, low], axis=0).T
-    cols = state.shape[1] // 2
-    left = jnp.concatenate([features[...], state[:own, cols:].T[:step]], axis=0)
     for k in range(groups):
         group = lax.rem(ids[0] + groups - k, groups)
         w_neigh = weights[k][pl.ds(base + pad, pad), :]
         total = mm(wide, jnp.concatenate([weights[k][pl.ds(base, pad), :], w_neigh, w_neigh], axis=0))
-        result = mm(left, (total * slope[k]).astype(BF16))
+        result = mm(left[...], (total * slope[k]).astype(BF16))
         if parts:
             for i in range(units // BLOCK):
                 out[group * (units // BLOCK) + i] = result[:, i * BLOCK : (i + 1) * BLOCK]
@@ -350,10 +351,10 @@
         moved=halo * own * 2,
     )
     source = swap(packed, nodes).reshape(halo, cols)
-    state, packed = call(
+    state, packed, left = call(
         first_kernel,
-        [((total_src, 2 * cols), BF16), ((halo, cols), BF16)],
-        (pick, a_mat, full, source),
+        [((total_src, 2 * cols), BF16), ((halo, cols), BF16), ((2 * step, own), BF16)],
+        (pick, a_mat, full, source, turned),
         flops=4 * own * total_src * cols,
         moved=4 * own * total_src,
     )
@@ -373,7 +374,7 @@
     (grads,) = call(
         functools.partial(backward_kernel, parts, groups),
         [((parts, 2 * step, BLOCK) if parts else (2 * step, width), F32)],
-        (ids, turned_grads, pick, a_mat, slope, turned, state, landed, *weights),
+        (ids, turned_grads, pick, a_mat, slope, left, landed, *weights),
         [((halo, pad), BF16)],
     )
     if not parts:

time: 84.9 us -> 84.9 us (level)
  no operation moved by 1% of the time
where the time goes in v20:
time: 84.9 us; the launch traced here: 84.5 us
  blocking collectives  63.7 us (75%)
  Pallas kernels  13.7 us (16%)
  starting transfers between devices  5.45 us (6%)
    all_to_all x5, blocking collectives, swap(): return lax.all_to_all(blocks, 'node', 0, 0, tiled=True)  63.7 us
    pallas_call x9, Pallas kernels, call(): pl.pallas_call(body, out_shape=[jax.ShapeDtypeStruct(shape, dtype) for sh...  13.7 us
    ppermute x3, starting transfers between devices, shards(): lax.ppermute(turned, 'feat', [(i, i ^ k) for i in range(groups)])  3.12 us
    ppermute x3, starting transfers between devices, gather_shifted(): lax.ppermute(value, 'feat', [(i, (i + k) % count) for i in range(count)])  2.05 us
  transfers between devices with their start and end apart: 7, of which 1 were waited for; matrix products, arithmetic and copies ran while one was open for 0% of the time, Pallas kernels for 9%

profile of v20, /device:TPU:0, one launch (start us, length us, event | category | flops | bytes accessed | tf_op | source)
XLA Modules:
  0.0 84.5 jit_solution(5396804362357052927)
XLA Ops:
  0.6 2.4 %collective-permute-start.2 = (bf16[32,512]{1,0:T(8,128)(2,1)}, bf16[32,512]{1,0:T(8,128)(2,1)S(1)}, u32[]{:S(2)}, u32[]{:S(2)}) collective-permute-start(bf16[32,512]{1,0:T(8,128)(2,1)} %bitcast.20), channel_id=1, source_target_pairs={{0,3},{1,2},{2,1},{3,0},{4,7},{5,6},{6,5},{7,4},{8,11},{9,10},{10,... | collective-permute-start | bytes 98312 | tf_op jit(solution)/shard_map/ppermute | solution.py:331
  3.1 0.6 collective-permute-start.1
  3.7 0.0 collective-permute-start
  3.8 0.7 copy-done.5
  4.5 2.5 %shard_map.137.a_ref = bf16[512,2048]{1,0:T(8,128)(2,1)S(1)} custom-call(s32[4,16]{1,0:T(4,128)S(1)} %copy-done.5, bf16[4,16,128,128]{3,2,1,0:T(8,128)(2,1)} %tile_val.1), custom_call_target="tpu_custom_call" | custom-call | bytes 4194304 | tf_op jit(solution)/shard_map/pallas_call | solution.py:63
  7.1 0.0 copy-start.7
  7.1 0.0 collective-permute-done.2.refs_3_
  7.1 0.1 collective-permute-done.1.refs_2_
  7.3 1.4 %collective-permute-start.5 = (bf16[608,256]{1,0:T(8,128)(2,1)S(1)}, bf16[608,256]{1,0:T(8,128)(2,1)S(1)}, u32[]{:S(2)}, u32[]{:S(2)}) collective-permute-start(bf16[608,256]{1,0:T(8,128)(2,1)S(1)} %shard_map.138.refs_0_), channel_id=1, source_target_pairs={{0,3},{1,0},{2,1},{3,2},{4,7},{5,4},{6,5},{7,6},{8,11},{9,8},{10,9... | collective-permute-start | bytes 933896 | tf_op jit(solution)/shard_map/ppermute | solution.py:309
  8.7 0.6 collective-permute-start.4
  9.3 1.0 %shard_map.139 = (bf16[512,512]{1,0:T(8,128)(2,1)S(1)}, bf16[512,128]{1,0:T(8,128)(2,1)S(1)}, bf16[512,128]{1,0:T(8,128)(2,1)S(1)}) custom-call(s32[1]{0:T(128)} %bitcast.2.ids, s32[1,8]{1,0:T(1,128)S(1)} %copy-done.8, s32[8,64]{1,0:T(8,128)S(1)} %bitcast.25, bf16[32,512]{1,0:T(8,128)(2,1)S(1)} %bitcast.23, ...), custom_call_target="tpu_custom_call" | custom-call | flops 67108864 | bytes 524288 | tf_op jit(solution)/shard_map/pallas_call | solution.py:63
  10.3 13.6 %all_to_all.25 = bf16[8,64,128]{2,1,0:T(8,128)(2,1)S(1)} all-to-all(bf16[8,64,128]{2,1,0:T(8,128)(2,1)S(1)} %bitcast.16), channel_id=1, replica_groups=mesh['node'=8,'feat'=4] {'node'}, dimensions={0} | all-to-all | bytes 262144 | tf_op jit(solution)/shard_map/all_to_all | solution.py:305
  23.9 1.2 %shard_map.140 = (bf16[1024,256]{1,0:T(8,128)(2,1)S(1)}, bf16[512,128]{1,0:T(8,128)(2,1)S(1)}, bf16[64,512]{1,0:T(8,128)(2,1)S(1)}) custom-call(bf16[512,512]{1,0:T(8,128)(2,1)S(1)} %get-tuple-element.50.pick, bf16[512,2048]{1,0:T(8,128)(2,1)S(1)} %shard_map.137.a_ref, bf16[512,128]{1,0:T(8,128)(2,1)S(1)} %get-tuple-element.52.full, ...), custom_call_target="tpu_custom_call" | custom-call | flops 268435456 | bytes 2097152 | tf_op jit(solution)/shard_map/pallas_call | solution.py:63
  25.1 0.0 collective-permute-done.4.refs_2_
  25.1 0.0 collective-permute-done.3.refs_1_
  25.1 11.7 %all_to_all.26 = bf16[8,64,128]{2,1,0:T(8,128)(2,1)S(1)} all-to-all(bf16[8,64,128]{2,1,0:T(8,128)(2,1)S(1)} %bitcast.15), channel_id=1, replica_groups=mesh['node'=8,'feat'=4] {'node'}, dimensions={0} | all-to-all | bytes 262144 | tf_op jit(solution)/shard_map/all_to_all | solution.py:305
  36.9 5.2 %shard_map.141 = (bf16[176,512]{1,0:T(8,128)(2,1)S(1)}, f32[4,512,256]{2,1,0:T(8,128)S(1)}, bf16[8,96,128]{2,1,0:T(8,128)(2,1)S(1)}, f32[2,176,256]{2,1,0:T(8,128)S(1)}) custom-call(s32[1]{0:T(128)} %bitcast.2.ids, bf16[512,2048]{1,0:T(8,128)(2,1)S(1)} %shard_map.137.a_ref, bf16[1024,256]{1,0:T(8,128)(2,1)S(1)} %get-tuple-element.59.state, ...), custom_call_target="tpu_custom_call" | custom-call | flops 4294967296 | bytes 8388608 | tf_op jit(solution)/shard_map/pallas_call | solution.py:63
  42.1 0.3 collective-permute-start.6
  42.4 10.7 %all_to_all.27.landed = bf16[8,96,128]{2,1,0:T(8,128)(2,1)S(1)} all-to-all(bf16[8,96,128]{2,1,0:T(8,128)(2,1)S(1)} %get-tuple-element.68), channel_id=1, replica_groups=mesh['node'=8,'feat'=4] {'node'}, dimensions={0} | all-to-all | bytes 393216 | tf_op jit(solution)/shard_map/all_to_all | solution.py:305
  53.1 2.8 %shard_map.142.grads = f32[8,64,128]{2,1,0:T(8,128)S(1)} custom-call(s32[1]{0:T(128)} %bitcast.2.ids, bf16[176,512]{1,0:T(8,128)(2,1)S(1)} %get-tuple-element.65.turned, bf16[512,512]{1,0:T(8,128)(2,1)S(1)} %get-tuple-element.50.pick, bf16[512,2048]{1,0:T(8,128)(2,1)S(1)} %shard_map.137.a_ref, f32[4,512,256]{2,1,0:T(8,128)S(1)} %get-tuple-element.66.slope, ...), custom_call_target="tpu_custom_call" | custom-call | tf_op jit(solution)/shard_map/pallas_call | solution.py:63
  56.0 12.3 %all_to_all.28.pieces = f32[8,112,128]{2,1,0:T(8,128)S(1)} all-to-all(f32[8,112,128]{2,1,0:T(8,128)S(1)} %shard_map.143), channel_id=1, replica_groups=mesh['node'=8,'feat'=4] {'node'}, dimensions={0} | all-to-all | bytes 917504 | tf_op jit(solution)/shard_map/all_to_all | solution.py:305
  68.3 0.1 shard_map.144
  68.3 15.4 %all_to_all.29.pieces = f32[8,152,128]{2,1,0:T(8,128)S(1)} all-to-all(f32[8,152,128]{2,1,0:T(8,128)S(1)} %shard_map.144), channel_id=1, replica_groups=mesh['node'=8,'feat'=4] {'node'}, dimensions={0} | all-to-all | bytes 1245184 | tf_op jit(solution)/shard_map/all_to_all | solution.py:305
  83.7 0.8 shard_map.145
  (22 shorter events, 0.1 us)
Async XLA Ops:
  0.6 6.5 %collective-permute-start.2 = (bf16[32,512]{1,0:T(8,128)(2,1)}, bf16[32,512]{1,0:T(8,128)(2,1)S(1)}, u32[]{:S(2)}, u32[]{:S(2)}) collective-permute-start(bf16[32,512]{1,0:T(8,128)(2,1)} %bitcast.20), channel_id=1, source_target_pairs={{0,3},{1,2},{2,1},{3,0},{4,7},{5,6},{6,5},{7,4},{8,11},{9,10},{10,... | collective-permute-start | bytes 98312 | tf_op jit(solution)/shard_map/ppermute | solution.py:331
  3.1 4.2 %collective-permute-start.1 = (bf16[32,512]{1,0:T(8,128)(2,1)}, bf16[32,512]{1,0:T(8,128)(2,1)S(1)}, u32[]{:S(2)}, u32[]{:S(2)}) collective-permute-start(bf16[32,512]{1,0:T(8,128)(2,1)} %bitcast.21), channel_id=1, source_target_pairs={{0,2},{1,3},{2,0},{3,1},{4,6},{5,7},{6,4},{7,5},{8,10},{9,11},{10,... | collective-permute-start | bytes 98312 | tf_op jit(solution)/shard_map/ppermute | solution.py:331
  3.7 3.5 %collective-permute-start = (bf16[32,512]{1,0:T(8,128)(2,1)}, bf16[32,512]{1,0:T(8,128)(2,1)S(1)}, u32[]{:S(2)}, u32[]{:S(2)}) collective-permute-start(bf16[32,512]{1,0:T(8,128)(2,1)} %bitcast.22), channel_id=1, source_target_pairs={{0,1},{1,0},{2,3},{3,2},{4,5},{5,4},{6,7},{7,6},{8,9},{9,8},{10,11... | collective-permute-start | bytes 98312 | tf_op jit(solution)/shard_map/ppermute | solution.py:331
  3.8 0.7 copy-start.5
  4.4 2.6 %copy-start = (bf16[256,172]{0,1:T(8,128)(2,1)S(1)}, bf16[256,172]{0,1:T(8,128)(2,1)}, u32[]{:S(2)}) copy-start(bf16[256,172]{0,1:T(8,128)(2,1)} %param.18) | copy-start | bytes 264196
  4.4 2.6 %copy-start.1 = (bf16[256,172]{0,1:T(8,128)(2,1)S(1)}, bf16[256,172]{0,1:T(8,128)(2,1)}, u32[]{:S(2)}) copy-start(bf16[256,172]{0,1:T(8,128)(2,1)} %param.19) | copy-start | bytes 264196
  4.4 2.6 %copy-start.2 = (bf16[32,1024]{1,0:T(8,128)(2,1)S(1)}, bf16[32,1024]{1,0:T(8,128)(2,1)}, u32[]{:S(2)}) copy-start(bf16[32,1024]{1,0:T(8,128)(2,1)} %w_self1) | copy-start | bytes 196612
  4.4 2.6 %copy-start.3 = (bf16[32,1024]{1,0:T(8,128)(2,1)S(1)}, bf16[32,1024]{1,0:T(8,128)(2,1)}, u32[]{:S(2)}) copy-start(bf16[32,1024]{1,0:T(8,128)(2,1)} %w_neigh1) | copy-start | bytes 196612
  4.5 4.9 %copy-start.4 = (bf16[512,32]{0,1:T(8,128)(2,1)S(1)}, bf16[512,32]{0,1:T(8,128)(2,1)}, u32[]{:S(2)}) copy-start(bf16[512,32]{0,1:T(8,128)(2,1)} %param.10) | copy-start | bytes 98308
  4.5 4.9 %copy-start.6 = (s32[1,8,64]{2,1,0:T(8,128)S(1)}, s32[1,8,64]{2,1,0:T(8,128)}, u32[]{:S(2)}) copy-start(s32[1,8,64]{2,1,0:T(8,128)} %param.11) | copy-start | bytes 6148
  4.5 4.9 %copy-start.8 = (s32[1,8]{1,0:T(1,128)S(1)}, s32[1,8]{1,0:T(1,128)}, u32[]{:S(2)}) copy-start(s32[1,8]{1,0:T(1,128)} %count.1) | copy-start | bytes 100
  7.1 29.8 %copy-start.7 = (s32[512]{0:T(512)S(1)}, s32[512]{0:T(512)}, u32[]{:S(2)}) copy-start(s32[512]{0:T(512)} %param.15) | copy-start | bytes 6148
  7.3 17.9 %collective-permute-start.5 = (bf16[608,256]{1,0:T(8,128)(2,1)S(1)}, bf16[608,256]{1,0:T(8,128)(2,1)S(1)}, u32[]{:S(2)}, u32[]{:S(2)}) collective-permute-start(bf16[608,256]{1,0:T(8,128)(2,1)S(1)} %shard_map.138.refs_0_), channel_id=1, source_target_pairs={{0,3},{1,0},{2,1},{3,2},{4,7},{5,4},{6,5},{7,6},{8,11},{9,8},{10,9... | collective-permute-start | bytes 933896 | tf_op jit(solution)/shard_map/ppermute | solution.py:309
  8.7 16.5 %collective-permute-start.4 = (bf16[608,256]{1,0:T(8,128)(2,1)S(1)}, bf16[608,256]{1,0:T(8,128)(2,1)S(1)}, u32[]{:S(2)}, u32[]{:S(2)}) collective-permute-start(bf16[608,256]{1,0:T(8,128)(2,1)S(1)} %shard_map.138.refs_0_), channel_id=1, source_target_pairs={{0,2},{1,3},{2,0},{3,1},{4,6},{5,7},{6,4},{7,5},{8,10},{9,11},{10,... | collective-permute-start | bytes 933896 | tf_op jit(solution)/shard_map/ppermute | solution.py:309
  9.3 15.8 %collective-permute-start.3 = (bf16[608,256]{1,0:T(8,128)(2,1)S(1)}, bf16[608,256]{1,0:T(8,128)(2,1)S(1)}, u32[]{:S(2)}, u32[]{:S(2)}) collective-permute-start(bf16[608,256]{1,0:T(8,128)(2,1)S(1)} %shard_map.138.refs_0_), channel_id=1, source_target_pairs={{0,1},{1,2},{2,3},{3,0},{4,5},{5,6},{6,7},{7,4},{8,9},{9,10},{10,1... | collective-permute-start | bytes 933896 | tf_op jit(solution)/shard_map/ppermute | solution.py:309
  42.1 13.8 %collective-permute-start.6 = (f32[2,176,256]{2,1,0:T(8,128)S(1)}, f32[2,176,256]{2,1,0:T(8,128)S(1)}, u32[]{:S(2)}, u32[]{:S(2)}) collective-permute-start(f32[2,176,256]{2,1,0:T(8,128)S(1)} %get-tuple-element.69.second), channel_id=1, source_target_pairs={{0,4},{4,0},{8,12},{12,8},{16,20},{20,16},{24,28},{28,24},{1,5},{5... | collective-permute-start | bytes 1081352 | tf_op jit(solution)/shard_map/ppermute | solution.py:372

commit v21 on v19

--- a/solution.py
+++ b/solution.py
@@ -139,7 +139,6 @@
     state[:own, :cols] = full[...]
     state[:own, cols:] = agg
     state[own:, :cols] = source[...]
-    state[own:, cols:] = jnp.zeros_like(source)
 
 
 def forward_kernel(

time: 84.9 us -> 84.9 us (level)
  no operation moved by 1% of the time
where the time goes in v21:
time: 84.9 us; the launch traced here: 84.5 us
  blocking collectives  63.7 us (75%)
  Pallas kernels  13.7 us (16%)
  starting transfers between devices  5.45 us (6%)
    all_to_all x5, blocking collectives, swap(): return lax.all_to_all(blocks, 'node', 0, 0, tiled=True)  63.7 us
    pallas_call x9, Pallas kernels, call(): pl.pallas_call(body, out_shape=[jax.ShapeDtypeStruct(shape, dtype) for sh...  13.7 us
    ppermute x3, starting transfers between devices, shards(): lax.ppermute(turned, 'feat', [(i, i ^ k) for i in range(groups)])  3.12 us
    ppermute x3, starting transfers between devices, gather_shifted(): lax.ppermute(value, 'feat', [(i, (i + k) % count) for i in range(count)])  2.05 us
  transfers between devices with their start and end apart: 7, of which 1 were waited for; matrix products, arithmetic and copies ran while one was open for 0% of the time, Pallas kernels for 9%

profile of v21, /device:TPU:0, one launch (start us, length us, event | category | flops | bytes accessed | tf_op | source)
XLA Modules:
  0.0 84.5 jit_solution(9341156336920667347)
XLA Ops:
  0.6 2.4 %collective-permute-start.2 = (bf16[32,512]{1,0:T(8,128)(2,1)}, bf16[32,512]{1,0:T(8,128)(2,1)S(1)}, u32[]{:S(2)}, u32[]{:S(2)}) collective-permute-start(bf16[32,512]{1,0:T(8,128)(2,1)} %bitcast.20), channel_id=1, source_target_pairs={{0,3},{1,2},{2,1},{3,0},{4,7},{5,6},{6,5},{7,4},{8,11},{9,10},{10,... | collective-permute-start | bytes 98312 | tf_op jit(solution)/shard_map/ppermute | solution.py:329
  3.1 0.6 collective-permute-start.1
  3.7 0.0 collective-permute-start
  3.8 0.7 copy-done.5
  4.5 2.5 %shard_map.137.a_ref = bf16[512,2048]{1,0:T(8,128)(2,1)S(1)} custom-call(s32[4,16]{1,0:T(4,128)S(1)} %copy-done.5, bf16[4,16,128,128]{3,2,1,0:T(8,128)(2,1)} %tile_val.1), custom_call_target="tpu_custom_call" | custom-call | bytes 4194304 | tf_op jit(solution)/shard_map/pallas_call | solution.py:63
  7.1 0.0 copy-start.7
  7.1 0.1 collective-permute-done.1.refs_2_
  7.3 0.0 collective-permute-done.refs_1_
  7.3 1.4 %collective-permute-start.5 = (bf16[608,256]{1,0:T(8,128)(2,1)S(1)}, bf16[608,256]{1,0:T(8,128)(2,1)S(1)}, u32[]{:S(2)}, u32[]{:S(2)}) collective-permute-start(bf16[608,256]{1,0:T(8,128)(2,1)S(1)} %shard_map.138.refs_0_), channel_id=1, source_target_pairs={{0,3},{1,0},{2,1},{3,2},{4,7},{5,4},{6,5},{7,6},{8,11},{9,8},{10,9... | collective-permute-start | bytes 933896 | tf_op jit(solution)/shard_map/ppermute | solution.py:307
  8.7 0.6 collective-permute-start.4
  9.3 0.0 collective-permute-start.3
  9.3 1.0 %shard_map.139 = (bf16[512,512]{1,0:T(8,128)(2,1)S(1)}, bf16[512,128]{1,0:T(8,128)(2,1)S(1)}, bf16[512,128]{1,0:T(8,128)(2,1)S(1)}) custom-call(s32[1]{0:T(128)} %bitcast.2.ids, s32[1,8]{1,0:T(1,128)S(1)} %copy-done.8, s32[8,64]{1,0:T(8,128)S(1)} %bitcast.25, bf16[32,512]{1,0:T(8,128)(2,1)S(1)} %bitcast.23, ...), custom_call_target="tpu_custom_call" | custom-call | flops 67108864 | bytes 524288 | tf_op jit(solution)/shard_map/pallas_call | solution.py:63
  10.3 13.6 %all_to_all.25 = bf16[8,64,128]{2,1,0:T(8,128)(2,1)S(1)} all-to-all(bf16[8,64,128]{2,1,0:T(8,128)(2,1)S(1)} %bitcast.16), channel_id=1, replica_groups=mesh['node'=8,'feat'=4] {'node'}, dimensions={0} | all-to-all | bytes 262144 | tf_op jit(solution)/shard_map/all_to_all | solution.py:303
  24.0 1.2 %shard_map.140 = (bf16[1024,256]{1,0:T(8,128)(2,1)S(1)}, bf16[512,128]{1,0:T(8,128)(2,1)S(1)}) custom-call(bf16[512,512]{1,0:T(8,128)(2,1)S(1)} %get-tuple-element.49.pick, bf16[512,2048]{1,0:T(8,128)(2,1)S(1)} %shard_map.137.a_ref, bf16[512,128]{1,0:T(8,128)(2,1)S(1)} %get-tuple-element.51.full, bf16[512,128]{1,0:T(8,128)(2,1)S(1)} %bitcast.14), custom_call_target="tpu_custom_call" | custom-call | flops 268435456 | bytes 2097152 | tf_op jit(solution)/shard_map/pallas_call | solution.py:63
  25.2 11.7 %all_to_all.26 = bf16[8,64,128]{2,1,0:T(8,128)(2,1)S(1)} all-to-all(bf16[8,64,128]{2,1,0:T(8,128)(2,1)S(1)} %bitcast.15), channel_id=1, replica_groups=mesh['node'=8,'feat'=4] {'node'}, dimensions={0} | all-to-all | bytes 262144 | tf_op jit(solution)/shard_map/all_to_all | solution.py:303
  36.9 5.3 %shard_map.141 = (bf16[176,512]{1,0:T(8,128)(2,1)S(1)}, f32[4,512,256]{2,1,0:T(8,128)S(1)}, bf16[8,96,128]{2,1,0:T(8,128)(2,1)S(1)}, f32[2,176,256]{2,1,0:T(8,128)S(1)}) custom-call(s32[1]{0:T(128)} %bitcast.2.ids, bf16[512,2048]{1,0:T(8,128)(2,1)S(1)} %shard_map.137.a_ref, bf16[1024,256]{1,0:T(8,128)(2,1)S(1)} %get-tuple-element.58.state, ...), custom_call_target="tpu_custom_call" | custom-call | flops 4294967296 | bytes 8388608 | tf_op jit(solution)/shard_map/pallas_call | solution.py:63
  42.1 0.3 collective-permute-start.6
  42.4 10.7 %all_to_all.27.landed = bf16[8,96,128]{2,1,0:T(8,128)(2,1)S(1)} all-to-all(bf16[8,96,128]{2,1,0:T(8,128)(2,1)S(1)} %get-tuple-element.66), channel_id=1, replica_groups=mesh['node'=8,'feat'=4] {'node'}, dimensions={0} | all-to-all | bytes 393216 | tf_op jit(solution)/shard_map/all_to_all | solution.py:303
  53.1 2.8 %shard_map.142.grads = f32[8,64,128]{2,1,0:T(8,128)S(1)} custom-call(s32[1]{0:T(128)} %bitcast.2.ids, bf16[176,512]{1,0:T(8,128)(2,1)S(1)} %get-tuple-element.64.turned, bf16[512,512]{1,0:T(8,128)(2,1)S(1)} %get-tuple-element.49.pick, bf16[512,2048]{1,0:T(8,128)(2,1)S(1)} %shard_map.137.a_ref, f32[4,512,256]{2,1,0:T(8,128)S(1)} %get-tuple-element.65.slope, ...), custom_call_target="tpu_custom_call" | custom-call | tf_op jit(solution)/shard_map/pallas_call | solution.py:63
  55.9 0.1 shard_map.143
  56.0 12.3 %all_to_all.28.pieces = f32[8,112,128]{2,1,0:T(8,128)S(1)} all-to-all(f32[8,112,128]{2,1,0:T(8,128)S(1)} %shard_map.143), channel_id=1, replica_groups=mesh['node'=8,'feat'=4] {'node'}, dimensions={0} | all-to-all | bytes 917504 | tf_op jit(solution)/shard_map/all_to_all | solution.py:303
  68.3 0.1 shard_map.144
  68.3 15.4 %all_to_all.29.pieces = f32[8,152,128]{2,1,0:T(8,128)S(1)} all-to-all(f32[8,152,128]{2,1,0:T(8,128)S(1)} %shard_map.144), channel_id=1, replica_groups=mesh['node'=8,'feat'=4] {'node'}, dimensions={0} | all-to-all | bytes 1245184 | tf_op jit(solution)/shard_map/all_to_all | solution.py:303
  83.7 0.8 shard_map.145
  (22 shorter events, 0.1 us)
Async XLA Ops:
  0.6 6.5 %collective-permute-start.2 = (bf16[32,512]{1,0:T(8,128)(2,1)}, bf16[32,512]{1,0:T(8,128)(2,1)S(1)}, u32[]{:S(2)}, u32[]{:S(2)}) collective-permute-start(bf16[32,512]{1,0:T(8,128)(2,1)} %bitcast.20), channel_id=1, source_target_pairs={{0,3},{1,2},{2,1},{3,0},{4,7},{5,6},{6,5},{7,4},{8,11},{9,10},{10,... | collective-permute-start | bytes 98312 | tf_op jit(solution)/shard_map/ppermute | solution.py:329
  3.1 4.2 %collective-permute-start.1 = (bf16[32,512]{1,0:T(8,128)(2,1)}, bf16[32,512]{1,0:T(8,128)(2,1)S(1)}, u32[]{:S(2)}, u32[]{:S(2)}) collective-permute-start(bf16[32,512]{1,0:T(8,128)(2,1)} %bitcast.21), channel_id=1, source_target_pairs={{0,2},{1,3},{2,0},{3,1},{4,6},{5,7},{6,4},{7,5},{8,10},{9,11},{10,... | collective-permute-start | bytes 98312 | tf_op jit(solution)/shard_map/ppermute | solution.py:329
  3.7 3.5 %collective-permute-start = (bf16[32,512]{1,0:T(8,128)(2,1)}, bf16[32,512]{1,0:T(8,128)(2,1)S(1)}, u32[]{:S(2)}, u32[]{:S(2)}) collective-permute-start(bf16[32,512]{1,0:T(8,128)(2,1)} %bitcast.22), channel_id=1, source_target_pairs={{0,1},{1,0},{2,3},{3,2},{4,5},{5,4},{6,7},{7,6},{8,9},{9,8},{10,11... | collective-permute-start | bytes 98312 | tf_op jit(solution)/shard_map/ppermute | solution.py:329
  3.8 0.7 copy-start.5
  4.4 2.6 %copy-start = (bf16[256,172]{0,1:T(8,128)(2,1)S(1)}, bf16[256,172]{0,1:T(8,128)(2,1)}, u32[]{:S(2)}) copy-start(bf16[256,172]{0,1:T(8,128)(2,1)} %param.18) | copy-start | bytes 264196
  4.4 2.6 %copy-start.1 = (bf16[256,172]{0,1:T(8,128)(2,1)S(1)}, bf16[256,172]{0,1:T(8,128)(2,1)}, u32[]{:S(2)}) copy-start(bf16[256,172]{0,1:T(8,128)(2,1)} %param.19) | copy-start | bytes 264196
  4.4 2.6 %copy-start.2 = (bf16[32,1024]{1,0:T(8,128)(2,1)S(1)}, bf16[32,1024]{1,0:T(8,128)(2,1)}, u32[]{:S(2)}) copy-start(bf16[32,1024]{1,0:T(8,128)(2,1)} %w_self1) | copy-start | bytes 196612
  4.4 2.6 %copy-start.3 = (bf16[32,1024]{1,0:T(8,128)(2,1)S(1)}, bf16[32,1024]{1,0:T(8,128)(2,1)}, u32[]{:S(2)}) copy-start(bf16[32,1024]{1,0:T(8,128)(2,1)} %w_neigh1) | copy-start | bytes 196612
  4.5 4.9 %copy-start.4 = (bf16[512,32]{0,1:T(8,128)(2,1)S(1)}, bf16[512,32]{0,1:T(8,128)(2,1)}, u32[]{:S(2)}) copy-start(bf16[512,32]{0,1:T(8,128)(2,1)} %param.10) | copy-start | bytes 98308
  4.5 4.9 %copy-start.6 = (s32[1,8,64]{2,1,0:T(8,128)S(1)}, s32[1,8,64]{2,1,0:T(8,128)}, u32[]{:S(2)}) copy-start(s32[1,8,64]{2,1,0:T(8,128)} %param.11) | copy-start | bytes 6148
  4.5 4.8 %copy-start.8 = (s32[1,8]{1,0:T(1,128)S(1)}, s32[1,8]{1,0:T(1,128)}, u32[]{:S(2)}) copy-start(s32[1,8]{1,0:T(1,128)} %count.1) | copy-start | bytes 100
  7.1 29.8 %copy-start.7 = (s32[512]{0:T(512)S(1)}, s32[512]{0:T(512)}, u32[]{:S(2)}) copy-start(s32[512]{0:T(512)} %param.15) | copy-start | bytes 6148
  7.3 17.9 %collective-permute-start.5 = (bf16[608,256]{1,0:T(8,128)(2,1)S(1)}, bf16[608,256]{1,0:T(8,128)(2,1)S(1)}, u32[]{:S(2)}, u32[]{:S(2)}) collective-permute-start(bf16[608,256]{1,0:T(8,128)(2,1)S(1)} %shard_map.138.refs_0_), channel_id=1, source_target_pairs={{0,3},{1,0},{2,1},{3,2},{4,7},{5,4},{6,5},{7,6},{8,11},{9,8},{10,9... | collective-permute-start | bytes 933896 | tf_op jit(solution)/shard_map/ppermute | solution.py:307
  8.7 16.5 %collective-permute-start.4 = (bf16[608,256]{1,0:T(8,128)(2,1)S(1)}, bf16[608,256]{1,0:T(8,128)(2,1)S(1)}, u32[]{:S(2)}, u32[]{:S(2)}) collective-permute-start(bf16[608,256]{1,0:T(8,128)(2,1)S(1)} %shard_map.138.refs_0_), channel_id=1, source_target_pairs={{0,2},{1,3},{2,0},{3,1},{4,6},{5,7},{6,4},{7,5},{8,10},{9,11},{10,... | collective-permute-start | bytes 933896 | tf_op jit(solution)/shard_map/ppermute | solution.py:307
  9.3 15.8 %collective-permute-start.3 = (bf16[608,256]{1,0:T(8,128)(2,1)S(1)}, bf16[608,256]{1,0:T(8,128)(2,1)S(1)}, u32[]{:S(2)}, u32[]{:S(2)}) collective-permute-start(bf16[608,256]{1,0:T(8,128)(2,1)S(1)} %shard_map.138.refs_0_), channel_id=1, source_target_pairs={{0,1},{1,2},{2,3},{3,0},{4,5},{5,6},{6,7},{7,4},{8,9},{9,10},{10,1... | collective-permute-start | bytes 933896 | tf_op jit(solution)/shard_map/ppermute | solution.py:307
  42.1 13.8 %collective-permute-start.6 = (f32[2,176,256]{2,1,0:T(8,128)S(1)}, f32[2,176,256]{2,1,0:T(8,128)S(1)}, u32[]{:S(2)}, u32[]{:S(2)}) collective-permute-start(f32[2,176,256]{2,1,0:T(8,128)S(1)} %get-tuple-element.67.second), channel_id=1, source_target_pairs={{0,4},{4,0},{8,12},{12,8},{16,20},{20,16},{24,28},{28,24},{1,5},{5... | collective-permute-start | bytes 1081352 | tf_op jit(solution)/shard_map/ppermute | solution.py:370
